TPU v7x, 32 devices: a whole 2x2x4 slice. The times are simulated.
32 devices in a mesh: lat: 4 (over z), lon: 8 (over y, x, core).
Axes of the slice: x: 2, y: 2, z: 4, core: 2. Of those that a mesh axis runs over, the one named last changes fastest.
Arguments:
- basis: bfloat16 [131072, 128], P(('lat', 'lon'))
- order: int32 [131072], P(('lat', 'lon')), may hold values from 0 to 4095, as said below
- land: int32 [128, 1024], P('lat', 'lon'), may hold values 0 or 1
- conduct: float32 [128, 1024], P('lat', 'lon'), may hold values from 0.6 to 1
Outputs:
- variance: float32 [128, 1024], P('lat', 'lon')
Inputs may be any that keep to these rules, and one draw needn't show every extreme that they name: `order`: each aligned block of 4096 entries starting at a multiple of 4096 holds every number from 0 to 4095 once.
All inputs are finite; a program needn't handle non-finite values. No bound on the sum of `land` on one device may be relied on, other than what follows from the above.
Results may differ from a plain program's by a relative error of at most 0.00053.
Values may be sent and summed in bfloat16 or wider, within the bound.
No kernel may reach another device: no remote copies, remote signals or barrier semaphores. Data moves between devices by JAX's collectives and lax.ppermute only.
A program may use at most 64 MiB of HBM per device.

v0:
```python
import jax
import jax.numpy as jnp
from jax import lax
from jax.sharding import PartitionSpec as P

SWEEPS = 10


def padded_2(cells, sides, width, closed):
    for axis, dim in sides:
        count = lax.axis_size(axis)
        ends = count if closed else count - 1
        head = lax.slice_in_dim(cells, 0, width, axis=dim)
        tail = lax.slice_in_dim(cells, cells.shape[dim] - width, cells.shape[dim], axis=dim)
        cells = jnp.concatenate(
            [
                lax.ppermute(tail, axis, [(i, (i + 1) % count) for i in range(ends)]),
                cells,
                lax.ppermute(head, axis, [((i + 1) % count, i) for i in range(ends)]),
            ],
            axis=dim,
        )
    return cells


def rotate_rows(rows_in, gram):
    lower = jnp.linalg.cholesky(gram)
    inverse = jax.scipy.linalg.solve_triangular(
        lower, jnp.eye(gram.shape[0], dtype=jnp.float32), lower=True
    )
    return jnp.dot(
        rows_in, inverse.T, precision=lax.Precision.HIGHEST, preferred_element_type=jnp.float32
    ).astype(jnp.bfloat16)


def update(padded, coeffs):
    centre = padded[1:-1, 1:-1]
    coef_here = coeffs[1:-1, 1:-1]
    total = centre
    nearby = (
        (padded[:-2, 1:-1], coeffs[:-2, 1:-1]),
        (padded[2:, 1:-1], coeffs[2:, 1:-1]),
        (padded[1:-1, :-2], coeffs[1:-1, :-2]),
        (padded[1:-1, 2:], coeffs[1:-1, 2:]),
    )
    for beside, coef_near in nearby:
        total = total + (0.124 * (coef_here + coef_near))[:, :, None] * (beside - centre)
    return total


def per_device(basis, order, land, conduct):
    rows_here, width = basis.shape
    tile_lat, tile_lon = land.shape
    cells = rows_here * lax.axis_size("lat") * lax.axis_size("lon")
    partial_gram = lax.dot_general(
        basis, basis, (((0,), (0,)), ((), ())), preferred_element_type=jnp.float32
    )
    gram = lax.psum(partial_gram, ("lat", "lon"))
    moving = rotate_rows(basis, gram)[order]
    arrived = lax.all_to_all(moving, ("lat", "lon"), split_axis=0, concat_axis=0, tiled=True)
    field = arrived.reshape(tile_lat, tile_lon, width).astype(jnp.float32)
    coefficient = conduct * (0.35 + 0.65 * land.astype(jnp.float32))
    coef_wide = padded_2(coefficient, (("lon", 1),), 2, True)
    coef_wide = padded_2(coef_wide, (("lat", 0),), 2, False)
    coef_near = coef_wide[1:-1, 1:-1]
    total_sq = jnp.zeros((tile_lat, tile_lon), jnp.float32)

    def one_sweep(index, state):
        plane, summed = state
        padded = padded_2(plane, (("lon", 1),), 1, True)
        padded = padded_2(padded, (("lat", 0),), 1, False)
        plane = update(padded, coef_near)
        return (plane, summed + jnp.sum(plane * plane, axis=-1))

    field, total_sq = lax.fori_loop(0, SWEEPS, one_sweep, (field, total_sq))
    return total_sq * (cells / (width * SWEEPS))


def solution(mesh):
    in_specs = (P(("lat", "lon"), None), P(("lat", "lon")), P("lat", "lon"), P("lat", "lon"))
    out_specs = P("lat", "lon")
    return jax.shard_map(
        per_device, mesh=mesh, in_specs=in_specs, out_specs=out_specs, check_vma=False
    )
```

profile of v0, /device:TPU:0, one launch (start us, length us, event | category | flops | bytes accessed | tf_op | source)
XLA Modules:
  0.0 403.5 jit_solution(5095322749766462267)
XLA Ops:
  8.9 124.3 %all-reduce.2.cloned.1.call-done = f32[128,128]{0,1:T(8,128)} async-done(((f32[128,128]{0,1:T(8,128)}), f32[128,128]{0,1:T(8,128)}) %all-reduce.2.cloned.1.call-update) | async-done | bytes 65552 | tf_op jit(solution)/shard_map/psum | solution.py:58
  135.0 11.7 %cholesky.17 = f32[128,128]{1,0:T(8,128)S(1)} custom-call(f32[128,128]{1,0:T(8,128)S(1)} %fusion.16), custom_call_target="Cholesky" | custom-call | tf_op jit(solution)/shard_map/jit(cholesky)/cholesky | solution.py:27
  148.1 9.8 %custom-call.7 = f32[1,128,128]{1,2,0:T(8,128)S(1)} custom-call(f32[1,128,128]{2,1,0:T(8,128)S(1)} %fusion.13), custom_call_target="InvertDiagBlocksLowerTriangular" | custom-call | tf_op jit(solution)/shard_map/jit(_solve_triangular)/triangular_solve | solution.py:28
  159.8 14.9 %gather_fusion = bf16[4096,128]{1,0:T(8,128)(2,1)} fusion(bf16[4096,128]{1,0:T(8,128)(2,1)S(1)} %copy.7, s32[4096]{0:T(1024)S(1)} %fusion.17), kind=kCustom, calls=%fused_computation | custom fusion | bytes 2113536 | tf_op jit(solution)/shard_map/gather | solution.py:59
  174.7 5.4 %all-to-all-start = ((bf16[32,128,128]{2,1,0:T(8,128)(2,1)}), bf16[32,128,128]{2,1,0:T(8,128)(2,1)S(1)}, u32[]{:S(2)}, u32[]{:S(2)}) async-start(bf16[32,128,128]{2,1,0:T(8,128)(2,1)} %bitcast.4), calls=%async_computation | async-start | bytes 2097152 | tf_op jit(solution)/shard_map/all_to_all | solution.py:60
  182.8 6.6 %collective-permute-done.4 = f32[32,2]{1,0:T(8,128)S(1)} collective-permute-done((f32[32,2]{1,0:T(8,128)S(1)}, f32[32,2]{1,0:T(8,128)S(1)}, u32[]{:S(2)}, u32[]{:S(2)}) %collective-permute-start.4) | collective-permute-done | bytes 288 | tf_op jit(solution)/shard_map/ppermute | solution.py:17
  192.8 5.1 %collective-permute-done.6 = f32[2,132]{1,0:T(2,128)S(1)} collective-permute-done((f32[2,132]{1,0:T(2,128)S(1)}, f32[2,132]{1,0:T(2,128)S(1)}, u32[]{:S(2)}, u32[]{:S(2)}) %collective-permute-start.6) | collective-permute-done | bytes 1088 | tf_op jit(solution)/shard_map/ppermute | solution.py:17
  198.6 7.8 %all-to-all-done = bf16[32,128,128]{2,1,0:T(8,128)(2,1)S(1)} async-done(((bf16[32,128,128]{2,1,0:T(8,128)(2,1)}), bf16[32,128,128]{2,1,0:T(8,128)(2,1)S(1)}, u32[]{:S(2)}, u32[]{:S(2)}) %all-to-all-start) | async-done | bytes 1048608 | tf_op jit(solution)/shard_map/all_to_all | solution.py:60
  207.9 188.1 %while.15 = (s32[]{:T(128)}, f32[32,128,128]{2,1,0:T(8,128)}, f32[32,128]{1,0:T(8,128)S(1)}, f32[32,128]{1,0:T(8,128)}, f32[32,128]{1,0:T(8,128)S(1)}, /*index=5...) while((s32[]{:T(128)}, f32[32,128,128]{2,1,0:T(8,128)}, f32[32,128]{1,0:T(8,128)S(1)}, ...), condition=%wide.region_5.6_spmd.clone, body=%wide.region_3.5_spmd.clone.sunk | while | flops 11621379 | bytes 11874595 | solution.py:75
  216.4 4.5 %collective-permute-start.3 = (f32[1,130,128]{2,1,0:T(8,128)S(1)}, f32[1,130,128]{2,1,0:T(8,128)S(1)}, u32[]{:S(2)}, u32[]{:S(2)}) collective-permute-start(f32[1,130,128]{2,1,0:T(8,128)S(1)} %get-tuple-element.186), channel_id=1, source_target_pairs={{0,8},{8,16},{16,24},{1,9},{9,17},{17,25},{2,10},{10,18},{18,26},{... | collective-permute-start | bytes 199688 | tf_op jit(solution)/shard_map/while/body/eval_jaxpr/ppermute | solution.py:17
  222.9 4.8 %multiply_reduce_fusion.2 = (f32[32,128]{1,0:T(8,128)S(1)}, f32[32,128,128]{2,1,0:T(8,128)}) fusion(f32[32,128,128]{2,1,0:T(8,128)S(1)} %copy.20, f32[32,1,128]{2,1,0:T(1,128)S(1)} %collective-permute-done, f32[32,128]{1,0:T(8,128)S(1)} %get-tuple-element.181, f32[32,1,128]{2,1,0:T(1,128)S(1)} %collective-permute-done.1, ...), kind=kLoop, calls=%fused_computation.21.clone.1 | loop fusion | flops 11530240 | bytes 4442112 | tf_op jit(solution)/shard_map/while/body/eval_jaxpr/reduce_sum | solution.py:73
  230.8 2.7 collective-permute-done.1
  234.8 4.9 %collective-permute-start.3 = (f32[1,130,128]{2,1,0:T(8,128)S(1)}, f32[1,130,128]{2,1,0:T(8,128)S(1)}, u32[]{:S(2)}, u32[]{:S(2)}) collective-permute-start(f32[1,130,128]{2,1,0:T(8,128)S(1)} %get-tuple-element.186), channel_id=1, source_target_pairs={{0,8},{8,16},{16,24},{1,9},{9,17},{17,25},{2,10},{10,18},{18,26},{... | collective-permute-start | bytes 199688 | tf_op jit(solution)/shard_map/while/body/eval_jaxpr/ppermute | solution.py:17
  241.6 4.8 %multiply_reduce_fusion.2 = (f32[32,128]{1,0:T(8,128)S(1)}, f32[32,128,128]{2,1,0:T(8,128)}) fusion(f32[32,128,128]{2,1,0:T(8,128)S(1)} %copy.20, f32[32,1,128]{2,1,0:T(1,128)S(1)} %collective-permute-done, f32[32,128]{1,0:T(8,128)S(1)} %get-tuple-element.181, f32[32,1,128]{2,1,0:T(1,128)S(1)} %collective-permute-done.1, ...), kind=kLoop, calls=%fused_computation.21.clone.1 | loop fusion | flops 11530240 | bytes 4442112 | tf_op jit(solution)/shard_map/while/body/eval_jaxpr/reduce_sum | solution.py:73
  249.5 2.7 collective-permute-done.1
  253.5 4.9 %collective-permute-start.3 = (f32[1,130,128]{2,1,0:T(8,128)S(1)}, f32[1,130,128]{2,1,0:T(8,128)S(1)}, u32[]{:S(2)}, u32[]{:S(2)}) collective-permute-start(f32[1,130,128]{2,1,0:T(8,128)S(1)} %get-tuple-element.186), channel_id=1, source_target_pairs={{0,8},{8,16},{16,24},{1,9},{9,17},{17,25},{2,10},{10,18},{18,26},{... | collective-permute-start | bytes 199688 | tf_op jit(solution)/shard_map/while/body/eval_jaxpr/ppermute | solution.py:17
  260.3 4.8 %multiply_reduce_fusion.2 = (f32[32,128]{1,0:T(8,128)S(1)}, f32[32,128,128]{2,1,0:T(8,128)}) fusion(f32[32,128,128]{2,1,0:T(8,128)S(1)} %copy.20, f32[32,1,128]{2,1,0:T(1,128)S(1)} %collective-permute-done, f32[32,128]{1,0:T(8,128)S(1)} %get-tuple-element.181, f32[32,1,128]{2,1,0:T(1,128)S(1)} %collective-permute-done.1, ...), kind=kLoop, calls=%fused_computation.21.clone.1 | loop fusion | flops 11530240 | bytes 4442112 | tf_op jit(solution)/shard_map/while/body/eval_jaxpr/reduce_sum | solution.py:73
  268.2 2.7 collective-permute-done.1
  272.2 4.9 %collective-permute-start.3 = (f32[1,130,128]{2,1,0:T(8,128)S(1)}, f32[1,130,128]{2,1,0:T(8,128)S(1)}, u32[]{:S(2)}, u32[]{:S(2)}) collective-permute-start(f32[1,130,128]{2,1,0:T(8,128)S(1)} %get-tuple-element.186), channel_id=1, source_target_pairs={{0,8},{8,16},{16,24},{1,9},{9,17},{17,25},{2,10},{10,18},{18,26},{... | collective-permute-start | bytes 199688 | tf_op jit(solution)/shard_map/while/body/eval_jaxpr/ppermute | solution.py:17
  279.0 4.8 %multiply_reduce_fusion.2 = (f32[32,128]{1,0:T(8,128)S(1)}, f32[32,128,128]{2,1,0:T(8,128)}) fusion(f32[32,128,128]{2,1,0:T(8,128)S(1)} %copy.20, f32[32,1,128]{2,1,0:T(1,128)S(1)} %collective-permute-done, f32[32,128]{1,0:T(8,128)S(1)} %get-tuple-element.181, f32[32,1,128]{2,1,0:T(1,128)S(1)} %collective-permute-done.1, ...), kind=kLoop, calls=%fused_computation.21.clone.1 | loop fusion | flops 11530240 | bytes 4442112 | tf_op jit(solution)/shard_map/while/body/eval_jaxpr/reduce_sum | solution.py:73
  290.9 4.9 %collective-permute-start.3 = (f32[1,130,128]{2,1,0:T(8,128)S(1)}, f32[1,130,128]{2,1,0:T(8,128)S(1)}, u32[]{:S(2)}, u32[]{:S(2)}) collective-permute-start(f32[1,130,128]{2,1,0:T(8,128)S(1)} %get-tuple-element.186), channel_id=1, source_target_pairs={{0,8},{8,16},{16,24},{1,9},{9,17},{17,25},{2,10},{10,18},{18,26},{... | collective-permute-start | bytes 199688 | tf_op jit(solution)/shard_map/while/body/eval_jaxpr/ppermute | solution.py:17
  297.8 4.8 %multiply_reduce_fusion.2 = (f32[32,128]{1,0:T(8,128)S(1)}, f32[32,128,128]{2,1,0:T(8,128)}) fusion(f32[32,128,128]{2,1,0:T(8,128)S(1)} %copy.20, f32[32,1,128]{2,1,0:T(1,128)S(1)} %collective-permute-done, f32[32,128]{1,0:T(8,128)S(1)} %get-tuple-element.181, f32[32,1,128]{2,1,0:T(1,128)S(1)} %collective-permute-done.1, ...), kind=kLoop, calls=%fused_computation.21.clone.1 | loop fusion | flops 11530240 | bytes 4442112 | tf_op jit(solution)/shard_map/while/body/eval_jaxpr/reduce_sum | solution.py:73
  309.6 4.9 %collective-permute-start.3 = (f32[1,130,128]{2,1,0:T(8,128)S(1)}, f32[1,130,128]{2,1,0:T(8,128)S(1)}, u32[]{:S(2)}, u32[]{:S(2)}) collective-permute-start(f32[1,130,128]{2,1,0:T(8,128)S(1)} %get-tuple-element.186), channel_id=1, source_target_pairs={{0,8},{8,16},{16,24},{1,9},{9,17},{17,25},{2,10},{10,18},{18,26},{... | collective-permute-start | bytes 199688 | tf_op jit(solution)/shard_map/while/body/eval_jaxpr/ppermute | solution.py:17
  316.5 4.8 %multiply_reduce_fusion.2 = (f32[32,128]{1,0:T(8,128)S(1)}, f32[32,128,128]{2,1,0:T(8,128)}) fusion(f32[32,128,128]{2,1,0:T(8,128)S(1)} %copy.20, f32[32,1,128]{2,1,0:T(1,128)S(1)} %collective-permute-done, f32[32,128]{1,0:T(8,128)S(1)} %get-tuple-element.181, f32[32,1,128]{2,1,0:T(1,128)S(1)} %collective-permute-done.1, ...), kind=kLoop, calls=%fused_computation.21.clone.1 | loop fusion | flops 11530240 | bytes 4442112 | tf_op jit(solution)/shard_map/while/body/eval_jaxpr/reduce_sum | solution.py:73
  328.3 4.9 %collective-permute-start.3 = (f32[1,130,128]{2,1,0:T(8,128)S(1)}, f32[1,130,128]{2,1,0:T(8,128)S(1)}, u32[]{:S(2)}, u32[]{:S(2)}) collective-permute-start(f32[1,130,128]{2,1,0:T(8,128)S(1)} %get-tuple-element.186), channel_id=1, source_target_pairs={{0,8},{8,16},{16,24},{1,9},{9,17},{17,25},{2,10},{10,18},{18,26},{... | collective-permute-start | bytes 199688 | tf_op jit(solution)/shard_map/while/body/eval_jaxpr/ppermute | solution.py:17
  335.2 4.8 %multiply_reduce_fusion.2 = (f32[32,128]{1,0:T(8,128)S(1)}, f32[32,128,128]{2,1,0:T(8,128)}) fusion(f32[32,128,128]{2,1,0:T(8,128)S(1)} %copy.20, f32[32,1,128]{2,1,0:T(1,128)S(1)} %collective-permute-done, f32[32,128]{1,0:T(8,128)S(1)} %get-tuple-element.181, f32[32,1,128]{2,1,0:T(1,128)S(1)} %collective-permute-done.1, ...), kind=kLoop, calls=%fused_computation.21.clone.1 | loop fusion | flops 11530240 | bytes 4442112 | tf_op jit(solution)/shard_map/while/body/eval_jaxpr/reduce_sum | solution.py:73
  347.1 4.9 %collective-permute-start.3 = (f32[1,130,128]{2,1,0:T(8,128)S(1)}, f32[1,130,128]{2,1,0:T(8,128)S(1)}, u32[]{:S(2)}, u32[]{:S(2)}) collective-permute-start(f32[1,130,128]{2,1,0:T(8,128)S(1)} %get-tuple-element.186), channel_id=1, source_target_pairs={{0,8},{8,16},{16,24},{1,9},{9,17},{17,25},{2,10},{10,18},{18,26},{... | collective-permute-start | bytes 199688 | tf_op jit(solution)/shard_map/while/body/eval_jaxpr/ppermute | solution.py:17
  353.9 4.8 %multiply_reduce_fusion.2 = (f32[32,128]{1,0:T(8,128)S(1)}, f32[32,128,128]{2,1,0:T(8,128)}) fusion(f32[32,128,128]{2,1,0:T(8,128)S(1)} %copy.20, f32[32,1,128]{2,1,0:T(1,128)S(1)} %collective-permute-done, f32[32,128]{1,0:T(8,128)S(1)} %get-tuple-element.181, f32[32,1,128]{2,1,0:T(1,128)S(1)} %collective-permute-done.1, ...), kind=kLoop, calls=%fused_computation.21.clone.1 | loop fusion | flops 11530240 | bytes 4442112 | tf_op jit(solution)/shard_map/while/body/eval_jaxpr/reduce_sum | solution.py:73
  365.8 4.9 %collective-permute-start.3 = (f32[1,130,128]{2,1,0:T(8,128)S(1)}, f32[1,130,128]{2,1,0:T(8,128)S(1)}, u32[]{:S(2)}, u32[]{:S(2)}) collective-permute-start(f32[1,130,128]{2,1,0:T(8,128)S(1)} %get-tuple-element.186), channel_id=1, source_target_pairs={{0,8},{8,16},{16,24},{1,9},{9,17},{17,25},{2,10},{10,18},{18,26},{... | collective-permute-start | bytes 199688 | tf_op jit(solution)/shard_map/while/body/eval_jaxpr/ppermute | solution.py:17
  372.6 4.8 %multiply_reduce_fusion.2 = (f32[32,128]{1,0:T(8,128)S(1)}, f32[32,128,128]{2,1,0:T(8,128)}) fusion(f32[32,128,128]{2,1,0:T(8,128)S(1)} %copy.20, f32[32,1,128]{2,1,0:T(1,128)S(1)} %collective-permute-done, f32[32,128]{1,0:T(8,128)S(1)} %get-tuple-element.181, f32[32,1,128]{2,1,0:T(1,128)S(1)} %collective-permute-done.1, ...), kind=kLoop, calls=%fused_computation.21.clone.1 | loop fusion | flops 11530240 | bytes 4442112 | tf_op jit(solution)/shard_map/while/body/eval_jaxpr/reduce_sum | solution.py:73
  384.5 4.9 %collective-permute-start.3 = (f32[1,130,128]{2,1,0:T(8,128)S(1)}, f32[1,130,128]{2,1,0:T(8,128)S(1)}, u32[]{:S(2)}, u32[]{:S(2)}) collective-permute-start(f32[1,130,128]{2,1,0:T(8,128)S(1)} %get-tuple-element.186), channel_id=1, source_target_pairs={{0,8},{8,16},{16,24},{1,9},{9,17},{17,25},{2,10},{10,18},{18,26},{... | collective-permute-start | bytes 199688 | tf_op jit(solution)/shard_map/while/body/eval_jaxpr/ppermute | solution.py:17
  391.3 4.8 %multiply_reduce_fusion.2 = (f32[32,128]{1,0:T(8,128)S(1)}, f32[32,128,128]{2,1,0:T(8,128)}) fusion(f32[32,128,128]{2,1,0:T(8,128)S(1)} %copy.20, f32[32,1,128]{2,1,0:T(1,128)S(1)} %collective-permute-done, f32[32,128]{1,0:T(8,128)S(1)} %get-tuple-element.181, f32[32,1,128]{2,1,0:T(1,128)S(1)} %collective-permute-done.1, ...), kind=kLoop, calls=%fused_computation.21.clone.1 | loop fusion | flops 11530240 | bytes 4442112 | tf_op jit(solution)/shard_map/while/body/eval_jaxpr/reduce_sum | solution.py:73
  (180 shorter events, 99.7 us)
Async XLA Ops:
  6.5 126.7 %all-reduce.2.cloned.1.call-start = ((), (), s32[]{:S(2)}) async-start(), calls=%async_computation.1 | async-start | bytes 131072 | tf_op jit(solution)/shard_map/psum | solution.py:58
  174.7 31.6 %all-to-all-start = ((bf16[32,128,128]{2,1,0:T(8,128)(2,1)}), bf16[32,128,128]{2,1,0:T(8,128)(2,1)S(1)}, u32[]{:S(2)}, u32[]{:S(2)}) async-start(bf16[32,128,128]{2,1,0:T(8,128)(2,1)} %bitcast.4), calls=%async_computation | async-start | bytes 2097152 | tf_op jit(solution)/shard_map/all_to_all | solution.py:60
  180.2 9.3 %collective-permute-start.4 = (f32[32,2]{1,0:T(8,128)S(1)}, f32[32,2]{1,0:T(8,128)S(1)}, u32[]{:S(2)}, u32[]{:S(2)}) collective-permute-start(f32[32,2]{1,0:T(8,128)S(1)} %get-tuple-element.125), channel_id=1, source_target_pairs={{0,1},{1,2},{2,3},{3,4},{4,5},{5,6},{6,7},{7,0},{8,9},{9,10},{10,1... | collective-permute-start | bytes 776 | tf_op jit(solution)/shard_map/ppermute | solution.py:17
  180.4 9.0 %collective-permute-start.5 = (f32[32,2]{1,0:T(8,128)S(1)}, f32[32,2]{1,0:T(8,128)S(1)}, u32[]{:S(2)}, u32[]{:S(2)}) collective-permute-start(f32[32,2]{1,0:T(8,128)S(1)} %get-tuple-element.126), channel_id=1, source_target_pairs={{1,0},{2,1},{3,2},{4,3},{5,4},{6,5},{7,6},{0,7},{9,8},{10,9},{11,1... | collective-permute-start | bytes 776 | tf_op jit(solution)/shard_map/ppermute | solution.py:19
  189.6 8.3 %collective-permute-start.6 = (f32[2,132]{1,0:T(2,128)S(1)}, f32[2,132]{1,0:T(2,128)S(1)}, u32[]{:S(2)}, u32[]{:S(2)}) collective-permute-start(f32[2,132]{1,0:T(2,128)S(1)} %get-tuple-element.122), channel_id=1, source_target_pairs={{0,8},{8,16},{16,24},{1,9},{9,17},{17,25},{2,10},{10,18},{18,26},{... | collective-permute-start | bytes 3176 | tf_op jit(solution)/shard_map/ppermute | solution.py:17
  191.5 6.4 %collective-permute-start.7 = (f32[2,132]{1,0:T(2,128)S(1)}, f32[2,132]{1,0:T(2,128)S(1)}, u32[]{:S(2)}, u32[]{:S(2)}) collective-permute-start(f32[2,132]{1,0:T(2,128)S(1)} %get-tuple-element.121), channel_id=1, source_target_pairs={{8,0},{16,8},{24,16},{9,1},{17,9},{25,17},{10,2},{18,10},{26,18},{... | collective-permute-start | bytes 3176 | tf_op jit(solution)/shard_map/ppermute | solution.py:19
  215.1 6.2 %collective-permute-start.2 = (f32[1,130,128]{2,1,0:T(8,128)S(1)}, f32[1,130,128]{2,1,0:T(8,128)S(1)}, u32[]{:S(2)}, u32[]{:S(2)}) collective-permute-start(f32[1,130,128]{2,1,0:T(8,128)S(1)} %get-tuple-element.184), channel_id=1, source_target_pairs={{8,0},{16,8},{24,16},{9,1},{17,9},{25,17},{10,2},{18,10},{26,18},{... | collective-permute-start | bytes 199688 | tf_op jit(solution)/shard_map/while/body/eval_jaxpr/ppermute | solution.py:19
  216.4 6.5 %collective-permute-start.3 = (f32[1,130,128]{2,1,0:T(8,128)S(1)}, f32[1,130,128]{2,1,0:T(8,128)S(1)}, u32[]{:S(2)}, u32[]{:S(2)}) collective-permute-start(f32[1,130,128]{2,1,0:T(8,128)S(1)} %get-tuple-element.186), channel_id=1, source_target_pairs={{0,8},{8,16},{16,24},{1,9},{9,17},{17,25},{2,10},{10,18},{18,26},{... | collective-permute-start | bytes 199688 | tf_op jit(solution)/shard_map/while/body/eval_jaxpr/ppermute | solution.py:17
  229.3 4.1 %collective-permute-start.1 = (f32[32,1,128]{2,1,0:T(1,128)S(1)}, f32[32,1,128]{2,1,0:T(1,128)S(1)}, u32[]{:S(2)}, u32[]{:S(2)}) collective-permute-start(f32[32,1,128]{2,1,0:T(1,128)S(1)} %get-tuple-element.182), channel_id=1, source_target_pairs={{0,1},{1,2},{2,3},{3,4},{4,5},{5,6},{6,7},{7,0},{8,9},{9,10},{10,1... | collective-permute-start | bytes 49160 | tf_op jit(solution)/shard_map/while/body/eval_jaxpr/ppermute | solution.py:17
  233.5 6.6 %collective-permute-start.2 = (f32[1,130,128]{2,1,0:T(8,128)S(1)}, f32[1,130,128]{2,1,0:T(8,128)S(1)}, u32[]{:S(2)}, u32[]{:S(2)}) collective-permute-start(f32[1,130,128]{2,1,0:T(8,128)S(1)} %get-tuple-element.184), channel_id=1, source_target_pairs={{8,0},{16,8},{24,16},{9,1},{17,9},{25,17},{10,2},{18,10},{26,18},{... | collective-permute-start | bytes 199688 | tf_op jit(solution)/shard_map/while/body/eval_jaxpr/ppermute | solution.py:19
  234.8 6.8 %collective-permute-start.3 = (f32[1,130,128]{2,1,0:T(8,128)S(1)}, f32[1,130,128]{2,1,0:T(8,128)S(1)}, u32[]{:S(2)}, u32[]{:S(2)}) collective-permute-start(f32[1,130,128]{2,1,0:T(8,128)S(1)} %get-tuple-element.186), channel_id=1, source_target_pairs={{0,8},{8,16},{16,24},{1,9},{9,17},{17,25},{2,10},{10,18},{18,26},{... | collective-permute-start | bytes 199688 | tf_op jit(solution)/shard_map/while/body/eval_jaxpr/ppermute | solution.py:17
  248.1 4.1 %collective-permute-start.1 = (f32[32,1,128]{2,1,0:T(1,128)S(1)}, f32[32,1,128]{2,1,0:T(1,128)S(1)}, u32[]{:S(2)}, u32[]{:S(2)}) collective-permute-start(f32[32,1,128]{2,1,0:T(1,128)S(1)} %get-tuple-element.182), channel_id=1, source_target_pairs={{0,1},{1,2},{2,3},{3,4},{4,5},{5,6},{6,7},{7,0},{8,9},{9,10},{10,1... | collective-permute-start | bytes 49160 | tf_op jit(solution)/shard_map/while/body/eval_jaxpr/ppermute | solution.py:17
  252.2 6.6 %collective-permute-start.2 = (f32[1,130,128]{2,1,0:T(8,128)S(1)}, f32[1,130,128]{2,1,0:T(8,128)S(1)}, u32[]{:S(2)}, u32[]{:S(2)}) collective-permute-start(f32[1,130,128]{2,1,0:T(8,128)S(1)} %get-tuple-element.184), channel_id=1, source_target_pairs={{8,0},{16,8},{24,16},{9,1},{17,9},{25,17},{10,2},{18,10},{26,18},{... | collective-permute-start | bytes 199688 | tf_op jit(solution)/shard_map/while/body/eval_jaxpr/ppermute | solution.py:19
  253.5 6.8 %collective-permute-start.3 = (f32[1,130,128]{2,1,0:T(8,128)S(1)}, f32[1,130,128]{2,1,0:T(8,128)S(1)}, u32[]{:S(2)}, u32[]{:S(2)}) collective-permute-start(f32[1,130,128]{2,1,0:T(8,128)S(1)} %get-tuple-element.186), channel_id=1, source_target_pairs={{0,8},{8,16},{16,24},{1,9},{9,17},{17,25},{2,10},{10,18},{18,26},{... | collective-permute-start | bytes 199688 | tf_op jit(solution)/shard_map/while/body/eval_jaxpr/ppermute | solution.py:17
  266.8 4.1 %collective-permute-start.1 = (f32[32,1,128]{2,1,0:T(1,128)S(1)}, f32[32,1,128]{2,1,0:T(1,128)S(1)}, u32[]{:S(2)}, u32[]{:S(2)}) collective-permute-start(f32[32,1,128]{2,1,0:T(1,128)S(1)} %get-tuple-element.182), channel_id=1, source_target_pairs={{0,1},{1,2},{2,3},{3,4},{4,5},{5,6},{6,7},{7,0},{8,9},{9,10},{10,1... | collective-permute-start | bytes 49160 | tf_op jit(solution)/shard_map/while/body/eval_jaxpr/ppermute | solution.py:17
  270.9 6.6 %collective-permute-start.2 = (f32[1,130,128]{2,1,0:T(8,128)S(1)}, f32[1,130,128]{2,1,0:T(8,128)S(1)}, u32[]{:S(2)}, u32[]{:S(2)}) collective-permute-start(f32[1,130,128]{2,1,0:T(8,128)S(1)} %get-tuple-element.184), channel_id=1, source_target_pairs={{8,0},{16,8},{24,16},{9,1},{17,9},{25,17},{10,2},{18,10},{26,18},{... | collective-permute-start | bytes 199688 | tf_op jit(solution)/shard_map/while/body/eval_jaxpr/ppermute | solution.py:19
  272.2 6.8 %collective-permute-start.3 = (f32[1,130,128]{2,1,0:T(8,128)S(1)}, f32[1,130,128]{2,1,0:T(8,128)S(1)}, u32[]{:S(2)}, u32[]{:S(2)}) collective-permute-start(f32[1,130,128]{2,1,0:T(8,128)S(1)} %get-tuple-element.186), channel_id=1, source_target_pairs={{0,8},{8,16},{16,24},{1,9},{9,17},{17,25},{2,10},{10,18},{18,26},{... | collective-permute-start | bytes 199688 | tf_op jit(solution)/shard_map/while/body/eval_jaxpr/ppermute | solution.py:17
  285.5 4.1 %collective-permute-start.1 = (f32[32,1,128]{2,1,0:T(1,128)S(1)}, f32[32,1,128]{2,1,0:T(1,128)S(1)}, u32[]{:S(2)}, u32[]{:S(2)}) collective-permute-start(f32[32,1,128]{2,1,0:T(1,128)S(1)} %get-tuple-element.182), channel_id=1, source_target_pairs={{0,1},{1,2},{2,3},{3,4},{4,5},{5,6},{6,7},{7,0},{8,9},{9,10},{10,1... | collective-permute-start | bytes 49160 | tf_op jit(solution)/shard_map/while/body/eval_jaxpr/ppermute | solution.py:17
  289.6 6.6 %collective-permute-start.2 = (f32[1,130,128]{2,1,0:T(8,128)S(1)}, f32[1,130,128]{2,1,0:T(8,128)S(1)}, u32[]{:S(2)}, u32[]{:S(2)}) collective-permute-start(f32[1,130,128]{2,1,0:T(8,128)S(1)} %get-tuple-element.184), channel_id=1, source_target_pairs={{8,0},{16,8},{24,16},{9,1},{17,9},{25,17},{10,2},{18,10},{26,18},{... | collective-permute-start | bytes 199688 | tf_op jit(solution)/shard_map/while/body/eval_jaxpr/ppermute | solution.py:19
  290.9 6.8 %collective-permute-start.3 = (f32[1,130,128]{2,1,0:T(8,128)S(1)}, f32[1,130,128]{2,1,0:T(8,128)S(1)}, u32[]{:S(2)}, u32[]{:S(2)}) collective-permute-start(f32[1,130,128]{2,1,0:T(8,128)S(1)} %get-tuple-element.186), channel_id=1, source_target_pairs={{0,8},{8,16},{16,24},{1,9},{9,17},{17,25},{2,10},{10,18},{18,26},{... | collective-permute-start | bytes 199688 | tf_op jit(solution)/shard_map/while/body/eval_jaxpr/ppermute | solution.py:17
  304.2 4.1 %collective-permute-start.1 = (f32[32,1,128]{2,1,0:T(1,128)S(1)}, f32[32,1,128]{2,1,0:T(1,128)S(1)}, u32[]{:S(2)}, u32[]{:S(2)}) collective-permute-start(f32[32,1,128]{2,1,0:T(1,128)S(1)} %get-tuple-element.182), channel_id=1, source_target_pairs={{0,1},{1,2},{2,3},{3,4},{4,5},{5,6},{6,7},{7,0},{8,9},{9,10},{10,1... | collective-permute-start | bytes 49160 | tf_op jit(solution)/shard_map/while/body/eval_jaxpr/ppermute | solution.py:17
  308.3 6.6 %collective-permute-start.2 = (f32[1,130,128]{2,1,0:T(8,128)S(1)}, f32[1,130,128]{2,1,0:T(8,128)S(1)}, u32[]{:S(2)}, u32[]{:S(2)}) collective-permute-start(f32[1,130,128]{2,1,0:T(8,128)S(1)} %get-tuple-element.184), channel_id=1, source_target_pairs={{8,0},{16,8},{24,16},{9,1},{17,9},{25,17},{10,2},{18,10},{26,18},{... | collective-permute-start | bytes 199688 | tf_op jit(solution)/shard_map/while/body/eval_jaxpr/ppermute | solution.py:19
  309.6 6.8 %collective-permute-start.3 = (f32[1,130,128]{2,1,0:T(8,128)S(1)}, f32[1,130,128]{2,1,0:T(8,128)S(1)}, u32[]{:S(2)}, u32[]{:S(2)}) collective-permute-start(f32[1,130,128]{2,1,0:T(8,128)S(1)} %get-tuple-element.186), channel_id=1, source_target_pairs={{0,8},{8,16},{16,24},{1,9},{9,17},{17,25},{2,10},{10,18},{18,26},{... | collective-permute-start | bytes 199688 | tf_op jit(solution)/shard_map/while/body/eval_jaxpr/ppermute | solution.py:17
  327.0 6.6 %collective-permute-start.2 = (f32[1,130,128]{2,1,0:T(8,128)S(1)}, f32[1,130,128]{2,1,0:T(8,128)S(1)}, u32[]{:S(2)}, u32[]{:S(2)}) collective-permute-start(f32[1,130,128]{2,1,0:T(8,128)S(1)} %get-tuple-element.184), channel_id=1, source_target_pairs={{8,0},{16,8},{24,16},{9,1},{17,9},{25,17},{10,2},{18,10},{26,18},{... | collective-permute-start | bytes 199688 | tf_op jit(solution)/shard_map/while/body/eval_jaxpr/ppermute | solution.py:19
  328.3 6.8 %collective-permute-start.3 = (f32[1,130,128]{2,1,0:T(8,128)S(1)}, f32[1,130,128]{2,1,0:T(8,128)S(1)}, u32[]{:S(2)}, u32[]{:S(2)}) collective-permute-start(f32[1,130,128]{2,1,0:T(8,128)S(1)} %get-tuple-element.186), channel_id=1, source_target_pairs={{0,8},{8,16},{16,24},{1,9},{9,17},{17,25},{2,10},{10,18},{18,26},{... | collective-permute-start | bytes 199688 | tf_op jit(solution)/shard_map/while/body/eval_jaxpr/ppermute | solution.py:17
  341.6 4.1 %collective-permute-start.1 = (f32[32,1,128]{2,1,0:T(1,128)S(1)}, f32[32,1,128]{2,1,0:T(1,128)S(1)}, u32[]{:S(2)}, u32[]{:S(2)}) collective-permute-start(f32[32,1,128]{2,1,0:T(1,128)S(1)} %get-tuple-element.182), channel_id=1, source_target_pairs={{0,1},{1,2},{2,3},{3,4},{4,5},{5,6},{6,7},{7,0},{8,9},{9,10},{10,1... | collective-permute-start | bytes 49160 | tf_op jit(solution)/shard_map/while/body/eval_jaxpr/ppermute | solution.py:17
  345.8 6.6 %collective-permute-start.2 = (f32[1,130,128]{2,1,0:T(8,128)S(1)}, f32[1,130,128]{2,1,0:T(8,128)S(1)}, u32[]{:S(2)}, u32[]{:S(2)}) collective-permute-start(f32[1,130,128]{2,1,0:T(8,128)S(1)} %get-tuple-element.184), channel_id=1, source_target_pairs={{8,0},{16,8},{24,16},{9,1},{17,9},{25,17},{10,2},{18,10},{26,18},{... | collective-permute-start | bytes 199688 | tf_op jit(solution)/shard_map/while/body/eval_jaxpr/ppermute | solution.py:19
  347.1 6.8 %collective-permute-start.3 = (f32[1,130,128]{2,1,0:T(8,128)S(1)}, f32[1,130,128]{2,1,0:T(8,128)S(1)}, u32[]{:S(2)}, u32[]{:S(2)}) collective-permute-start(f32[1,130,128]{2,1,0:T(8,128)S(1)} %get-tuple-element.186), channel_id=1, source_target_pairs={{0,8},{8,16},{16,24},{1,9},{9,17},{17,25},{2,10},{10,18},{18,26},{... | collective-permute-start | bytes 199688 | tf_op jit(solution)/shard_map/while/body/eval_jaxpr/ppermute | solution.py:17
  364.5 6.6 %collective-permute-start.2 = (f32[1,130,128]{2,1,0:T(8,128)S(1)}, f32[1,130,128]{2,1,0:T(8,128)S(1)}, u32[]{:S(2)}, u32[]{:S(2)}) collective-permute-start(f32[1,130,128]{2,1,0:T(8,128)S(1)} %get-tuple-element.184), channel_id=1, source_target_pairs={{8,0},{16,8},{24,16},{9,1},{17,9},{25,17},{10,2},{18,10},{26,18},{... | collective-permute-start | bytes 199688 | tf_op jit(solution)/shard_map/while/body/eval_jaxpr/ppermute | solution.py:19
  365.8 6.8 %collective-permute-start.3 = (f32[1,130,128]{2,1,0:T(8,128)S(1)}, f32[1,130,128]{2,1,0:T(8,128)S(1)}, u32[]{:S(2)}, u32[]{:S(2)}) collective-permute-start(f32[1,130,128]{2,1,0:T(8,128)S(1)} %get-tuple-element.186), channel_id=1, source_target_pairs={{0,8},{8,16},{16,24},{1,9},{9,17},{17,25},{2,10},{10,18},{18,26},{... | collective-permute-start | bytes 199688 | tf_op jit(solution)/shard_map/while/body/eval_jaxpr/ppermute | solution.py:17
  383.2 6.6 %collective-permute-start.2 = (f32[1,130,128]{2,1,0:T(8,128)S(1)}, f32[1,130,128]{2,1,0:T(8,128)S(1)}, u32[]{:S(2)}, u32[]{:S(2)}) collective-permute-start(f32[1,130,128]{2,1,0:T(8,128)S(1)} %get-tuple-element.184), channel_id=1, source_target_pairs={{8,0},{16,8},{24,16},{9,1},{17,9},{25,17},{10,2},{18,10},{26,18},{... | collective-permute-start | bytes 199688 | tf_op jit(solution)/shard_map/while/body/eval_jaxpr/ppermute | solution.py:19
  384.5 6.8 %collective-permute-start.3 = (f32[1,130,128]{2,1,0:T(8,128)S(1)}, f32[1,130,128]{2,1,0:T(8,128)S(1)}, u32[]{:S(2)}, u32[]{:S(2)}) collective-permute-start(f32[1,130,128]{2,1,0:T(8,128)S(1)} %get-tuple-element.186), channel_id=1, source_target_pairs={{0,8},{8,16},{16,24},{1,9},{9,17},{17,25},{2,10},{10,18},{18,26},{... | collective-permute-start | bytes 199688 | tf_op jit(solution)/shard_map/while/body/eval_jaxpr/ppermute | solution.py:17
  (28 other events, 152.6 us)
Sparse Core Ops, SparseCore 0:
  12.9 120.2 all-reduce.1
where the time goes:
time: 406 us; the launch traced here: 404 us
  waiting for transfers between devices  192 us (47%)
  other arithmetic  81.9 us (20%)
  starting transfers between devices  79.3 us (20%)
  local copies, waits for them, and re-layouts  34 us (8%)
  between operations  13.5 us (3%)
    psum x1, waiting for transfers between devices, per_device(): gram = lax.psum(partial_gram, ('lat', 'lon'))  124 us
    ppermute x22, starting transfers between devices, padded_2(): lax.ppermute(tail, axis, [(i, (i + 1) % count) for i in range(ends)])  55.3 us
    ppermute x22, waiting for transfers between devices, padded_2(): lax.ppermute(tail, axis, [(i, (i + 1) % count) for i in range(ends)])  54.2 us
    reduce_sum x10, other arithmetic, one_sweep(): return (plane, summed + jnp.sum(plane * plane, axis=-1))  47.5 us
    ppermute x22, starting transfers between devices, padded_2(): lax.ppermute(head, axis, [((i + 1) % count, i) for i in range(ends)])  18.6 us
    while x30, local copies, waits for them, and re-layouts  15.9 us
    gather x1, local copies, waits for them, and re-layouts, per_device(): moving = rotate_rows(basis, gram)[order]  14.9 us
    another operation x3, other arithmetic, rotate_rows(): lower = jnp.linalg.cholesky(gram)  12.4 us
  transfers between devices with their start and end apart: 46, of which 44 were waited for; matrix products, arithmetic and copies ran while one was open for 2% of the time, Pallas kernels for 0%

commit v1 on v0

v1 whole, which is shorter than its diff:
```python
import functools

import jax
import jax.numpy as jnp
from jax import lax
from jax.experimental import pallas as pl
from jax.experimental.pallas import tpu as pltpu
from jax.sharding import PartitionSpec as P

SWEEPS = 10
HALO = SWEEPS
LANES = 128
ONE_HOT = 1024
CHUNK = 256
GROUP = 16
STRIP = 64
SIDE = 3 * HALO
VMEM_BYTES = 56 * 1024 * 1024

bf16, f32, i32 = jnp.bfloat16, jnp.float32, jnp.int32


def iota(shape, dim):
    return lax.broadcasted_iota(i32, shape, dim)


def dot(a, b):
    return jnp.dot(a, b, preferred_element_type=f32)


def deal_kernel(basis_ref, order_ref, out_ref, turned):
    rows, width = basis_ref.shape
    parts = rows // ONE_HOT
    for q in range(parts):
        turned[q * width : (q + 1) * width, :] = basis_ref[
            q * ONE_HOT : (q + 1) * ONE_HOT, :
        ].T

    def step(c, carry):
        order = order_ref[pl.ds(c, 1), :]
        within = order % ONE_HOT
        part = order // ONE_HOT
        hot = (iota((ONE_HOT, CHUNK), 0) == within).astype(f32).astype(bf16)
        found = dot(turned[...], hot)
        picked = found[:width]
        for q in range(1, parts):
            picked = jnp.where(part == q, found[q * width : (q + 1) * width], picked)
        picked = picked.astype(bf16)
        for h in range(CHUNK // LANES):
            out_ref[c * (CHUNK // LANES) + h] = picked[:, h * LANES : (h + 1) * LANES]
        return carry

    lax.fori_loop(0, rows // CHUNK, step, 0)


def deal(basis, order):
    rows, width = basis.shape
    return pl.pallas_call(
        deal_kernel,
        out_shape=jax.ShapeDtypeStruct((rows // LANES, width, LANES), bf16),
        scratch_shapes=[pltpu.VMEM((rows // ONE_HOT * width, ONE_HOT), bf16)],
        compiler_params=pltpu.CompilerParams(vmem_limit_bytes=VMEM_BYTES),
        name="deal",
    )(basis, order.reshape(rows // CHUNK, CHUNK))


def rotate_kernel(rows_ref, inverse_ref, field_ref, edge_ref):
    tall, width, lanes = rows_ref.shape
    whole = inverse_ref[...]
    high = whole.astype(bf16)
    rest = whole - high.astype(f32)
    mid = rest.astype(bf16)
    low = (rest - mid.astype(f32)).astype(bf16)
    split = jnp.concatenate([high, mid, low], axis=0)
    for r in range(tall):
        parts = dot(split, rows_ref[r])
        turned = parts[:width] + (parts[width : 2 * width] + parts[2 * width :])
        field_ref[r] = turned.astype(bf16)
    groups = width // GROUP
    column = iota((lanes, 2 * LANES), 0)
    place = iota((lanes, 2 * LANES), 1)
    side, group, offset = place // LANES, (place % LANES) // GROUP, place % GROUP
    wanted = jnp.where(side == 0, offset, lanes - HALO + offset)
    keep = (offset < HALO) & (column == wanted)
    packed = jnp.zeros((tall * GROUP, 2 * LANES), f32)
    for g in range(groups):
        select = (keep & (group == g)).astype(f32).astype(bf16)
        piece = field_ref[:, g * GROUP : (g + 1) * GROUP, :].reshape(tall * GROUP, lanes)
        packed = packed + dot(piece, select)
    packed = packed.astype(bf16)
    edge_ref[0] = packed[:, :LANES].reshape(tall, GROUP, LANES)
    edge_ref[1] = packed[:, LANES:].reshape(tall, GROUP, LANES)


def rotate(rows, inverse):
    tall, width, lanes = rows.shape
    return pl.pallas_call(
        rotate_kernel,
        out_shape=(
            jax.ShapeDtypeStruct(rows.shape, bf16),
            jax.ShapeDtypeStruct((2, tall, GROUP, LANES), bf16),
        ),
        compiler_params=pltpu.CompilerParams(vmem_limit_bytes=VMEM_BYTES),
        name="rotate",
    )(rows, inverse)


def sweep_kernel(
    scale,
    ends_ref,
    north_ref,
    own_ref,
    south_ref,
    left_n_ref,
    left_ref,
    left_s_ref,
    right_n_ref,
    right_ref,
    right_s_ref,
    coef_ref,
    out_ref,
    u_ref,
    across_ref,
    down_ref,
    sum_ref,
):
    tall, width, lanes = own_ref.shape
    rows = tall + 2 * HALO
    main_groups = width // 8
    strip_groups = width // 2 // 8
    chunk = strip_groups
    half = width // 2

    for kind in range(2):
        coef = coef_ref[kind]
        across = 0.124 * (coef + pltpu.roll(coef, lanes - 1, 1))
        below = jnp.concatenate([coef[1:], coef[:1]], axis=0)
        down = 0.124 * (coef + below)
        across_ref[kind] = jnp.broadcast_to(across[:, None, :], (rows, 8, lanes))
        down_ref[kind] = jnp.broadcast_to(down[:, None, :], (rows, 8, lanes))
    sum_ref[...] = jnp.zeros_like(sum_ref)

    source = iota((2 * lanes, lanes), 0)
    place = iota((2 * lanes, lanes), 1)
    group, m = place // STRIP, place % STRIP
    from_half, column = source // lanes, source % lanes
    left_part = (m >= HALO) & (m < SIDE) & (column == m - HALO)
    right_part = (m >= SIDE) & (m < 2 * SIDE - HALO) & (column == m - SIDE + lanes - 2 * HALO)
    inner = ((group == from_half) & (left_part | right_part)).astype(f32).astype(bf16)
    halves = half // GROUP
    outers = []
    for gg in range(halves):
        slot = (group * halves + gg) * GROUP
        left_halo = (from_half == 0) & (m < HALO) & (column == slot + m)
        right_halo = (
            (from_half == 1)
            & (m >= 2 * SIDE - HALO)
            & (m < 2 * SIDE)
            & (column == slot + m - (2 * SIDE - HALO))
        )
        outers.append((left_halo | right_halo).astype(f32).astype(bf16))

    def fill(row, field, left, right):
        u_ref[row, :main_groups] = field.astype(f32).reshape(main_groups, 8, lanes)
        strip = dot(jnp.concatenate([field[:half], field[half:]], axis=1), inner)
        edge = jnp.concatenate([left, right], axis=1)
        outer = jnp.concatenate([dot(edge, o) for o in outers], axis=0)
        u_ref[row, main_groups:] = (strip + outer).reshape(strip_groups, 8, lanes)

    def fill_north(r, carry):
        fill(r, north_ref[r], left_n_ref[r], right_n_ref[r])
        fill(r + HALO + tall, south_ref[r], left_s_ref[r], right_s_ref[r])
        return carry

    def fill_own(r, carry):
        fill(r + HALO, own_ref[r], left_ref[r], right_ref[r])
        return carry

    lax.fori_loop(0, HALO, fill_north, 0)
    lax.fori_loop(0, tall, fill_own, 0)

    def sweep(s, carry):
        first = s + 1
        for c in range((main_groups + strip_groups) // chunk):
            kind = (c * chunk) // main_groups
            part = pl.ds(c * chunk, chunk)
            start = u_ref[first, part]
            above = down_ref[kind, first - 1] * (start - u_ref[first - 1, part])

            def one(row, here, above):
                below = u_ref[row + 1, part]
                under = down_ref[kind, row] * (below - here)
                east = pltpu.roll(here, lanes - 1, 2)
                flux = across_ref[kind, row] * (east - here)
                new = here + (under - above) + (flux - pltpu.roll(flux, 1, 2))
                u_ref[row, part] = new
                sum_ref[c, row] += jnp.sum(new * new, axis=0)
                return below, under

            def pair(p, state):
                row = first + 2 * p
                state = one(row, *state)
                return one(row + 1, *state)

            lax.fori_loop(0, (rows - 2 * first) // 2, pair, (start, above))

        @pl.when(ends_ref[0] == 1)
        def _():
            u_ref[HALO - 1] = jnp.zeros(u_ref.shape[1:], f32)

        @pl.when(ends_ref[1] == 1)
        def _():
            u_ref[HALO + tall] = jnp.zeros(u_ref.shape[1:], f32)

        return carry

    lax.fori_loop(0, SWEEPS, sweep, 0)

    inside = pl.ds(HALO, tall)
    middle = jnp.sum(sum_ref[0, inside] + sum_ref[1, inside], axis=1)
    strip = jnp.sum(sum_ref[2, inside], axis=1)
    strip = strip + pltpu.roll(strip, STRIP, 1)
    at = iota((tall, lanes), 1)
    left = pltpu.roll(strip, lanes - HALO, 1)
    right = pltpu.roll(strip, lanes - (2 * SIDE - HALO), 1)
    total = jnp.where(at < HALO, left, jnp.where(at >= lanes - HALO, right, middle))
    out_ref[...] = total * scale


def sweeps(scale, ends, fields, coef):
    own = fields[1]
    tall, width, lanes = own.shape
    rows = tall + 2 * HALO
    groups = (width + width // 2) // 8
    vmem = pl.BlockSpec(memory_space=pltpu.VMEM)
    return pl.pallas_call(
        functools.partial(sweep_kernel, scale),
        out_shape=jax.ShapeDtypeStruct((tall, lanes), f32),
        in_specs=[pl.BlockSpec(memory_space=pltpu.SMEM)] + [vmem] * (len(fields) + 1),
        out_specs=vmem,
        scratch_shapes=[
            pltpu.VMEM((rows, groups, 8, lanes), f32),
            pltpu.VMEM((2, rows, 8, lanes), f32),
            pltpu.VMEM((2, rows, 8, lanes), f32),
            pltpu.VMEM((3, rows, 8, lanes), f32),
        ],
        compiler_params=pltpu.CompilerParams(vmem_limit_bytes=VMEM_BYTES),
        name="sweeps",
    )(ends, *fields, coef)


def from_before(x, axis, closed):
    count = lax.axis_size(axis)
    return lax.ppermute(
        x, axis, [(i, (i + 1) % count) for i in range(count if closed else count - 1)]
    )


def from_after(x, axis, closed):
    count = lax.axis_size(axis)
    return lax.ppermute(
        x, axis, [((i + 1) % count, i) for i in range(count if closed else count - 1)]
    )


def summed(partial, axes, count):
    rows, width = partial.shape
    share = rows // count
    pieces = lax.all_to_all(partial, axes, split_axis=0, concat_axis=0, tiled=True)
    mine = jnp.sum(pieces.reshape(count, share, width), axis=0)
    copies = jnp.broadcast_to(mine[None], (count, share, width)).reshape(rows, width)
    return lax.all_to_all(copies, axes, split_axis=0, concat_axis=0, tiled=True)


def per_device(basis, order, land, conduct):
    axes = ("lat", "lon")
    rows_here, width = basis.shape
    tall, wide = land.shape
    count = lax.axis_size("lat") * lax.axis_size("lon")
    cells = rows_here * count
    share = rows_here // count

    partial = lax.dot_general(
        basis, basis, (((0,), (0,)), ((), ())), preferred_element_type=f32
    )
    gram = summed(partial, axes, count)

    dealt = deal(basis, order)
    split = LANES // share
    outgoing = dealt.reshape(-1, width, split, share).transpose(0, 2, 1, 3)
    outgoing = outgoing.reshape(count, width, share)
    arrived = lax.all_to_all(outgoing, axes, split_axis=0, concat_axis=0, tiled=True)
    raw = arrived.reshape(tall, wide // share, width, share).transpose(0, 2, 1, 3)
    raw = raw.reshape(tall, width, wide)

    lower = jnp.linalg.cholesky(gram)
    inverse = jax.scipy.linalg.solve_triangular(lower, jnp.eye(width, dtype=f32), lower=True)
    field, edges = rotate(raw, inverse)

    north = from_before(field[-HALO:], "lat", False)
    south = from_after(field[:HALO], "lat", False)
    left = from_before(edges[1], "lon", True)
    right = from_after(edges[0], "lon", True)
    left_n = from_before(left[-HALO:], "lat", False)
    left_s = from_after(left[:HALO], "lat", False)
    right_n = from_before(right[-HALO:], "lat", False)
    right_s = from_after(right[:HALO], "lat", False)

    coef = conduct * (0.35 + 0.65 * land.astype(f32))
    coef = jnp.concatenate(
        [from_before(coef[:, -HALO:], "lon", True), coef, from_after(coef[:, :HALO], "lon", True)],
        axis=1,
    )
    coef = jnp.concatenate(
        [from_before(coef[-HALO:], "lat", False), coef, from_after(coef[:HALO], "lat", False)],
        axis=0,
    )
    strip = jnp.concatenate([coef[:, :SIDE], coef[:, -SIDE:]], axis=1)
    strip = jnp.pad(strip, ((0, 0), (0, STRIP - 2 * SIDE)))
    coef = jnp.stack([coef[:, HALO:-HALO], jnp.concatenate([strip, strip], axis=1)])

    at = lax.axis_index("lat")
    ends = jnp.stack([at == 0, at == lax.axis_size("lat") - 1]).astype(i32)
    fields = (north, field, south, left_n, left, left_s, right_n, right, right_s)
    return sweeps(cells / (width * SWEEPS), ends, fields, coef)


def solution(mesh):
    in_specs = (P(("lat", "lon"), None), P(("lat", "lon")), P("lat", "lon"), P("lat", "lon"))
    out_specs = P("lat", "lon")
    return jax.shard_map(
        per_device, mesh=mesh, in_specs=in_specs, out_specs=out_specs, check_vma=False
    )
```

time: 406 us -> 230 us (0.57)
  waiting for transfers between devices: 192 us -> 22.7 us
  Pallas kernels: 0 us -> 122 us
  other arithmetic: 81.9 us -> 24.5 us
  starting transfers between devices: 79.3 us -> 50.2 us
  local copies, waits for them, and re-layouts: 34 us -> 6.06 us
  between operations: 13.5 us -> 0.32 us
    psum x1 -> x0, waiting for transfers between devices: 124 us -> none  [per_device(): gram = lax.psum(partial_gram, ('lat', 'lon'))]
    pallas_call x0 -> x3, Pallas kernels: none -> 122 us  [the longest x1 109 us: sweeps(): pl.pallas_call(functools.partial(sweep_kernel, scale), out_shape=jax.Shap...]
    reduce_sum x10 -> x1, other arithmetic: 47.5 us -> 0.04 us  [summed(): mine = jnp.sum(pieces.reshape(count, share, width), axis=0)]
    ppermute x44 -> x12, waiting for transfers between devices: 59.9 us -> 15.4 us  [the longest x6 11.3 us: from_after(): lax.ppermute(x, axis, [((i + 1) % count, i) for i in range(count if close...]
    ppermute x44 -> x12, starting transfers between devices: 73.9 us -> 34.4 us  [the longest x6 24.5 us: from_before(): lax.ppermute(x, axis, [(i, (i + 1) % count) for i in range(count if close...]
    while x30 -> x0, local copies, waits for them, and re-layouts: 15.9 us -> none
    gather x1 -> x0, local copies, waits for them, and re-layouts: 14.9 us -> none  [per_device(): moving = rotate_rows(basis, gram)[order]]
    all_to_all x1 -> x3, starting transfers between devices: 5.36 us -> 15.8 us  [the longest x1 7.29 us: summed(): lax.all_to_all(partial, axes, split_axis=0, concat_axis=0, tiled=True)]
  transfers between devices with their start and end apart: 46 -> 15, of which waited for: 44 -> 4; matrix products, arithmetic and copies ran while one was open for 2% -> 12% of each run, Pallas kernels for 0% -> 4%
where the time goes in v1:
time: 230 us; the launch traced here: 229 us
  Pallas kernels  122 us (53%)
  starting transfers between devices  50.2 us (22%)
  other arithmetic  24.5 us (11%)
  waiting for transfers between devices  22.7 us (10%)
  local copies, waits for them, and re-layouts  6.06 us (3%)
  matrix products  3.52 us (2%)
    pallas_call x1, Pallas kernels, sweeps(): pl.pallas_call(functools.partial(sweep_kernel, scale), out_shape=jax.Shap...  109 us
    ppermute x6, starting transfers between devices, from_before(): lax.ppermute(x, axis, [(i, (i + 1) % count) for i in range(count if close...  24.5 us
    another operation x3, other arithmetic, per_device(): lower = jnp.linalg.cholesky(gram)  12.4 us
    ppermute x6, waiting for transfers between devices, from_after(): lax.ppermute(x, axis, [((i + 1) % count, i) for i in range(count if close...  11.3 us
    another operation x2, other arithmetic, per_device(): jax.scipy.linalg.solve_triangular(lower, jnp.eye(width, dtype=f32), lower...  10.5 us
    ppermute x6, starting transfers between devices, from_after(): lax.ppermute(x, axis, [((i + 1) % count, i) for i in range(count if close...  9.89 us
    pallas_call x1, Pallas kernels, deal(): pl.pallas_call(deal_kernel, out_shape=jax.ShapeDtypeStruct((rows // LANES...  9.8 us
    all_to_all x1, waiting for transfers between devices, summed(): lax.all_to_all(partial, axes, split_axis=0, concat_axis=0, tiled=True)  7.37 us
  transfers between devices with their start and end apart: 15, of which 4 were waited for; matrix products, arithmetic and copies ran while one was open for 12% of the time, Pallas kernels for 4%

profile of v1, /device:TPU:0, one launch (start us, length us, event | category | flops | bytes accessed | tf_op | source)
XLA Modules:
  0.0 229.5 jit_solution(17796869839927044535)
XLA Ops:
  0.0 2.6 %fusion.10 = f32[128,128]{1,0:T(8,128)} fusion(bf16[4096,128]{1,0:T(8,128)(2,1)} %basis_ref.1), kind=kOutput, calls=%fused_computation.27 | convolution fusion | flops 134217728 | bytes 1114112 | tf_op jit(solution)/shard_map/dot_general | solution.py:283
  2.6 7.3 %all-to-all-start.1 = ((f32[32,4,128]{2,1,0:T(4,128)}), f32[32,4,128]{2,1,0:T(4,128)S(1)}, u32[]{:S(2)}, u32[]{:S(2)}) async-start(f32[32,4,128]{2,1,0:T(4,128)} %bitcast.2), calls=%async_computation.1 | async-start | bytes 131072 | tf_op jit(solution)/shard_map/all_to_all | solution.py:269
  10.0 7.4 %all-to-all-done.1 = f32[32,4,128]{2,1,0:T(4,128)S(1)} async-done(((f32[32,4,128]{2,1,0:T(4,128)}), f32[32,4,128]{2,1,0:T(4,128)S(1)}, u32[]{:S(2)}, u32[]{:S(2)}) %all-to-all-start.1) | async-done | bytes 65568 | tf_op jit(solution)/shard_map/all_to_all | solution.py:269
  17.4 0.6 broadcast_in_dim.3
  18.0 2.6 %all-to-all-start.2 = ((f32[32,4,128]{2,1,0:T(4,128)}), f32[32,4,128]{2,1,0:T(4,128)S(1)}, u32[]{:S(2)}, u32[]{:S(2)}) async-start(f32[32,4,128]{2,1,0:T(4,128)} %broadcast_in_dim.3), calls=%async_computation.2 | async-start | bytes 131072 | tf_op jit(solution)/shard_map/all_to_all | solution.py:272
  20.7 2.3 %collective-permute-start.9 = (f32[32,10]{1,0:T(8,128)S(1)}, f32[32,10]{1,0:T(8,128)S(1)}, u32[]{:S(2)}, u32[]{:S(2)}) collective-permute-start(f32[32,10]{1,0:T(8,128)S(1)} %get-tuple-element.22), channel_id=1, source_target_pairs={{1,0},{2,1},{3,2},{4,3},{5,4},{6,5},{7,6},{0,7},{9,8},{10,9},{11,1... | collective-permute-start | bytes 3848 | tf_op jit(solution)/shard_map/ppermute | solution.py:261
  23.6 9.8 %deal.1 = bf16[32,128,128]{2,1,0:T(8,128)(2,1)} custom-call(bf16[4096,128]{1,0:T(8,128)(2,1)} %basis_ref.1, s32[16,256]{1,0:T(8,128)} %reshape.22.order_ref), custom_call_target="tpu_custom_call" | custom-call | tf_op jit(solution)/shard_map/deal/pallas_call | solution.py:58
  33.4 5.9 %all-to-all-start = ((bf16[32,128,128]{2,1,0:T(8,128)(2,1)}), bf16[32,128,128]{2,1,0:T(8,128)(2,1)S(1)}, u32[]{:S(2)}, u32[]{:S(2)}) async-start(bf16[32,128,128]{2,1,0:T(8,128)(2,1)} %deal.1), calls=%async_computation | async-start | bytes 2097152 | tf_op jit(solution)/shard_map/all_to_all | solution.py:292
  39.5 1.3 collective-permute-start.11
  40.8 4.5 %collective-permute-start.10 = (f32[10,148]{1,0:T(8,128)S(1)}, f32[10,148]{1,0:T(8,128)S(1)}, u32[]{:S(2)}, u32[]{:S(2)}) collective-permute-start(f32[10,148]{1,0:T(8,128)S(1)} %get-tuple-element.19), channel_id=1, source_target_pairs={{0,8},{8,16},{16,24},{1,9},{9,17},{17,25},{2,10},{10,18},{18,26},{... | collective-permute-start | bytes 17768 | tf_op jit(solution)/shard_map/ppermute | solution.py:254
  45.9 7.4 %collective-permute-done.11 = f32[10,148]{1,0:T(8,128)S(1)} collective-permute-done((f32[10,148]{1,0:T(8,128)S(1)}, f32[10,148]{1,0:T(8,128)S(1)}, u32[]{:S(2)}, u32[]{:S(2)}) %collective-permute-start.11) | collective-permute-done | bytes 5952 | tf_op jit(solution)/shard_map/ppermute | solution.py:261
  53.3 4.0 %collective-permute-done.10 = f32[10,148]{1,0:T(8,128)S(1)} collective-permute-done((f32[10,148]{1,0:T(8,128)S(1)}, f32[10,148]{1,0:T(8,128)S(1)}, u32[]{:S(2)}, u32[]{:S(2)}) %collective-permute-start.10) | collective-permute-done | bytes 5952 | tf_op jit(solution)/shard_map/ppermute | solution.py:254
  57.8 11.7 %cholesky.17 = f32[128,128]{1,0:T(8,128)S(1)} custom-call(f32[128,128]{1,0:T(8,128)S(1)} %fusion.3), custom_call_target="Cholesky" | custom-call | tf_op jit(solution)/shard_map/jit(cholesky)/cholesky | solution.py:296
  69.6 0.6 compare_reduce_fusion
  70.2 0.7 fusion
  70.9 9.8 %custom-call.7 = f32[1,128,128]{1,2,0:T(8,128)S(1)} custom-call(f32[1,128,128]{2,1,0:T(8,128)S(1)} %fusion), custom_call_target="InvertDiagBlocksLowerTriangular" | custom-call | tf_op jit(solution)/shard_map/jit(_solve_triangular)/triangular_solve | solution.py:297
  80.7 0.9 fusion.1.inverse_ref
  81.6 1.0 copy-done
  82.5 3.4 %rotate.1 = (bf16[32,128,128]{2,1,0:T(8,128)(2,1)}, bf16[2,32,16,128]{3,2,1,0:T(8,128)(2,1)}) custom-call(bf16[32,128,128]{2,1,0:T(8,128)(2,1)} %copy-done, f32[128,128]{1,0:T(8,128)} %fusion.1.inverse_ref), custom_call_target="tpu_custom_call" | custom-call | tf_op jit(solution)/shard_map/rotate/pallas_call | solution.py:97
  86.0 1.0 slice_bitcast_fusion
  87.0 1.1 fusion.4
  88.2 11.1 %collective-permute-start = (bf16[10,128,128]{2,1,0:T(8,128)(2,1)S(1)}, bf16[10,128,128]{2,1,0:T(8,128)(2,1)S(1)}, u32[]{:S(2)}, u32[]{:S(2)}) collective-permute-start(bf16[10,128,128]{2,1,0:T(8,128)(2,1)S(1)} %get-tuple-element.10), channel_id=1, source_target_pairs={{0,8},{8,16},{16,24},{1,9},{9,17},{17,25},{2,10},{10,18},{18,26},{... | collective-permute-start | bytes 983048 | tf_op jit(solution)/shard_map/ppermute | solution.py:254
  99.2 1.3 collective-permute-start.1
  100.5 2.4 %collective-permute-start.5 = (bf16[32,16,128]{2,1,0:T(8,128)(2,1)S(1)}, bf16[32,16,128]{2,1,0:T(8,128)(2,1)S(1)}, u32[]{:S(2)}, u32[]{:S(2)}) collective-permute-start(bf16[32,16,128]{2,1,0:T(8,128)(2,1)S(1)} %get-tuple-element.11), channel_id=1, source_target_pairs={{1,0},{2,1},{3,2},{4,3},{5,4},{6,5},{7,6},{0,7},{9,8},{10,9},{11,1... | collective-permute-start | bytes 393224 | tf_op jit(solution)/shard_map/ppermute | solution.py:261
  103.0 4.3 %collective-permute-start.3 = (bf16[10,16,128]{2,1,0:T(8,128)(2,1)S(1)}, bf16[10,16,128]{2,1,0:T(8,128)(2,1)S(1)}, u32[]{:S(2)}, u32[]{:S(2)}) collective-permute-start(bf16[10,16,128]{2,1,0:T(8,128)(2,1)S(1)} %get-tuple-element.16), channel_id=1, source_target_pairs={{0,8},{8,16},{16,24},{1,9},{9,17},{17,25},{2,10},{10,18},{18,26},{... | collective-permute-start | bytes 122888 | tf_op jit(solution)/shard_map/ppermute | solution.py:254
  107.2 1.3 collective-permute-start.4
  108.6 4.5 %collective-permute-start.6 = (bf16[10,16,128]{2,1,0:T(8,128)(2,1)S(1)}, bf16[10,16,128]{2,1,0:T(8,128)(2,1)S(1)}, u32[]{:S(2)}, u32[]{:S(2)}) collective-permute-start(bf16[10,16,128]{2,1,0:T(8,128)(2,1)S(1)} %get-tuple-element.14), channel_id=1, source_target_pairs={{0,8},{8,16},{16,24},{1,9},{9,17},{17,25},{2,10},{10,18},{18,26},{... | collective-permute-start | bytes 122888 | tf_op jit(solution)/shard_map/ppermute | solution.py:254
  113.2 1.3 collective-permute-start.7
  114.5 0.6 pad_maximum_fusion.1.coef_ref
  115.1 3.9 %collective-permute-done.7.right_s_ref = bf16[10,16,128]{2,1,0:T(8,128)(2,1)S(1)} collective-permute-done((bf16[10,16,128]{2,1,0:T(8,128)(2,1)S(1)}, bf16[10,16,128]{2,1,0:T(8,128)(2,1)S(1)}, u32[]{:S(2)}, u32[]{:S(2)}) %collective-permute-start.7) | collective-permute-done | bytes 40992 | tf_op jit(solution)/shard_map/ppermute | solution.py:261
  119.8 0.7 copy-done.4
  120.5 108.9 %sweeps.1 = f32[32,128]{1,0:T(8,128)} custom-call(s32[2]{0:T(128)} %add_convert_fusion.ends_ref, bf16[10,128,128]{2,1,0:T(8,128)(2,1)} %copy-done.3, bf16[32,128,128]{2,1,0:T(8,128)(2,1)} %get-tuple-element.7.own_ref, bf16[10,128,128]{2,1,0:T(8,128)(2,1)} %copy-done.4, bf16[10,16,128]{2,1,0:T(8,128)(2,1)} %copy-done.5, bf16[32,16,128]{2,1,0:T(8,128)(2,1)} %copy-done.1, ...), custom_call_target="tpu_custom_call" | custom-call | tf_op jit(solution)/shard_map/sweeps/pallas_call | solution.py:236
  (51 shorter events, 2.8 us)
Async XLA Ops:
  2.6 7.3 %copy-start.9 = (f32[32,128]{1,0:T(8,128)S(1)}, f32[32,128]{1,0:T(8,128)}, u32[]{:S(2)}) copy-start(f32[32,128]{1,0:T(8,128)} %param.7) | copy-start | bytes 49156
  2.6 7.3 %copy-start.10 = (s32[32,128]{1,0:T(8,128)S(1)}, s32[32,128]{1,0:T(8,128)}, u32[]{:S(2)}) copy-start(s32[32,128]{1,0:T(8,128)} %param.6) | copy-start | bytes 49156
  2.6 14.7 %all-to-all-start.1 = ((f32[32,4,128]{2,1,0:T(4,128)}), f32[32,4,128]{2,1,0:T(4,128)S(1)}, u32[]{:S(2)}, u32[]{:S(2)}) async-start(f32[32,4,128]{2,1,0:T(4,128)} %bitcast.2), calls=%async_computation.1 | async-start | bytes 131072 | tf_op jit(solution)/shard_map/all_to_all | solution.py:269
  18.0 15.4 %all-to-all-start.2 = ((f32[32,4,128]{2,1,0:T(4,128)}), f32[32,4,128]{2,1,0:T(4,128)S(1)}, u32[]{:S(2)}, u32[]{:S(2)}) async-start(f32[32,4,128]{2,1,0:T(4,128)} %broadcast_in_dim.3), calls=%async_computation.2 | async-start | bytes 131072 | tf_op jit(solution)/shard_map/all_to_all | solution.py:272
  20.6 2.4 %copy-start.11 = (s32[4096]{0:T(1024)S(1)}, s32[4096]{0:T(1024)}, u32[]{:S(2)}) copy-start(s32[4096]{0:T(1024)} %param.5) | copy-start | bytes 49156
  20.7 18.7 %collective-permute-start.9 = (f32[32,10]{1,0:T(8,128)S(1)}, f32[32,10]{1,0:T(8,128)S(1)}, u32[]{:S(2)}, u32[]{:S(2)}) collective-permute-start(f32[32,10]{1,0:T(8,128)S(1)} %get-tuple-element.22), channel_id=1, source_target_pairs={{1,0},{2,1},{3,2},{4,3},{5,4},{6,5},{7,6},{0,7},{9,8},{10,9},{11,1... | collective-permute-start | bytes 3848 | tf_op jit(solution)/shard_map/ppermute | solution.py:261
  23.0 16.3 %collective-permute-start.8 = (f32[32,10]{1,0:T(8,128)S(1)}, f32[32,10]{1,0:T(8,128)S(1)}, u32[]{:S(2)}, u32[]{:S(2)}) collective-permute-start(f32[32,10]{1,0:T(8,128)S(1)} %get-tuple-element.21), channel_id=1, source_target_pairs={{0,1},{1,2},{2,3},{3,4},{4,5},{5,6},{6,7},{7,0},{8,9},{9,10},{10,1... | collective-permute-start | bytes 3848 | tf_op jit(solution)/shard_map/ppermute | solution.py:254
  33.4 48.1 %all-to-all-start = ((bf16[32,128,128]{2,1,0:T(8,128)(2,1)}), bf16[32,128,128]{2,1,0:T(8,128)(2,1)S(1)}, u32[]{:S(2)}, u32[]{:S(2)}) async-start(bf16[32,128,128]{2,1,0:T(8,128)(2,1)} %deal.1), calls=%async_computation | async-start | bytes 2097152 | tf_op jit(solution)/shard_map/all_to_all | solution.py:292
  39.5 13.9 %collective-permute-start.11 = (f32[10,148]{1,0:T(8,128)S(1)}, f32[10,148]{1,0:T(8,128)S(1)}, u32[]{:S(2)}, u32[]{:S(2)}) collective-permute-start(f32[10,148]{1,0:T(8,128)S(1)} %get-tuple-element.20), channel_id=1, source_target_pairs={{8,0},{16,8},{24,16},{9,1},{17,9},{25,17},{10,2},{18,10},{26,18},{... | collective-permute-start | bytes 17768 | tf_op jit(solution)/shard_map/ppermute | solution.py:261
  40.8 16.6 %collective-permute-start.10 = (f32[10,148]{1,0:T(8,128)S(1)}, f32[10,148]{1,0:T(8,128)S(1)}, u32[]{:S(2)}, u32[]{:S(2)}) collective-permute-start(f32[10,148]{1,0:T(8,128)S(1)} %get-tuple-element.19), channel_id=1, source_target_pairs={{0,8},{8,16},{16,24},{1,9},{9,17},{17,25},{2,10},{10,18},{18,26},{... | collective-permute-start | bytes 17768 | tf_op jit(solution)/shard_map/ppermute | solution.py:254
  81.5 1.0 copy-start
  87.0 16.0 %collective-permute-start.2 = (bf16[32,16,128]{2,1,0:T(8,128)(2,1)S(1)}, bf16[32,16,128]{2,1,0:T(8,128)(2,1)S(1)}, u32[]{:S(2)}, u32[]{:S(2)}) collective-permute-start(bf16[32,16,128]{2,1,0:T(8,128)(2,1)S(1)} %get-tuple-element.12), channel_id=1, source_target_pairs={{0,1},{1,2},{2,3},{3,4},{4,5},{5,6},{6,7},{7,0},{8,9},{9,10},{10,1... | collective-permute-start | bytes 393224 | tf_op jit(solution)/shard_map/ppermute | solution.py:254
  88.2 30.9 %collective-permute-start = (bf16[10,128,128]{2,1,0:T(8,128)(2,1)S(1)}, bf16[10,128,128]{2,1,0:T(8,128)(2,1)S(1)}, u32[]{:S(2)}, u32[]{:S(2)}) collective-permute-start(bf16[10,128,128]{2,1,0:T(8,128)(2,1)S(1)} %get-tuple-element.10), channel_id=1, source_target_pairs={{0,8},{8,16},{16,24},{1,9},{9,17},{17,25},{2,10},{10,18},{18,26},{... | collective-permute-start | bytes 983048 | tf_op jit(solution)/shard_map/ppermute | solution.py:254
  99.2 19.8 %collective-permute-start.1 = (bf16[10,128,128]{2,1,0:T(8,128)(2,1)S(1)}, bf16[10,128,128]{2,1,0:T(8,128)(2,1)S(1)}, u32[]{:S(2)}, u32[]{:S(2)}) collective-permute-start(bf16[10,128,128]{2,1,0:T(8,128)(2,1)S(1)} %get-tuple-element.9), channel_id=1, source_target_pairs={{8,0},{16,8},{24,16},{9,1},{17,9},{25,17},{10,2},{18,10},{26,18},{... | collective-permute-start | bytes 983048 | tf_op jit(solution)/shard_map/ppermute | solution.py:261
  100.5 8.0 %collective-permute-start.5 = (bf16[32,16,128]{2,1,0:T(8,128)(2,1)S(1)}, bf16[32,16,128]{2,1,0:T(8,128)(2,1)S(1)}, u32[]{:S(2)}, u32[]{:S(2)}) collective-permute-start(bf16[32,16,128]{2,1,0:T(8,128)(2,1)S(1)} %get-tuple-element.11), channel_id=1, source_target_pairs={{1,0},{2,1},{3,2},{4,3},{5,4},{6,5},{7,6},{0,7},{9,8},{10,9},{11,1... | collective-permute-start | bytes 393224 | tf_op jit(solution)/shard_map/ppermute | solution.py:261
  103.0 5.6 %copy-start.1 = (bf16[32,16,128]{2,1,0:T(8,128)(2,1)}, bf16[32,16,128]{2,1,0:T(8,128)(2,1)S(1)}, u32[]{:S(2)}) copy-start(bf16[32,16,128]{2,1,0:T(8,128)(2,1)S(1)} %collective-permute-done.2.left_ref) | copy-start | bytes 393220
  103.0 10.2 %collective-permute-start.3 = (bf16[10,16,128]{2,1,0:T(8,128)(2,1)S(1)}, bf16[10,16,128]{2,1,0:T(8,128)(2,1)S(1)}, u32[]{:S(2)}, u32[]{:S(2)}) collective-permute-start(bf16[10,16,128]{2,1,0:T(8,128)(2,1)S(1)} %get-tuple-element.16), channel_id=1, source_target_pairs={{0,8},{8,16},{16,24},{1,9},{9,17},{17,25},{2,10},{10,18},{18,26},{... | collective-permute-start | bytes 122888 | tf_op jit(solution)/shard_map/ppermute | solution.py:254
  107.2 7.9 %collective-permute-start.4 = (bf16[10,16,128]{2,1,0:T(8,128)(2,1)S(1)}, bf16[10,16,128]{2,1,0:T(8,128)(2,1)S(1)}, u32[]{:S(2)}, u32[]{:S(2)}) collective-permute-start(bf16[10,16,128]{2,1,0:T(8,128)(2,1)S(1)} %get-tuple-element.15), channel_id=1, source_target_pairs={{8,0},{16,8},{24,16},{9,1},{17,9},{25,17},{10,2},{18,10},{26,18},{... | collective-permute-start | bytes 122888 | tf_op jit(solution)/shard_map/ppermute | solution.py:261
  108.6 6.5 %copy-start.2 = (bf16[32,16,128]{2,1,0:T(8,128)(2,1)}, bf16[32,16,128]{2,1,0:T(8,128)(2,1)S(1)}, u32[]{:S(2)}) copy-start(bf16[32,16,128]{2,1,0:T(8,128)(2,1)S(1)} %collective-permute-done.5.right_ref) | copy-start | bytes 393220
  108.6 6.5 %collective-permute-start.6 = (bf16[10,16,128]{2,1,0:T(8,128)(2,1)S(1)}, bf16[10,16,128]{2,1,0:T(8,128)(2,1)S(1)}, u32[]{:S(2)}, u32[]{:S(2)}) collective-permute-start(bf16[10,16,128]{2,1,0:T(8,128)(2,1)S(1)} %get-tuple-element.14), channel_id=1, source_target_pairs={{0,8},{8,16},{16,24},{1,9},{9,17},{17,25},{2,10},{10,18},{18,26},{... | collective-permute-start | bytes 122888 | tf_op jit(solution)/shard_map/ppermute | solution.py:254
  113.2 1.9 copy-start.5
  113.2 5.9 %collective-permute-start.7 = (bf16[10,16,128]{2,1,0:T(8,128)(2,1)S(1)}, bf16[10,16,128]{2,1,0:T(8,128)(2,1)S(1)}, u32[]{:S(2)}, u32[]{:S(2)}) collective-permute-start(bf16[10,16,128]{2,1,0:T(8,128)(2,1)S(1)} %get-tuple-element.13), channel_id=1, source_target_pairs={{8,0},{16,8},{24,16},{9,1},{17,9},{25,17},{10,2},{18,10},{26,18},{... | collective-permute-start | bytes 122888 | tf_op jit(solution)/shard_map/ppermute | solution.py:261
  115.1 4.0 %copy-start.6 = (bf16[10,16,128]{2,1,0:T(8,128)(2,1)}, bf16[10,16,128]{2,1,0:T(8,128)(2,1)S(1)}, u32[]{:S(2)}) copy-start(bf16[10,16,128]{2,1,0:T(8,128)(2,1)S(1)} %collective-permute-done.4.left_s_ref) | copy-start | bytes 122884
  115.1 4.0 %copy-start.7 = (bf16[10,16,128]{2,1,0:T(8,128)(2,1)}, bf16[10,16,128]{2,1,0:T(8,128)(2,1)S(1)}, u32[]{:S(2)}) copy-start(bf16[10,16,128]{2,1,0:T(8,128)(2,1)S(1)} %collective-permute-done.6.right_n_ref) | copy-start | bytes 122884
  119.1 0.6 copy-start.8
  119.1 0.7 copy-start.3
  119.8 0.7 copy-start.4

commit v2 on v0

v2 whole, which is shorter than its diff:
```python
import functools

import jax
import jax.numpy as jnp
from jax import lax
from jax.experimental import pallas as pl
from jax.experimental.pallas import tpu as pltpu
from jax.sharding import PartitionSpec as P

SWEEPS = 10
HALO = SWEEPS
LANES = 128
SUB = 8
ONE_HOT = 1024
BLOCK = 4
VMEM_BYTES = 56 * 1024 * 1024

bf16, f32, i32 = jnp.bfloat16, jnp.float32, jnp.int32


def iota(shape, dim):
    return lax.broadcasted_iota(i32, shape, dim)


def dot(a, b):
    return jnp.dot(a, b, preferred_element_type=f32)


def split3(x):
    high = x.astype(bf16)
    rest = x - high.astype(f32)
    mid = rest.astype(bf16)
    low = (rest - mid.astype(f32)).astype(bf16)
    return high, mid, low


def slots(wide):
    return -(-(wide + 2 * HALO) // SUB) * SUB


def circle(own, right, left, axis):
    wide = own.shape[axis]
    count = slots(wide)
    gap = list(own.shape)
    gap[axis] = count - wide - 2 * HALO
    around = jnp.concatenate([own, right, jnp.zeros(gap, own.dtype), left], axis=axis)
    shape = around.shape
    around = around.reshape(shape[:axis] + (SUB, count // SUB) + shape[axis + 1 :])
    return jnp.swapaxes(around, axis, axis + 1).reshape(shape)


def deal_kernel(basis_ref, order_ref, out_ref, hot_ref):
    rows, width = basis_ref.shape
    parts = rows // ONE_HOT
    blocks = order_ref.shape[0]
    lane = iota((LANES, LANES), 1)

    def mark(c, carry):
        order = jnp.broadcast_to(order_ref[pl.ds(c, 1), :], (LANES, LANES)).T
        within = order % ONE_HOT
        for b in range(ONE_HOT // LANES):
            hot = (within == lane + b * LANES).astype(f32).astype(bf16)
            hot_ref[pl.ds(c * LANES, LANES), b * LANES : (b + 1) * LANES] = hot
        return carry

    lax.fori_loop(0, blocks, mark, 0)
    stacked = jnp.concatenate(
        [basis_ref[q * ONE_HOT : (q + 1) * ONE_HOT, :] for q in range(parts)], axis=1
    )
    per_step = 2

    def pick(c, carry):
        found = dot(hot_ref[pl.ds(c * per_step * LANES, per_step * LANES), :], stacked)
        for h in range(per_step):
            at = c * per_step + h
            part = jnp.broadcast_to(order_ref[pl.ds(at, 1), :], (LANES, LANES)).T // ONE_HOT
            here = found[h * LANES : (h + 1) * LANES]
            picked = here[:, :width]
            for q in range(1, parts):
                picked = jnp.where(part == q, here[:, q * width : (q + 1) * width], picked)
            out_ref[pl.ds(at * LANES, LANES), :] = picked.astype(bf16)
        return carry

    lax.fori_loop(0, blocks // per_step, pick, 0)


def deal(basis, order):
    rows, width = basis.shape
    total = order.size
    return pl.pallas_call(
        deal_kernel,
        out_shape=jax.ShapeDtypeStruct((total, width), bf16),
        scratch_shapes=[pltpu.VMEM((total, ONE_HOT), bf16)],
        compiler_params=pltpu.CompilerParams(vmem_limit_bytes=VMEM_BYTES),
        name="deal",
    )(basis, order.reshape(total // LANES, LANES))


def sweep_kernel(
    scale, ends_ref, north_ref, own_ref, south_ref, inverse_ref, coef_ref, out_ref,
    first_ref, second_ref, across_ref, down_ref, sum_ref,
):
    tall = own_ref.shape[0]
    rows, groups = first_ref.shape[:2]
    lanes = first_ref.shape[3]
    places = groups * SUB

    spread = second_ref
    turned = coef_ref[...].T
    depth = turned.shape[1]
    pieces = jnp.concatenate(split3(turned[:places]), axis=1)
    per_step = 4

    def put(c, carry):
        row = iota((3 * depth, per_step * lanes), 0) % depth
        wanted = c * per_step + iota((3 * depth, per_step * lanes), 1) // lanes
        values = dot(pieces, (row == wanted).astype(f32).astype(bf16))
        for h in range(per_step):
            spread[c * per_step + h] = values[:, h * lanes : (h + 1) * lanes].reshape(
                groups, SUB, lanes
            )
        return carry

    lax.fori_loop(0, rows // per_step, put, 0)

    def weigh(r, carry):
        for g in range(groups):
            here = spread[r, g]
            east = spread[r, g + 1] if g + 1 < groups else pltpu.roll(spread[r, 0], SUB - 1, 0)
            across_ref[r, g] = 0.124 * (here + east)
            down_ref[r, g] = 0.124 * (here + spread[r + 1, g])
        return carry

    lax.fori_loop(0, rows - 1, weigh, 0)
    sum_ref[...] = jnp.zeros_like(sum_ref)

    turn = jnp.concatenate(split3(inverse_ref[...].T), axis=1)

    def rotate(source, start, take, offset):
        raw = source[pl.ds(start, take)].astype(f32).reshape(take * places, lanes).astype(bf16)
        parts = dot(raw, turn)
        field = parts[:, :lanes] + (parts[:, lanes : 2 * lanes] + parts[:, 2 * lanes :])
        field = field.astype(bf16).astype(f32)
        first_ref[pl.ds(start + offset, take)] = field.reshape(take, groups, SUB, lanes)

    def rotate_own(c, carry):
        rotate(own_ref, c * 4, 4, HALO)
        return carry

    def rotate_halo(c, carry):
        rotate(north_ref, c * 2, 2, 0)
        rotate(south_ref, c * 2, 2, HALO + tall)
        return carry

    lax.fori_loop(0, tall // 4, rotate_own, 0)
    lax.fori_loop(0, HALO // 2, rotate_halo, 0)

    def update(src, dst, row, take, kept):
        last = groups - 1
        west = []
        closing = []
        for r in range(take):
            here = src[row + r, last]
            east = pltpu.roll(src[row + r, 0], SUB - 1, 0)
            flux = across_ref[row + r, last] * (east - here)
            closing.append(flux)
            west.append(pltpu.roll(flux, 1, 0))
        here = [src[row + r, 0] for r in range(take)]
        for g in range(groups):
            above = down_ref[row - 1, g] * (here[0] - src[row - 1, g])
            following = []
            for r in range(take):
                below = here[r + 1] if r + 1 < take else src[row + take, g]
                under = down_ref[row + r, g] * (below - here[r])
                if g < last:
                    east = src[row + r, g + 1]
                    following.append(east)
                    flux = across_ref[row + r, g] * (east - here[r])
                else:
                    flux = closing[r]
                new = here[r] + ((under - above) + (flux - west[r]))
                dst[row + r, g] = new
                if kept:
                    sum_ref[row + r - HALO, g] += new * new
                above = under
                west[r] = flux
            here = following

    def sweep(s, src, dst):
        def inside(c, carry):
            update(src, dst, HALO + c * BLOCK, BLOCK, True)
            return carry

        def outside(r, carry):
            update(src, dst, r, 1, False)
            update(src, dst, rows - 1 - r, 1, False)
            return carry

        lax.fori_loop(0, tall // BLOCK, inside, 0)
        lax.fori_loop(s + 1, HALO, outside, 0)

        @pl.when(ends_ref[0] == 1)
        def _():
            dst[HALO - 1] = jnp.zeros(dst.shape[1:], f32)

        @pl.when(ends_ref[1] == 1)
        def _():
            dst[HALO + tall] = jnp.zeros(dst.shape[1:], f32)

    def two(t, carry):
        sweep(2 * t, first_ref, second_ref)
        sweep(2 * t + 1, second_ref, first_ref)
        return carry

    lax.fori_loop(0, SWEEPS // 2, two, 0)

    lane = iota((SUB, lanes), 1)

    def gather(r, totals):
        kept = []
        for g in range(groups):
            total = jnp.sum(sum_ref[r, g], axis=1, keepdims=True)
            kept.append(jnp.where(lane == r, total, totals[g]))
        return tuple(kept)

    totals = lax.fori_loop(
        0, tall, gather, tuple(jnp.zeros((SUB, lanes), f32) for _ in range(groups))
    )
    totals = jnp.concatenate(totals, axis=0).T[:tall]
    slot = iota((places, out_ref.shape[1]), 0)
    column = iota((places, out_ref.shape[1]), 1)
    back = (column == (slot % SUB) * groups + slot // SUB).astype(f32).astype(bf16)
    high, mid, low = split3(totals)
    out_ref[...] = (dot(high, back) + (dot(mid, back) + dot(low, back))) * scale


def sweeps(scale, ends, fields, inverse, coef, wide):
    own = fields[1]
    tall, places, lanes = own.shape
    rows = tall + 2 * HALO
    coef = jnp.pad(coef, ((0, 64 - rows), (0, 2 * LANES - places)))
    vmem = pl.BlockSpec(memory_space=pltpu.VMEM)
    grid_rows = (rows, places // SUB, SUB, lanes)
    return pl.pallas_call(
        functools.partial(sweep_kernel, scale),
        out_shape=jax.ShapeDtypeStruct((tall, wide), f32),
        in_specs=[pl.BlockSpec(memory_space=pltpu.SMEM)] + [vmem] * (len(fields) + 2),
        out_specs=vmem,
        scratch_shapes=[
            pltpu.VMEM(grid_rows, f32),
            pltpu.VMEM(grid_rows, f32),
            pltpu.VMEM(grid_rows, f32),
            pltpu.VMEM(grid_rows, f32),
            pltpu.VMEM((tall,) + grid_rows[1:], f32),
        ],
        compiler_params=pltpu.CompilerParams(vmem_limit_bytes=VMEM_BYTES),
        name="sweeps",
    )(ends, *fields, inverse, coef)


def from_before(x, axis, closed):
    count = lax.axis_size(axis)
    return lax.ppermute(
        x, axis, [(i, (i + 1) % count) for i in range(count if closed else count - 1)]
    )


def from_after(x, axis, closed):
    count = lax.axis_size(axis)
    return lax.ppermute(
        x, axis, [((i + 1) % count, i) for i in range(count if closed else count - 1)]
    )


def summed(partial, axes, count):
    rows, width = partial.shape
    share = rows // count
    pieces = lax.all_to_all(partial, axes, split_axis=0, concat_axis=0, tiled=True)
    mine = jnp.sum(pieces.reshape(count, share, width), axis=0)
    copies = jnp.broadcast_to(mine[None], (count, share, width)).reshape(rows, width)
    return lax.all_to_all(copies, axes, split_axis=0, concat_axis=0, tiled=True)


def dealt_rows(basis, order, tall, wide, axes, count):
    width = basis.shape[1]
    share = order.size // count
    if share == wide:
        order = order.reshape(lax.axis_size("lat"), lax.axis_size("lon"), wide)
        right = jnp.roll(order, -1, axis=1)[:, :, :HALO]
        left = jnp.roll(order, 1, axis=1)[:, :, -HALO:]
        moving = deal(basis, circle(order, right, left, 2))
        arrived = lax.all_to_all(moving, axes, split_axis=0, concat_axis=0, tiled=True)
        return arrived.reshape(tall, slots(wide), width)
    arrived = lax.all_to_all(basis[order], axes, split_axis=0, concat_axis=0, tiled=True)
    own = arrived.reshape(tall, wide, width)
    left = from_before(own[:, -HALO:], "lon", True)
    right = from_after(own[:, :HALO], "lon", True)
    return circle(own, right, left, 1)


def per_device(basis, order, land, conduct):
    axes = ("lat", "lon")
    rows_here, width = basis.shape
    tall, wide = land.shape
    count = lax.axis_size("lat") * lax.axis_size("lon")
    cells = rows_here * count

    partial = lax.dot_general(
        basis, basis, (((0,), (0,)), ((), ())), preferred_element_type=f32
    )
    gram = summed(partial, axes, count)
    raw = dealt_rows(basis, order, tall, wide, axes, count)
    north = from_before(raw[-HALO:], "lat", False)
    south = from_after(raw[:HALO], "lat", False)

    lower = jnp.linalg.cholesky(gram)
    inverse = jax.scipy.linalg.solve_triangular(lower, jnp.eye(width, dtype=f32), lower=True)

    coef = conduct * (0.35 + 0.65 * land.astype(f32))
    coef = circle(
        coef,
        from_after(coef[:, :HALO], "lon", True),
        from_before(coef[:, -HALO:], "lon", True),
        1,
    )
    coef = jnp.concatenate(
        [from_before(coef[-HALO:], "lat", False), coef, from_after(coef[:HALO], "lat", False)],
        axis=0,
    )
    at = lax.axis_index("lat")
    ends = jnp.stack([at == 0, at == lax.axis_size("lat") - 1]).astype(i32)
    scale = cells / (width * SWEEPS)
    return sweeps(scale, ends, (north, raw, south), inverse, coef, wide)


def solution(mesh):
    in_specs = (P(("lat", "lon"), None), P(("lat", "lon")), P("lat", "lon"), P("lat", "lon"))
    out_specs = P("lat", "lon")
    return jax.shard_map(
        per_device, mesh=mesh, in_specs=in_specs, out_specs=out_specs, check_vma=False
    )
```

time: 406 us -> 131 us (0.32)
  waiting for transfers between devices: 192 us -> 21.4 us
  other arithmetic: 81.9 us -> 24.4 us
  starting transfers between devices: 79.3 us -> 34.4 us
  Pallas kernels: 0 us -> 42.4 us
  local copies, waits for them, and re-layouts: 34 us -> 4.42 us
  between operations: 13.5 us -> 0.22 us
    psum x1 -> x0, waiting for transfers between devices: 124 us -> none  [per_device(): gram = lax.psum(partial_gram, ('lat', 'lon'))]
    ppermute x44 -> x6, starting transfers between devices: 73.9 us -> 18.7 us  [the longest x3 13.7 us: from_before(): lax.ppermute(x, axis, [(i, (i + 1) % count) for i in range(count if close...]
    reduce_sum x10 -> x1, other arithmetic: 47.5 us -> 0.04 us  [summed(): mine = jnp.sum(pieces.reshape(count, share, width), axis=0)]
    ppermute x44 -> x6, waiting for transfers between devices: 59.9 us -> 14.2 us  [the longest x3 11.6 us: from_before(): lax.ppermute(x, axis, [(i, (i + 1) % count) for i in range(count if close...]
    pallas_call x0 -> x2, Pallas kernels: none -> 42.4 us  [the longest x1 25.8 us: sweeps(): pl.pallas_call(functools.partial(sweep_kernel, scale), out_shape=jax.Shap...]
    while x30 -> x0, local copies, waits for them, and re-layouts: 15.9 us -> none
    gather x1 -> x0, local copies, waits for them, and re-layouts: 14.9 us -> none  [per_device(): moving = rotate_rows(basis, gram)[order]]
    all_to_all x1 -> x3, starting transfers between devices: 5.36 us -> 15.7 us  [the longest x1 7.3 us: summed(): lax.all_to_all(partial, axes, split_axis=0, concat_axis=0, tiled=True)]
  transfers between devices with their start and end apart: 46 -> 9, of which waited for: 44 -> 4; matrix products, arithmetic and copies ran while one was open for 2% -> 21% of each run, Pallas kernels for 0% -> 13%
where the time goes in v2:
time: 131 us
  Pallas kernels  42.4 us (32%)
  starting transfers between devices  34.4 us (26%)
  other arithmetic  24.4 us (19%)
  waiting for transfers between devices  21.4 us (16%)
  local copies, waits for them, and re-layouts  4.42 us (3%)
  matrix products  3.53 us (3%)
    pallas_call x1, Pallas kernels, sweeps(): pl.pallas_call(functools.partial(sweep_kernel, scale), out_shape=jax.Shap...  25.8 us
    pallas_call x1, Pallas kernels, deal(): pl.pallas_call(deal_kernel, out_shape=jax.ShapeDtypeStruct((total, width)...  16.6 us
    ppermute x3, starting transfers between devices, from_before(): lax.ppermute(x, axis, [(i, (i + 1) % count) for i in range(count if close...  13.7 us
    another operation x3, other arithmetic, per_device(): lower = jnp.linalg.cholesky(gram)  12.4 us
    ppermute x3, waiting for transfers between devices, from_before(): lax.ppermute(x, axis, [(i, (i + 1) % count) for i in range(count if close...  11.6 us
    another operation x2, other arithmetic, per_device(): jax.scipy.linalg.solve_triangular(lower, jnp.eye(width, dtype=f32), lower...  10.5 us
    all_to_all x1, starting transfers between devices, summed(): lax.all_to_all(partial, axes, split_axis=0, concat_axis=0, tiled=True)  7.3 us
    all_to_all x1, waiting for transfers between devices, summed(): lax.all_to_all(partial, axes, split_axis=0, concat_axis=0, tiled=True)  7.21 us
  transfers between devices with their start and end apart: 9, of which 4 were waited for; matrix products, arithmetic and copies ran while one was open for 21% of the time, Pallas kernels for 13%

profile of v2, /device:TPU:0, one launch (start us, length us, event | category | flops | bytes accessed | tf_op | source)
XLA Modules:
  0.0 130.8 jit_solution(8526625229249593539)
XLA Ops:
  0.0 2.7 %fusion.9 = f32[128,128]{1,0:T(8,128)} fusion(bf16[4096,128]{1,0:T(8,128)(2,1)} %basis_ref.1), kind=kOutput, calls=%fused_computation.25 | convolution fusion | flops 134217728 | bytes 1114112 | tf_op jit(solution)/shard_map/dot_general | solution.py:308
  2.7 7.3 %all-to-all-start.1 = ((f32[32,4,128]{2,1,0:T(4,128)}), f32[32,4,128]{2,1,0:T(4,128)S(1)}, u32[]{:S(2)}, u32[]{:S(2)}) async-start(f32[32,4,128]{2,1,0:T(4,128)} %bitcast.5), calls=%async_computation.1 | async-start | bytes 131072 | tf_op jit(solution)/shard_map/all_to_all | solution.py:278
  10.2 7.2 %all-to-all-done.1 = f32[32,4,128]{2,1,0:T(4,128)S(1)} async-done(((f32[32,4,128]{2,1,0:T(4,128)}), f32[32,4,128]{2,1,0:T(4,128)S(1)}, u32[]{:S(2)}, u32[]{:S(2)}) %all-to-all-start.1) | async-done | bytes 65568 | tf_op jit(solution)/shard_map/all_to_all | solution.py:278
  17.4 0.6 broadcast_in_dim.15
  18.1 2.5 %all-to-all-start.2 = ((f32[32,4,128]{2,1,0:T(4,128)}), f32[32,4,128]{2,1,0:T(4,128)S(1)}, u32[]{:S(2)}, u32[]{:S(2)}) async-start(f32[32,4,128]{2,1,0:T(4,128)} %broadcast_in_dim.15), calls=%async_computation.2 | async-start | bytes 131072 | tf_op jit(solution)/shard_map/all_to_all | solution.py:281
  20.8 0.3 copy.7
  21.1 0.8 reshape_reshape.3.order_ref
  21.8 16.6 %deal.1 = bf16[4864,128]{1,0:T(8,128)(2,1)} custom-call(bf16[4096,128]{1,0:T(8,128)(2,1)} %basis_ref.1, s32[38,128]{1,0:T(8,128)} %reshape_reshape.3.order_ref), custom_call_target="tpu_custom_call" | custom-call | tf_op jit(solution)/shard_map/deal/pallas_call | solution.py:90
  38.5 5.8 %all-to-all-start = ((bf16[32,152,128]{2,1,0:T(8,128)(2,1)}), bf16[32,152,128]{2,1,0:T(8,128)(2,1)S(1)}, u32[]{:S(2)}, u32[]{:S(2)}) async-start(bf16[32,152,128]{2,1,0:T(8,128)(2,1)} %bitcast.20), calls=%async_computation | async-start | bytes 2490368 | tf_op jit(solution)/shard_map/all_to_all | solution.py:292
  44.4 2.4 %collective-permute-start.2 = (f32[32,10]{1,0:T(8,128)S(1)}, f32[32,10]{1,0:T(8,128)S(1)}, u32[]{:S(2)}, u32[]{:S(2)}) collective-permute-start(f32[32,10]{1,0:T(8,128)S(1)} %get-tuple-element.9), channel_id=1, source_target_pairs={{1,0},{2,1},{3,2},{4,3},{5,4},{6,5},{7,6},{0,7},{9,8},{10,9},{11,1... | collective-permute-start | bytes 3848 | tf_op jit(solution)/shard_map/ppermute | solution.py:270
  46.9 2.6 %collective-permute-done.2 = f32[32,10]{1,0:T(8,128)S(1)} collective-permute-done((f32[32,10]{1,0:T(8,128)S(1)}, f32[32,10]{1,0:T(8,128)S(1)}, u32[]{:S(2)}, u32[]{:S(2)}) %collective-permute-start.2) | collective-permute-done | bytes 1312 | tf_op jit(solution)/shard_map/ppermute | solution.py:270
  49.5 5.4 %collective-permute-done.3 = f32[32,10]{1,0:T(8,128)S(1)} collective-permute-done((f32[32,10]{1,0:T(8,128)S(1)}, f32[32,10]{1,0:T(8,128)S(1)}, u32[]{:S(2)}, u32[]{:S(2)}) %collective-permute-start.3) | collective-permute-done | bytes 1312 | tf_op jit(solution)/shard_map/ppermute | solution.py:263
  55.1 0.1 copy.9
  55.3 0.1 slice.73
  55.4 1.6 %collective-permute-start.4 = (f32[10,152]{1,0:T(8,128)S(1)}, f32[10,152]{1,0:T(8,128)S(1)}, u32[]{:S(2)}, u32[]{:S(2)}) collective-permute-start(f32[10,152]{1,0:T(8,128)S(1)} %slice.73), channel_id=1, source_target_pairs={{0,8},{8,16},{16,24},{1,9},{9,17},{17,25},{2,10},{10,18},{18,26},{... | collective-permute-start | bytes 18248 | tf_op jit(solution)/shard_map/ppermute | solution.py:263
  57.0 0.1 copy.11
  57.1 0.1 slice.75
  57.2 1.3 collective-permute-start.5
  58.5 0.7 add_convert_fusion.ends_ref
  59.2 0.1 copy.10
  59.4 6.2 %collective-permute-done.4 = f32[10,152]{1,0:T(8,128)S(1)} collective-permute-done((f32[10,152]{1,0:T(8,128)S(1)}, f32[10,152]{1,0:T(8,128)S(1)}, u32[]{:S(2)}, u32[]{:S(2)}) %collective-permute-start.4) | collective-permute-done | bytes 6112 | tf_op jit(solution)/shard_map/ppermute | solution.py:263
  65.6 0.6 select_maximum_fusion.coef_ref
  66.3 11.7 %cholesky.17 = f32[128,128]{1,0:T(8,128)S(1)} custom-call(f32[128,128]{1,0:T(8,128)S(1)} %fusion.3), custom_call_target="Cholesky" | custom-call | tf_op jit(solution)/shard_map/jit(cholesky)/cholesky | solution.py:316
  78.1 0.6 compare_reduce_fusion
  78.8 12.1 %collective-permute-start = (bf16[10,152,128]{2,1,0:T(8,128)(2,1)S(1)}, bf16[10,152,128]{2,1,0:T(8,128)(2,1)S(1)}, u32[]{:S(2)}, u32[]{:S(2)}) collective-permute-start(bf16[10,152,128]{2,1,0:T(8,128)(2,1)S(1)} %get-tuple-element.6), channel_id=1, source_target_pairs={{0,8},{8,16},{16,24},{1,9},{9,17},{17,25},{2,10},{10,18},{18,26},{... | collective-permute-start | bytes 1167368 | tf_op jit(solution)/shard_map/ppermute | solution.py:263
  90.9 1.3 collective-permute-start.1
  92.2 0.7 fusion
  92.8 9.8 %custom-call.7 = f32[1,128,128]{1,2,0:T(8,128)S(1)} custom-call(f32[1,128,128]{2,1,0:T(8,128)S(1)} %fusion), custom_call_target="InvertDiagBlocksLowerTriangular" | custom-call | tf_op jit(solution)/shard_map/jit(_solve_triangular)/triangular_solve | solution.py:317
  102.6 0.9 fusion.1.inverse_ref
  103.5 0.7 copy-done.1
  104.3 0.8 copy-done.2
  105.0 25.8 %sweeps.1 = f32[32,128]{1,0:T(8,128)} custom-call(s32[2]{0:T(128)} %add_convert_fusion.ends_ref, bf16[10,152,128]{2,1,0:T(8,128)(2,1)} %copy-done.1, bf16[32,152,128]{2,1,0:T(8,128)(2,1)} %copy-done, bf16[10,152,128]{2,1,0:T(8,128)(2,1)} %copy-done.2, f32[128,128]{1,0:T(8,128)} %fusion.1.inverse_ref, f32[64,256]{1,0:T(8,128)} %select_maximum_fusion.coef_ref), custom_call_target="tpu_custom_call" | custom-call | tf_op jit(solution)/shard_map/sweeps/pallas_call | solution.py:244
  (36 shorter events, 1.0 us)
Async XLA Ops:
  0.0 10.0 %copy-start.3 = (s32[4096]{0:T(1024)S(1)}, s32[4096]{0:T(1024)}, u32[]{:S(2)}) copy-start(s32[4096]{0:T(1024)} %param.5) | copy-start | bytes 49156
  2.7 14.7 %all-to-all-start.1 = ((f32[32,4,128]{2,1,0:T(4,128)}), f32[32,4,128]{2,1,0:T(4,128)S(1)}, u32[]{:S(2)}, u32[]{:S(2)}) async-start(f32[32,4,128]{2,1,0:T(4,128)} %bitcast.5), calls=%async_computation.1 | async-start | bytes 131072 | tf_op jit(solution)/shard_map/all_to_all | solution.py:278
  18.1 20.4 %all-to-all-start.2 = ((f32[32,4,128]{2,1,0:T(4,128)}), f32[32,4,128]{2,1,0:T(4,128)S(1)}, u32[]{:S(2)}, u32[]{:S(2)}) async-start(f32[32,4,128]{2,1,0:T(4,128)} %broadcast_in_dim.15), calls=%async_computation.2 | async-start | bytes 131072 | tf_op jit(solution)/shard_map/all_to_all | solution.py:281
  38.5 5.9 %copy-start.4 = (f32[32,128]{1,0:T(8,128)S(1)}, f32[32,128]{1,0:T(8,128)}, u32[]{:S(2)}) copy-start(f32[32,128]{1,0:T(8,128)} %param.7) | copy-start | bytes 49156
  38.5 5.9 %copy-start.5 = (s32[32,128]{1,0:T(8,128)S(1)}, s32[32,128]{1,0:T(8,128)}, u32[]{:S(2)}) copy-start(s32[32,128]{1,0:T(8,128)} %param.6) | copy-start | bytes 49156
  38.5 40.2 %all-to-all-start = ((bf16[32,152,128]{2,1,0:T(8,128)(2,1)}), bf16[32,152,128]{2,1,0:T(8,128)(2,1)S(1)}, u32[]{:S(2)}, u32[]{:S(2)}) async-start(bf16[32,152,128]{2,1,0:T(8,128)(2,1)} %bitcast.20), calls=%async_computation | async-start | bytes 2490368 | tf_op jit(solution)/shard_map/all_to_all | solution.py:292
  44.4 5.1 %collective-permute-start.2 = (f32[32,10]{1,0:T(8,128)S(1)}, f32[32,10]{1,0:T(8,128)S(1)}, u32[]{:S(2)}, u32[]{:S(2)}) collective-permute-start(f32[32,10]{1,0:T(8,128)S(1)} %get-tuple-element.9), channel_id=1, source_target_pairs={{1,0},{2,1},{3,2},{4,3},{5,4},{6,5},{7,6},{0,7},{9,8},{10,9},{11,1... | collective-permute-start | bytes 3848 | tf_op jit(solution)/shard_map/ppermute | solution.py:270
  46.8 8.1 %collective-permute-start.3 = (f32[32,10]{1,0:T(8,128)S(1)}, f32[32,10]{1,0:T(8,128)S(1)}, u32[]{:S(2)}, u32[]{:S(2)}) collective-permute-start(f32[32,10]{1,0:T(8,128)S(1)} %get-tuple-element.10), channel_id=1, source_target_pairs={{0,1},{1,2},{2,3},{3,4},{4,5},{5,6},{6,7},{7,0},{8,9},{9,10},{10,1... | collective-permute-start | bytes 3848 | tf_op jit(solution)/shard_map/ppermute | solution.py:263
  55.4 10.2 %collective-permute-start.4 = (f32[10,152]{1,0:T(8,128)S(1)}, f32[10,152]{1,0:T(8,128)S(1)}, u32[]{:S(2)}, u32[]{:S(2)}) collective-permute-start(f32[10,152]{1,0:T(8,128)S(1)} %slice.73), channel_id=1, source_target_pairs={{0,8},{8,16},{16,24},{1,9},{9,17},{17,25},{2,10},{10,18},{18,26},{... | collective-permute-start | bytes 18248 | tf_op jit(solution)/shard_map/ppermute | solution.py:263
  57.2 8.4 %collective-permute-start.5 = (f32[10,152]{1,0:T(8,128)S(1)}, f32[10,152]{1,0:T(8,128)S(1)}, u32[]{:S(2)}, u32[]{:S(2)}) collective-permute-start(f32[10,152]{1,0:T(8,128)S(1)} %slice.75), channel_id=1, source_target_pairs={{8,0},{16,8},{24,16},{9,1},{17,9},{25,17},{10,2},{18,10},{26,18},{... | collective-permute-start | bytes 18248 | tf_op jit(solution)/shard_map/ppermute | solution.py:270
  78.7 24.8 %copy-start = (bf16[32,152,128]{2,1,0:T(8,128)(2,1)}, bf16[32,152,128]{2,1,0:T(8,128)(2,1)S(1)}, u32[]{:S(2)}) copy-start(bf16[32,152,128]{2,1,0:T(8,128)(2,1)S(1)} %all-to-all-done.own_ref) | copy-start | bytes 3735556
  78.8 24.7 %collective-permute-start = (bf16[10,152,128]{2,1,0:T(8,128)(2,1)S(1)}, bf16[10,152,128]{2,1,0:T(8,128)(2,1)S(1)}, u32[]{:S(2)}, u32[]{:S(2)}) collective-permute-start(bf16[10,152,128]{2,1,0:T(8,128)(2,1)S(1)} %get-tuple-element.6), channel_id=1, source_target_pairs={{0,8},{8,16},{16,24},{1,9},{9,17},{17,25},{2,10},{10,18},{18,26},{... | collective-permute-start | bytes 1167368 | tf_op jit(solution)/shard_map/ppermute | solution.py:263
  90.9 12.7 %collective-permute-start.1 = (bf16[10,152,128]{2,1,0:T(8,128)(2,1)S(1)}, bf16[10,152,128]{2,1,0:T(8,128)(2,1)S(1)}, u32[]{:S(2)}, u32[]{:S(2)}) collective-permute-start(bf16[10,152,128]{2,1,0:T(8,128)(2,1)S(1)} %get-tuple-element.5), channel_id=1, source_target_pairs={{8,0},{16,8},{24,16},{9,1},{17,9},{25,17},{10,2},{18,10},{26,18},{... | collective-permute-start | bytes 1167368 | tf_op jit(solution)/shard_map/ppermute | solution.py:270
  103.5 0.7 copy-start.1
  104.3 0.8 copy-start.2

commit v3 on v2

--- a/solution.py
+++ b/solution.py
@@ -49,39 +49,48 @@
     return jnp.swapaxes(around, axis, axis + 1).reshape(shape)
 
 
-def deal_kernel(basis_ref, order_ref, out_ref, hot_ref):
+def deal_kernel(basis_ref, order_ref, out_ref):
     rows, width = basis_ref.shape
     parts = rows // ONE_HOT
     blocks = order_ref.shape[0]
     lane = iota((LANES, LANES), 1)
-
-    def mark(c, carry):
-        order = jnp.broadcast_to(order_ref[pl.ds(c, 1), :], (LANES, LANES)).T
-        within = order % ONE_HOT
-        for b in range(ONE_HOT // LANES):
-            hot = (within == lane + b * LANES).astype(f32).astype(bf16)
-            hot_ref[pl.ds(c * LANES, LANES), b * LANES : (b + 1) * LANES] = hot
-        return carry
-
-    lax.fori_loop(0, blocks, mark, 0)
     stacked = jnp.concatenate(
         [basis_ref[q * ONE_HOT : (q + 1) * ONE_HOT, :] for q in range(parts)], axis=1
     )
-    per_step = 2
-
-    def pick(c, carry):
-        found = dot(hot_ref[pl.ds(c * per_step * LANES, per_step * LANES), :], stacked)
-        for h in range(per_step):
-            at = c * per_step + h
-            part = jnp.broadcast_to(order_ref[pl.ds(at, 1), :], (LANES, LANES)).T // ONE_HOT
+
+    def pick(start, take):
+        marks, part = [], []
+        for h in range(take):
+            order = jnp.broadcast_to(order_ref[pl.ds(start + h, 1), :], (LANES, LANES)).T
+            within = order & (ONE_HOT - 1)
+            part.append(order - within)
+            marks.append(
+                jnp.concatenate(
+                    [
+                        (within == lane + b * LANES).astype(f32).astype(bf16)
+                        for b in range(ONE_HOT // LANES)
+                    ],
+                    axis=1,
+                )
+            )
+        found = dot(jnp.concatenate(marks, axis=0), stacked)
+        for h in range(take):
             here = found[h * LANES : (h + 1) * LANES]
             picked = here[:, :width]
             for q in range(1, parts):
-                picked = jnp.where(part == q, here[:, q * width : (q + 1) * width], picked)
-            out_ref[pl.ds(at * LANES, LANES), :] = picked.astype(bf16)
-        return carry
-
-    lax.fori_loop(0, blocks // per_step, pick, 0)
+                chosen = part[h] == q * ONE_HOT
+                picked = jnp.where(chosen, here[:, q * width : (q + 1) * width], picked)
+            out_ref[pl.ds((start + h) * LANES, LANES), :] = picked.astype(bf16)
+
+    take = 4
+
+    def step(c, carry):
+        pick(c * take, take)
+        return carry
+
+    lax.fori_loop(0, blocks // take, step, 0)
+    if blocks % take:
+        pick(blocks - blocks % take, blocks % take)
 
 
 def deal(basis, order):
@@ -90,10 +99,51 @@
     return pl.pallas_call(
         deal_kernel,
         out_shape=jax.ShapeDtypeStruct((total, width), bf16),
-        scratch_shapes=[pltpu.VMEM((total, ONE_HOT), bf16)],
         compiler_params=pltpu.CompilerParams(vmem_limit_bytes=VMEM_BYTES),
+        cost_estimate=pl.CostEstimate(
+            flops=2 * total * rows * width, bytes_accessed=4 * total * width, transcendentals=0
+        ),
         name="deal",
     )(basis, order.reshape(total // LANES, LANES))
+
+
+def inverse_kernel(gram_ref, out_ref):
+    size = gram_ref.shape[0]
+    tiles = [gram_ref[t * SUB : (t + 1) * SUB, :] for t in range(size // SUB)]
+    lane = iota((SUB, size), 1)
+    sub = iota((SUB, size), 0)
+    pivots = [jnp.zeros((SUB, size), f32) for _ in tiles]
+    for j in range(size):
+        top, at = j // SUB, j % SUB
+        is_lane = lane == j
+        row = jnp.broadcast_to(tiles[top][at : at + 1, :], (SUB, size))
+        columns = [
+            jnp.broadcast_to(tiles[t][:, j : j + 1], (SUB, size)) for t in range(top, len(tiles))
+        ]
+        pivot = jnp.broadcast_to(columns[0][at : at + 1, :], (SUB, size))
+        scaled = jnp.where(is_lane, 1.0, row) * (1.0 / pivot)
+        pivots[top] = jnp.where(sub == at, pivot, pivots[top])
+        for t in range(top, len(tiles)):
+            rest = jnp.where(is_lane, 0.0, tiles[t]) - columns[t - top] * scaled
+            if t == top:
+                rest = jnp.where(sub > at, rest, jnp.where(is_lane & (sub == at), 1.0, tiles[t]))
+            tiles[t] = rest
+    for t in range(len(tiles)):
+        kept = jnp.where(lane <= sub + t * SUB, tiles[t], 0.0)
+        out_ref[t * SUB : (t + 1) * SUB, :] = kept * (1.0 / jnp.sqrt(pivots[t]))
+
+
+def factor_inverse(gram):
+    size = gram.shape[0]
+    return pl.pallas_call(
+        inverse_kernel,
+        out_shape=jax.ShapeDtypeStruct(gram.shape, f32),
+        compiler_params=pltpu.CompilerParams(vmem_limit_bytes=VMEM_BYTES),
+        cost_estimate=pl.CostEstimate(
+            flops=4 * size**4, bytes_accessed=8 * size * size, transcendentals=0
+        ),
+        name="factor_inverse",
+    )(gram)
 
 
 def sweep_kernel(
@@ -272,15 +322,6 @@
     )
 
 
-def summed(partial, axes, count):
-    rows, width = partial.shape
-    share = rows // count
-    pieces = lax.all_to_all(partial, axes, split_axis=0, concat_axis=0, tiled=True)
-    mine = jnp.sum(pieces.reshape(count, share, width), axis=0)
-    copies = jnp.broadcast_to(mine[None], (count, share, width)).reshape(rows, width)
-    return lax.all_to_all(copies, axes, split_axis=0, concat_axis=0, tiled=True)
-
-
 def dealt_rows(basis, order, tall, wide, axes, count):
     width = basis.shape[1]
     share = order.size // count
@@ -289,13 +330,15 @@
         right = jnp.roll(order, -1, axis=1)[:, :, :HALO]
         left = jnp.roll(order, 1, axis=1)[:, :, -HALO:]
         moving = deal(basis, circle(order, right, left, 2))
-        arrived = lax.all_to_all(moving, axes, split_axis=0, concat_axis=0, tiled=True)
-        return arrived.reshape(tall, slots(wide), width)
-    arrived = lax.all_to_all(basis[order], axes, split_axis=0, concat_axis=0, tiled=True)
-    own = arrived.reshape(tall, wide, width)
-    left = from_before(own[:, -HALO:], "lon", True)
-    right = from_after(own[:, :HALO], "lon", True)
-    return circle(own, right, left, 1)
+        return moving, lambda arrived: arrived.reshape(tall, slots(wide), width)
+
+    def last_step(arrived):
+        own = arrived.reshape(tall, wide, width)
+        left = from_before(own[:, -HALO:], "lon", True)
+        right = from_after(own[:, :HALO], "lon", True)
+        return circle(own, right, left, 1)
+
+    return basis[order], last_step
 
 
 def per_device(basis, order, land, conduct):
@@ -304,29 +347,42 @@
     tall, wide = land.shape
     count = lax.axis_size("lat") * lax.axis_size("lon")
     cells = rows_here * count
+    share = width // count
+    tied = lax.optimization_barrier
+
+    def exchange(x):
+        return lax.all_to_all(x, axes, split_axis=0, concat_axis=0, tiled=True)
+
+    moving, last_step = dealt_rows(basis, order, tall, wide, axes, count)
+    moving, basis = tied((moving, basis))
+    raw = last_step(exchange(moving))
 
     partial = lax.dot_general(
         basis, basis, (((0,), (0,)), ((), ())), preferred_element_type=f32
     )
-    gram = summed(partial, axes, count)
-    raw = dealt_rows(basis, order, tall, wide, axes, count)
-    north = from_before(raw[-HALO:], "lat", False)
-    south = from_after(raw[:HALO], "lat", False)
-
-    lower = jnp.linalg.cholesky(gram)
-    inverse = jax.scipy.linalg.solve_triangular(lower, jnp.eye(width, dtype=f32), lower=True)
-
     coef = conduct * (0.35 + 0.65 * land.astype(f32))
+    partial, coef = tied((partial, coef))
+    pieces = exchange(partial)
     coef = circle(
         coef,
         from_after(coef[:, :HALO], "lon", True),
         from_before(coef[:, -HALO:], "lon", True),
         1,
     )
+    pieces, coef = tied((pieces, coef))
+    mine = jnp.sum(pieces.reshape(count, share, width), axis=0)
+    copies = jnp.broadcast_to(mine[None], (count, share, width)).reshape(width, width)
+    gram = exchange(copies)
     coef = jnp.concatenate(
         [from_before(coef[-HALO:], "lat", False), coef, from_after(coef[:HALO], "lat", False)],
         axis=0,
     )
+    gram, coef, raw = tied((gram, coef, raw))
+
+    north = from_before(raw[-HALO:], "lat", False)
+    south = from_after(raw[:HALO], "lat", False)
+    inverse = factor_inverse(gram)
+
     at = lax.axis_index("lat")
     ends = jnp.stack([at == 0, at == lax.axis_size("lat") - 1]).astype(i32)
     scale = cells / (width * SWEEPS)

time: 131 us -> 129 us (0.985)
  other arithmetic: 24.4 us -> 1.65 us
  Pallas kernels: 42.4 us -> 54.2 us
  starting transfers between devices: 34.4 us -> 22.8 us
  waiting for transfers between devices: 21.4 us -> 32.7 us
  blocking collectives: 0 us -> 9.78 us
  matrix products: 3.53 us -> 1.1 us
    another operation x5 -> x0, other arithmetic: 22.9 us -> none  [the longest x3 12.4 us: per_device(): lower = jnp.linalg.cholesky(gram)]
    pallas_call x0 -> x1, Pallas kernels: none -> 18.6 us  [factor_inverse(): pl.pallas_call(inverse_kernel, out_shape=jax.ShapeDtypeStruct(gram.shape,...]
    all_to_all x0 -> x1, blocking collectives: none -> 9.78 us  [exchange(): return lax.all_to_all(x, axes, split_axis=0, concat_axis=0, tiled=True)]
    all_to_all x3 -> x2, waiting for transfers between devices: 7.22 us -> 16.6 us  [exchange(): return lax.all_to_all(x, axes, split_axis=0, concat_axis=0, tiled=True)]
    all_to_all x3 -> x2, starting transfers between devices: 15.7 us -> 8.72 us  [exchange(): return lax.all_to_all(x, axes, split_axis=0, concat_axis=0, tiled=True)]
    pallas_call x1, Pallas kernels: 16.6 us -> 9.76 us  [deal(): pl.pallas_call(deal_kernel, out_shape=jax.ShapeDtypeStruct((total, width)...]
    ppermute x3, starting transfers between devices: 13.7 us -> 8.16 us  [from_before(): lax.ppermute(x, axis, [(i, (i + 1) % count) for i in range(count if close...]
    ppermute x3, waiting for transfers between devices: 11.6 us -> 16 us  [from_before(): lax.ppermute(x, axis, [(i, (i + 1) % count) for i in range(count if close...]
  transfers between devices with their start and end apart: 9 -> 8, of which waited for: 4 -> 3; matrix products, arithmetic and copies ran while one was open for 21% -> 1% of each run, Pallas kernels for 13% -> 15%
where the time goes in v3:
time: 129 us; the launch traced here: 128 us
  Pallas kernels  54.2 us (42%)
  waiting for transfers between devices  32.7 us (25%)
  starting transfers between devices  22.8 us (18%)
  blocking collectives  9.78 us (8%)
  local copies, waits for them, and re-layouts  5.46 us (4%)
  other arithmetic  1.65 us (1%)
    pallas_call x1, Pallas kernels, sweeps(): pl.pallas_call(functools.partial(sweep_kernel, scale), out_shape=jax.Shap...  25.8 us
    pallas_call x1, Pallas kernels, factor_inverse(): pl.pallas_call(inverse_kernel, out_shape=jax.ShapeDtypeStruct(gram.shape,...  18.6 us
    all_to_all x2, waiting for transfers between devices, exchange(): return lax.all_to_all(x, axes, split_axis=0, concat_axis=0, tiled=True)  16.6 us
    ppermute x3, waiting for transfers between devices, from_before(): lax.ppermute(x, axis, [(i, (i + 1) % count) for i in range(count if close...  16 us
    all_to_all x1, blocking collectives, exchange(): return lax.all_to_all(x, axes, split_axis=0, concat_axis=0, tiled=True)  9.78 us
    pallas_call x1, Pallas kernels, deal(): pl.pallas_call(deal_kernel, out_shape=jax.ShapeDtypeStruct((total, width)...  9.76 us
    all_to_all x2, starting transfers between devices, exchange(): return lax.all_to_all(x, axes, split_axis=0, concat_axis=0, tiled=True)  8.72 us
    ppermute x3, starting transfers between devices, from_before(): lax.ppermute(x, axis, [(i, (i + 1) % count) for i in range(count if close...  8.16 us
  transfers between devices with their start and end apart: 8, of which 3 were waited for; matrix products, arithmetic and copies ran while one was open for 1% of the time, Pallas kernels for 15%

profile of v3, /device:TPU:0, one launch (start us, length us, event | category | flops | bytes accessed | tf_op | source)
XLA Modules:
  0.0 127.8 jit_solution(13074377997574568486)
XLA Ops:
  0.0 0.8 fusion.4
  0.8 0.8 fusion.3
  1.6 0.1 pad.14.clone
  1.7 0.1 pad_add_fusion.1
  1.7 0.8 pad_add_fusion
  2.5 0.1 reshape.27
  2.6 0.3 copy.6
  2.9 0.8 reshape_reshape.3.order_ref
  3.7 9.8 %deal.1 = bf16[4864,128]{1,0:T(8,128)(2,1)} custom-call(bf16[4096,128]{1,0:T(8,128)(2,1)} %basis_ref.1, s32[38,128]{1,0:T(8,128)} %reshape_reshape.3.order_ref), custom_call_target="tpu_custom_call" | custom-call | flops 5100273664 | bytes 2490368 | tf_op jit(solution)/shard_map/deal/pallas_call | solution.py:99
  13.5 1.1 fusion.5
  14.6 0.1 fusion.2
  14.6 3.3 %collective-permute-start = (f32[32,10]{1,0:T(8,128)S(1)}, f32[32,10]{1,0:T(8,128)S(1)}, u32[]{:S(2)}, u32[]{:S(2)}) collective-permute-start(f32[32,10]{1,0:T(8,128)S(1)} %get-tuple-element.27), channel_id=1, source_target_pairs={{1,0},{2,1},{3,2},{4,3},{5,4},{6,5},{7,6},{0,7},{9,8},{10,9},{11,1... | collective-permute-start | bytes 3848 | tf_op jit(solution)/shard_map/ppermute | solution.py:320
  18.0 6.1 %all-to-all-start = ((f32[32,4,128]{2,1,0:T(4,128)}), f32[32,4,128]{2,1,0:T(4,128)S(1)}, u32[]{:S(2)}, u32[]{:S(2)}) async-start(f32[32,4,128]{2,1,0:T(4,128)} %bitcast.4), calls=%async_computation | async-start | bytes 131072 | tf_op jit(solution)/shard_map/all_to_all | solution.py:354
  24.1 0.1 pad.10.clone
  24.1 0.1 pad_maximum_fusion.1
  24.2 0.1 reshape.28
  24.3 0.1 copy.7
  24.5 7.0 %all-to-all-done = f32[32,4,128]{2,1,0:T(4,128)S(1)} async-done(((f32[32,4,128]{2,1,0:T(4,128)}), f32[32,4,128]{2,1,0:T(4,128)S(1)}, u32[]{:S(2)}, u32[]{:S(2)}) %all-to-all-start) | async-done | bytes 65568 | tf_op jit(solution)/shard_map/all_to_all | solution.py:354
  31.5 9.8 %all_to_all.30 = f32[32,4,128]{2,1,0:T(4,128)} all-to-all(f32[32,4,128]{2,1,0:T(4,128)S(1)} %broadcast_in_dim.14), channel_id=1, replica_groups=mesh['lat'=4,'lon'=8] {'lat','lon'}, dimensions={0} | all-to-all | bytes 131072 | tf_op jit(solution)/shard_map/all_to_all | solution.py:354
  41.3 2.7 %all-to-all-start.2 = ((bf16[32,152,128]{2,1,0:T(8,128)(2,1)}), bf16[32,152,128]{2,1,0:T(8,128)(2,1)S(1)}, u32[]{:S(2)}, u32[]{:S(2)}) async-start(bf16[32,152,128]{2,1,0:T(8,128)(2,1)} %bitcast.10), calls=%async_computation.2 | async-start | bytes 2490368 | tf_op jit(solution)/shard_map/all_to_all | solution.py:354
  44.0 3.6 %collective-permute-start.2 = (f32[10,152]{1,0:T(8,128)S(1)}, f32[10,152]{1,0:T(8,128)S(1)}, u32[]{:S(2)}, u32[]{:S(2)}) collective-permute-start(f32[10,152]{1,0:T(8,128)S(1)} %get-tuple-element.25), channel_id=1, source_target_pairs={{0,8},{8,16},{16,24},{1,9},{9,17},{17,25},{2,10},{10,18},{18,26},{... | collective-permute-start | bytes 18248 | tf_op jit(solution)/shard_map/ppermute | solution.py:313
  47.6 1.3 %collective-permute-start.3 = (f32[10,152]{1,0:T(8,128)S(1)}, f32[10,152]{1,0:T(8,128)S(1)}, u32[]{:S(2)}, u32[]{:S(2)}) collective-permute-start(f32[10,152]{1,0:T(8,128)S(1)} %get-tuple-element.26), channel_id=1, source_target_pairs={{8,0},{16,8},{24,16},{9,1},{17,9},{25,17},{10,2},{18,10},{26,18},{... | collective-permute-start | bytes 18248 | tf_op jit(solution)/shard_map/ppermute | solution.py:320
  48.9 16.0 %collective-permute-done.2 = f32[10,152]{1,0:T(8,128)S(1)} collective-permute-done((f32[10,152]{1,0:T(8,128)S(1)}, f32[10,152]{1,0:T(8,128)S(1)}, u32[]{:S(2)}, u32[]{:S(2)}) %collective-permute-start.2) | collective-permute-done | bytes 6112 | tf_op jit(solution)/shard_map/ppermute | solution.py:313
  65.0 9.6 %all-to-all-done.2.own_ref = bf16[32,152,128]{2,1,0:T(8,128)(2,1)S(1)} async-done(((bf16[32,152,128]{2,1,0:T(8,128)(2,1)}), bf16[32,152,128]{2,1,0:T(8,128)(2,1)S(1)}, u32[]{:S(2)}, u32[]{:S(2)}) %all-to-all-start.2) | async-done | bytes 1245216 | tf_op jit(solution)/shard_map/all_to_all | solution.py:354
  74.7 1.3 %collective-permute-start.5 = (bf16[10,152,128]{2,1,0:T(8,128)(2,1)S(1)}, bf16[10,152,128]{2,1,0:T(8,128)(2,1)S(1)}, u32[]{:S(2)}, u32[]{:S(2)}) collective-permute-start(bf16[10,152,128]{2,1,0:T(8,128)(2,1)S(1)} %get-tuple-element.23), channel_id=1, source_target_pairs={{8,0},{16,8},{24,16},{9,1},{17,9},{25,17},{10,2},{18,10},{26,18},{... | collective-permute-start | bytes 1167368 | tf_op jit(solution)/shard_map/ppermute | solution.py:320
  76.0 4.6 %collective-permute-start.4 = (bf16[10,152,128]{2,1,0:T(8,128)(2,1)S(1)}, bf16[10,152,128]{2,1,0:T(8,128)(2,1)S(1)}, u32[]{:S(2)}, u32[]{:S(2)}) collective-permute-start(bf16[10,152,128]{2,1,0:T(8,128)(2,1)S(1)} %get-tuple-element.24), channel_id=1, source_target_pairs={{0,8},{8,16},{16,24},{1,9},{9,17},{17,25},{2,10},{10,18},{18,26},{... | collective-permute-start | bytes 1167368 | tf_op jit(solution)/shard_map/ppermute | solution.py:313
  80.6 0.6 add_convert_fusion.ends_ref
  81.2 0.6 pad.4.coef_ref
  81.8 18.6 %factor_inverse.1.inverse_ref = f32[128,128]{1,0:T(8,128)} custom-call(f32[128,128]{1,0:T(8,128)} %bitcast.19), custom_call_target="tpu_custom_call" | custom-call | flops 1073741824 | bytes 131072 | tf_op jit(solution)/shard_map/factor_inverse/pallas_call | solution.py:138
  100.5 0.7 copy-done.2
  101.2 0.7 copy-done.3
  102.0 25.8 %sweeps.1 = f32[32,128]{1,0:T(8,128)} custom-call(s32[2]{0:T(128)} %add_convert_fusion.ends_ref, bf16[10,152,128]{2,1,0:T(8,128)(2,1)} %copy-done.3, bf16[32,152,128]{2,1,0:T(8,128)(2,1)} %copy-done, bf16[10,152,128]{2,1,0:T(8,128)(2,1)} %copy-done.2, f32[128,128]{1,0:T(8,128)} %factor_inverse.1.inverse_ref, f32[64,256]{1,0:T(8,128)} %pad.4.coef_ref), custom_call_target="tpu_custom_call" | custom-call | tf_op jit(solution)/shard_map/sweeps/pallas_call | solution.py:294
  (25 shorter events, 0.2 us)
Async XLA Ops:
  3.7 9.8 %copy-start.1 = (bf16[4096,128]{1,0:T(8,128)(2,1)S(1)}, bf16[4096,128]{1,0:T(8,128)(2,1)}, u32[]{:S(2)}) copy-start(bf16[4096,128]{1,0:T(8,128)(2,1)} %basis_ref.1) | copy-start | bytes 3145732
  13.5 1.1 copy-start.4
  13.5 1.1 copy-start.5
  14.6 9.5 %collective-permute-start = (f32[32,10]{1,0:T(8,128)S(1)}, f32[32,10]{1,0:T(8,128)S(1)}, u32[]{:S(2)}, u32[]{:S(2)}) collective-permute-start(f32[32,10]{1,0:T(8,128)S(1)} %get-tuple-element.27), channel_id=1, source_target_pairs={{1,0},{2,1},{3,2},{4,3},{5,4},{6,5},{7,6},{0,7},{9,8},{10,9},{11,1... | collective-permute-start | bytes 3848 | tf_op jit(solution)/shard_map/ppermute | solution.py:320
  18.0 6.2 %collective-permute-start.1 = (f32[32,10]{1,0:T(8,128)S(1)}, f32[32,10]{1,0:T(8,128)S(1)}, u32[]{:S(2)}, u32[]{:S(2)}) collective-permute-start(f32[32,10]{1,0:T(8,128)S(1)} %get-tuple-element.28), channel_id=1, source_target_pairs={{0,1},{1,2},{2,3},{3,4},{4,5},{5,6},{6,7},{7,0},{8,9},{9,10},{10,1... | collective-permute-start | bytes 3848 | tf_op jit(solution)/shard_map/ppermute | solution.py:313
  18.0 13.5 %all-to-all-start = ((f32[32,4,128]{2,1,0:T(4,128)}), f32[32,4,128]{2,1,0:T(4,128)S(1)}, u32[]{:S(2)}, u32[]{:S(2)}) async-start(f32[32,4,128]{2,1,0:T(4,128)} %bitcast.4), calls=%async_computation | async-start | bytes 131072 | tf_op jit(solution)/shard_map/all_to_all | solution.py:354
  41.3 33.3 %all-to-all-start.2 = ((bf16[32,152,128]{2,1,0:T(8,128)(2,1)}), bf16[32,152,128]{2,1,0:T(8,128)(2,1)S(1)}, u32[]{:S(2)}, u32[]{:S(2)}) async-start(bf16[32,152,128]{2,1,0:T(8,128)(2,1)} %bitcast.10), calls=%async_computation.2 | async-start | bytes 2490368 | tf_op jit(solution)/shard_map/all_to_all | solution.py:354
  44.0 20.9 %collective-permute-start.2 = (f32[10,152]{1,0:T(8,128)S(1)}, f32[10,152]{1,0:T(8,128)S(1)}, u32[]{:S(2)}, u32[]{:S(2)}) collective-permute-start(f32[10,152]{1,0:T(8,128)S(1)} %get-tuple-element.25), channel_id=1, source_target_pairs={{0,8},{8,16},{16,24},{1,9},{9,17},{17,25},{2,10},{10,18},{18,26},{... | collective-permute-start | bytes 18248 | tf_op jit(solution)/shard_map/ppermute | solution.py:313
  47.6 17.3 %collective-permute-start.3 = (f32[10,152]{1,0:T(8,128)S(1)}, f32[10,152]{1,0:T(8,128)S(1)}, u32[]{:S(2)}, u32[]{:S(2)}) collective-permute-start(f32[10,152]{1,0:T(8,128)S(1)} %get-tuple-element.26), channel_id=1, source_target_pairs={{8,0},{16,8},{24,16},{9,1},{17,9},{25,17},{10,2},{18,10},{26,18},{... | collective-permute-start | bytes 18248 | tf_op jit(solution)/shard_map/ppermute | solution.py:320
  74.6 25.9 %copy-start = (bf16[32,152,128]{2,1,0:T(8,128)(2,1)}, bf16[32,152,128]{2,1,0:T(8,128)(2,1)S(1)}, u32[]{:S(2)}) copy-start(bf16[32,152,128]{2,1,0:T(8,128)(2,1)S(1)} %all-to-all-done.2.own_ref) | copy-start | bytes 3735556
  74.7 25.8 %collective-permute-start.5 = (bf16[10,152,128]{2,1,0:T(8,128)(2,1)S(1)}, bf16[10,152,128]{2,1,0:T(8,128)(2,1)S(1)}, u32[]{:S(2)}, u32[]{:S(2)}) collective-permute-start(bf16[10,152,128]{2,1,0:T(8,128)(2,1)S(1)} %get-tuple-element.23), channel_id=1, source_target_pairs={{8,0},{16,8},{24,16},{9,1},{17,9},{25,17},{10,2},{18,10},{26,18},{... | collective-permute-start | bytes 1167368 | tf_op jit(solution)/shard_map/ppermute | solution.py:320
  76.0 24.5 %collective-permute-start.4 = (bf16[10,152,128]{2,1,0:T(8,128)(2,1)S(1)}, bf16[10,152,128]{2,1,0:T(8,128)(2,1)S(1)}, u32[]{:S(2)}, u32[]{:S(2)}) collective-permute-start(bf16[10,152,128]{2,1,0:T(8,128)(2,1)S(1)} %get-tuple-element.24), channel_id=1, source_target_pairs={{0,8},{8,16},{16,24},{1,9},{9,17},{17,25},{2,10},{10,18},{18,26},{... | collective-permute-start | bytes 1167368 | tf_op jit(solution)/shard_map/ppermute | solution.py:313
  100.5 0.8 copy-start.2
  101.2 0.7 copy-start.3

commit v4 on v3

v4 whole, which is shorter than its diff:
```python
import functools

import jax
import jax.numpy as jnp
from jax import lax
from jax.experimental import pallas as pl
from jax.experimental.pallas import tpu as pltpu
from jax.sharding import PartitionSpec as P

SWEEPS = 10
HALO = SWEEPS
LANES = 128
SUB = 8
ONE_HOT = 1024
BLOCK = 4
VMEM_BYTES = 56 * 1024 * 1024

bf16, f32, i32 = jnp.bfloat16, jnp.float32, jnp.int32


def iota(shape, dim):
    return lax.broadcasted_iota(i32, shape, dim)


def dot(a, b):
    return jnp.dot(a, b, preferred_element_type=f32)


def split3(x):
    high = x.astype(bf16)
    rest = x - high.astype(f32)
    mid = rest.astype(bf16)
    low = (rest - mid.astype(f32)).astype(bf16)
    return high, mid, low


def slots(wide):
    return -(-(wide + 2 * HALO) // SUB) * SUB


def circle(own, right, left, axis):
    wide = own.shape[axis]
    count = slots(wide)
    gap = list(own.shape)
    gap[axis] = count - wide - 2 * HALO
    around = jnp.concatenate([own, right, jnp.zeros(gap, own.dtype), left], axis=axis)
    shape = around.shape
    around = around.reshape(shape[:axis] + (SUB, count // SUB) + shape[axis + 1 :])
    return jnp.swapaxes(around, axis, axis + 1).reshape(shape)


def deal_kernel(tiles_lon, basis_ref, order_ref, out_ref, slot_ref):
    rows, width = basis_ref.shape
    parts = rows // ONE_HOT
    tiles, places, _ = out_ref.shape
    wide = order_ref.shape[1]
    groups = places // SUB
    lane = iota((LANES, LANES), 1)
    stacked = jnp.concatenate(
        [basis_ref[q * ONE_HOT : (q + 1) * ONE_HOT, :] for q in range(parts)], axis=1
    )

    order = order_ref[...]
    at = iota(order.shape, 0) % tiles_lon
    after = jnp.where(
        at == tiles_lon - 1, pltpu.roll(order, tiles_lon - 1, 0), pltpu.roll(order, tiles - 1, 0)
    )
    before = jnp.where(
        at == 0, pltpu.roll(order, tiles - tiles_lon + 1, 0), pltpu.roll(order, 1, 0)
    )
    padded = slot_ref.shape[1]
    column = iota((wide, padded), 0)
    slot = iota((wide, padded), 1)
    place = jnp.where(slot < places, (slot % SUB) * groups + slot // SUB, -1)
    low = jnp.zeros((tiles, padded), f32)
    high = low
    for source, hit in (
        (order, (place < wide) & (column == place)),
        (after, (place < wide + HALO) & (column == place - wide)),
        (before, (place >= places - HALO) & (column == place - places + wide)),
    ):
        hot = hit.astype(f32).astype(bf16)
        low = low + dot((source & 63).astype(f32).astype(bf16), hot)
        high = high + dot((source >> 6).astype(f32).astype(bf16), hot)
    slot_ref[...] = (high * 64.0 + low).astype(i32)

    take = 4

    def step(c, carry):
        marks, part = [], []
        for h in range(take):
            order = slot_ref[pl.ds(c * take + h, 1), :]
            order = jnp.broadcast_to(order, (LANES, padded)).T[:places]
            within = order & (ONE_HOT - 1)
            part.append(order - within)
            lane = iota((places, LANES), 1)
            marks.append(
                jnp.concatenate(
                    [
                        (within == lane + b * LANES).astype(f32)
                        for b in range(ONE_HOT // LANES)
                    ],
                    axis=1,
                )
            )
        found = dot(jnp.concatenate(marks, axis=0).astype(bf16), stacked)
        for h in range(take):
            here = found[h * places : (h + 1) * places]
            picked = here[:, :width]
            for q in range(1, parts):
                chosen = part[h] == q * ONE_HOT
                picked = jnp.where(chosen, here[:, q * width : (q + 1) * width], picked)
            out_ref[c * take + h] = picked.astype(bf16)
        return carry

    lax.fori_loop(0, tiles // take, step, 0)


def deal(basis, order, tiles_lon, wide):
    rows, width = basis.shape
    tiles = rows // wide
    places = slots(wide)
    return pl.pallas_call(
        functools.partial(deal_kernel, tiles_lon),
        out_shape=jax.ShapeDtypeStruct((tiles, places, width), bf16),
        scratch_shapes=[pltpu.VMEM((tiles, -(-places // LANES) * LANES), i32)],
        compiler_params=pltpu.CompilerParams(vmem_limit_bytes=VMEM_BYTES),
        cost_estimate=pl.CostEstimate(
            flops=2 * tiles * places * rows * width, bytes_accessed=4 * rows * width, transcendentals=0
        ),
        name="deal",
    )(basis, order.reshape(tiles, wide))


def inverse_kernel(gram_ref, out_ref):
    size = gram_ref.shape[0]
    count = size // SUB
    shape = (SUB, size)
    tiles = [gram_ref[t * SUB : (t + 1) * SUB, :] for t in range(count)]
    lane = iota(shape, 1)
    sub = iota(shape, 0)
    for top in range(count):
        first = top * SUB
        inside = (lane >= first) & (lane < first + SUB)
        columns = [
            [jnp.broadcast_to(tiles[t][:, first + c : first + c + 1], shape) for t in range(top, count)]
            for c in range(SUB)
        ]
        core = {
            (r, c): jnp.broadcast_to(columns[c][0][r : r + 1, :], shape)
            for r in range(SUB)
            for c in range(r, SUB)
        }
        lines = [
            jnp.where(
                inside,
                jnp.where(lane == first + c, 1.0, 0.0),
                jnp.broadcast_to(tiles[top][c : c + 1, :], shape),
            )
            for c in range(SUB)
        ]
        scales = []
        for c in range(SUB):
            inverse = 1.0 / core[c, c]
            scales.append(inverse)
            for d in range(c + 1, SUB):
                factor = core[c, d] * inverse
                for e in range(d, SUB):
                    core[d, e] = core[d, e] - factor * core[c, e]
                lines[d] = lines[d] - factor * lines[c]
                for t in range(1, count - top):
                    columns[d][t] = columns[d][t] - factor * columns[c][t]
        for t in range(1, count - top):
            rest = jnp.where(inside, 0.0, tiles[top + t])
            for c in range(SUB):
                rest = rest - columns[c][t] * (scales[c] * lines[c])
            tiles[top + t] = rest
        merged = lines[0]
        pivot = core[0, 0]
        for c in range(1, SUB):
            merged = jnp.where(sub == c, lines[c], merged)
            pivot = jnp.where(sub == c, core[c, c], pivot)
        kept = jnp.where(lane <= sub + first, merged, 0.0)
        out_ref[first : first + SUB, :] = kept * (1.0 / jnp.sqrt(pivot))


def factor_inverse(gram):
    size = gram.shape[0]
    return pl.pallas_call(
        inverse_kernel,
        out_shape=jax.ShapeDtypeStruct(gram.shape, f32),
        compiler_params=pltpu.CompilerParams(vmem_limit_bytes=VMEM_BYTES),
        cost_estimate=pl.CostEstimate(
            flops=40 * size**4, bytes_accessed=8 * size * size, transcendentals=0
        ),
        name="factor_inverse",
    )(gram)


def weight_kernel(coef_ref, across_ref, down_ref, spread):
    rows, groups, _, lanes = spread.shape
    places = groups * SUB
    turned = coef_ref[...].T
    depth = turned.shape[1]
    pieces = jnp.concatenate(split3(turned[:places]), axis=1)
    per_step = 4

    def put(c, carry):
        row = iota((3 * depth, per_step * lanes), 0) % depth
        wanted = c * per_step + iota((3 * depth, per_step * lanes), 1) // lanes
        values = dot(pieces, (row == wanted).astype(f32).astype(bf16))
        for h in range(per_step):
            spread[c * per_step + h] = values[:, h * lanes : (h + 1) * lanes].reshape(
                groups, SUB, lanes
            )
        return carry

    lax.fori_loop(0, rows // per_step, put, 0)

    def weigh(r, carry):
        for g in range(groups):
            here = spread[r, g]
            east = spread[r, g + 1] if g + 1 < groups else pltpu.roll(spread[r, 0], SUB - 1, 0)
            across_ref[r, g] = 0.124 * (here + east)
            down_ref[r, g] = 0.124 * (here + spread[r + 1, g])
        return carry

    lax.fori_loop(0, rows - 1, weigh, 0)
    across_ref[rows - 1] = jnp.zeros((groups, SUB, lanes), f32)
    down_ref[rows - 1] = jnp.zeros((groups, SUB, lanes), f32)


def weights(coef, lanes):
    rows, places = coef.shape
    coef = jnp.pad(coef, ((0, -rows % 64), (0, -places % LANES)))
    shape = (rows, places // SUB, SUB, lanes)
    return pl.pallas_call(
        weight_kernel,
        out_shape=(jax.ShapeDtypeStruct(shape, f32),) * 2,
        scratch_shapes=[pltpu.VMEM(shape, f32)],
        compiler_params=pltpu.CompilerParams(vmem_limit_bytes=VMEM_BYTES),
        cost_estimate=pl.CostEstimate(
            flops=rows * places * lanes * 100, bytes_accessed=8 * rows * places * lanes, transcendentals=0
        ),
        name="weights",
    )(coef)


def rotation(inverse):
    return jnp.concatenate(split3(inverse.T), axis=1)


def rotated(raw, turn):
    take, places, lanes = raw.shape
    raw = raw.astype(f32).reshape(take * places, lanes).astype(bf16)
    parts = dot(raw, turn)
    field = parts[:, :lanes] + (parts[:, lanes : 2 * lanes] + parts[:, 2 * lanes :])
    return field.astype(bf16).astype(f32).reshape(take, places, lanes)


def rotate_kernel(raw_ref, inverse_ref, out_ref):
    turn = rotation(inverse_ref[...])
    take = 8

    def step(c, carry):
        rows = pl.ds(c * take, take)
        out_ref[rows] = rotated(raw_ref[rows], turn).astype(bf16)
        return carry

    lax.fori_loop(0, raw_ref.shape[0] // take, step, 0)


def rotate(raw, inverse):
    return pl.pallas_call(
        rotate_kernel,
        out_shape=jax.ShapeDtypeStruct(raw.shape, bf16),
        compiler_params=pltpu.CompilerParams(vmem_limit_bytes=VMEM_BYTES),
        cost_estimate=pl.CostEstimate(
            flops=raw.size * 2000, bytes_accessed=4 * raw.size, transcendentals=0
        ),
        name="rotate",
    )(raw, inverse)


def sweep_kernel(
    scale, ends_ref, north_ref, own_ref, south_ref, inverse_ref, across_hbm, down_hbm, out_ref,
    first_ref, second_ref, across_ref, down_ref, sum_ref, sems,
):
    tall = own_ref.shape[0]
    rows, groups = first_ref.shape[:2]
    lanes = first_ref.shape[3]
    places = groups * SUB
    fetches = [
        pltpu.make_async_copy(across_hbm, across_ref, sems.at[0]),
        pltpu.make_async_copy(down_hbm, down_ref, sems.at[1]),
    ]
    for fetch in fetches:
        fetch.start()
    sum_ref[...] = jnp.zeros_like(sum_ref)
    turn = rotation(inverse_ref[...])

    def fill_halo(c, carry):
        take = 5
        for source, offset in ((north_ref, 0), (south_ref, HALO + tall)):
            field = rotated(source[pl.ds(c * take, take)], turn)
            first_ref[pl.ds(offset + c * take, take)] = field.reshape(take, groups, SUB, lanes)
        return carry

    def fill_own(c, carry):
        take = 4
        field = own_ref[pl.ds(c * take, take)].astype(f32)
        first_ref[pl.ds(HALO + c * take, take)] = field.reshape(take, groups, SUB, lanes)
        return carry

    lax.fori_loop(0, HALO // 5, fill_halo, 0)
    lax.fori_loop(0, tall // 4, fill_own, 0)
    for fetch in fetches:
        fetch.wait()

    def update(src, dst, row, take, kept):
        last = groups - 1
        west = []
        closing = []
        for r in range(take):
            here = src[row + r, last]
            east = pltpu.roll(src[row + r, 0], SUB - 1, 0)
            flux = across_ref[row + r, last] * (east - here)
            closing.append(flux)
            west.append(pltpu.roll(flux, 1, 0))
        here = [src[row + r, 0] for r in range(take)]
        for g in range(groups):
            above = down_ref[row - 1, g] * (here[0] - src[row - 1, g])
            following = []
            for r in range(take):
                below = here[r + 1] if r + 1 < take else src[row + take, g]
                under = down_ref[row + r, g] * (below - here[r])
                if g < last:
                    east = src[row + r, g + 1]
                    following.append(east)
                    flux = across_ref[row + r, g] * (east - here[r])
                else:
                    flux = closing[r]
                new = here[r] + ((under - above) + (flux - west[r]))
                dst[row + r, g] = new
                if kept:
                    sum_ref[row + r - HALO, g] += new * new
                above = under
                west[r] = flux
            here = following

    def sweep(s, src, dst):
        def inside(c, carry):
            update(src, dst, HALO + c * BLOCK, BLOCK, True)
            return carry

        def outside(r, carry):
            update(src, dst, r, 1, False)
            update(src, dst, rows - 1 - r, 1, False)
            return carry

        lax.fori_loop(0, tall // BLOCK, inside, 0)
        lax.fori_loop(s + 1, HALO, outside, 0)

        @pl.when(ends_ref[0] == 1)
        def _():
            dst[HALO - 1] = jnp.zeros(dst.shape[1:], f32)

        @pl.when(ends_ref[1] == 1)
        def _():
            dst[HALO + tall] = jnp.zeros(dst.shape[1:], f32)

    def two(t, carry):
        sweep(2 * t, first_ref, second_ref)
        sweep(2 * t + 1, second_ref, first_ref)
        return carry

    lax.fori_loop(0, SWEEPS // 2, two, 0)

    lane = iota((SUB, lanes), 1)

    def gather(c, totals):
        totals = list(totals)
        for r in [c * 2, c * 2 + 1]:
            for g in range(groups):
                total = jnp.sum(sum_ref[r, g], axis=1, keepdims=True)
                totals[g] = jnp.where(lane == r, total, totals[g])
        return tuple(totals)

    totals = lax.fori_loop(
        0, tall // 2, gather, tuple(jnp.zeros((SUB, lanes), f32) for _ in range(groups))
    )
    totals = jnp.concatenate(totals, axis=0).T[:tall]
    slot = iota((places, out_ref.shape[1]), 0)
    column = iota((places, out_ref.shape[1]), 1)
    back = (column == (slot % SUB) * groups + slot // SUB).astype(f32).astype(bf16)
    high, mid, low = split3(totals)
    out_ref[...] = (dot(high, back) + (dot(mid, back) + dot(low, back))) * scale


def sweeps(scale, ends, fields, inverse, across_down, wide):
    own = fields[1]
    tall, places, lanes = own.shape
    rows = tall + 2 * HALO
    vmem = pl.BlockSpec(memory_space=pltpu.VMEM)
    far = pl.BlockSpec(memory_space=pl.ANY)
    grid_rows = (rows, places // SUB, SUB, lanes)
    return pl.pallas_call(
        functools.partial(sweep_kernel, scale),
        out_shape=jax.ShapeDtypeStruct((tall, wide), f32),
        in_specs=[pl.BlockSpec(memory_space=pltpu.SMEM)] + [vmem] * (len(fields) + 1) + [far] * 2,
        out_specs=vmem,
        scratch_shapes=[
            pltpu.VMEM(grid_rows, f32),
            pltpu.VMEM(grid_rows, f32),
            pltpu.VMEM(grid_rows, f32),
            pltpu.VMEM(grid_rows, f32),
            pltpu.VMEM((tall,) + grid_rows[1:], f32),
            pltpu.SemaphoreType.DMA((2,)),
        ],
        compiler_params=pltpu.CompilerParams(vmem_limit_bytes=VMEM_BYTES),
        name="sweeps",
    )(ends, *fields, inverse, *across_down)


def from_before(x, axis, closed):
    count = lax.axis_size(axis)
    return lax.ppermute(
        x, axis, [(i, (i + 1) % count) for i in range(count if closed else count - 1)]
    )


def from_after(x, axis, closed):
    count = lax.axis_size(axis)
    return lax.ppermute(
        x, axis, [((i + 1) % count, i) for i in range(count if closed else count - 1)]
    )


def summed(x):
    def partner(axis, bits):
        return lax.ppermute(x, axis, [(i, i ^ bits) for i in range(lax.axis_size(axis))])

    for axis in ("lon", "lat"):
        step, count = 1, lax.axis_size(axis)
        while step < count:
            if step * 4 <= count:
                one, two, three = (partner(axis, step * k) for k in (1, 2, 3))
                x = (x + one) + (two + three)
                step *= 4
            else:
                x = x + partner(axis, step)
                step *= 2
    return x


def dealt_rows(basis, order, tall, wide, axes, count):
    width = basis.shape[1]
    share = order.size // count
    if share == wide:
        moving = deal(basis, order, lax.axis_size("lon"), wide)
        return moving, lambda arrived: arrived

    def last_step(arrived):
        own = arrived.reshape(tall, wide, width)
        left = from_before(own[:, -HALO:], "lon", True)
        right = from_after(own[:, :HALO], "lon", True)
        return circle(own, right, left, 1)

    return basis[order], last_step


def per_device(basis, order, land, conduct):
    axes = ("lat", "lon")
    rows_here, width = basis.shape
    tall, wide = land.shape
    count = lax.axis_size("lat") * lax.axis_size("lon")
    cells = rows_here * count
    tied = lax.optimization_barrier

    moving, last_step = dealt_rows(basis, order, tall, wide, axes, count)
    moving, basis = tied((moving, basis))
    raw = last_step(lax.all_to_all(moving, axes, split_axis=0, concat_axis=0, tiled=True))

    partial = lax.dot_general(
        basis, basis, (((0,), (0,)), ((), ())), preferred_element_type=f32
    )
    coef = conduct * (0.35 + 0.65 * land.astype(f32))
    partial, coef = tied((partial, coef))
    gram = summed(partial)
    coef = circle(
        coef,
        from_after(coef[:, :HALO], "lon", True),
        from_before(coef[:, -HALO:], "lon", True),
        1,
    )
    coef = jnp.concatenate(
        [from_before(coef[-HALO:], "lat", False), coef, from_after(coef[:HALO], "lat", False)],
        axis=0,
    )
    across_down = weights(coef, width)
    inverse = factor_inverse(gram)

    north = from_before(raw[-HALO:], "lat", False)
    south = from_after(raw[:HALO], "lat", False)
    own = rotate(raw, inverse)

    at = lax.axis_index("lat")
    ends = jnp.stack([at == 0, at == lax.axis_size("lat") - 1]).astype(i32)
    scale = cells / (width * SWEEPS)
    return sweeps(scale, ends, (north, own, south), inverse, across_down, wide)


def solution(mesh):
    in_specs = (P(("lat", "lon"), None), P(("lat", "lon")), P("lat", "lon"), P("lat", "lon"))
    out_specs = P("lat", "lon")
    return jax.shard_map(
        per_device, mesh=mesh, in_specs=in_specs, out_specs=out_specs, check_vma=False
    )
```

time: 129 us -> 96.8 us (0.75)
  waiting for transfers between devices: 32.7 us -> 8.45 us
  starting transfers between devices: 22.8 us -> 35.2 us
  blocking collectives: 9.78 us -> 0 us
  Pallas kernels: 54.2 us -> 48.3 us
  local copies, waits for them, and re-layouts: 5.46 us -> 1.87 us
    all_to_all x2 -> x1, waiting for transfers between devices: 16.6 us -> 0.01 us  [per_device(): lax.all_to_all(moving, axes, split_axis=0, concat_axis=0, tiled=True)]
    ppermute x3, waiting for transfers between devices: 16 us -> 2.89 us  [from_before(): lax.ppermute(x, axis, [(i, (i + 1) % count) for i in range(count if close...]
    pallas_call x1, Pallas kernels: 18.6 us -> 5.9 us  [factor_inverse(): pl.pallas_call(inverse_kernel, out_shape=jax.ShapeDtypeStruct(gram.shape,...]
    pallas_call x1 -> x3, Pallas kernels: 9.76 us -> 22 us  [the longest x1 10.2 us: deal(): pl.pallas_call(functools.partial(deal_kernel, tiles_lon), out_shape=jax.S...]
    ppermute x0 -> x7, starting transfers between devices: none -> 12.2 us  [partner(): lax.ppermute(x, axis, [(i, i ^ bits) for i in range(lax.axis_size(axis))])]
    all_to_all x1 -> x0, blocking collectives: 9.78 us -> none  [exchange(): return lax.all_to_all(x, axes, split_axis=0, concat_axis=0, tiled=True)]
    pallas_call x1, Pallas kernels: 25.8 us -> 20.3 us  [sweeps(): pl.pallas_call(functools.partial(sweep_kernel, scale), out_shape=jax.Shap...]
    ppermute x0 -> x7, waiting for transfers between devices: none -> 2.82 us  [partner(): lax.ppermute(x, axis, [(i, i ^ bits) for i in range(lax.axis_size(axis))])]
  transfers between devices with their start and end apart: 8 -> 14, of which waited for: 3 -> 5; matrix products, arithmetic and copies ran while one was open for 1% -> 3% of each run, Pallas kernels for 15% -> 18%
where the time goes in v4:
time: 96.8 us; the launch traced here: 96.4 us
  Pallas kernels  48.3 us (50%)
  starting transfers between devices  35.2 us (36%)
  waiting for transfers between devices  8.45 us (9%)
  other arithmetic  1.96 us (2%)
  local copies, waits for them, and re-layouts  1.87 us (2%)
    pallas_call x1, Pallas kernels, sweeps(): pl.pallas_call(functools.partial(sweep_kernel, scale), out_shape=jax.Shap...  20.3 us
    ppermute x7, starting transfers between devices, partner(): lax.ppermute(x, axis, [(i, i ^ bits) for i in range(lax.axis_size(axis))])  12.2 us
    ppermute x3, starting transfers between devices, from_before(): lax.ppermute(x, axis, [(i, (i + 1) % count) for i in range(count if close...  10.7 us
    pallas_call x1, Pallas kernels, deal(): pl.pallas_call(functools.partial(deal_kernel, tiles_lon), out_shape=jax.S...  10.2 us
    pallas_call x1, Pallas kernels, weights(): pl.pallas_call(weight_kernel, out_shape=(jax.ShapeDtypeStruct(shape, f32)...  7.7 us
    all_to_all x1, starting transfers between devices, per_device(): lax.all_to_all(moving, axes, split_axis=0, concat_axis=0, tiled=True)  7.3 us
    pallas_call x1, Pallas kernels, factor_inverse(): pl.pallas_call(inverse_kernel, out_shape=jax.ShapeDtypeStruct(gram.shape,...  5.9 us
    ppermute x3, starting transfers between devices, from_after(): lax.ppermute(x, axis, [((i + 1) % count, i) for i in range(count if close...  5.01 us
  transfers between devices with their start and end apart: 14, of which 5 were waited for; matrix products, arithmetic and copies ran while one was open for 3% of the time, Pallas kernels for 18%

profile of v4, /device:TPU:0, one launch (start us, length us, event | category | flops | bytes accessed | tf_op | source)
XLA Modules:
  0.0 96.4 jit_solution(7739030573785997798)
XLA Ops:
  0.0 10.2 %deal.1 = bf16[32,152,128]{2,1,0:T(8,128)(2,1)} custom-call(bf16[4096,128]{1,0:T(8,128)(2,1)} %basis_ref.1, s32[32,128]{1,0:T(8,128)} %bitcast.10), custom_call_target="tpu_custom_call" | custom-call | flops 5100273664 | bytes 2097152 | tf_op jit(solution)/shard_map/deal/pallas_call | solution.py:123
  10.2 7.3 %all-to-all-start = ((bf16[32,152,128]{2,1,0:T(8,128)(2,1)}), bf16[32,152,128]{2,1,0:T(8,128)(2,1)S(1)}, u32[]{:S(2)}, u32[]{:S(2)}) async-start(bf16[32,152,128]{2,1,0:T(8,128)(2,1)} %deal.1), calls=%async_computation | async-start | bytes 2490368 | tf_op jit(solution)/shard_map/all_to_all | solution.py:482
  17.6 0.5 fusion.3
  18.1 2.4 %collective-permute-start.9 = (f32[32,10]{1,0:T(8,128)S(1)}, f32[32,10]{1,0:T(8,128)S(1)}, u32[]{:S(2)}, u32[]{:S(2)}) collective-permute-start(f32[32,10]{1,0:T(8,128)S(1)} %get-tuple-element.21), channel_id=1, source_target_pairs={{1,0},{2,1},{3,2},{4,3},{5,4},{6,5},{7,6},{0,7},{9,8},{10,9},{11,1... | collective-permute-start | bytes 3848 | tf_op jit(solution)/shard_map/ppermute | solution.py:434
  20.6 1.7 %collective-permute-start.3 = (f32[128,128]{1,0:T(8,128)S(1)}, f32[128,128]{1,0:T(8,128)S(1)}, u32[]{:S(2)}, u32[]{:S(2)}) collective-permute-start(f32[128,128]{1,0:T(8,128)S(1)} %fusion.3), channel_id=1, source_target_pairs={{0,3},{1,2},{2,1},{3,0},{4,7},{5,6},{6,5},{7,4},{8,11},{9,10},{10,... | collective-permute-start | bytes 196616 | tf_op jit(solution)/shard_map/ppermute | solution.py:441
  22.3 0.1 collective-permute-start.1
  22.5 2.7 %collective-permute-done.9 = f32[32,10]{1,0:T(8,128)S(1)} collective-permute-done((f32[32,10]{1,0:T(8,128)S(1)}, f32[32,10]{1,0:T(8,128)S(1)}, u32[]{:S(2)}, u32[]{:S(2)}) %collective-permute-start.9) | collective-permute-done | bytes 1312 | tf_op jit(solution)/shard_map/ppermute | solution.py:434
  25.3 2.9 %collective-permute-done.10 = f32[32,10]{1,0:T(8,128)S(1)} collective-permute-done((f32[32,10]{1,0:T(8,128)S(1)}, f32[32,10]{1,0:T(8,128)S(1)}, u32[]{:S(2)}, u32[]{:S(2)}) %collective-permute-start.10) | collective-permute-done | bytes 1312 | tf_op jit(solution)/shard_map/ppermute | solution.py:427
  28.4 0.1 copy.6
  28.5 0.1 slice.29
  28.6 1.6 %collective-permute-start.11 = (f32[10,152]{1,0:T(8,128)S(1)}, f32[10,152]{1,0:T(8,128)S(1)}, u32[]{:S(2)}, u32[]{:S(2)}) collective-permute-start(f32[10,152]{1,0:T(8,128)S(1)} %slice.29), channel_id=1, source_target_pairs={{0,8},{8,16},{16,24},{1,9},{9,17},{17,25},{2,10},{10,18},{18,26},{... | collective-permute-start | bytes 18248 | tf_op jit(solution)/shard_map/ppermute | solution.py:427
  30.2 0.1 copy.8
  30.3 0.1 slice.31
  30.4 1.3 %collective-permute-start.12 = (f32[10,152]{1,0:T(8,128)S(1)}, f32[10,152]{1,0:T(8,128)S(1)}, u32[]{:S(2)}, u32[]{:S(2)}) collective-permute-start(f32[10,152]{1,0:T(8,128)S(1)} %slice.31), channel_id=1, source_target_pairs={{8,0},{16,8},{24,16},{9,1},{17,9},{25,17},{10,2},{18,10},{26,18},{... | collective-permute-start | bytes 18248 | tf_op jit(solution)/shard_map/ppermute | solution.py:434
  31.7 0.8 collective-permute-done.2
  32.5 2.5 %collective-permute-start.4 = (f32[128,128]{1,0:T(8,128)S(1)}, f32[128,128]{1,0:T(8,128)S(1)}, u32[]{:S(2)}, u32[]{:S(2)}) collective-permute-start(f32[128,128]{1,0:T(8,128)S(1)} %add_add_fusion.1), channel_id=1, source_target_pairs={{0,4},{1,5},{2,6},{3,7},{4,0},{5,1},{6,2},{7,3},{8,12},{9,13},{10,... | collective-permute-start | bytes 196616 | tf_op jit(solution)/shard_map/ppermute | solution.py:441
  35.0 0.6 add_convert_fusion.ends_ref
  35.6 0.1 copy.7
  35.8 1.6 %collective-permute-done.4 = f32[128,128]{1,0:T(8,128)S(1)} collective-permute-done((f32[128,128]{1,0:T(8,128)S(1)}, f32[128,128]{1,0:T(8,128)S(1)}, u32[]{:S(2)}, u32[]{:S(2)}) %collective-permute-start.4) | collective-permute-done | bytes 65568 | tf_op jit(solution)/shard_map/ppermute | solution.py:441
  37.4 7.2 %collective-permute-start.7 = (f32[128,128]{1,0:T(8,128)S(1)}, f32[128,128]{1,0:T(8,128)S(1)}, u32[]{:S(2)}, u32[]{:S(2)}) collective-permute-start(f32[128,128]{1,0:T(8,128)S(1)} %add.34), channel_id=1, source_target_pairs={{0,24},{8,16},{16,8},{24,0},{1,25},{9,17},{17,9},{25,1},{2,26},{10... | collective-permute-start | bytes 196616 | tf_op jit(solution)/shard_map/ppermute | solution.py:441
  44.6 0.6 collective-permute-start.5
  45.3 0.6 select_maximum_fusion.coef_ref
  45.9 7.7 %weights.1 = (f32[52,19,8,128]{3,2,1,0:T(8,128)}, f32[52,19,8,128]{3,2,1,0:T(8,128)}) custom-call(f32[64,256]{1,0:T(8,128)} %select_maximum_fusion.coef_ref), custom_call_target="tpu_custom_call" | custom-call | flops 101171200 | bytes 8093696 | tf_op jit(solution)/shard_map/weights/pallas_call | solution.py:237
  53.6 0.4 collective-permute-done.6
  54.0 0.6 add_add_fusion.gram_ref
  54.7 1.3 %collective-permute-start.8 = (bf16[10,152,128]{2,1,0:T(8,128)(2,1)S(1)}, bf16[10,152,128]{2,1,0:T(8,128)(2,1)S(1)}, u32[]{:S(2)}, u32[]{:S(2)}) collective-permute-start(bf16[10,152,128]{2,1,0:T(8,128)(2,1)S(1)} %get-tuple-element.17), channel_id=1, source_target_pairs={{8,0},{16,8},{24,16},{9,1},{17,9},{25,17},{10,2},{18,10},{26,18},{... | collective-permute-start | bytes 1167368 | tf_op jit(solution)/shard_map/ppermute | solution.py:434
  56.0 9.1 %collective-permute-start = (bf16[10,152,128]{2,1,0:T(8,128)(2,1)S(1)}, bf16[10,152,128]{2,1,0:T(8,128)(2,1)S(1)}, u32[]{:S(2)}, u32[]{:S(2)}) collective-permute-start(bf16[10,152,128]{2,1,0:T(8,128)(2,1)S(1)} %get-tuple-element.18), channel_id=1, source_target_pairs={{0,8},{8,16},{16,24},{1,9},{9,17},{17,25},{2,10},{10,18},{18,26},{... | collective-permute-start | bytes 1167368 | tf_op jit(solution)/shard_map/ppermute | solution.py:427
  65.1 5.9 %factor_inverse.1.inverse_ref = f32[128,128]{1,0:T(8,128)} custom-call(f32[128,128]{1,0:T(8,128)} %add_add_fusion.gram_ref), custom_call_target="tpu_custom_call" | custom-call | flops 10737418240 | bytes 131072 | tf_op jit(solution)/shard_map/factor_inverse/pallas_call | solution.py:189
  71.0 4.1 %rotate.1.own_ref = bf16[32,152,128]{2,1,0:T(8,128)(2,1)} custom-call(bf16[32,152,128]{2,1,0:T(8,128)(2,1)} %copy-done.1, f32[128,128]{1,0:T(8,128)} %factor_inverse.1.inverse_ref), custom_call_target="tpu_custom_call" | custom-call | flops 1245184000 | bytes 2490368 | tf_op jit(solution)/shard_map/rotate/pallas_call | solution.py:274
  75.1 0.7 copy-done.2
  75.9 0.1 copy-done.3
  76.0 20.3 %sweeps.1 = f32[32,128]{1,0:T(8,128)} custom-call(s32[2]{0:T(128)} %add_convert_fusion.ends_ref, bf16[10,152,128]{2,1,0:T(8,128)(2,1)} %copy-done.3, bf16[32,152,128]{2,1,0:T(8,128)(2,1)} %rotate.1.own_ref, bf16[10,152,128]{2,1,0:T(8,128)(2,1)} %copy-done.2, f32[128,128]{1,0:T(8,128)} %factor_inverse.1.inverse_ref, ...), custom_call_target="tpu_custom_call" | custom-call | tf_op jit(solution)/shard_map/sweeps/pallas_call | solution.py:407
  (33 shorter events, 0.5 us)
Async XLA Ops:
  10.2 7.3 %copy-start.4 = (f32[32,128]{1,0:T(8,128)S(1)}, f32[32,128]{1,0:T(8,128)}, u32[]{:S(2)}) copy-start(f32[32,128]{1,0:T(8,128)} %param.7) | copy-start | bytes 49156
  10.2 7.3 %copy-start.5 = (s32[32,128]{1,0:T(8,128)S(1)}, s32[32,128]{1,0:T(8,128)}, u32[]{:S(2)}) copy-start(s32[32,128]{1,0:T(8,128)} %param.6) | copy-start | bytes 49156
  10.2 7.3 %copy-start = (bf16[4096,128]{1,0:T(8,128)(2,1)S(1)}, bf16[4096,128]{1,0:T(8,128)(2,1)}, u32[]{:S(2)}) copy-start(bf16[4096,128]{1,0:T(8,128)(2,1)} %basis_ref.1) | copy-start | bytes 3145732
  10.2 44.4 %all-to-all-start = ((bf16[32,152,128]{2,1,0:T(8,128)(2,1)}), bf16[32,152,128]{2,1,0:T(8,128)(2,1)S(1)}, u32[]{:S(2)}, u32[]{:S(2)}) async-start(bf16[32,152,128]{2,1,0:T(8,128)(2,1)} %deal.1), calls=%async_computation | async-start | bytes 2490368 | tf_op jit(solution)/shard_map/all_to_all | solution.py:482
  18.1 7.1 %collective-permute-start.9 = (f32[32,10]{1,0:T(8,128)S(1)}, f32[32,10]{1,0:T(8,128)S(1)}, u32[]{:S(2)}, u32[]{:S(2)}) collective-permute-start(f32[32,10]{1,0:T(8,128)S(1)} %get-tuple-element.21), channel_id=1, source_target_pairs={{1,0},{2,1},{3,2},{4,3},{5,4},{6,5},{7,6},{0,7},{9,8},{10,9},{11,1... | collective-permute-start | bytes 3848 | tf_op jit(solution)/shard_map/ppermute | solution.py:434
  20.6 7.6 %collective-permute-start.10 = (f32[32,10]{1,0:T(8,128)S(1)}, f32[32,10]{1,0:T(8,128)S(1)}, u32[]{:S(2)}, u32[]{:S(2)}) collective-permute-start(f32[32,10]{1,0:T(8,128)S(1)} %get-tuple-element.22), channel_id=1, source_target_pairs={{0,1},{1,2},{2,3},{3,4},{4,5},{5,6},{6,7},{7,0},{8,9},{9,10},{10,1... | collective-permute-start | bytes 3848 | tf_op jit(solution)/shard_map/ppermute | solution.py:427
  20.6 11.2 %collective-permute-start.3 = (f32[128,128]{1,0:T(8,128)S(1)}, f32[128,128]{1,0:T(8,128)S(1)}, u32[]{:S(2)}, u32[]{:S(2)}) collective-permute-start(f32[128,128]{1,0:T(8,128)S(1)} %fusion.3), channel_id=1, source_target_pairs={{0,3},{1,2},{2,1},{3,0},{4,7},{5,6},{6,5},{7,4},{8,11},{9,10},{10,... | collective-permute-start | bytes 196616 | tf_op jit(solution)/shard_map/ppermute | solution.py:441
  22.3 10.2 %collective-permute-start.2 = (f32[128,128]{1,0:T(8,128)S(1)}, f32[128,128]{1,0:T(8,128)S(1)}, u32[]{:S(2)}, u32[]{:S(2)}) collective-permute-start(f32[128,128]{1,0:T(8,128)S(1)} %fusion.3), channel_id=1, source_target_pairs={{0,2},{1,3},{2,0},{3,1},{4,6},{5,7},{6,4},{7,5},{8,10},{9,11},{10,... | collective-permute-start | bytes 196616 | tf_op jit(solution)/shard_map/ppermute | solution.py:441
  22.3 10.2 %collective-permute-start.1 = (f32[128,128]{1,0:T(8,128)S(1)}, f32[128,128]{1,0:T(8,128)S(1)}, u32[]{:S(2)}, u32[]{:S(2)}) collective-permute-start(f32[128,128]{1,0:T(8,128)S(1)} %fusion.3), channel_id=1, source_target_pairs={{0,1},{1,0},{2,3},{3,2},{4,5},{5,4},{6,7},{7,6},{8,9},{9,8},{10,11... | collective-permute-start | bytes 196616 | tf_op jit(solution)/shard_map/ppermute | solution.py:441
  28.6 16.7 %collective-permute-start.11 = (f32[10,152]{1,0:T(8,128)S(1)}, f32[10,152]{1,0:T(8,128)S(1)}, u32[]{:S(2)}, u32[]{:S(2)}) collective-permute-start(f32[10,152]{1,0:T(8,128)S(1)} %slice.29), channel_id=1, source_target_pairs={{0,8},{8,16},{16,24},{1,9},{9,17},{17,25},{2,10},{10,18},{18,26},{... | collective-permute-start | bytes 18248 | tf_op jit(solution)/shard_map/ppermute | solution.py:427
  30.4 14.9 %collective-permute-start.12 = (f32[10,152]{1,0:T(8,128)S(1)}, f32[10,152]{1,0:T(8,128)S(1)}, u32[]{:S(2)}, u32[]{:S(2)}) collective-permute-start(f32[10,152]{1,0:T(8,128)S(1)} %slice.31), channel_id=1, source_target_pairs={{8,0},{16,8},{24,16},{9,1},{17,9},{25,17},{10,2},{18,10},{26,18},{... | collective-permute-start | bytes 18248 | tf_op jit(solution)/shard_map/ppermute | solution.py:434
  32.5 4.9 %collective-permute-start.4 = (f32[128,128]{1,0:T(8,128)S(1)}, f32[128,128]{1,0:T(8,128)S(1)}, u32[]{:S(2)}, u32[]{:S(2)}) collective-permute-start(f32[128,128]{1,0:T(8,128)S(1)} %add_add_fusion.1), channel_id=1, source_target_pairs={{0,4},{1,5},{2,6},{3,7},{4,0},{5,1},{6,2},{7,3},{8,12},{9,13},{10,... | collective-permute-start | bytes 196616 | tf_op jit(solution)/shard_map/ppermute | solution.py:441
  37.4 16.2 %collective-permute-start.7 = (f32[128,128]{1,0:T(8,128)S(1)}, f32[128,128]{1,0:T(8,128)S(1)}, u32[]{:S(2)}, u32[]{:S(2)}) collective-permute-start(f32[128,128]{1,0:T(8,128)S(1)} %add.34), channel_id=1, source_target_pairs={{0,24},{8,16},{16,8},{24,0},{1,25},{9,17},{17,9},{25,1},{2,26},{10... | collective-permute-start | bytes 196616 | tf_op jit(solution)/shard_map/ppermute | solution.py:441
  44.6 9.4 %collective-permute-start.6 = (f32[128,128]{1,0:T(8,128)S(1)}, f32[128,128]{1,0:T(8,128)S(1)}, u32[]{:S(2)}, u32[]{:S(2)}) collective-permute-start(f32[128,128]{1,0:T(8,128)S(1)} %add.34), channel_id=1, source_target_pairs={{0,16},{8,24},{16,0},{24,8},{1,17},{9,25},{17,1},{25,9},{2,18},{10... | collective-permute-start | bytes 196616 | tf_op jit(solution)/shard_map/ppermute | solution.py:441
  44.6 9.4 %collective-permute-start.5 = (f32[128,128]{1,0:T(8,128)S(1)}, f32[128,128]{1,0:T(8,128)S(1)}, u32[]{:S(2)}, u32[]{:S(2)}) collective-permute-start(f32[128,128]{1,0:T(8,128)S(1)} %add.34), channel_id=1, source_target_pairs={{0,8},{8,0},{16,24},{24,16},{1,9},{9,1},{17,25},{25,17},{2,10},{10... | collective-permute-start | bytes 196616 | tf_op jit(solution)/shard_map/ppermute | solution.py:441
  54.6 16.4 %copy-start.1 = (bf16[32,152,128]{2,1,0:T(8,128)(2,1)}, bf16[32,152,128]{2,1,0:T(8,128)(2,1)S(1)}, u32[]{:S(2)}) copy-start(bf16[32,152,128]{2,1,0:T(8,128)(2,1)S(1)} %all-to-all-done.raw_ref) | copy-start | bytes 3735556
  54.7 20.4 %collective-permute-start.8 = (bf16[10,152,128]{2,1,0:T(8,128)(2,1)S(1)}, bf16[10,152,128]{2,1,0:T(8,128)(2,1)S(1)}, u32[]{:S(2)}, u32[]{:S(2)}) collective-permute-start(bf16[10,152,128]{2,1,0:T(8,128)(2,1)S(1)} %get-tuple-element.17), channel_id=1, source_target_pairs={{8,0},{16,8},{24,16},{9,1},{17,9},{25,17},{10,2},{18,10},{26,18},{... | collective-permute-start | bytes 1167368 | tf_op jit(solution)/shard_map/ppermute | solution.py:434
  56.0 19.1 %collective-permute-start = (bf16[10,152,128]{2,1,0:T(8,128)(2,1)S(1)}, bf16[10,152,128]{2,1,0:T(8,128)(2,1)S(1)}, u32[]{:S(2)}, u32[]{:S(2)}) collective-permute-start(bf16[10,152,128]{2,1,0:T(8,128)(2,1)S(1)} %get-tuple-element.18), channel_id=1, source_target_pairs={{0,8},{8,16},{16,24},{1,9},{9,17},{17,25},{2,10},{10,18},{18,26},{... | collective-permute-start | bytes 1167368 | tf_op jit(solution)/shard_map/ppermute | solution.py:427
  75.1 0.7 copy-start.2
  75.1 0.9 copy-start.3

commit v5 on v4

--- a/solution.py
+++ b/solution.py
@@ -203,19 +203,19 @@
     turned = coef_ref[...].T
     depth = turned.shape[1]
     pieces = jnp.concatenate(split3(turned[:places]), axis=1)
-    per_step = 4
+    per_step = rows // 4
+    offset = iota((3 * depth, per_step * lanes), 0) & (depth - 1)
+    offset = offset - (iota((3 * depth, per_step * lanes), 1) // lanes)
 
     def put(c, carry):
-        row = iota((3 * depth, per_step * lanes), 0) % depth
-        wanted = c * per_step + iota((3 * depth, per_step * lanes), 1) // lanes
-        values = dot(pieces, (row == wanted).astype(f32).astype(bf16))
+        values = dot(pieces, (offset == c * per_step).astype(f32).astype(bf16))
         for h in range(per_step):
             spread[c * per_step + h] = values[:, h * lanes : (h + 1) * lanes].reshape(
                 groups, SUB, lanes
             )
         return carry
 
-    lax.fori_loop(0, rows // per_step, put, 0)
+    lax.fori_loop(0, 4, put, 0)
 
     def weigh(r, carry):
         for g in range(groups):
@@ -258,108 +258,189 @@
     return field.astype(bf16).astype(f32).reshape(take, places, lanes)
 
 
-def rotate_kernel(raw_ref, inverse_ref, out_ref):
+def update(src, dst, across, down, sums, row, take):
+    groups = src.shape[1]
+    last = groups - 1
+    span = range(take)
+    start = [src[row + r, 0] for r in span]
+    closing = [
+        across[row + r, last] * (pltpu.roll(start[r], SUB - 1, 0) - src[row + r, last])
+        for r in span
+    ]
+    wrapped = [pltpu.roll(flux, 1, 0) for flux in closing]
+
+    def vertical(g, here):
+        above = down[row - 1, g] * (here[0] - src[row - 1, g])
+        change = []
+        for r in span:
+            below = here[r + 1] if r + 1 < take else src[row + take, g]
+            under = down[row + r, g] * (below - here[r])
+            change.append(under - above)
+            above = under
+        return change
+
+    def finish(r, g, new):
+        dst[row + r, g] = new
+        sums[row + r, g] += new * new
+
+    here = [src[row + r, 1] for r in span]
+    west = [across[row + r, 0] * (here[r] - start[r]) for r in span]
+    change = vertical(0, start)
+    pending = [start[r] + (change[r] + west[r]) for r in span]
+    for g in range(1, groups):
+        if g < last:
+            following = [src[row + r, g + 1] for r in span]
+            flux = [across[row + r, g] * (following[r] - here[r]) for r in span]
+        else:
+            following, flux = None, closing
+        change = vertical(g, here)
+        for r in span:
+            finish(r, g, here[r] + (change[r] + (flux[r] - west[r])))
+        here, west = following, flux
+    for r in span:
+        finish(r, 0, pending[r] - wrapped[r])
+
+
+def summed_lanes(sums, rows, totals):
+    lane = iota(totals[0].shape, 1)
+    for row, to in rows:
+        for g in range(len(totals)):
+            total = jnp.sum(sums[row, g], axis=1, keepdims=True)
+            totals[g] = totals[g] + jnp.where(lane == to, total, 0.0)
+    return totals
+
+
+def inner_kernel(
+    own_ref, inverse_ref, across_hbm, down_hbm, first_ref, second_ref, total_ref,
+    across_ref, down_ref, sum_ref, sems,
+):
+    tall, groups, _, lanes = first_ref.shape
+    inside = pl.ds(HALO, tall)
+    fetches = [
+        pltpu.make_async_copy(across_hbm.at[inside], across_ref, sems.at[0]),
+        pltpu.make_async_copy(down_hbm.at[inside], down_ref, sems.at[1]),
+    ]
+    for fetch in fetches:
+        fetch.start()
     turn = rotation(inverse_ref[...])
     take = 8
 
-    def step(c, carry):
-        rows = pl.ds(c * take, take)
-        out_ref[rows] = rotated(raw_ref[rows], turn).astype(bf16)
-        return carry
-
-    lax.fori_loop(0, raw_ref.shape[0] // take, step, 0)
-
-
-def rotate(raw, inverse):
+    def fill(c, carry):
+        field = rotated(own_ref[pl.ds(c * take, take)], turn)
+        first_ref[pl.ds(c * take, take)] = field.reshape(take, groups, SUB, lanes)
+        return carry
+
+    lax.fori_loop(0, tall // take, fill, 0)
+    sum_ref[...] = jnp.zeros_like(sum_ref)
+    second_ref[0] = jnp.zeros(second_ref.shape[1:], f32)
+    second_ref[tall - 1] = jnp.zeros(second_ref.shape[1:], f32)
+    for fetch in fetches:
+        fetch.wait()
+
+    def sweep(s, src, dst, odd_pair):
+        count = tall - 2 - 2 * s
+
+        def step(c, carry):
+            update(src, dst, across_ref, down_ref, sum_ref, s + 1 + c * BLOCK, BLOCK)
+            return carry
+
+        lax.fori_loop(0, count // BLOCK, step, 0)
+        if odd_pair:
+            update(src, dst, across_ref, down_ref, sum_ref, s + count - 1, 2)
+
+    def two(t, carry):
+        sweep(2 * t, first_ref, second_ref, (tall - 2) % BLOCK == 2)
+        sweep(2 * t + 1, second_ref, first_ref, (tall - 4) % BLOCK == 2)
+        return carry
+
+    lax.fori_loop(0, SWEEPS // 2, two, 0)
+
+    def gather(c, totals):
+        rows = [(c * 2 + h, c * 2 + h) for h in range(2)]
+        return tuple(summed_lanes(sum_ref, rows, list(totals)))
+
+    zeros = tuple(jnp.zeros((SUB, lanes), f32) for _ in range(groups))
+    totals = lax.fori_loop(0, tall // 2, gather, zeros)
+    total_ref[...] = jnp.concatenate(totals, axis=0)
+
+
+def inner_sweeps(own, inverse, across_down):
+    tall, places, lanes = own.shape
+    vmem = pl.BlockSpec(memory_space=pltpu.VMEM)
+    far = pl.BlockSpec(memory_space=pl.ANY)
+    shape = (tall, places // SUB, SUB, lanes)
     return pl.pallas_call(
-        rotate_kernel,
-        out_shape=jax.ShapeDtypeStruct(raw.shape, bf16),
+        inner_kernel,
+        out_shape=(
+            jax.ShapeDtypeStruct(shape, f32),
+            jax.ShapeDtypeStruct(shape, f32),
+            jax.ShapeDtypeStruct((places, lanes), f32),
+        ),
+        in_specs=[vmem, vmem, far, far],
+        out_specs=(vmem, vmem, vmem),
+        scratch_shapes=[
+            pltpu.VMEM(shape, f32),
+            pltpu.VMEM(shape, f32),
+            pltpu.VMEM(shape, f32),
+            pltpu.SemaphoreType.DMA((2,)),
+        ],
         compiler_params=pltpu.CompilerParams(vmem_limit_bytes=VMEM_BYTES),
         cost_estimate=pl.CostEstimate(
-            flops=raw.size * 2000, bytes_accessed=4 * raw.size, transcendentals=0
+            flops=12 * 10**9, bytes_accessed=8 * own.size, transcendentals=0
         ),
-        name="rotate",
-    )(raw, inverse)
-
-
-def sweep_kernel(
-    scale, ends_ref, north_ref, own_ref, south_ref, inverse_ref, across_hbm, down_hbm, out_ref,
-    first_ref, second_ref, across_ref, down_ref, sum_ref, sems,
+        name="inner_sweeps",
+    )(own, inverse, *across_down)
+
+
+def outer_kernel(
+    scale, ends_ref, north_ref, south_ref, inverse_ref, inner_ref, first_hbm, second_hbm,
+    across_hbm, down_hbm, out_ref, first_ref, second_ref, across_ref, down_ref, sum_ref, sems,
 ):
-    tall = own_ref.shape[0]
-    rows, groups = first_ref.shape[:2]
-    lanes = first_ref.shape[3]
+    rows, groups, _, lanes = first_ref.shape
+    tall = rows - 2 * HALO
     places = groups * SUB
-    fetches = [
-        pltpu.make_async_copy(across_hbm, across_ref, sems.at[0]),
-        pltpu.make_async_copy(down_hbm, down_ref, sems.at[1]),
-    ]
+    near = HALO + 1
+    fetches = []
+    for k, (source, target) in enumerate(((first_hbm, first_ref), (second_hbm, second_ref))):
+        for side, row in enumerate((0, tall - near)):
+            fetches.append(
+                pltpu.make_async_copy(
+                    source.at[pl.ds(row, near)],
+                    target.at[pl.ds(HALO + row, near)],
+                    sems.at[2 * k + side],
+                )
+            )
+    wide_part = 2 * HALO + 1
+    for k, (source, target) in enumerate(((across_hbm, across_ref), (down_hbm, down_ref))):
+        for side, row in enumerate((0, rows - wide_part)):
+            part = pl.ds(row, wide_part)
+            fetches.append(
+                pltpu.make_async_copy(source.at[part], target.at[part], sems.at[4 + 2 * k + side])
+            )
     for fetch in fetches:
         fetch.start()
     sum_ref[...] = jnp.zeros_like(sum_ref)
     turn = rotation(inverse_ref[...])
-
-    def fill_halo(c, carry):
-        take = 5
+    take = 5
+
+    def fill(c, carry):
         for source, offset in ((north_ref, 0), (south_ref, HALO + tall)):
             field = rotated(source[pl.ds(c * take, take)], turn)
             first_ref[pl.ds(offset + c * take, take)] = field.reshape(take, groups, SUB, lanes)
         return carry
 
-    def fill_own(c, carry):
-        take = 4
-        field = own_ref[pl.ds(c * take, take)].astype(f32)
-        first_ref[pl.ds(HALO + c * take, take)] = field.reshape(take, groups, SUB, lanes)
-        return carry
-
-    lax.fori_loop(0, HALO // 5, fill_halo, 0)
-    lax.fori_loop(0, tall // 4, fill_own, 0)
+    lax.fori_loop(0, HALO // take, fill, 0)
     for fetch in fetches:
         fetch.wait()
 
-    def update(src, dst, row, take, kept):
-        last = groups - 1
-        west = []
-        closing = []
-        for r in range(take):
-            here = src[row + r, last]
-            east = pltpu.roll(src[row + r, 0], SUB - 1, 0)
-            flux = across_ref[row + r, last] * (east - here)
-            closing.append(flux)
-            west.append(pltpu.roll(flux, 1, 0))
-        here = [src[row + r, 0] for r in range(take)]
-        for g in range(groups):
-            above = down_ref[row - 1, g] * (here[0] - src[row - 1, g])
-            following = []
-            for r in range(take):
-                below = here[r + 1] if r + 1 < take else src[row + take, g]
-                under = down_ref[row + r, g] * (below - here[r])
-                if g < last:
-                    east = src[row + r, g + 1]
-                    following.append(east)
-                    flux = across_ref[row + r, g] * (east - here[r])
-                else:
-                    flux = closing[r]
-                new = here[r] + ((under - above) + (flux - west[r]))
-                dst[row + r, g] = new
-                if kept:
-                    sum_ref[row + r - HALO, g] += new * new
-                above = under
-                west[r] = flux
-            here = following
-
     def sweep(s, src, dst):
-        def inside(c, carry):
-            update(src, dst, HALO + c * BLOCK, BLOCK, True)
+        def step(c, carry):
+            bottom = c // 2
+            row = jnp.where(bottom == 0, s + 1, rows - 1 - HALO - s) + (c % 2) * take
+            update(src, dst, across_ref, down_ref, sum_ref, row, take)
             return carry
 
-        def outside(r, carry):
-            update(src, dst, r, 1, False)
-            update(src, dst, rows - 1 - r, 1, False)
-            return carry
-
-        lax.fori_loop(0, tall // BLOCK, inside, 0)
-        lax.fori_loop(s + 1, HALO, outside, 0)
+        lax.fori_loop(0, 4, step, 0)
 
         @pl.when(ends_ref[0] == 1)
         def _():
@@ -376,19 +457,12 @@
 
     lax.fori_loop(0, SWEEPS // 2, two, 0)
 
-    lane = iota((SUB, lanes), 1)
-
     def gather(c, totals):
-        totals = list(totals)
-        for r in [c * 2, c * 2 + 1]:
-            for g in range(groups):
-                total = jnp.sum(sum_ref[r, g], axis=1, keepdims=True)
-                totals[g] = jnp.where(lane == r, total, totals[g])
-        return tuple(totals)
-
-    totals = lax.fori_loop(
-        0, tall // 2, gather, tuple(jnp.zeros((SUB, lanes), f32) for _ in range(groups))
-    )
+        pairs = [(HALO + c, c), (tall + c, tall - HALO + c)]
+        return tuple(summed_lanes(sum_ref, pairs, list(totals)))
+
+    totals = tuple(inner_ref[g * SUB : (g + 1) * SUB, :] for g in range(groups))
+    totals = lax.fori_loop(0, HALO, gather, totals)
     totals = jnp.concatenate(totals, axis=0).T[:tall]
     slot = iota((places, out_ref.shape[1]), 0)
     column = iota((places, out_ref.shape[1]), 1)
@@ -397,29 +471,21 @@
     out_ref[...] = (dot(high, back) + (dot(mid, back) + dot(low, back))) * scale
 
 
-def sweeps(scale, ends, fields, inverse, across_down, wide):
-    own = fields[1]
-    tall, places, lanes = own.shape
-    rows = tall + 2 * HALO
+def outer_sweeps(scale, ends, north, south, inverse, inner, across_down, wide):
+    first, second, total = inner
+    tall, groups, _, lanes = first.shape
+    shape = (tall + 2 * HALO, groups, SUB, lanes)
     vmem = pl.BlockSpec(memory_space=pltpu.VMEM)
     far = pl.BlockSpec(memory_space=pl.ANY)
-    grid_rows = (rows, places // SUB, SUB, lanes)
     return pl.pallas_call(
-        functools.partial(sweep_kernel, scale),
+        functools.partial(outer_kernel, scale),
         out_shape=jax.ShapeDtypeStruct((tall, wide), f32),
-        in_specs=[pl.BlockSpec(memory_space=pltpu.SMEM)] + [vmem] * (len(fields) + 1) + [far] * 2,
+        in_specs=[pl.BlockSpec(memory_space=pltpu.SMEM)] + [vmem] * 4 + [far] * 4,
         out_specs=vmem,
-        scratch_shapes=[
-            pltpu.VMEM(grid_rows, f32),
-            pltpu.VMEM(grid_rows, f32),
-            pltpu.VMEM(grid_rows, f32),
-            pltpu.VMEM(grid_rows, f32),
-            pltpu.VMEM((tall,) + grid_rows[1:], f32),
-            pltpu.SemaphoreType.DMA((2,)),
-        ],
+        scratch_shapes=[pltpu.VMEM(shape, f32)] * 5 + [pltpu.SemaphoreType.DMA((8,))],
         compiler_params=pltpu.CompilerParams(vmem_limit_bytes=VMEM_BYTES),
-        name="sweeps",
-    )(ends, *fields, inverse, *across_down)
+        name="outer_sweeps",
+    )(ends, north, south, inverse, total, first, second, *across_down)
 
 
 def from_before(x, axis, closed):
@@ -436,21 +502,21 @@
     )
 
 
-def summed(x):
-    def partner(axis, bits):
-        return lax.ppermute(x, axis, [(i, i ^ bits) for i in range(lax.axis_size(axis))])
-
-    for axis in ("lon", "lat"):
-        step, count = 1, lax.axis_size(axis)
-        while step < count:
-            if step * 4 <= count:
-                one, two, three = (partner(axis, step * k) for k in (1, 2, 3))
-                x = (x + one) + (two + three)
-                step *= 4
-            else:
-                x = x + partner(axis, step)
-                step *= 2
-    return x
+def summed(x, extra, axis):
+    size = x.shape[0]
+    count = lax.axis_size(axis)
+
+    def ahead(values, step):
+        return lax.ppermute(values, axis, [((i + step) % count, i) for i in range(count)])
+
+    sent = jnp.concatenate([x, extra], axis=0)
+    after, before, second = ahead(sent, 1), ahead(sent, count - 1), ahead(x, 2)
+    x = (x + before[:size]) + (after[:size] + second)
+    step = 4
+    while step < count:
+        x = x + ahead(x, step)
+        step *= 2
+    return x, before[size:], after[size:]
 
 
 def dealt_rows(basis, order, tall, wide, axes, count):
@@ -476,6 +542,8 @@
     count = lax.axis_size("lat") * lax.axis_size("lon")
     cells = rows_here * count
     tied = lax.optimization_barrier
+    at = lax.axis_index("lat")
+    top, bottom = at == 0, at == lax.axis_size("lat") - 1
 
     moving, last_step = dealt_rows(basis, order, tall, wide, axes, count)
     moving, basis = tied((moving, basis))
@@ -485,29 +553,31 @@
         basis, basis, (((0,), (0,)), ((), ())), preferred_element_type=f32
     )
     coef = conduct * (0.35 + 0.65 * land.astype(f32))
-    partial, coef = tied((partial, coef))
-    gram = summed(partial)
-    coef = circle(
-        coef,
-        from_after(coef[:, :HALO], "lon", True),
-        from_before(coef[:, -HALO:], "lon", True),
-        1,
-    )
+    edges = jnp.concatenate([coef[:, :HALO], coef[:, -HALO:]], axis=1).T
+    edges = jnp.pad(edges, ((0, 4), (0, width - tall)))
+    partial, before, after = summed(partial, edges, "lon")
+    coef = circle(coef, after[:HALO, :tall].T, before[HALO : 2 * HALO, :tall].T, 1)
+    ends = jnp.concatenate([coef[:HALO], coef[-HALO:]], axis=0)
+    rest = coef.shape[1] - width
+    edges = jnp.concatenate(
+        [ends[:, :width], jnp.pad(ends[:, width:], ((0, 0), (0, width - rest)))], axis=0
+    )
+    gram, before, after = summed(partial, edges, "lat")
+    before = jnp.concatenate([before[: 2 * HALO], before[2 * HALO :, :rest]], axis=1)[HALO:]
+    after = jnp.concatenate([after[: 2 * HALO], after[2 * HALO :, :rest]], axis=1)[:HALO]
     coef = jnp.concatenate(
-        [from_before(coef[-HALO:], "lat", False), coef, from_after(coef[:HALO], "lat", False)],
-        axis=0,
-    )
+        [jnp.where(top, 0.0, before), coef, jnp.where(bottom, 0.0, after)], axis=0
+    )
+    inverse = factor_inverse(gram)
     across_down = weights(coef, width)
-    inverse = factor_inverse(gram)
+    raw, inverse = tied((raw, inverse))
 
     north = from_before(raw[-HALO:], "lat", False)
     south = from_after(raw[:HALO], "lat", False)
-    own = rotate(raw, inverse)
-
-    at = lax.axis_index("lat")
-    ends = jnp.stack([at == 0, at == lax.axis_size("lat") - 1]).astype(i32)
+    inner = inner_sweeps(raw, inverse, across_down)
+    ends = jnp.stack([top, bottom]).astype(i32)
     scale = cells / (width * SWEEPS)
-    return sweeps(scale, ends, (north, own, south), inverse, across_down, wide)
+    return outer_sweeps(scale, ends, north, south, inverse, inner, across_down, wide)
 
 
 def solution(mesh):

time: 96.8 us -> 106 us (1.095)
  waiting for transfers between devices: 8.45 us -> 20.9 us
  starting transfers between devices: 35.2 us -> 27.7 us
  Pallas kernels: 48.3 us -> 50.3 us
  local copies, waits for them, and re-layouts: 1.87 us -> 2.98 us
    ppermute x7, waiting for transfers between devices: 2.82 us -> 20.9 us  [ahead(): lax.ppermute(values, axis, [((i + step) % count, i) for i in range(count)])]
    ppermute x3 -> x1, starting transfers between devices: 5.01 us -> 1.29 us  [from_after(): lax.ppermute(x, axis, [((i + 1) % count, i) for i in range(count if close...]
    pallas_call x2, Pallas kernels: 24.4 us -> 27.8 us  [the longest x1 14.5 us: inner_sweeps(): pl.pallas_call(inner_kernel, out_shape=(jax.ShapeDtypeStruct(shape, f32),...]
    ppermute x3 -> x1, waiting for transfers between devices: 2.89 us -> 0.01 us  [from_before(): lax.ppermute(x, axis, [(i, (i + 1) % count) for i in range(count if close...]
    ppermute x3 -> x1, waiting for transfers between devices: 2.74 us -> 0.01 us  [from_after(): lax.ppermute(x, axis, [((i + 1) % count, i) for i in range(count if close...]
    ppermute x3 -> x1, starting transfers between devices: 10.7 us -> 9.23 us  [from_before(): lax.ppermute(x, axis, [(i, (i + 1) % count) for i in range(count if close...]
    all_to_all x1, starting transfers between devices: 7.3 us -> 5.89 us  [per_device(): lax.all_to_all(moving, axes, split_axis=0, concat_axis=0, tiled=True)]
    pallas_call x1, Pallas kernels: 7.7 us -> 6.32 us  [weights(): pl.pallas_call(weight_kernel, out_shape=(jax.ShapeDtypeStruct(shape, f32)...]
  transfers between devices with their start and end apart: 14 -> 10, of which waited for: 5 -> 4; matrix products, arithmetic and copies ran while one was open for 3% -> 3% of each run, Pallas kernels for 18% -> 25%
where the time goes in v5:
time: 106 us; the launch traced here: 105 us
  Pallas kernels  50.3 us (47%)
  starting transfers between devices  27.7 us (26%)
  waiting for transfers between devices  20.9 us (20%)
  local copies, waits for them, and re-layouts  2.98 us (3%)
  other arithmetic  2.8 us (3%)
    ppermute x7, waiting for transfers between devices, ahead(): lax.ppermute(values, axis, [((i + step) % count, i) for i in range(count)])  20.9 us
    pallas_call x1, Pallas kernels, inner_sweeps(): pl.pallas_call(inner_kernel, out_shape=(jax.ShapeDtypeStruct(shape, f32),...  14.5 us
    pallas_call x1, Pallas kernels, outer_sweeps(): pl.pallas_call(functools.partial(outer_kernel, scale), out_shape=jax.Shap...  13.3 us
    ppermute x7, starting transfers between devices, ahead(): lax.ppermute(values, axis, [((i + step) % count, i) for i in range(count)])  11.3 us
    pallas_call x1, Pallas kernels, deal(): pl.pallas_call(functools.partial(deal_kernel, tiles_lon), out_shape=jax.S...  10.3 us
    ppermute x1, starting transfers between devices, from_before(): lax.ppermute(x, axis, [(i, (i + 1) % count) for i in range(count if close...  9.23 us
    pallas_call x1, Pallas kernels, weights(): pl.pallas_call(weight_kernel, out_shape=(jax.ShapeDtypeStruct(shape, f32)...  6.32 us
    pallas_call x1, Pallas kernels, factor_inverse(): pl.pallas_call(inverse_kernel, out_shape=jax.ShapeDtypeStruct(gram.shape,...  5.89 us
  transfers between devices with their start and end apart: 10, of which 4 were waited for; matrix products, arithmetic and copies ran while one was open for 3% of the time, Pallas kernels for 25%

profile of v5, /device:TPU:0, one launch (start us, length us, event | category | flops | bytes accessed | tf_op | source)
XLA Modules:
  0.0 105.5 jit_solution(13396685016898905050)
XLA Ops:
  0.0 0.7 convert_element_type.13
  0.7 0.1 copy.24
  0.8 0.8 copy.25
  1.7 10.3 %deal.1 = bf16[32,152,128]{2,1,0:T(8,128)(2,1)} custom-call(bf16[4096,128]{1,0:T(8,128)(2,1)} %basis_ref.1, s32[32,128]{1,0:T(8,128)} %bitcast.16), custom_call_target="tpu_custom_call" | custom-call | flops 5100273664 | bytes 2097152 | tf_op jit(solution)/shard_map/deal/pallas_call | solution.py:123
  12.0 0.5 fusion.8
  12.5 3.4 %collective-permute-start.1 = (f32[152,128]{1,0:T(8,128)S(1)}, f32[152,128]{1,0:T(8,128)S(1)}, u32[]{:S(2)}, u32[]{:S(2)}) collective-permute-start(f32[152,128]{1,0:T(8,128)S(1)} %select_maximum_fusion), channel_id=1, source_target_pairs={{1,0},{2,1},{3,2},{4,3},{5,4},{6,5},{7,6},{0,7},{9,8},{10,9},{11,1... | collective-permute-start | bytes 233480 | tf_op jit(solution)/shard_map/ppermute | solution.py:510
  15.9 0.6 collective-permute-start.2
  16.5 0.2 collective-permute-start
  16.7 5.9 %all-to-all-start = ((bf16[32,152,128]{2,1,0:T(8,128)(2,1)}), bf16[32,152,128]{2,1,0:T(8,128)(2,1)S(1)}, u32[]{:S(2)}, u32[]{:S(2)}) async-start(bf16[32,152,128]{2,1,0:T(8,128)(2,1)} %deal.1), calls=%async_computation | async-start | bytes 2490368 | tf_op jit(solution)/shard_map/all_to_all | solution.py:550
  23.0 1.8 %collective-permute-start.3 = (f32[128,128]{1,0:T(8,128)S(1)}, f32[128,128]{1,0:T(8,128)S(1)}, u32[]{:S(2)}, u32[]{:S(2)}) collective-permute-start(f32[128,128]{1,0:T(8,128)S(1)} %fusion.1), channel_id=1, source_target_pairs={{4,0},{5,1},{6,2},{7,3},{0,4},{1,5},{2,6},{3,7},{12,8},{13,9},{14,... | collective-permute-start | bytes 196616 | tf_op jit(solution)/shard_map/ppermute | solution.py:510
  24.9 0.1 copy.29
  25.1 0.1 slice.83
  25.2 0.1 copy.30
  25.3 0.1 slice.85
  25.4 6.6 %collective-permute-done.3 = f32[128,128]{1,0:T(8,128)S(1)} collective-permute-done((f32[128,128]{1,0:T(8,128)S(1)}, f32[128,128]{1,0:T(8,128)S(1)}, u32[]{:S(2)}, u32[]{:S(2)}) %collective-permute-start.3) | collective-permute-done | bytes 65568 | tf_op jit(solution)/shard_map/ppermute | solution.py:510
  32.1 4.7 %collective-permute-start.5 = (f32[168,128]{1,0:T(8,128)S(1)}, f32[168,128]{1,0:T(8,128)S(1)}, u32[]{:S(2)}, u32[]{:S(2)}) collective-permute-start(f32[168,128]{1,0:T(8,128)S(1)} %pad_maximum_fusion), channel_id=1, source_target_pairs={{8,0},{16,8},{24,16},{0,24},{9,1},{17,9},{25,17},{1,25},{10,2},{18... | collective-permute-start | bytes 258056 | tf_op jit(solution)/shard_map/ppermute | solution.py:510
  36.8 0.6 add_convert_fusion.ends_ref
  37.4 0.1 copy.31
  37.6 0.7 collective-permute-start.6
  38.3 7.3 %collective-permute-done.5 = f32[168,128]{1,0:T(8,128)S(1)} collective-permute-done((f32[168,128]{1,0:T(8,128)S(1)}, f32[168,128]{1,0:T(8,128)S(1)}, u32[]{:S(2)}, u32[]{:S(2)}) %collective-permute-start.5) | collective-permute-done | bytes 86048 | tf_op jit(solution)/shard_map/ppermute | solution.py:510
  45.5 6.0 %collective-permute-done.4 = f32[168,128]{1,0:T(8,128)S(1)} collective-permute-done((f32[168,128]{1,0:T(8,128)S(1)}, f32[168,128]{1,0:T(8,128)S(1)}, u32[]{:S(2)}, u32[]{:S(2)}) %collective-permute-start.4) | collective-permute-done | bytes 86048 | tf_op jit(solution)/shard_map/ppermute | solution.py:510
  51.6 0.6 select_maximum_fusion.1.coef_ref
  52.3 6.3 %weights.1 = (f32[52,19,8,128]{3,2,1,0:T(8,128)}, f32[52,19,8,128]{3,2,1,0:T(8,128)}) custom-call(f32[64,256]{1,0:T(8,128)} %select_maximum_fusion.1.coef_ref), custom_call_target="tpu_custom_call" | custom-call | flops 101171200 | bytes 8093696 | tf_op jit(solution)/shard_map/weights/pallas_call | solution.py:237
  58.6 1.0 collective-permute-done.6
  59.6 0.6 fusion.gram_ref
  60.2 5.9 %factor_inverse.1.inverse_ref = f32[128,128]{1,0:T(8,128)} custom-call(f32[128,128]{1,0:T(8,128)} %fusion.gram_ref), custom_call_target="tpu_custom_call" | custom-call | flops 10737418240 | bytes 131072 | tf_op jit(solution)/shard_map/factor_inverse/pallas_call | solution.py:189
  66.2 1.3 %collective-permute-start.8 = (bf16[10,152,128]{2,1,0:T(8,128)(2,1)S(1)}, bf16[10,152,128]{2,1,0:T(8,128)(2,1)S(1)}, u32[]{:S(2)}, u32[]{:S(2)}) collective-permute-start(bf16[10,152,128]{2,1,0:T(8,128)(2,1)S(1)} %get-tuple-element.23), channel_id=1, source_target_pairs={{8,0},{16,8},{24,16},{9,1},{17,9},{25,17},{10,2},{18,10},{26,18},{... | collective-permute-start | bytes 1167368 | tf_op jit(solution)/shard_map/ppermute | solution.py:500
  67.5 9.2 %collective-permute-start.7 = (bf16[10,152,128]{2,1,0:T(8,128)(2,1)S(1)}, bf16[10,152,128]{2,1,0:T(8,128)(2,1)S(1)}, u32[]{:S(2)}, u32[]{:S(2)}) collective-permute-start(bf16[10,152,128]{2,1,0:T(8,128)(2,1)S(1)} %get-tuple-element.24), channel_id=1, source_target_pairs={{0,8},{8,16},{16,24},{1,9},{9,17},{17,25},{2,10},{10,18},{18,26},{... | collective-permute-start | bytes 1167368 | tf_op jit(solution)/shard_map/ppermute | solution.py:493
  76.7 14.5 %inner_sweeps.1 = (f32[32,19,8,128]{3,2,1,0:T(8,128)}, f32[32,19,8,128]{3,2,1,0:T(8,128)}, f32[152,128]{1,0:T(8,128)}) custom-call(bf16[32,152,128]{2,1,0:T(8,128)(2,1)} %copy-done.1, f32[128,128]{1,0:T(8,128)} %factor_inverse.1.inverse_ref, f32[52,19,8,128]{3,2,1,0:T(8,128)} %get-tuple-element.18.across_hbm, f32[52,19,8,128]{3,2,1,0:T(8,128)} %get-tuple-element.19.down_hbm), custom_call_target="tpu_custom_call" | custom-call | flops 12000000000 | bytes 4980736 | tf_op jit(solution)/shard_map/inner_sweeps/pallas_call | solution.py:372
  91.3 0.7 copy-done.2
  92.0 0.2 copy-done.3
  92.2 13.3 %outer_sweeps.1 = f32[32,128]{1,0:T(8,128)} custom-call(s32[2]{0:T(128)} %add_convert_fusion.ends_ref, bf16[10,152,128]{2,1,0:T(8,128)(2,1)} %copy-done.3, bf16[10,152,128]{2,1,0:T(8,128)(2,1)} %copy-done.2, f32[128,128]{1,0:T(8,128)} %factor_inverse.1.inverse_ref, f32[152,128]{1,0:T(8,128)} %get-tuple-element.20.inner_ref, ...), custom_call_target="tpu_custom_call" | custom-call | tf_op jit(solution)/shard_map/outer_sweeps/pallas_call | solution.py:480
  (39 shorter events, 0.8 us)
Async XLA Ops:
  1.7 10.3 %copy-start = (bf16[4096,128]{1,0:T(8,128)(2,1)S(1)}, bf16[4096,128]{1,0:T(8,128)(2,1)}, u32[]{:S(2)}) copy-start(bf16[4096,128]{1,0:T(8,128)(2,1)} %basis_ref.1) | copy-start | bytes 3145732
  12.5 10.2 %collective-permute-start.1 = (f32[152,128]{1,0:T(8,128)S(1)}, f32[152,128]{1,0:T(8,128)S(1)}, u32[]{:S(2)}, u32[]{:S(2)}) collective-permute-start(f32[152,128]{1,0:T(8,128)S(1)} %select_maximum_fusion), channel_id=1, source_target_pairs={{1,0},{2,1},{3,2},{4,3},{5,4},{6,5},{7,6},{0,7},{9,8},{10,9},{11,1... | collective-permute-start | bytes 233480 | tf_op jit(solution)/shard_map/ppermute | solution.py:510
  15.9 6.8 %collective-permute-start.2 = (f32[128,128]{1,0:T(8,128)S(1)}, f32[128,128]{1,0:T(8,128)S(1)}, u32[]{:S(2)}, u32[]{:S(2)}) collective-permute-start(f32[128,128]{1,0:T(8,128)S(1)} %fusion.8), channel_id=1, source_target_pairs={{2,0},{3,1},{4,2},{5,3},{6,4},{7,5},{0,6},{1,7},{10,8},{11,9},{12,... | collective-permute-start | bytes 196616 | tf_op jit(solution)/shard_map/ppermute | solution.py:510
  16.5 6.2 %collective-permute-start = (f32[152,128]{1,0:T(8,128)S(1)}, f32[152,128]{1,0:T(8,128)S(1)}, u32[]{:S(2)}, u32[]{:S(2)}) collective-permute-start(f32[152,128]{1,0:T(8,128)S(1)} %select_maximum_fusion), channel_id=1, source_target_pairs={{7,0},{0,1},{1,2},{2,3},{3,4},{4,5},{5,6},{6,7},{15,8},{8,9},{9,10... | collective-permute-start | bytes 233480 | tf_op jit(solution)/shard_map/ppermute | solution.py:510
  16.7 49.4 %all-to-all-start = ((bf16[32,152,128]{2,1,0:T(8,128)(2,1)}), bf16[32,152,128]{2,1,0:T(8,128)(2,1)S(1)}, u32[]{:S(2)}, u32[]{:S(2)}) async-start(bf16[32,152,128]{2,1,0:T(8,128)(2,1)} %deal.1), calls=%async_computation | async-start | bytes 2490368 | tf_op jit(solution)/shard_map/all_to_all | solution.py:550
  23.0 9.1 %collective-permute-start.3 = (f32[128,128]{1,0:T(8,128)S(1)}, f32[128,128]{1,0:T(8,128)S(1)}, u32[]{:S(2)}, u32[]{:S(2)}) collective-permute-start(f32[128,128]{1,0:T(8,128)S(1)} %fusion.1), channel_id=1, source_target_pairs={{4,0},{5,1},{6,2},{7,3},{0,4},{1,5},{2,6},{3,7},{12,8},{13,9},{14,... | collective-permute-start | bytes 196616 | tf_op jit(solution)/shard_map/ppermute | solution.py:510
  32.1 13.4 %collective-permute-start.5 = (f32[168,128]{1,0:T(8,128)S(1)}, f32[168,128]{1,0:T(8,128)S(1)}, u32[]{:S(2)}, u32[]{:S(2)}) collective-permute-start(f32[168,128]{1,0:T(8,128)S(1)} %pad_maximum_fusion), channel_id=1, source_target_pairs={{8,0},{16,8},{24,16},{0,24},{9,1},{17,9},{25,17},{1,25},{10,2},{18... | collective-permute-start | bytes 258056 | tf_op jit(solution)/shard_map/ppermute | solution.py:510
  36.8 14.8 %collective-permute-start.4 = (f32[168,128]{1,0:T(8,128)S(1)}, f32[168,128]{1,0:T(8,128)S(1)}, u32[]{:S(2)}, u32[]{:S(2)}) collective-permute-start(f32[168,128]{1,0:T(8,128)S(1)} %pad_maximum_fusion), channel_id=1, source_target_pairs={{24,0},{0,8},{8,16},{16,24},{25,1},{1,9},{9,17},{17,25},{26,2},{2,... | collective-permute-start | bytes 258056 | tf_op jit(solution)/shard_map/ppermute | solution.py:510
  37.6 22.0 %collective-permute-start.6 = (f32[128,128]{1,0:T(8,128)S(1)}, f32[128,128]{1,0:T(8,128)S(1)}, u32[]{:S(2)}, u32[]{:S(2)}) collective-permute-start(f32[128,128]{1,0:T(8,128)S(1)} %add.38), channel_id=1, source_target_pairs={{16,0},{24,8},{0,16},{8,24},{17,1},{25,9},{1,17},{9,25},{18,2},{26... | collective-permute-start | bytes 196616 | tf_op jit(solution)/shard_map/ppermute | solution.py:510
  66.1 10.6 %copy-start.1 = (bf16[32,152,128]{2,1,0:T(8,128)(2,1)}, bf16[32,152,128]{2,1,0:T(8,128)(2,1)S(1)}, u32[]{:S(2)}) copy-start(bf16[32,152,128]{2,1,0:T(8,128)(2,1)S(1)} %all-to-all-done.own_ref) | copy-start | bytes 3735556
  66.2 25.1 %collective-permute-start.8 = (bf16[10,152,128]{2,1,0:T(8,128)(2,1)S(1)}, bf16[10,152,128]{2,1,0:T(8,128)(2,1)S(1)}, u32[]{:S(2)}, u32[]{:S(2)}) collective-permute-start(bf16[10,152,128]{2,1,0:T(8,128)(2,1)S(1)} %get-tuple-element.23), channel_id=1, source_target_pairs={{8,0},{16,8},{24,16},{9,1},{17,9},{25,17},{10,2},{18,10},{26,18},{... | collective-permute-start | bytes 1167368 | tf_op jit(solution)/shard_map/ppermute | solution.py:500
  67.5 23.8 %collective-permute-start.7 = (bf16[10,152,128]{2,1,0:T(8,128)(2,1)S(1)}, bf16[10,152,128]{2,1,0:T(8,128)(2,1)S(1)}, u32[]{:S(2)}, u32[]{:S(2)}) collective-permute-start(bf16[10,152,128]{2,1,0:T(8,128)(2,1)S(1)} %get-tuple-element.24), channel_id=1, source_target_pairs={{0,8},{8,16},{16,24},{1,9},{9,17},{17,25},{2,10},{10,18},{18,26},{... | collective-permute-start | bytes 1167368 | tf_op jit(solution)/shard_map/ppermute | solution.py:493
  91.3 0.7 copy-start.2
  91.3 0.9 copy-start.3

commit v6 on v5

--- a/solution.py
+++ b/solution.py
@@ -12,6 +12,7 @@
 LANES = 128
 SUB = 8
 ONE_HOT = 1024
+TILES = 4
 BLOCK = 4
 VMEM_BYTES = 56 * 1024 * 1024
 
@@ -49,13 +50,13 @@
     return jnp.swapaxes(around, axis, axis + 1).reshape(shape)
 
 
-def deal_kernel(tiles_lon, basis_ref, order_ref, out_ref, slot_ref):
+def deal_kernel(tiles_lon, first, count, basis_ref, order_ref, *refs):
+    out_ref, slot_ref, ready_ref, sems = refs[-4:]
     rows, width = basis_ref.shape
     parts = rows // ONE_HOT
     tiles, places, _ = out_ref.shape
     wide = order_ref.shape[1]
     groups = places // SUB
-    lane = iota((LANES, LANES), 1)
     stacked = jnp.concatenate(
         [basis_ref[q * ONE_HOT : (q + 1) * ONE_HOT, :] for q in range(parts)], axis=1
     )
@@ -84,52 +85,68 @@
         high = high + dot((source >> 6).astype(f32).astype(bf16), hot)
     slot_ref[...] = (high * 64.0 + low).astype(i32)
 
-    take = 4
-
-    def step(c, carry):
-        marks, part = [], []
+    take = TILES
+    steps = count // take
+
+    def leave(c):
+        return pltpu.make_async_copy(
+            ready_ref.at[pl.ds(c * take, take)],
+            out_ref.at[pl.ds(first + c * take, take)],
+            sems.at[c],
+        )
+
+    lane = iota((take * places, LANES), 1)
+    for c in range(steps):
+        wanted = []
         for h in range(take):
-            order = slot_ref[pl.ds(c * take + h, 1), :]
-            order = jnp.broadcast_to(order, (LANES, padded)).T[:places]
-            within = order & (ONE_HOT - 1)
-            part.append(order - within)
-            lane = iota((places, LANES), 1)
-            marks.append(
-                jnp.concatenate(
-                    [
-                        (within == lane + b * LANES).astype(f32)
-                        for b in range(ONE_HOT // LANES)
-                    ],
-                    axis=1,
-                )
+            order = slot_ref[first + c * take + h : first + c * take + h + 1, :]
+            wanted.append(jnp.broadcast_to(order, (LANES, padded)).T[:places])
+        wanted = jnp.concatenate(wanted, axis=0)
+        within = wanted & (ONE_HOT - 1)
+        part = wanted - within
+        marks = [
+            (within == lane + b * LANES).astype(f32).astype(bf16)
+            for b in range(ONE_HOT // LANES)
+        ]
+        found = dot(jnp.concatenate(marks, axis=1), stacked)
+        picked = found[:, :width]
+        for q in range(1, parts):
+            picked = jnp.where(
+                part == q * ONE_HOT, found[:, q * width : (q + 1) * width], picked
             )
-        found = dot(jnp.concatenate(marks, axis=0).astype(bf16), stacked)
         for h in range(take):
-            here = found[h * places : (h + 1) * places]
-            picked = here[:, :width]
-            for q in range(1, parts):
-                chosen = part[h] == q * ONE_HOT
-                picked = jnp.where(chosen, here[:, q * width : (q + 1) * width], picked)
-            out_ref[c * take + h] = picked.astype(bf16)
-        return carry
-
-    lax.fori_loop(0, tiles // take, step, 0)
-
-
-def deal(basis, order, tiles_lon, wide):
+            ready_ref[c * take + h] = picked[h * places : (h + 1) * places].astype(bf16)
+        leave(c).start()
+    for c in range(steps):
+        leave(c).wait()
+
+
+def deal(basis, order, tiles_lon, wide, first, count, so_far):
     rows, width = basis.shape
     tiles = rows // wide
     places = slots(wide)
+    vmem = pl.BlockSpec(memory_space=pltpu.VMEM)
+    far = pl.BlockSpec(memory_space=pl.ANY)
+    before = [] if so_far is None else [so_far]
     return pl.pallas_call(
-        functools.partial(deal_kernel, tiles_lon),
+        functools.partial(deal_kernel, tiles_lon, first, count),
         out_shape=jax.ShapeDtypeStruct((tiles, places, width), bf16),
-        scratch_shapes=[pltpu.VMEM((tiles, -(-places // LANES) * LANES), i32)],
+        in_specs=[vmem, vmem] + [far] * len(before),
+        out_specs=far,
+        input_output_aliases={2: 0} if before else {},
+        scratch_shapes=[
+            pltpu.VMEM((tiles, -(-places // LANES) * LANES), i32),
+            pltpu.VMEM((count, places, width), bf16),
+            pltpu.SemaphoreType.DMA((count // TILES,)),
+        ],
         compiler_params=pltpu.CompilerParams(vmem_limit_bytes=VMEM_BYTES),
         cost_estimate=pl.CostEstimate(
-            flops=2 * tiles * places * rows * width, bytes_accessed=4 * rows * width, transcendentals=0
+            flops=2 * count * places * rows * width,
+            bytes_accessed=4 * rows * width,
+            transcendentals=0,
         ),
-        name="deal",
-    )(basis, order.reshape(tiles, wide))
+        name=f"deal_{first}",
+    )(basis, order.reshape(tiles, wide), *before)
 
 
 def inverse_kernel(gram_ref, out_ref):
@@ -247,15 +264,17 @@
 
 
 def rotation(inverse):
-    return jnp.concatenate(split3(inverse.T), axis=1)
+    high, mid, low = split3(inverse.T)
+    return jnp.concatenate(
+        [jnp.concatenate([high, low], axis=1), jnp.concatenate([mid, jnp.zeros_like(mid)], axis=1)],
+        axis=0,
+    )
 
 
 def rotated(raw, turn):
-    take, places, lanes = raw.shape
-    raw = raw.astype(f32).reshape(take * places, lanes).astype(bf16)
-    parts = dot(raw, turn)
-    field = parts[:, :lanes] + (parts[:, lanes : 2 * lanes] + parts[:, 2 * lanes :])
-    return field.astype(bf16).astype(f32).reshape(take, places, lanes)
+    lanes = raw.shape[1]
+    parts = dot(jnp.concatenate([raw, raw], axis=1), turn)
+    return (parts[:, :lanes] + parts[:, lanes:]).astype(bf16).astype(f32)
 
 
 def update(src, dst, across, down, sums, row, take):
@@ -323,10 +342,11 @@
     for fetch in fetches:
         fetch.start()
     turn = rotation(inverse_ref[...])
-    take = 8
+    take = 4
+    cells = take * groups * SUB
 
     def fill(c, carry):
-        field = rotated(own_ref[pl.ds(c * take, take)], turn)
+        field = rotated(own_ref[pl.ds(pl.multiple_of(c * cells, 16), cells), :], turn)
         first_ref[pl.ds(c * take, take)] = field.reshape(take, groups, SUB, lanes)
         return carry
 
@@ -356,16 +376,17 @@
     lax.fori_loop(0, SWEEPS // 2, two, 0)
 
     def gather(c, totals):
-        rows = [(c * 2 + h, c * 2 + h) for h in range(2)]
+        rows = [(c * 4 + h, c * 4 + h) for h in range(4)]
         return tuple(summed_lanes(sum_ref, rows, list(totals)))
 
     zeros = tuple(jnp.zeros((SUB, lanes), f32) for _ in range(groups))
-    totals = lax.fori_loop(0, tall // 2, gather, zeros)
+    totals = lax.fori_loop(0, tall // 4, gather, zeros)
     total_ref[...] = jnp.concatenate(totals, axis=0)
 
 
 def inner_sweeps(own, inverse, across_down):
     tall, places, lanes = own.shape
+    own = own.reshape(tall * places, lanes)
     vmem = pl.BlockSpec(memory_space=pltpu.VMEM)
     far = pl.BlockSpec(memory_space=pl.ANY)
     shape = (tall, places // SUB, SUB, lanes)
@@ -421,15 +442,17 @@
         fetch.start()
     sum_ref[...] = jnp.zeros_like(sum_ref)
     turn = rotation(inverse_ref[...])
-    take = 5
+    take = 2
+    cells = take * places
 
     def fill(c, carry):
         for source, offset in ((north_ref, 0), (south_ref, HALO + tall)):
-            field = rotated(source[pl.ds(c * take, take)], turn)
+            field = rotated(source[pl.ds(pl.multiple_of(c * cells, 16), cells), :], turn)
             first_ref[pl.ds(offset + c * take, take)] = field.reshape(take, groups, SUB, lanes)
         return carry
 
     lax.fori_loop(0, HALO // take, fill, 0)
+    take = HALO // 2
     for fetch in fetches:
         fetch.wait()
 
@@ -458,11 +481,13 @@
     lax.fori_loop(0, SWEEPS // 2, two, 0)
 
     def gather(c, totals):
-        pairs = [(HALO + c, c), (tall + c, tall - HALO + c)]
+        pairs = []
+        for row in (2 * c, 2 * c + 1):
+            pairs += [(HALO + row, row), (tall + row, tall - HALO + row)]
         return tuple(summed_lanes(sum_ref, pairs, list(totals)))
 
     totals = tuple(inner_ref[g * SUB : (g + 1) * SUB, :] for g in range(groups))
-    totals = lax.fori_loop(0, HALO, gather, totals)
+    totals = lax.fori_loop(0, HALO // 2, gather, totals)
     totals = jnp.concatenate(totals, axis=0).T[:tall]
     slot = iota((places, out_ref.shape[1]), 0)
     column = iota((places, out_ref.shape[1]), 1)
@@ -475,6 +500,7 @@
     first, second, total = inner
     tall, groups, _, lanes = first.shape
     shape = (tall + 2 * HALO, groups, SUB, lanes)
+    north, south = (x.reshape(-1, lanes) for x in (north, south))
     vmem = pl.BlockSpec(memory_space=pltpu.VMEM)
     far = pl.BlockSpec(memory_space=pl.ANY)
     return pl.pallas_call(
@@ -502,37 +528,25 @@
     )
 
 
-def summed(x, extra, axis):
+def ahead(values, axis, step):
+    count = lax.axis_size(axis)
+    return lax.ppermute(values, axis, [((i + step) % count, i) for i in range(count)])
+
+
+def neighbours(x, extra, axis):
     size = x.shape[0]
-    count = lax.axis_size(axis)
-
-    def ahead(values, step):
-        return lax.ppermute(values, axis, [((i + step) % count, i) for i in range(count)])
-
     sent = jnp.concatenate([x, extra], axis=0)
-    after, before, second = ahead(sent, 1), ahead(sent, count - 1), ahead(x, 2)
+    after, before, second = ahead(sent, axis, 1), ahead(sent, axis, -1), ahead(x, axis, 2)
     x = (x + before[:size]) + (after[:size] + second)
+    return x, before[size:], after[size:]
+
+
+def rest_of_ring(x, axis):
     step = 4
-    while step < count:
-        x = x + ahead(x, step)
+    while step < lax.axis_size(axis):
+        x = x + ahead(x, axis, step)
         step *= 2
-    return x, before[size:], after[size:]
-
-
-def dealt_rows(basis, order, tall, wide, axes, count):
-    width = basis.shape[1]
-    share = order.size // count
-    if share == wide:
-        moving = deal(basis, order, lax.axis_size("lon"), wide)
-        return moving, lambda arrived: arrived
-
-    def last_step(arrived):
-        own = arrived.reshape(tall, wide, width)
-        left = from_before(own[:, -HALO:], "lon", True)
-        right = from_after(own[:, :HALO], "lon", True)
-        return circle(own, right, left, 1)
-
-    return basis[order], last_step
+    return x
 
 
 def per_device(basis, order, land, conduct):
@@ -544,25 +558,50 @@
     tied = lax.optimization_barrier
     at = lax.axis_index("lat")
     top, bottom = at == 0, at == lax.axis_size("lat") - 1
-
-    moving, last_step = dealt_rows(basis, order, tall, wide, axes, count)
-    moving, basis = tied((moving, basis))
-    raw = last_step(lax.all_to_all(moving, axes, split_axis=0, concat_axis=0, tiled=True))
+    whole_rows = rows_here // count == wide
+
+    def dealt(part, so_far):
+        if not whole_rows:
+            return basis[order] if so_far is None else so_far
+        bounds = [0, 3 * tall // 8, 5 * tall // 8, tall]
+        return deal(
+            basis, order, lax.axis_size("lon"), wide, bounds[part],
+            bounds[part + 1] - bounds[part], so_far,
+        )
 
     partial = lax.dot_general(
         basis, basis, (((0,), (0,)), ((), ())), preferred_element_type=f32
     )
     coef = conduct * (0.35 + 0.65 * land.astype(f32))
-    edges = jnp.concatenate([coef[:, :HALO], coef[:, -HALO:]], axis=1).T
-    edges = jnp.pad(edges, ((0, 4), (0, width - tall)))
-    partial, before, after = summed(partial, edges, "lon")
-    coef = circle(coef, after[:HALO, :tall].T, before[HALO : 2 * HALO, :tall].T, 1)
+    edges = jnp.pad(
+        jnp.concatenate([coef[:, :HALO], coef[:, -HALO:]], axis=1),
+        ((0, 0), (0, width - 2 * HALO)),
+    )
+    partial, edges, basis = tied((partial, edges, basis))
+    moving = dealt(0, None)
+    partial, before, after = neighbours(partial, edges, "lon")
+    partial, moving = tied((partial, moving))
+    moving = dealt(1, moving)
+    partial = rest_of_ring(partial, "lon")
+    coef = circle(coef, after[:, :HALO], before[:, HALO : 2 * HALO], 1)
     ends = jnp.concatenate([coef[:HALO], coef[-HALO:]], axis=0)
     rest = coef.shape[1] - width
     edges = jnp.concatenate(
         [ends[:, :width], jnp.pad(ends[:, width:], ((0, 0), (0, width - rest)))], axis=0
     )
-    gram, before, after = summed(partial, edges, "lat")
+    partial, edges, moving = tied((partial, edges, moving))
+    moving = dealt(2, moving)
+    partial, before, after = neighbours(partial, edges, "lat")
+    gram = rest_of_ring(partial, "lat")
+    gram, before, after, moving = tied((gram, before, after, moving))
+
+    raw = lax.all_to_all(moving, axes, split_axis=0, concat_axis=0, tiled=True)
+    if not whole_rows:
+        raw = raw.reshape(tall, wide, width)
+        left = from_before(raw[:, -HALO:], "lon", True)
+        right = from_after(raw[:, :HALO], "lon", True)
+        raw = circle(raw, right, left, 1)
+
     before = jnp.concatenate([before[: 2 * HALO], before[2 * HALO :, :rest]], axis=1)[HALO:]
     after = jnp.concatenate([after[: 2 * HALO], after[2 * HALO :, :rest]], axis=1)[:HALO]
     coef = jnp.concatenate(
@@ -570,12 +609,12 @@
     )
     inverse = factor_inverse(gram)
     across_down = weights(coef, width)
-    raw, inverse = tied((raw, inverse))
+    ends = jnp.stack([top, bottom]).astype(i32)
+    raw, inverse, across_down, ends = tied((raw, inverse, across_down, ends))
 
     north = from_before(raw[-HALO:], "lat", False)
     south = from_after(raw[:HALO], "lat", False)
     inner = inner_sweeps(raw, inverse, across_down)
-    ends = jnp.stack([top, bottom]).astype(i32)
     scale = cells / (width * SWEEPS)
     return outer_sweeps(scale, ends, north, south, inverse, inner, across_down, wide)
 

time: 106 us -> 99.8 us (0.942)
  starting transfers between devices: 27.7 us -> 19.3 us
  matrix products: 0.47 us -> 2.05 us
    all_to_all x1, waiting for transfers between devices: 0.01 us -> 16.7 us  [per_device(): raw = lax.all_to_all(moving, axes, split_axis=0, concat_axis=0, tiled=True)]
    ppermute x7, waiting for transfers between devices: 20.9 us -> 5 us  [ahead(): lax.ppermute(values, axis, [((i + step) % count, i) for i in range(count)])]
    ppermute x1, starting transfers between devices: 9.23 us -> 4.57 us  [from_before(): lax.ppermute(x, axis, [(i, (i + 1) % count) for i in range(count if close...]
    all_to_all x1, starting transfers between devices: 5.89 us -> 3.08 us  [per_device(): raw = lax.all_to_all(moving, axes, split_axis=0, concat_axis=0, tiled=True)]
    pallas_call x1 -> x3, Pallas kernels: 10.3 us -> 12.1 us  [deal(): pl.pallas_call(functools.partial(deal_kernel, tiles_lon, first, count), o...]
    dot_general x1, matrix products: 0.47 us -> 2.05 us  [per_device(): lax.dot_general(basis, basis, (((0,), (0,)), ((), ())), preferred_element...]
  transfers between devices with their start and end apart: 10 -> 10, of which waited for: 4 -> 3; matrix products, arithmetic and copies ran while one was open for 3% -> 2% of each run, Pallas kernels for 25% -> 35%
where the time goes in v6:
time: 99.8 us; the launch traced here: 99.3 us
  Pallas kernels  51.1 us (51%)
  waiting for transfers between devices  21.7 us (22%)
  starting transfers between devices  19.3 us (19%)
  other arithmetic  2.85 us (3%)
  matrix products  2.05 us (2%)
  local copies, waits for them, and re-layouts  2 us (2%)
    all_to_all x1, waiting for transfers between devices, per_device(): raw = lax.all_to_all(moving, axes, split_axis=0, concat_axis=0, tiled=True)  16.7 us
    pallas_call x1, Pallas kernels, inner_sweeps(): pl.pallas_call(inner_kernel, out_shape=(jax.ShapeDtypeStruct(shape, f32),...  13.9 us
    pallas_call x1, Pallas kernels, outer_sweeps(): pl.pallas_call(functools.partial(outer_kernel, scale), out_shape=jax.Shap...  12.9 us
    pallas_call x3, Pallas kernels, deal(): pl.pallas_call(functools.partial(deal_kernel, tiles_lon, first, count), o...  12.1 us
    ppermute x7, starting transfers between devices, ahead(): lax.ppermute(values, axis, [((i + step) % count, i) for i in range(count)])  10.3 us
    pallas_call x1, Pallas kernels, weights(): pl.pallas_call(weight_kernel, out_shape=(jax.ShapeDtypeStruct(shape, f32)...  6.32 us
    pallas_call x1, Pallas kernels, factor_inverse(): pl.pallas_call(inverse_kernel, out_shape=jax.ShapeDtypeStruct(gram.shape,...  5.89 us
    ppermute x7, waiting for transfers between devices, ahead(): lax.ppermute(values, axis, [((i + step) % count, i) for i in range(count)])  5 us
  transfers between devices with their start and end apart: 10, of which 3 were waited for; matrix products, arithmetic and copies ran while one was open for 2% of the time, Pallas kernels for 35%

profile of v6, /device:TPU:0, one launch (start us, length us, event | category | flops | bytes accessed | tf_op | source)
XLA Modules:
  0.0 99.3 jit_solution(8641732619157201361)
XLA Ops:
  0.0 0.7 add_multiply_fusion
  0.8 2.1 %fusion.8 = f32[128,128]{1,0:T(8,128)S(1)} fusion(bf16[4096,128]{1,0:T(8,128)(2,1)} %basis_ref.2), kind=kOutput, calls=%fused_computation.32 | convolution fusion | flops 134217728 | bytes 1114112 | tf_op jit(solution)/shard_map/dot_general | solution.py:572
  2.9 3.9 %collective-permute-start.2 = (f32[128,128]{1,0:T(8,128)S(1)}, f32[128,128]{1,0:T(8,128)S(1)}, u32[]{:S(2)}, u32[]{:S(2)}) collective-permute-start(f32[128,128]{1,0:T(8,128)S(1)} %fusion.8), channel_id=1, source_target_pairs={{2,0},{3,1},{4,2},{5,3},{6,4},{7,5},{0,6},{1,7},{10,8},{11,9},{12,... | collective-permute-start | bytes 196616 | tf_op jit(solution)/shard_map/ppermute | solution.py:533
  6.9 0.5 collective-permute-start
  7.4 4.2 %deal_0.1.refs_0_ = bf16[32,152,128]{2,1,0:T(8,128)(2,1)} custom-call(bf16[4096,128]{1,0:T(8,128)(2,1)} %basis_ref.2, s32[32,128]{1,0:T(8,128)} %bitcast.16), custom_call_target="tpu_custom_call" | custom-call | flops 1912602624 | bytes 2097152 | tf_op jit(solution)/shard_map/deal_0/pallas_call | solution.py:131
  11.9 0.1 reshape.23
  12.0 0.1 copy.8
  12.2 0.1 slice.83
  12.3 0.1 copy.9
  12.4 0.1 slice.85
  12.6 3.6 %deal_12.1.refs_0_ = bf16[32,152,128]{2,1,0:T(8,128)(2,1)} custom-call(bf16[4096,128]{1,0:T(8,128)(2,1)} %basis_ref.2, s32[32,128]{1,0:T(8,128)} %bitcast.17, bf16[32,152,128]{2,1,0:T(8,128)(2,1)} %deal_0.1.refs_0_), custom_call_target="tpu_custom_call", output_to_operand_aliasing={{}: (2, {})} | custom-call | flops 1275068416 | bytes 2097152 | tf_op jit(solution)/shard_map/deal_12/pallas_call | solution.py:131
  16.2 1.1 %collective-permute-start.3 = (f32[128,128]{1,0:T(8,128)S(1)}, f32[128,128]{1,0:T(8,128)S(1)}, u32[]{:S(2)}, u32[]{:S(2)}) collective-permute-start(f32[128,128]{1,0:T(8,128)S(1)} %fusion.1), channel_id=1, source_target_pairs={{4,0},{5,1},{6,2},{7,3},{0,4},{1,5},{2,6},{3,7},{12,8},{13,9},{14,... | collective-permute-start | bytes 196616 | tf_op jit(solution)/shard_map/ppermute | solution.py:533
  17.4 3.7 %collective-permute-done.3 = f32[128,128]{1,0:T(8,128)S(1)} collective-permute-done((f32[128,128]{1,0:T(8,128)S(1)}, f32[128,128]{1,0:T(8,128)S(1)}, u32[]{:S(2)}, u32[]{:S(2)}) %collective-permute-start.3) | collective-permute-done | bytes 65568 | tf_op jit(solution)/shard_map/ppermute | solution.py:533
  21.1 2.7 %collective-permute-start.6 = (f32[128,128]{1,0:T(8,128)S(1)}, f32[128,128]{1,0:T(8,128)S(1)}, u32[]{:S(2)}, u32[]{:S(2)}) collective-permute-start(f32[128,128]{1,0:T(8,128)S(1)} %add.38), channel_id=1, source_target_pairs={{16,0},{24,8},{0,16},{8,24},{17,1},{25,9},{1,17},{9,25},{18,2},{26... | collective-permute-start | bytes 196616 | tf_op jit(solution)/shard_map/ppermute | solution.py:533
  23.7 1.4 %collective-permute-start.5 = (f32[168,128]{1,0:T(8,128)S(1)}, f32[168,128]{1,0:T(8,128)S(1)}, u32[]{:S(2)}, u32[]{:S(2)}) collective-permute-start(f32[168,128]{1,0:T(8,128)S(1)} %constant_dynamic-update-slice_fusion.2), channel_id=1, source_target_pairs={{8,0},{16,8},{24,16},{0,24},{9,1},{17,9},{25,17},{1,25},{10,2},{18... | collective-permute-start | bytes 258056 | tf_op jit(solution)/shard_map/ppermute | solution.py:533
  25.1 0.7 collective-permute-start.4
  25.8 4.3 %deal_20.1 = bf16[32,152,128]{2,1,0:T(8,128)(2,1)} custom-call(bf16[4096,128]{1,0:T(8,128)(2,1)} %basis_ref.2, s32[32,128]{1,0:T(8,128)} %bitcast.18, bf16[32,152,128]{2,1,0:T(8,128)(2,1)} %deal_12.1.refs_0_), custom_call_target="tpu_custom_call", output_to_operand_aliasing={{}: (2, {})} | custom-call | flops 1912602624 | bytes 2097152 | tf_op jit(solution)/shard_map/deal_20/pallas_call | solution.py:131
  30.1 1.3 %collective-permute-done.4 = f32[168,128]{1,0:T(8,128)S(1)} collective-permute-done((f32[168,128]{1,0:T(8,128)S(1)}, f32[168,128]{1,0:T(8,128)S(1)}, u32[]{:S(2)}, u32[]{:S(2)}) %collective-permute-start.4) | collective-permute-done | bytes 86048 | tf_op jit(solution)/shard_map/ppermute | solution.py:533
  31.4 0.6 fusion.gram_ref
  32.1 3.1 %all-to-all-start = ((bf16[32,152,128]{2,1,0:T(8,128)(2,1)}), bf16[32,152,128]{2,1,0:T(8,128)(2,1)S(1)}, u32[]{:S(2)}, u32[]{:S(2)}) async-start(bf16[32,152,128]{2,1,0:T(8,128)(2,1)} %deal_20.1), calls=%async_computation | async-start | bytes 2490368 | tf_op jit(solution)/shard_map/all_to_all | solution.py:598
  35.2 0.6 add_convert_fusion.ends_ref
  35.8 0.1 copy.10
  36.1 0.6 select_maximum_fusion.coef_ref
  36.7 6.3 %weights.1 = (f32[52,19,8,128]{3,2,1,0:T(8,128)}, f32[52,19,8,128]{3,2,1,0:T(8,128)}) custom-call(f32[64,256]{1,0:T(8,128)} %select_maximum_fusion.coef_ref), custom_call_target="tpu_custom_call" | custom-call | flops 101171200 | bytes 8093696 | tf_op jit(solution)/shard_map/weights/pallas_call | solution.py:254
  43.0 5.9 %factor_inverse.1.inverse_ref = f32[128,128]{1,0:T(8,128)} custom-call(f32[128,128]{1,0:T(8,128)} %fusion.gram_ref), custom_call_target="tpu_custom_call" | custom-call | flops 10737418240 | bytes 131072 | tf_op jit(solution)/shard_map/factor_inverse/pallas_call | solution.py:206
  48.9 16.7 %all-to-all-done = bf16[32,152,128]{2,1,0:T(8,128)(2,1)S(1)} async-done(((bf16[32,152,128]{2,1,0:T(8,128)(2,1)}), bf16[32,152,128]{2,1,0:T(8,128)(2,1)S(1)}, u32[]{:S(2)}, u32[]{:S(2)}) %all-to-all-start) | async-done | bytes 1245216 | tf_op jit(solution)/shard_map/all_to_all | solution.py:598
  65.7 1.3 %collective-permute-start.8 = (bf16[10,152,128]{2,1,0:T(8,128)(2,1)S(1)}, bf16[10,152,128]{2,1,0:T(8,128)(2,1)S(1)}, u32[]{:S(2)}, u32[]{:S(2)}) collective-permute-start(bf16[10,152,128]{2,1,0:T(8,128)(2,1)S(1)} %get-tuple-element.49), channel_id=1, source_target_pairs={{8,0},{16,8},{24,16},{9,1},{17,9},{25,17},{10,2},{18,10},{26,18},{... | collective-permute-start | bytes 1167368 | tf_op jit(solution)/shard_map/ppermute | solution.py:526
  67.0 4.6 %collective-permute-start.7 = (bf16[10,152,128]{2,1,0:T(8,128)(2,1)S(1)}, bf16[10,152,128]{2,1,0:T(8,128)(2,1)S(1)}, u32[]{:S(2)}, u32[]{:S(2)}) collective-permute-start(bf16[10,152,128]{2,1,0:T(8,128)(2,1)S(1)} %get-tuple-element.50), channel_id=1, source_target_pairs={{0,8},{8,16},{16,24},{1,9},{9,17},{17,25},{2,10},{10,18},{18,26},{... | collective-permute-start | bytes 1167368 | tf_op jit(solution)/shard_map/ppermute | solution.py:519
  71.6 13.9 %inner_sweeps.1 = (f32[32,19,8,128]{3,2,1,0:T(8,128)}, f32[32,19,8,128]{3,2,1,0:T(8,128)}, f32[152,128]{1,0:T(8,128)}) custom-call(bf16[4864,128]{1,0:T(8,128)(2,1)} %bitcast.10, f32[128,128]{1,0:T(8,128)} %factor_inverse.1.inverse_ref, f32[52,19,8,128]{3,2,1,0:T(8,128)} %get-tuple-element.44.across_hbm, f32[52,19,8,128]{3,2,1,0:T(8,128)} %get-tuple-element.45.down_hbm), custom_call_target="tpu_custom_call" | custom-call | flops 12000000000 | bytes 4980736 | tf_op jit(solution)/shard_map/inner_sweeps/pallas_call | solution.py:393
  85.5 0.7 copy-done.1
  86.2 0.2 copy-done.2
  86.4 12.9 %outer_sweeps.1 = f32[32,128]{1,0:T(8,128)} custom-call(s32[2]{0:T(128)} %add_convert_fusion.ends_ref, bf16[1520,128]{1,0:T(8,128)(2,1)} %bitcast.14, bf16[1520,128]{1,0:T(8,128)(2,1)} %bitcast.13, f32[128,128]{1,0:T(8,128)} %factor_inverse.1.inverse_ref, f32[152,128]{1,0:T(8,128)} %get-tuple-element.46.inner_ref, ...), custom_call_target="tpu_custom_call" | custom-call | tf_op jit(solution)/shard_map/outer_sweeps/pallas_call | solution.py:506
  (37 shorter events, 0.7 us)
Async XLA Ops:
  2.9 9.6 %collective-permute-start.2 = (f32[128,128]{1,0:T(8,128)S(1)}, f32[128,128]{1,0:T(8,128)S(1)}, u32[]{:S(2)}, u32[]{:S(2)}) collective-permute-start(f32[128,128]{1,0:T(8,128)S(1)} %fusion.8), channel_id=1, source_target_pairs={{2,0},{3,1},{4,2},{5,3},{6,4},{7,5},{0,6},{1,7},{10,8},{11,9},{12,... | collective-permute-start | bytes 196616 | tf_op jit(solution)/shard_map/ppermute | solution.py:533
  6.9 4.9 %collective-permute-start.1 = (f32[160,128]{1,0:T(8,128)S(1)}, f32[160,128]{1,0:T(8,128)S(1)}, u32[]{:S(2)}, u32[]{:S(2)}) collective-permute-start(f32[160,128]{1,0:T(8,128)S(1)} %constant_dynamic-update-slice_fusion), channel_id=1, source_target_pairs={{1,0},{2,1},{3,2},{4,3},{5,4},{6,5},{7,6},{0,7},{9,8},{10,9},{11,1... | collective-permute-start | bytes 245768 | tf_op jit(solution)/shard_map/ppermute | solution.py:533
  6.9 4.8 %collective-permute-start = (f32[160,128]{1,0:T(8,128)S(1)}, f32[160,128]{1,0:T(8,128)S(1)}, u32[]{:S(2)}, u32[]{:S(2)}) collective-permute-start(f32[160,128]{1,0:T(8,128)S(1)} %constant_dynamic-update-slice_fusion), channel_id=1, source_target_pairs={{7,0},{0,1},{1,2},{2,3},{3,4},{4,5},{5,6},{6,7},{15,8},{8,9},{9,10... | collective-permute-start | bytes 245768 | tf_op jit(solution)/shard_map/ppermute | solution.py:533
  16.2 4.8 %collective-permute-start.3 = (f32[128,128]{1,0:T(8,128)S(1)}, f32[128,128]{1,0:T(8,128)S(1)}, u32[]{:S(2)}, u32[]{:S(2)}) collective-permute-start(f32[128,128]{1,0:T(8,128)S(1)} %fusion.1), channel_id=1, source_target_pairs={{4,0},{5,1},{6,2},{7,3},{0,4},{1,5},{2,6},{3,7},{12,8},{13,9},{14,... | collective-permute-start | bytes 196616 | tf_op jit(solution)/shard_map/ppermute | solution.py:533
  21.1 10.4 %collective-permute-start.6 = (f32[128,128]{1,0:T(8,128)S(1)}, f32[128,128]{1,0:T(8,128)S(1)}, u32[]{:S(2)}, u32[]{:S(2)}) collective-permute-start(f32[128,128]{1,0:T(8,128)S(1)} %add.38), channel_id=1, source_target_pairs={{16,0},{24,8},{0,16},{8,24},{17,1},{25,9},{1,17},{9,25},{18,2},{26... | collective-permute-start | bytes 196616 | tf_op jit(solution)/shard_map/ppermute | solution.py:533
  23.7 6.4 %collective-permute-start.5 = (f32[168,128]{1,0:T(8,128)S(1)}, f32[168,128]{1,0:T(8,128)S(1)}, u32[]{:S(2)}, u32[]{:S(2)}) collective-permute-start(f32[168,128]{1,0:T(8,128)S(1)} %constant_dynamic-update-slice_fusion.2), channel_id=1, source_target_pairs={{8,0},{16,8},{24,16},{0,24},{9,1},{17,9},{25,17},{1,25},{10,2},{18... | collective-permute-start | bytes 258056 | tf_op jit(solution)/shard_map/ppermute | solution.py:533
  25.1 6.3 %collective-permute-start.4 = (f32[168,128]{1,0:T(8,128)S(1)}, f32[168,128]{1,0:T(8,128)S(1)}, u32[]{:S(2)}, u32[]{:S(2)}) collective-permute-start(f32[168,128]{1,0:T(8,128)S(1)} %constant_dynamic-update-slice_fusion.2), channel_id=1, source_target_pairs={{24,0},{0,8},{8,16},{16,24},{25,1},{1,9},{9,17},{17,25},{26,2},{2,... | collective-permute-start | bytes 258056 | tf_op jit(solution)/shard_map/ppermute | solution.py:533
  32.1 33.6 %all-to-all-start = ((bf16[32,152,128]{2,1,0:T(8,128)(2,1)}), bf16[32,152,128]{2,1,0:T(8,128)(2,1)S(1)}, u32[]{:S(2)}, u32[]{:S(2)}) async-start(bf16[32,152,128]{2,1,0:T(8,128)(2,1)} %deal_20.1), calls=%async_computation | async-start | bytes 2490368 | tf_op jit(solution)/shard_map/all_to_all | solution.py:598
  65.7 5.9 %copy-start = (bf16[32,152,128]{2,1,0:T(8,128)(2,1)}, bf16[32,152,128]{2,1,0:T(8,128)(2,1)S(1)}, u32[]{:S(2)}) copy-start(bf16[32,152,128]{2,1,0:T(8,128)(2,1)S(1)} %all-to-all-done) | copy-start | bytes 3735556
  65.7 19.8 %collective-permute-start.8 = (bf16[10,152,128]{2,1,0:T(8,128)(2,1)S(1)}, bf16[10,152,128]{2,1,0:T(8,128)(2,1)S(1)}, u32[]{:S(2)}, u32[]{:S(2)}) collective-permute-start(bf16[10,152,128]{2,1,0:T(8,128)(2,1)S(1)} %get-tuple-element.49), channel_id=1, source_target_pairs={{8,0},{16,8},{24,16},{9,1},{17,9},{25,17},{10,2},{18,10},{26,18},{... | collective-permute-start | bytes 1167368 | tf_op jit(solution)/shard_map/ppermute | solution.py:526
  67.0 18.5 %collective-permute-start.7 = (bf16[10,152,128]{2,1,0:T(8,128)(2,1)S(1)}, bf16[10,152,128]{2,1,0:T(8,128)(2,1)S(1)}, u32[]{:S(2)}, u32[]{:S(2)}) collective-permute-start(bf16[10,152,128]{2,1,0:T(8,128)(2,1)S(1)} %get-tuple-element.50), channel_id=1, source_target_pairs={{0,8},{8,16},{16,24},{1,9},{9,17},{17,25},{2,10},{10,18},{18,26},{... | collective-permute-start | bytes 1167368 | tf_op jit(solution)/shard_map/ppermute | solution.py:519
  85.5 0.7 copy-start.1
  85.5 0.9 copy-start.2

commit v7 on v6

--- a/solution.py
+++ b/solution.py
@@ -50,8 +50,7 @@
     return jnp.swapaxes(around, axis, axis + 1).reshape(shape)
 
 
-def deal_kernel(tiles_lon, first, count, basis_ref, order_ref, *refs):
-    out_ref, slot_ref, ready_ref, sems = refs[-4:]
+def deal_kernel(tiles_lon, basis_ref, order_ref, out_ref, slot_ref, ready_ref, sems):
     rows, width = basis_ref.shape
     parts = rows // ONE_HOT
     tiles, places, _ = out_ref.shape
@@ -86,20 +85,21 @@
     slot_ref[...] = (high * 64.0 + low).astype(i32)
 
     take = TILES
-    steps = count // take
+    steps = tiles // take
 
     def leave(c):
         return pltpu.make_async_copy(
             ready_ref.at[pl.ds(c * take, take)],
-            out_ref.at[pl.ds(first + c * take, take)],
+            out_ref.at[pl.ds(c * take, take)],
             sems.at[c],
         )
 
     lane = iota((take * places, LANES), 1)
-    for c in range(steps):
+
+    def step(c, carry):
         wanted = []
         for h in range(take):
-            order = slot_ref[first + c * take + h : first + c * take + h + 1, :]
+            order = slot_ref[pl.ds(c * take + h, 1), :]
             wanted.append(jnp.broadcast_to(order, (LANES, padded)).T[:places])
         wanted = jnp.concatenate(wanted, axis=0)
         within = wanted & (ONE_HOT - 1)
@@ -117,36 +117,36 @@
         for h in range(take):
             ready_ref[c * take + h] = picked[h * places : (h + 1) * places].astype(bf16)
         leave(c).start()
+        return carry
+
+    lax.fori_loop(0, steps, step, 0)
     for c in range(steps):
         leave(c).wait()
 
 
-def deal(basis, order, tiles_lon, wide, first, count, so_far):
+def deal(basis, order, tiles_lon, wide):
     rows, width = basis.shape
     tiles = rows // wide
     places = slots(wide)
     vmem = pl.BlockSpec(memory_space=pltpu.VMEM)
-    far = pl.BlockSpec(memory_space=pl.ANY)
-    before = [] if so_far is None else [so_far]
     return pl.pallas_call(
-        functools.partial(deal_kernel, tiles_lon, first, count),
+        functools.partial(deal_kernel, tiles_lon),
         out_shape=jax.ShapeDtypeStruct((tiles, places, width), bf16),
-        in_specs=[vmem, vmem] + [far] * len(before),
-        out_specs=far,
-        input_output_aliases={2: 0} if before else {},
+        in_specs=[vmem, vmem],
+        out_specs=pl.BlockSpec(memory_space=pl.ANY),
         scratch_shapes=[
             pltpu.VMEM((tiles, -(-places // LANES) * LANES), i32),
-            pltpu.VMEM((count, places, width), bf16),
-            pltpu.SemaphoreType.DMA((count // TILES,)),
+            pltpu.VMEM((tiles, places, width), bf16),
+            pltpu.SemaphoreType.DMA((tiles // TILES,)),
         ],
         compiler_params=pltpu.CompilerParams(vmem_limit_bytes=VMEM_BYTES),
         cost_estimate=pl.CostEstimate(
-            flops=2 * count * places * rows * width,
+            flops=2 * tiles * places * rows * width,
             bytes_accessed=4 * rows * width,
             transcendentals=0,
         ),
-        name=f"deal_{first}",
-    )(basis, order.reshape(tiles, wide), *before)
+        name="deal",
+    )(basis, order.reshape(tiles, wide))
 
 
 def inverse_kernel(gram_ref, out_ref):
@@ -330,8 +330,8 @@
 
 
 def inner_kernel(
-    own_ref, inverse_ref, across_hbm, down_hbm, first_ref, second_ref, total_ref,
-    across_ref, down_ref, sum_ref, sems,
+    own_ref, inverse_ref, across_hbm, down_hbm, first_hbm, second_hbm, total_ref,
+    first_ref, second_ref, across_ref, down_ref, sum_ref, sems,
 ):
     tall, groups, _, lanes = first_ref.shape
     inside = pl.ds(HALO, tall)
@@ -375,6 +375,17 @@
 
     lax.fori_loop(0, SWEEPS // 2, two, 0)
 
+    near = HALO + 1
+    leaving = []
+    for k, (source, target) in enumerate(((first_ref, first_hbm), (second_ref, second_hbm))):
+        for side, row in enumerate((0, tall - near)):
+            part = pl.ds(row, near)
+            leaving.append(
+                pltpu.make_async_copy(source.at[part], target.at[part], sems.at[2 + 2 * k + side])
+            )
+    for copy in leaving:
+        copy.start()
+
     def gather(c, totals):
         rows = [(c * 4 + h, c * 4 + h) for h in range(4)]
         return tuple(summed_lanes(sum_ref, rows, list(totals)))
@@ -382,6 +393,8 @@
     zeros = tuple(jnp.zeros((SUB, lanes), f32) for _ in range(groups))
     totals = lax.fori_loop(0, tall // 4, gather, zeros)
     total_ref[...] = jnp.concatenate(totals, axis=0)
+    for copy in leaving:
+        copy.wait()
 
 
 def inner_sweeps(own, inverse, across_down):
@@ -398,13 +411,8 @@
             jax.ShapeDtypeStruct((places, lanes), f32),
         ),
         in_specs=[vmem, vmem, far, far],
-        out_specs=(vmem, vmem, vmem),
-        scratch_shapes=[
-            pltpu.VMEM(shape, f32),
-            pltpu.VMEM(shape, f32),
-            pltpu.VMEM(shape, f32),
-            pltpu.SemaphoreType.DMA((2,)),
-        ],
+        out_specs=(far, far, vmem),
+        scratch_shapes=[pltpu.VMEM(shape, f32)] * 5 + [pltpu.SemaphoreType.DMA((6,))],
         compiler_params=pltpu.CompilerParams(vmem_limit_bytes=VMEM_BYTES),
         cost_estimate=pl.CostEstimate(
             flops=12 * 10**9, bytes_accessed=8 * own.size, transcendentals=0
@@ -558,43 +566,10 @@
     tied = lax.optimization_barrier
     at = lax.axis_index("lat")
     top, bottom = at == 0, at == lax.axis_size("lat") - 1
+
     whole_rows = rows_here // count == wide
-
-    def dealt(part, so_far):
-        if not whole_rows:
-            return basis[order] if so_far is None else so_far
-        bounds = [0, 3 * tall // 8, 5 * tall // 8, tall]
-        return deal(
-            basis, order, lax.axis_size("lon"), wide, bounds[part],
-            bounds[part + 1] - bounds[part], so_far,
-        )
-
-    partial = lax.dot_general(
-        basis, basis, (((0,), (0,)), ((), ())), preferred_element_type=f32
-    )
-    coef = conduct * (0.35 + 0.65 * land.astype(f32))
-    edges = jnp.pad(
-        jnp.concatenate([coef[:, :HALO], coef[:, -HALO:]], axis=1),
-        ((0, 0), (0, width - 2 * HALO)),
-    )
-    partial, edges, basis = tied((partial, edges, basis))
-    moving = dealt(0, None)
-    partial, before, after = neighbours(partial, edges, "lon")
-    partial, moving = tied((partial, moving))
-    moving = dealt(1, moving)
-    partial = rest_of_ring(partial, "lon")
-    coef = circle(coef, after[:, :HALO], before[:, HALO : 2 * HALO], 1)
-    ends = jnp.concatenate([coef[:HALO], coef[-HALO:]], axis=0)
-    rest = coef.shape[1] - width
-    edges = jnp.concatenate(
-        [ends[:, :width], jnp.pad(ends[:, width:], ((0, 0), (0, width - rest)))], axis=0
-    )
-    partial, edges, moving = tied((partial, edges, moving))
-    moving = dealt(2, moving)
-    partial, before, after = neighbours(partial, edges, "lat")
-    gram = rest_of_ring(partial, "lat")
-    gram, before, after, moving = tied((gram, before, after, moving))
-
+    moving = deal(basis, order, lax.axis_size("lon"), wide) if whole_rows else basis[order]
+    moving, basis = tied((moving, basis))
     raw = lax.all_to_all(moving, axes, split_axis=0, concat_axis=0, tiled=True)
     if not whole_rows:
         raw = raw.reshape(tall, wide, width)
@@ -602,11 +577,23 @@
         right = from_after(raw[:, :HALO], "lon", True)
         raw = circle(raw, right, left, 1)
 
-    before = jnp.concatenate([before[: 2 * HALO], before[2 * HALO :, :rest]], axis=1)[HALO:]
-    after = jnp.concatenate([after[: 2 * HALO], after[2 * HALO :, :rest]], axis=1)[:HALO]
-    coef = jnp.concatenate(
-        [jnp.where(top, 0.0, before), coef, jnp.where(bottom, 0.0, after)], axis=0
-    )
+    partial = lax.dot_general(
+        basis, basis, (((0,), (0,)), ((), ())), preferred_element_type=f32
+    )
+    coef = conduct * (0.35 + 0.65 * land.astype(f32))
+    edges = jnp.concatenate([coef[:HALO], coef[-HALO:]], axis=0)
+    edges = jnp.pad(edges, ((0, 4), (0, width - wide)))
+    partial, before, after = neighbours(partial, edges, "lat")
+    partial = rest_of_ring(partial, "lat")
+    before = jnp.where(top, 0.0, before[HALO : 2 * HALO, :wide])
+    after = jnp.where(bottom, 0.0, after[:HALO, :wide])
+    coef = jnp.concatenate([before, coef, after], axis=0)
+    edges = jnp.concatenate([coef[:, :HALO], coef[:, -HALO:]], axis=1)
+    edges = jnp.pad(edges, ((0, 4), (0, width - 2 * HALO)))
+    partial, before, after = neighbours(partial, edges, "lon")
+    rows = coef.shape[0]
+    coef = circle(coef, after[:rows, :HALO], before[:rows, HALO : 2 * HALO], 1)
+    gram = rest_of_ring(partial, "lon")
     inverse = factor_inverse(gram)
     across_down = weights(coef, width)
     ends = jnp.stack([top, bottom]).astype(i32)

time: 99.8 us -> 86.7 us (0.87)
  waiting for transfers between devices: 21.7 us -> 12.5 us
  Pallas kernels: 51.1 us -> 47.9 us
  matrix products: 2.05 us -> 0.48 us
  starting transfers between devices: 19.3 us -> 20.7 us
    all_to_all x1, waiting for transfers between devices: 16.7 us -> 0.16 us  [per_device(): raw = lax.all_to_all(moving, axes, split_axis=0, concat_axis=0, tiled=True)]
    ppermute x7, waiting for transfers between devices: 5 us -> 12.4 us  [ahead(): lax.ppermute(values, axis, [((i + step) % count, i) for i in range(count)])]
    all_to_all x1, starting transfers between devices: 3.08 us -> 5.62 us  [per_device(): raw = lax.all_to_all(moving, axes, split_axis=0, concat_axis=0, tiled=True)]
    pallas_call x3 -> x1, Pallas kernels: 12.1 us -> 9.94 us  [deal(): pl.pallas_call(functools.partial(deal_kernel, tiles_lon), out_shape=jax.S...]
    dot_general x1, matrix products: 2.05 us -> 0.48 us  [per_device(): lax.dot_general(basis, basis, (((0,), (0,)), ((), ())), preferred_element...]
    ppermute x7, starting transfers between devices: 10.3 us -> 9.23 us  [ahead(): lax.ppermute(values, axis, [((i + step) % count, i) for i in range(count)])]
    pallas_call x1, Pallas kernels: 13.9 us -> 12.9 us  [inner_sweeps(): pl.pallas_call(inner_kernel, out_shape=(jax.ShapeDtypeStruct(shape, f32),...]
  transfers between devices with their start and end apart: 10 -> 10, of which waited for: 3 -> 5; matrix products, arithmetic and copies ran while one was open for 2% -> 3% of each run, Pallas kernels for 35% -> 29%
where the time goes in v7:
time: 86.7 us; the launch traced here: 86.1 us
  Pallas kernels  47.9 us (55%)
  starting transfers between devices  20.7 us (24%)
  waiting for transfers between devices  12.5 us (14%)
  other arithmetic  2.24 us (3%)
  local copies, waits for them, and re-layouts  2.01 us (2%)
    pallas_call x1, Pallas kernels, outer_sweeps(): pl.pallas_call(functools.partial(outer_kernel, scale), out_shape=jax.Shap...  12.9 us
    pallas_call x1, Pallas kernels, inner_sweeps(): pl.pallas_call(inner_kernel, out_shape=(jax.ShapeDtypeStruct(shape, f32),...  12.9 us
    ppermute x7, waiting for transfers between devices, ahead(): lax.ppermute(values, axis, [((i + step) % count, i) for i in range(count)])  12.4 us
    pallas_call x1, Pallas kernels, deal(): pl.pallas_call(functools.partial(deal_kernel, tiles_lon), out_shape=jax.S...  9.94 us
    ppermute x7, starting transfers between devices, ahead(): lax.ppermute(values, axis, [((i + step) % count, i) for i in range(count)])  9.23 us
    pallas_call x1, Pallas kernels, weights(): pl.pallas_call(weight_kernel, out_shape=(jax.ShapeDtypeStruct(shape, f32)...  6.31 us
    pallas_call x1, Pallas kernels, factor_inverse(): pl.pallas_call(inverse_kernel, out_shape=jax.ShapeDtypeStruct(gram.shape,...  5.89 us
    all_to_all x1, starting transfers between devices, per_device(): raw = lax.all_to_all(moving, axes, split_axis=0, concat_axis=0, tiled=True)  5.62 us
  transfers between devices with their start and end apart: 10, of which 5 were waited for; matrix products, arithmetic and copies ran while one was open for 3% of the time, Pallas kernels for 29%

profile of v7, /device:TPU:0, one launch (start us, length us, event | category | flops | bytes accessed | tf_op | source)
XLA Modules:
  0.0 86.1 jit_solution(13115784189167676770)
XLA Ops:
  0.0 0.7 add_multiply_fusion
  0.8 9.9 %deal.1 = bf16[32,152,128]{2,1,0:T(8,128)(2,1)} custom-call(bf16[4096,128]{1,0:T(8,128)(2,1)} %basis_ref.1, s32[32,128]{1,0:T(8,128)} %bitcast.19), custom_call_target="tpu_custom_call" | custom-call | flops 5100273664 | bytes 2097152 | tf_op jit(solution)/shard_map/deal/pallas_call | solution.py:132
  10.7 0.5 fusion.5
  11.2 5.1 %collective-permute-start.1 = (f32[152,128]{1,0:T(8,128)S(1)}, f32[152,128]{1,0:T(8,128)S(1)}, u32[]{:S(2)}, u32[]{:S(2)}) collective-permute-start(f32[152,128]{1,0:T(8,128)S(1)} %pad_maximum_fusion.1), channel_id=1, source_target_pairs={{8,0},{16,8},{24,16},{0,24},{9,1},{17,9},{25,17},{1,25},{10,2},{18... | collective-permute-start | bytes 233480 | tf_op jit(solution)/shard_map/ppermute | solution.py:541
  16.3 1.0 %collective-permute-start.2 = (f32[128,128]{1,0:T(8,128)S(1)}, f32[128,128]{1,0:T(8,128)S(1)}, u32[]{:S(2)}, u32[]{:S(2)}) collective-permute-start(f32[128,128]{1,0:T(8,128)S(1)} %fusion.5), channel_id=1, source_target_pairs={{16,0},{24,8},{0,16},{8,24},{17,1},{25,9},{1,17},{9,25},{18,2},{26... | collective-permute-start | bytes 196616 | tf_op jit(solution)/shard_map/ppermute | solution.py:541
  17.3 5.6 %all-to-all-start = ((bf16[32,152,128]{2,1,0:T(8,128)(2,1)}), bf16[32,152,128]{2,1,0:T(8,128)(2,1)S(1)}, u32[]{:S(2)}, u32[]{:S(2)}) async-start(bf16[32,152,128]{2,1,0:T(8,128)(2,1)} %deal.1), calls=%async_computation | async-start | bytes 2490368 | tf_op jit(solution)/shard_map/all_to_all | solution.py:573
  23.0 0.1 pad.21.clone
  23.1 1.0 %collective-permute-done.2 = f32[128,128]{1,0:T(8,128)S(1)} collective-permute-done((f32[128,128]{1,0:T(8,128)S(1)}, f32[128,128]{1,0:T(8,128)S(1)}, u32[]{:S(2)}, u32[]{:S(2)}) %collective-permute-start.2) | collective-permute-done | bytes 65568 | tf_op jit(solution)/shard_map/ppermute | solution.py:541
  24.1 2.5 %collective-permute-start.5 = (f32[128,128]{1,0:T(8,128)S(1)}, f32[128,128]{1,0:T(8,128)S(1)}, u32[]{:S(2)}, u32[]{:S(2)}) collective-permute-start(f32[128,128]{1,0:T(8,128)S(1)} %fusion.1), channel_id=1, source_target_pairs={{2,0},{3,1},{4,2},{5,3},{6,4},{7,5},{0,6},{1,7},{10,8},{11,9},{12,... | collective-permute-start | bytes 196616 | tf_op jit(solution)/shard_map/ppermute | solution.py:541
  26.6 0.1 fusion.3
  26.7 0.1 select_maximum_fusion
  26.8 0.5 collective-permute-start.3
  27.3 0.6 add_convert_fusion.ends_ref
  28.0 7.8 %collective-permute-done.5 = f32[128,128]{1,0:T(8,128)S(1)} collective-permute-done((f32[128,128]{1,0:T(8,128)S(1)}, f32[128,128]{1,0:T(8,128)S(1)}, u32[]{:S(2)}, u32[]{:S(2)}) %collective-permute-start.5) | collective-permute-done | bytes 65568 | tf_op jit(solution)/shard_map/ppermute | solution.py:541
  35.8 0.8 collective-permute-done.4
  36.5 2.8 %collective-permute-done.3 = f32[184,128]{1,0:T(8,128)S(1)} collective-permute-done((f32[184,128]{1,0:T(8,128)S(1)}, f32[184,128]{1,0:T(8,128)S(1)}, u32[]{:S(2)}, u32[]{:S(2)}) %collective-permute-start.3) | collective-permute-done | bytes 94240 | tf_op jit(solution)/shard_map/ppermute | solution.py:541
  39.4 0.1 collective-permute-start.6
  39.4 0.1 slice.75
  39.5 0.1 pad_maximum_fusion.2
  39.6 0.1 copy.15
  39.8 0.1 copy.17
  39.8 0.6 pad.14.coef_ref
  40.5 6.3 %weights.1 = (f32[52,19,8,128]{3,2,1,0:T(8,128)}, f32[52,19,8,128]{3,2,1,0:T(8,128)}) custom-call(f32[64,256]{1,0:T(8,128)} %pad.14.coef_ref), custom_call_target="tpu_custom_call" | custom-call | flops 101171200 | bytes 8093696 | tf_op jit(solution)/shard_map/weights/pallas_call | solution.py:254
  46.8 0.6 add.41.gram_ref
  47.4 5.9 %factor_inverse.1.inverse_ref = f32[128,128]{1,0:T(8,128)} custom-call(f32[128,128]{1,0:T(8,128)} %add.41.gram_ref), custom_call_target="tpu_custom_call" | custom-call | flops 10737418240 | bytes 131072 | tf_op jit(solution)/shard_map/factor_inverse/pallas_call | solution.py:206
  53.3 0.2 all-to-all-done
  53.5 1.3 %collective-permute-start.8 = (bf16[10,152,128]{2,1,0:T(8,128)(2,1)S(1)}, bf16[10,152,128]{2,1,0:T(8,128)(2,1)S(1)}, u32[]{:S(2)}, u32[]{:S(2)}) collective-permute-start(bf16[10,152,128]{2,1,0:T(8,128)(2,1)S(1)} %get-tuple-element.29), channel_id=1, source_target_pairs={{8,0},{16,8},{24,16},{9,1},{17,9},{25,17},{10,2},{18,10},{26,18},{... | collective-permute-start | bytes 1167368 | tf_op jit(solution)/shard_map/ppermute | solution.py:534
  54.8 4.6 %collective-permute-start.7 = (bf16[10,152,128]{2,1,0:T(8,128)(2,1)S(1)}, bf16[10,152,128]{2,1,0:T(8,128)(2,1)S(1)}, u32[]{:S(2)}, u32[]{:S(2)}) collective-permute-start(bf16[10,152,128]{2,1,0:T(8,128)(2,1)S(1)} %get-tuple-element.30), channel_id=1, source_target_pairs={{0,8},{8,16},{16,24},{1,9},{9,17},{17,25},{2,10},{10,18},{18,26},{... | collective-permute-start | bytes 1167368 | tf_op jit(solution)/shard_map/ppermute | solution.py:527
  59.4 12.9 %inner_sweeps.1 = (f32[32,19,8,128]{3,2,1,0:T(8,128)}, f32[32,19,8,128]{3,2,1,0:T(8,128)}, f32[152,128]{1,0:T(8,128)}) custom-call(bf16[4864,128]{1,0:T(8,128)(2,1)} %bitcast.14, f32[128,128]{1,0:T(8,128)} %factor_inverse.1.inverse_ref, f32[52,19,8,128]{3,2,1,0:T(8,128)} %get-tuple-element.24.across_hbm, f32[52,19,8,128]{3,2,1,0:T(8,128)} %get-tuple-element.25.down_hbm), custom_call_target="tpu_custom_call" | custom-call | flops 12000000000 | bytes 4980736 | tf_op jit(solution)/shard_map/inner_sweeps/pallas_call | solution.py:406
  72.3 0.7 copy-done.2
  73.0 0.1 copy-done.3
  73.2 12.9 %outer_sweeps.1 = f32[32,128]{1,0:T(8,128)} custom-call(s32[2]{0:T(128)} %add_convert_fusion.ends_ref, bf16[1520,128]{1,0:T(8,128)(2,1)} %bitcast.17, bf16[1520,128]{1,0:T(8,128)(2,1)} %bitcast.16, f32[128,128]{1,0:T(8,128)} %factor_inverse.1.inverse_ref, f32[152,128]{1,0:T(8,128)} %get-tuple-element.26.inner_ref, ...), custom_call_target="tpu_custom_call" | custom-call | tf_op jit(solution)/shard_map/outer_sweeps/pallas_call | solution.py:514
  (27 shorter events, 0.3 us)
Async XLA Ops:
  0.7 10.0 %copy-start = (bf16[4096,128]{1,0:T(8,128)(2,1)S(1)}, bf16[4096,128]{1,0:T(8,128)(2,1)}, u32[]{:S(2)}) copy-start(bf16[4096,128]{1,0:T(8,128)(2,1)} %basis_ref.1) | copy-start | bytes 3145732
  11.2 12.8 %collective-permute-start.1 = (f32[152,128]{1,0:T(8,128)S(1)}, f32[152,128]{1,0:T(8,128)S(1)}, u32[]{:S(2)}, u32[]{:S(2)}) collective-permute-start(f32[152,128]{1,0:T(8,128)S(1)} %pad_maximum_fusion.1), channel_id=1, source_target_pairs={{8,0},{16,8},{24,16},{0,24},{9,1},{17,9},{25,17},{1,25},{10,2},{18... | collective-permute-start | bytes 233480 | tf_op jit(solution)/shard_map/ppermute | solution.py:541
  16.3 7.7 %collective-permute-start = (f32[152,128]{1,0:T(8,128)S(1)}, f32[152,128]{1,0:T(8,128)S(1)}, u32[]{:S(2)}, u32[]{:S(2)}) collective-permute-start(f32[152,128]{1,0:T(8,128)S(1)} %pad_maximum_fusion.1), channel_id=1, source_target_pairs={{24,0},{0,8},{8,16},{16,24},{25,1},{1,9},{9,17},{17,25},{26,2},{2,... | collective-permute-start | bytes 233480 | tf_op jit(solution)/shard_map/ppermute | solution.py:541
  16.3 7.7 %collective-permute-start.2 = (f32[128,128]{1,0:T(8,128)S(1)}, f32[128,128]{1,0:T(8,128)S(1)}, u32[]{:S(2)}, u32[]{:S(2)}) collective-permute-start(f32[128,128]{1,0:T(8,128)S(1)} %fusion.5), channel_id=1, source_target_pairs={{16,0},{24,8},{0,16},{8,24},{17,1},{25,9},{1,17},{9,25},{18,2},{26... | collective-permute-start | bytes 196616 | tf_op jit(solution)/shard_map/ppermute | solution.py:541
  17.3 36.1 %all-to-all-start = ((bf16[32,152,128]{2,1,0:T(8,128)(2,1)}), bf16[32,152,128]{2,1,0:T(8,128)(2,1)S(1)}, u32[]{:S(2)}, u32[]{:S(2)}) async-start(bf16[32,152,128]{2,1,0:T(8,128)(2,1)} %deal.1), calls=%async_computation | async-start | bytes 2490368 | tf_op jit(solution)/shard_map/all_to_all | solution.py:573
  24.1 11.7 %collective-permute-start.5 = (f32[128,128]{1,0:T(8,128)S(1)}, f32[128,128]{1,0:T(8,128)S(1)}, u32[]{:S(2)}, u32[]{:S(2)}) collective-permute-start(f32[128,128]{1,0:T(8,128)S(1)} %fusion.1), channel_id=1, source_target_pairs={{2,0},{3,1},{4,2},{5,3},{6,4},{7,5},{0,6},{1,7},{10,8},{11,9},{12,... | collective-permute-start | bytes 196616 | tf_op jit(solution)/shard_map/ppermute | solution.py:541
  26.8 9.7 %collective-permute-start.4 = (f32[184,128]{1,0:T(8,128)S(1)}, f32[184,128]{1,0:T(8,128)S(1)}, u32[]{:S(2)}, u32[]{:S(2)}) collective-permute-start(f32[184,128]{1,0:T(8,128)S(1)} %pad_maximum_fusion), channel_id=1, source_target_pairs={{1,0},{2,1},{3,2},{4,3},{5,4},{6,5},{7,6},{0,7},{9,8},{10,9},{11,1... | collective-permute-start | bytes 282632 | tf_op jit(solution)/shard_map/ppermute | solution.py:541
  26.8 12.5 %collective-permute-start.3 = (f32[184,128]{1,0:T(8,128)S(1)}, f32[184,128]{1,0:T(8,128)S(1)}, u32[]{:S(2)}, u32[]{:S(2)}) collective-permute-start(f32[184,128]{1,0:T(8,128)S(1)} %pad_maximum_fusion), channel_id=1, source_target_pairs={{7,0},{0,1},{1,2},{2,3},{3,4},{4,5},{5,6},{6,7},{15,8},{8,9},{9,10... | collective-permute-start | bytes 282632 | tf_op jit(solution)/shard_map/ppermute | solution.py:541
  39.4 7.4 %collective-permute-start.6 = (f32[128,128]{1,0:T(8,128)S(1)}, f32[128,128]{1,0:T(8,128)S(1)}, u32[]{:S(2)}, u32[]{:S(2)}) collective-permute-start(f32[128,128]{1,0:T(8,128)S(1)} %fusion), channel_id=1, source_target_pairs={{4,0},{5,1},{6,2},{7,3},{0,4},{1,5},{2,6},{3,7},{12,8},{13,9},{14,... | collective-permute-start | bytes 196616 | tf_op jit(solution)/shard_map/ppermute | solution.py:541
  53.5 5.9 %copy-start.1 = (bf16[32,152,128]{2,1,0:T(8,128)(2,1)}, bf16[32,152,128]{2,1,0:T(8,128)(2,1)S(1)}, u32[]{:S(2)}) copy-start(bf16[32,152,128]{2,1,0:T(8,128)(2,1)S(1)} %all-to-all-done) | copy-start | bytes 3735556
  53.5 18.8 %collective-permute-start.8 = (bf16[10,152,128]{2,1,0:T(8,128)(2,1)S(1)}, bf16[10,152,128]{2,1,0:T(8,128)(2,1)S(1)}, u32[]{:S(2)}, u32[]{:S(2)}) collective-permute-start(bf16[10,152,128]{2,1,0:T(8,128)(2,1)S(1)} %get-tuple-element.29), channel_id=1, source_target_pairs={{8,0},{16,8},{24,16},{9,1},{17,9},{25,17},{10,2},{18,10},{26,18},{... | collective-permute-start | bytes 1167368 | tf_op jit(solution)/shard_map/ppermute | solution.py:534
  54.8 17.5 %collective-permute-start.7 = (bf16[10,152,128]{2,1,0:T(8,128)(2,1)S(1)}, bf16[10,152,128]{2,1,0:T(8,128)(2,1)S(1)}, u32[]{:S(2)}, u32[]{:S(2)}) collective-permute-start(bf16[10,152,128]{2,1,0:T(8,128)(2,1)S(1)} %get-tuple-element.30), channel_id=1, source_target_pairs={{0,8},{8,16},{16,24},{1,9},{9,17},{17,25},{2,10},{10,18},{18,26},{... | collective-permute-start | bytes 1167368 | tf_op jit(solution)/shard_map/ppermute | solution.py:527
  72.3 0.7 copy-start.2
  72.3 0.9 copy-start.3

commit v8 on v7

--- a/solution.py
+++ b/solution.py
@@ -72,17 +72,17 @@
     column = iota((wide, padded), 0)
     slot = iota((wide, padded), 1)
     place = jnp.where(slot < places, (slot % SUB) * groups + slot // SUB, -1)
-    low = jnp.zeros((tiles, padded), f32)
-    high = low
+    sources, hits = [], []
     for source, hit in (
         (order, (place < wide) & (column == place)),
         (after, (place < wide + HALO) & (column == place - wide)),
         (before, (place >= places - HALO) & (column == place - places + wide)),
     ):
-        hot = hit.astype(f32).astype(bf16)
-        low = low + dot((source & 63).astype(f32).astype(bf16), hot)
-        high = high + dot((source >> 6).astype(f32).astype(bf16), hot)
-    slot_ref[...] = (high * 64.0 + low).astype(i32)
+        hits.append(hit.astype(f32).astype(bf16))
+        halves = jnp.concatenate([source & 63, source >> 6], axis=0)
+        sources.append(halves.astype(f32).astype(bf16))
+    halves = dot(jnp.concatenate(sources, axis=1), jnp.concatenate(hits, axis=0))
+    slot_ref[...] = (halves[tiles:] * 64.0 + halves[:tiles]).astype(i32)
 
     take = TILES
     steps = tiles // take
@@ -96,10 +96,10 @@
 
     lane = iota((take * places, LANES), 1)
 
-    def step(c, carry):
+    for c in range(steps):
         wanted = []
         for h in range(take):
-            order = slot_ref[pl.ds(c * take + h, 1), :]
+            order = slot_ref[c * take + h : c * take + h + 1, :]
             wanted.append(jnp.broadcast_to(order, (LANES, padded)).T[:places])
         wanted = jnp.concatenate(wanted, axis=0)
         within = wanted & (ONE_HOT - 1)
@@ -117,9 +117,6 @@
         for h in range(take):
             ready_ref[c * take + h] = picked[h * places : (h + 1) * places].astype(bf16)
         leave(c).start()
-        return carry
-
-    lax.fori_loop(0, steps, step, 0)
     for c in range(steps):
         leave(c).wait()
 
@@ -357,23 +354,23 @@
     for fetch in fetches:
         fetch.wait()
 
-    def sweep(s, src, dst, odd_pair):
+    for s in range(SWEEPS):
+        src, dst = (first_ref, second_ref) if s % 2 == 0 else (second_ref, first_ref)
         count = tall - 2 - 2 * s
+        steps = count // (2 * BLOCK)
 
         def step(c, carry):
-            update(src, dst, across_ref, down_ref, sum_ref, s + 1 + c * BLOCK, BLOCK)
+            for h in range(2):
+                row = s + 1 + (2 * c + h) * BLOCK
+                update(src, dst, across_ref, down_ref, sum_ref, row, BLOCK)
             return carry
 
-        lax.fori_loop(0, count // BLOCK, step, 0)
-        if odd_pair:
-            update(src, dst, across_ref, down_ref, sum_ref, s + count - 1, 2)
-
-    def two(t, carry):
-        sweep(2 * t, first_ref, second_ref, (tall - 2) % BLOCK == 2)
-        sweep(2 * t + 1, second_ref, first_ref, (tall - 4) % BLOCK == 2)
-        return carry
-
-    lax.fori_loop(0, SWEEPS // 2, two, 0)
+        lax.fori_loop(0, steps, step, 0)
+        done = steps * 2 * BLOCK
+        while done < count:
+            take = min(BLOCK, count - done)
+            update(src, dst, across_ref, down_ref, sum_ref, s + 1 + done, take)
+            done += take
 
     near = HALO + 1
     leaving = []
@@ -422,13 +419,20 @@
 
 
 def outer_kernel(
-    scale, ends_ref, north_ref, south_ref, inverse_ref, inner_ref, first_hbm, second_hbm,
-    across_hbm, down_hbm, out_ref, first_ref, second_ref, across_ref, down_ref, sum_ref, sems,
+    scale, ends_ref, inverse_ref, inner_ref, north_hbm, south_hbm, first_hbm, second_hbm,
+    across_hbm, down_hbm, out_ref, first_ref, second_ref, across_ref, down_ref, sum_ref,
+    north_ref, south_ref, sems,
 ):
     rows, groups, _, lanes = first_ref.shape
     tall = rows - 2 * HALO
     places = groups * SUB
     near = HALO + 1
+    halos = [
+        pltpu.make_async_copy(north_hbm, north_ref, sems.at[8]),
+        pltpu.make_async_copy(south_hbm, south_ref, sems.at[9]),
+    ]
+    for halo in halos:
+        halo.start()
     fetches = []
     for k, (source, target) in enumerate(((first_hbm, first_ref), (second_hbm, second_ref))):
         for side, row in enumerate((0, tall - near)):
@@ -450,6 +454,8 @@
         fetch.start()
     sum_ref[...] = jnp.zeros_like(sum_ref)
     turn = rotation(inverse_ref[...])
+    for halo in halos:
+        halo.wait()
     take = 2
     cells = take * places
 
@@ -465,13 +471,9 @@
         fetch.wait()
 
     def sweep(s, src, dst):
-        def step(c, carry):
-            bottom = c // 2
-            row = jnp.where(bottom == 0, s + 1, rows - 1 - HALO - s) + (c % 2) * take
-            update(src, dst, across_ref, down_ref, sum_ref, row, take)
-            return carry
-
-        lax.fori_loop(0, 4, step, 0)
+        for start in (s + 1, rows - 1 - HALO - s):
+            for c in range(HALO // take):
+                update(src, dst, across_ref, down_ref, sum_ref, start + c * take, take)
 
         @pl.when(ends_ref[0] == 1)
         def _():
@@ -514,12 +516,14 @@
     return pl.pallas_call(
         functools.partial(outer_kernel, scale),
         out_shape=jax.ShapeDtypeStruct((tall, wide), f32),
-        in_specs=[pl.BlockSpec(memory_space=pltpu.SMEM)] + [vmem] * 4 + [far] * 4,
+        in_specs=[pl.BlockSpec(memory_space=pltpu.SMEM)] + [vmem] * 2 + [far] * 6,
         out_specs=vmem,
-        scratch_shapes=[pltpu.VMEM(shape, f32)] * 5 + [pltpu.SemaphoreType.DMA((8,))],
-        compiler_params=pltpu.CompilerParams(vmem_limit_bytes=VMEM_BYTES),
+        scratch_shapes=[pltpu.VMEM(shape, f32)] * 5
+        + [pltpu.VMEM(north.shape, bf16)] * 2
+        + [pltpu.SemaphoreType.DMA((10,))],
+        compiler_params=pltpu.CompilerParams(vmem_limit_bytes=VMEM_BYTES // 2),
         name="outer_sweeps",
-    )(ends, north, south, inverse, total, first, second, *across_down)
+    )(ends, inverse, total, north, south, first, second, *across_down)
 
 
 def from_before(x, axis, closed):
@@ -569,7 +573,7 @@
 
     whole_rows = rows_here // count == wide
     moving = deal(basis, order, lax.axis_size("lon"), wide) if whole_rows else basis[order]
-    moving, basis = tied((moving, basis))
+    moving, basis, land, conduct = tied((moving, basis, land, conduct))
     raw = lax.all_to_all(moving, axes, split_axis=0, concat_axis=0, tiled=True)
     if not whole_rows:
         raw = raw.reshape(tall, wide, width)

time: 86.7 us -> 92.4 us (1.066)
  local copies, waits for them, and re-layouts: 2.01 us -> 6.45 us
  other arithmetic: 2.24 us -> 0.95 us
  Pallas kernels: 47.9 us -> 49 us
    unnamed x8 -> x20, local copies, waits for them, and re-layouts: 0.86 us -> 4.31 us
    pallas_call x1, Pallas kernels: 12.9 us -> 16.3 us  [outer_sweeps(): pl.pallas_call(functools.partial(outer_kernel, scale), out_shape=jax.Shap...]
    pallas_call x1, Pallas kernels: 9.94 us -> 7.63 us  [deal(): pl.pallas_call(functools.partial(deal_kernel, tiles_lon), out_shape=jax.S...]
    slice x1, local copies, waits for them, and re-layouts: 0.06 us -> 1.05 us  [per_device(): south = from_after(raw[:HALO], 'lat', False)]
  transfers between devices with their start and end apart: 10 -> 10, of which waited for: 5 -> 5; matrix products, arithmetic and copies ran while one was open for 3% -> 2% of each run, Pallas kernels for 29% -> 27%
where the time goes in v8:
time: 92.4 us; the launch traced here: 91.8 us
  Pallas kernels  49 us (53%)
  starting transfers between devices  21.5 us (23%)
  waiting for transfers between devices  13 us (14%)
  local copies, waits for them, and re-layouts  6.45 us (7%)
  other arithmetic  0.95 us (1%)
    pallas_call x1, Pallas kernels, outer_sweeps(): pl.pallas_call(functools.partial(outer_kernel, scale), out_shape=jax.Shap...  16.3 us
    ppermute x7, waiting for transfers between devices, ahead(): lax.ppermute(values, axis, [((i + step) % count, i) for i in range(count)])  12.9 us
    pallas_call x1, Pallas kernels, inner_sweeps(): pl.pallas_call(inner_kernel, out_shape=(jax.ShapeDtypeStruct(shape, f32),...  12.9 us
    ppermute x7, starting transfers between devices, ahead(): lax.ppermute(values, axis, [((i + step) % count, i) for i in range(count)])  9.24 us
    pallas_call x1, Pallas kernels, deal(): pl.pallas_call(functools.partial(deal_kernel, tiles_lon), out_shape=jax.S...  7.63 us
    pallas_call x1, Pallas kernels, weights(): pl.pallas_call(weight_kernel, out_shape=(jax.ShapeDtypeStruct(shape, f32)...  6.33 us
    pallas_call x1, Pallas kernels, factor_inverse(): pl.pallas_call(inverse_kernel, out_shape=jax.ShapeDtypeStruct(gram.shape,...  5.9 us
    all_to_all x1, starting transfers between devices, per_device(): raw = lax.all_to_all(moving, axes, split_axis=0, concat_axis=0, tiled=True)  5.62 us
  transfers between devices with their start and end apart: 10, of which 5 were waited for; matrix products, arithmetic and copies ran while one was open for 2% of the time, Pallas kernels for 27%

profile of v8, /device:TPU:0, one launch (start us, length us, event | category | flops | bytes accessed | tf_op | source)
XLA Modules:
  0.0 91.8 jit_solution(7328088054561235931)
XLA Ops:
  0.0 7.6 %deal.1 = bf16[32,152,128]{2,1,0:T(8,128)(2,1)} custom-call(bf16[4096,128]{1,0:T(8,128)(2,1)} %basis_ref.1, s32[32,128]{1,0:T(8,128)} %bitcast.17), custom_call_target="tpu_custom_call" | custom-call | flops 5100273664 | bytes 2097152 | tf_op jit(solution)/shard_map/deal/pallas_call | solution.py:129
  7.7 0.5 fusion.5
  8.2 5.1 %collective-permute-start.1 = (f32[152,128]{1,0:T(8,128)S(1)}, f32[152,128]{1,0:T(8,128)S(1)}, u32[]{:S(2)}, u32[]{:S(2)}) collective-permute-start(f32[152,128]{1,0:T(8,128)S(1)} %pad_maximum_fusion.1), channel_id=1, source_target_pairs={{8,0},{16,8},{24,16},{0,24},{9,1},{17,9},{25,17},{1,25},{10,2},{18... | collective-permute-start | bytes 233480 | tf_op jit(solution)/shard_map/ppermute | solution.py:545
  13.3 1.0 %collective-permute-start.2 = (f32[128,128]{1,0:T(8,128)S(1)}, f32[128,128]{1,0:T(8,128)S(1)}, u32[]{:S(2)}, u32[]{:S(2)}) collective-permute-start(f32[128,128]{1,0:T(8,128)S(1)} %fusion.5), channel_id=1, source_target_pairs={{16,0},{24,8},{0,16},{8,24},{17,1},{25,9},{1,17},{9,25},{18,2},{26... | collective-permute-start | bytes 196616 | tf_op jit(solution)/shard_map/ppermute | solution.py:545
  14.3 5.6 %all-to-all-start = ((bf16[32,152,128]{2,1,0:T(8,128)(2,1)}), bf16[32,152,128]{2,1,0:T(8,128)(2,1)S(1)}, u32[]{:S(2)}, u32[]{:S(2)}) async-start(bf16[32,152,128]{2,1,0:T(8,128)(2,1)} %deal.1), calls=%async_computation | async-start | bytes 2490368 | tf_op jit(solution)/shard_map/all_to_all | solution.py:577
  20.0 0.1 pad.21.clone
  20.1 1.0 %collective-permute-done.2 = f32[128,128]{1,0:T(8,128)S(1)} collective-permute-done((f32[128,128]{1,0:T(8,128)S(1)}, f32[128,128]{1,0:T(8,128)S(1)}, u32[]{:S(2)}, u32[]{:S(2)}) %collective-permute-start.2) | collective-permute-done | bytes 65568 | tf_op jit(solution)/shard_map/ppermute | solution.py:545
  21.1 2.5 %collective-permute-start.5 = (f32[128,128]{1,0:T(8,128)S(1)}, f32[128,128]{1,0:T(8,128)S(1)}, u32[]{:S(2)}, u32[]{:S(2)}) collective-permute-start(f32[128,128]{1,0:T(8,128)S(1)} %fusion.1), channel_id=1, source_target_pairs={{2,0},{3,1},{4,2},{5,3},{6,4},{7,5},{0,6},{1,7},{10,8},{11,9},{12,... | collective-permute-start | bytes 196616 | tf_op jit(solution)/shard_map/ppermute | solution.py:545
  23.6 0.1 fusion.3
  23.7 0.1 select_maximum_fusion
  23.8 0.5 collective-permute-start.3
  24.3 0.1 add_convert_fusion.ends_ref
  24.4 8.3 %collective-permute-done.5 = f32[128,128]{1,0:T(8,128)S(1)} collective-permute-done((f32[128,128]{1,0:T(8,128)S(1)}, f32[128,128]{1,0:T(8,128)S(1)}, u32[]{:S(2)}, u32[]{:S(2)}) %collective-permute-start.5) | collective-permute-done | bytes 65568 | tf_op jit(solution)/shard_map/ppermute | solution.py:545
  32.7 0.8 collective-permute-done.4
  33.5 2.8 %collective-permute-done.3 = f32[184,128]{1,0:T(8,128)S(1)} collective-permute-done((f32[184,128]{1,0:T(8,128)S(1)}, f32[184,128]{1,0:T(8,128)S(1)}, u32[]{:S(2)}, u32[]{:S(2)}) %collective-permute-start.3) | collective-permute-done | bytes 94240 | tf_op jit(solution)/shard_map/ppermute | solution.py:545
  36.4 0.1 slice.75
  36.5 0.1 pad_maximum_fusion.2
  36.6 0.1 copy.15
  36.7 0.1 copy.17
  36.8 0.6 pad.14.coef_ref
  37.5 6.3 %weights.1 = (f32[52,19,8,128]{3,2,1,0:T(8,128)}, f32[52,19,8,128]{3,2,1,0:T(8,128)}) custom-call(f32[64,256]{1,0:T(8,128)} %pad.14.coef_ref), custom_call_target="tpu_custom_call" | custom-call | flops 101171200 | bytes 8093696 | tf_op jit(solution)/shard_map/weights/pallas_call | solution.py:251
  43.8 0.6 add.41.gram_ref
  44.4 5.9 %factor_inverse.1.inverse_ref = f32[128,128]{1,0:T(8,128)} custom-call(f32[128,128]{1,0:T(8,128)} %add.41.gram_ref), custom_call_target="tpu_custom_call" | custom-call | flops 10737418240 | bytes 131072 | tf_op jit(solution)/shard_map/factor_inverse/pallas_call | solution.py:203
  50.3 0.1 all-to-all-done
  50.5 1.0 %fusion.2 = (bf16[10,152,128]{2,1,0:T(8,128)(2,1)}, bf16[10,152,128]{2,1,0:T(8,128)(2,1)}) fusion(bf16[32,152,128]{2,1,0:T(8,128)(2,1)S(1)} %all-to-all-done), kind=kLoop, calls=%fused_computation.20 | loop fusion | bytes 1556480 | tf_op jit(solution)/shard_map/slice | solution.py:607
  51.5 1.3 %collective-permute-start.8 = (bf16[10,152,128]{2,1,0:T(8,128)(2,1)}, bf16[10,152,128]{2,1,0:T(8,128)(2,1)}, u32[]{:S(2)}, u32[]{:S(2)}) collective-permute-start(bf16[10,152,128]{2,1,0:T(8,128)(2,1)} %get-tuple-element.33), channel_id=1, source_target_pairs={{8,0},{16,8},{24,16},{9,1},{17,9},{25,17},{10,2},{18,10},{26,18},{... | collective-permute-start | bytes 1167368 | tf_op jit(solution)/shard_map/ppermute | solution.py:538
  52.8 5.3 %collective-permute-start.7 = (bf16[10,152,128]{2,1,0:T(8,128)(2,1)}, bf16[10,152,128]{2,1,0:T(8,128)(2,1)}, u32[]{:S(2)}, u32[]{:S(2)}) collective-permute-start(bf16[10,152,128]{2,1,0:T(8,128)(2,1)} %get-tuple-element.34), channel_id=1, source_target_pairs={{0,8},{8,16},{16,24},{1,9},{9,17},{17,25},{2,10},{10,18},{18,26},{... | collective-permute-start | bytes 1167368 | tf_op jit(solution)/shard_map/ppermute | solution.py:531
  58.1 12.9 %inner_sweeps.1 = (f32[32,19,8,128]{3,2,1,0:T(8,128)}, f32[32,19,8,128]{3,2,1,0:T(8,128)}, f32[152,128]{1,0:T(8,128)}) custom-call(bf16[4864,128]{1,0:T(8,128)(2,1)} %bitcast.14, f32[128,128]{1,0:T(8,128)} %factor_inverse.1.inverse_ref, f32[52,19,8,128]{3,2,1,0:T(8,128)} %get-tuple-element.28.across_hbm, f32[52,19,8,128]{3,2,1,0:T(8,128)} %get-tuple-element.29.down_hbm), custom_call_target="tpu_custom_call" | custom-call | flops 12000000000 | bytes 4980736 | tf_op jit(solution)/shard_map/inner_sweeps/pallas_call | solution.py:403
  71.1 1.7 %copy-done.2 = f32[32,19,8,128]{3,2,1,0:T(8,128)S(1)} copy-done((f32[32,19,8,128]{3,2,1,0:T(8,128)S(1)}, f32[32,19,8,128]{3,2,1,0:T(8,128)}, u32[]{:S(2)}) %copy-start.2) | copy-done | bytes 2490392
  72.8 1.7 %copy-done.3 = f32[32,19,8,128]{3,2,1,0:T(8,128)S(1)} copy-done((f32[32,19,8,128]{3,2,1,0:T(8,128)S(1)}, f32[32,19,8,128]{3,2,1,0:T(8,128)}, u32[]{:S(2)}) %copy-start.3) | copy-done | bytes 2490392
  74.5 0.9 copy-done.4
  75.4 16.3 %outer_sweeps.1 = f32[32,128]{1,0:T(8,128)} custom-call(s32[2]{0:T(128)S(1)} %add_convert_fusion.ends_ref, f32[128,128]{1,0:T(8,128)S(1)} %copy-done.5, f32[152,128]{1,0:T(8,128)S(1)} %copy-done.4, bf16[1520,128]{1,0:T(8,128)(2,1)} %bitcast.6.north_hbm, bf16[1520,128]{1,0:T(8,128)(2,1)} %bitcast.7.south_hbm, f32[32,19,8,128]{3,2,1,0:T(8,128)S(1)} %copy-done.2, ...), custom_call_target="tpu_custom_call" | custom-call | tf_op jit(solution)/shard_map/outer_sweeps/pallas_call | solution.py:516
  (39 shorter events, 0.3 us)
Async XLA Ops:
  0.0 7.6 %copy-start.8 = (f32[32,128]{1,0:T(8,128)S(1)}, f32[32,128]{1,0:T(8,128)}, u32[]{:S(2)}) copy-start(f32[32,128]{1,0:T(8,128)} %param.7) | copy-start | bytes 49156
  0.0 7.7 %copy-start.9 = (s32[32,128]{1,0:T(8,128)S(1)}, s32[32,128]{1,0:T(8,128)}, u32[]{:S(2)}) copy-start(s32[32,128]{1,0:T(8,128)} %param.6) | copy-start | bytes 49156
  0.0 7.7 %copy-start.6 = (bf16[4096,128]{1,0:T(8,128)(2,1)S(1)}, bf16[4096,128]{1,0:T(8,128)(2,1)}, u32[]{:S(2)}) copy-start(bf16[4096,128]{1,0:T(8,128)(2,1)} %basis_ref.1) | copy-start | bytes 3145732
  8.2 12.8 %collective-permute-start.1 = (f32[152,128]{1,0:T(8,128)S(1)}, f32[152,128]{1,0:T(8,128)S(1)}, u32[]{:S(2)}, u32[]{:S(2)}) collective-permute-start(f32[152,128]{1,0:T(8,128)S(1)} %pad_maximum_fusion.1), channel_id=1, source_target_pairs={{8,0},{16,8},{24,16},{0,24},{9,1},{17,9},{25,17},{1,25},{10,2},{18... | collective-permute-start | bytes 233480 | tf_op jit(solution)/shard_map/ppermute | solution.py:545
  13.3 7.7 %collective-permute-start = (f32[152,128]{1,0:T(8,128)S(1)}, f32[152,128]{1,0:T(8,128)S(1)}, u32[]{:S(2)}, u32[]{:S(2)}) collective-permute-start(f32[152,128]{1,0:T(8,128)S(1)} %pad_maximum_fusion.1), channel_id=1, source_target_pairs={{24,0},{0,8},{8,16},{16,24},{25,1},{1,9},{9,17},{17,25},{26,2},{2,... | collective-permute-start | bytes 233480 | tf_op jit(solution)/shard_map/ppermute | solution.py:545
  13.3 7.7 %collective-permute-start.2 = (f32[128,128]{1,0:T(8,128)S(1)}, f32[128,128]{1,0:T(8,128)S(1)}, u32[]{:S(2)}, u32[]{:S(2)}) collective-permute-start(f32[128,128]{1,0:T(8,128)S(1)} %fusion.5), channel_id=1, source_target_pairs={{16,0},{24,8},{0,16},{8,24},{17,1},{25,9},{1,17},{9,25},{18,2},{26... | collective-permute-start | bytes 196616 | tf_op jit(solution)/shard_map/ppermute | solution.py:545
  14.3 36.1 %all-to-all-start = ((bf16[32,152,128]{2,1,0:T(8,128)(2,1)}), bf16[32,152,128]{2,1,0:T(8,128)(2,1)S(1)}, u32[]{:S(2)}, u32[]{:S(2)}) async-start(bf16[32,152,128]{2,1,0:T(8,128)(2,1)} %deal.1), calls=%async_computation | async-start | bytes 2490368 | tf_op jit(solution)/shard_map/all_to_all | solution.py:577
  21.1 11.7 %collective-permute-start.5 = (f32[128,128]{1,0:T(8,128)S(1)}, f32[128,128]{1,0:T(8,128)S(1)}, u32[]{:S(2)}, u32[]{:S(2)}) collective-permute-start(f32[128,128]{1,0:T(8,128)S(1)} %fusion.1), channel_id=1, source_target_pairs={{2,0},{3,1},{4,2},{5,3},{6,4},{7,5},{0,6},{1,7},{10,8},{11,9},{12,... | collective-permute-start | bytes 196616 | tf_op jit(solution)/shard_map/ppermute | solution.py:545
  23.8 9.7 %collective-permute-start.4 = (f32[184,128]{1,0:T(8,128)S(1)}, f32[184,128]{1,0:T(8,128)S(1)}, u32[]{:S(2)}, u32[]{:S(2)}) collective-permute-start(f32[184,128]{1,0:T(8,128)S(1)} %pad_maximum_fusion), channel_id=1, source_target_pairs={{1,0},{2,1},{3,2},{4,3},{5,4},{6,5},{7,6},{0,7},{9,8},{10,9},{11,1... | collective-permute-start | bytes 282632 | tf_op jit(solution)/shard_map/ppermute | solution.py:545
  23.8 12.5 %collective-permute-start.3 = (f32[184,128]{1,0:T(8,128)S(1)}, f32[184,128]{1,0:T(8,128)S(1)}, u32[]{:S(2)}, u32[]{:S(2)}) collective-permute-start(f32[184,128]{1,0:T(8,128)S(1)} %pad_maximum_fusion), channel_id=1, source_target_pairs={{7,0},{0,1},{1,2},{2,3},{3,4},{4,5},{5,6},{6,7},{15,8},{8,9},{9,10... | collective-permute-start | bytes 282632 | tf_op jit(solution)/shard_map/ppermute | solution.py:545
  36.3 7.5 %collective-permute-start.6 = (f32[128,128]{1,0:T(8,128)S(1)}, f32[128,128]{1,0:T(8,128)S(1)}, u32[]{:S(2)}, u32[]{:S(2)}) collective-permute-start(f32[128,128]{1,0:T(8,128)S(1)} %fusion), channel_id=1, source_target_pairs={{4,0},{5,1},{6,2},{7,3},{0,4},{1,5},{2,6},{3,7},{12,8},{13,9},{14,... | collective-permute-start | bytes 196616 | tf_op jit(solution)/shard_map/ppermute | solution.py:545
  50.5 7.7 %copy-start.7 = (bf16[32,152,128]{2,1,0:T(8,128)(2,1)}, bf16[32,152,128]{2,1,0:T(8,128)(2,1)S(1)}, u32[]{:S(2)}) copy-start(bf16[32,152,128]{2,1,0:T(8,128)(2,1)S(1)} %all-to-all-done) | copy-start | bytes 3735556
  51.5 19.5 %collective-permute-start.8 = (bf16[10,152,128]{2,1,0:T(8,128)(2,1)}, bf16[10,152,128]{2,1,0:T(8,128)(2,1)}, u32[]{:S(2)}, u32[]{:S(2)}) collective-permute-start(bf16[10,152,128]{2,1,0:T(8,128)(2,1)} %get-tuple-element.33), channel_id=1, source_target_pairs={{8,0},{16,8},{24,16},{9,1},{17,9},{25,17},{10,2},{18,10},{26,18},{... | collective-permute-start | bytes 1167368 | tf_op jit(solution)/shard_map/ppermute | solution.py:538
  52.8 18.2 %collective-permute-start.7 = (bf16[10,152,128]{2,1,0:T(8,128)(2,1)}, bf16[10,152,128]{2,1,0:T(8,128)(2,1)}, u32[]{:S(2)}, u32[]{:S(2)}) collective-permute-start(bf16[10,152,128]{2,1,0:T(8,128)(2,1)} %get-tuple-element.34), channel_id=1, source_target_pairs={{0,8},{8,16},{16,24},{1,9},{9,17},{17,25},{2,10},{10,18},{18,26},{... | collective-permute-start | bytes 1167368 | tf_op jit(solution)/shard_map/ppermute | solution.py:531
  58.1 12.9 %copy-start = (f32[52,19,8,128]{3,2,1,0:T(8,128)S(1)}, f32[52,19,8,128]{3,2,1,0:T(8,128)}, u32[]{:S(2)}) copy-start(f32[52,19,8,128]{3,2,1,0:T(8,128)} %get-tuple-element.28.across_hbm) | copy-start | bytes 12140548
  58.1 12.9 %copy-start.1 = (f32[52,19,8,128]{3,2,1,0:T(8,128)S(1)}, f32[52,19,8,128]{3,2,1,0:T(8,128)}, u32[]{:S(2)}) copy-start(f32[52,19,8,128]{3,2,1,0:T(8,128)} %get-tuple-element.29.down_hbm) | copy-start | bytes 12140548
  58.1 12.9 %copy-start.5 = (f32[128,128]{1,0:T(8,128)S(1)}, f32[128,128]{1,0:T(8,128)}, u32[]{:S(2)}) copy-start(f32[128,128]{1,0:T(8,128)} %factor_inverse.1.inverse_ref) | copy-start | bytes 196612
  71.1 1.7 %copy-start.2 = (f32[32,19,8,128]{3,2,1,0:T(8,128)S(1)}, f32[32,19,8,128]{3,2,1,0:T(8,128)}, u32[]{:S(2)}) copy-start(f32[32,19,8,128]{3,2,1,0:T(8,128)} %get-tuple-element.31.first_hbm) | copy-start | bytes 7471108
  72.8 1.7 %copy-start.3 = (f32[32,19,8,128]{3,2,1,0:T(8,128)S(1)}, f32[32,19,8,128]{3,2,1,0:T(8,128)}, u32[]{:S(2)}) copy-start(f32[32,19,8,128]{3,2,1,0:T(8,128)} %get-tuple-element.32.second_hbm) | copy-start | bytes 7471108
  74.5 0.9 copy-start.4

commit v9 on v8

--- a/solution.py
+++ b/solution.py
@@ -354,23 +354,23 @@
     for fetch in fetches:
         fetch.wait()
 
-    for s in range(SWEEPS):
-        src, dst = (first_ref, second_ref) if s % 2 == 0 else (second_ref, first_ref)
+    def sweep(s, src, dst, odd_pair):
         count = tall - 2 - 2 * s
-        steps = count // (2 * BLOCK)
 
         def step(c, carry):
-            for h in range(2):
-                row = s + 1 + (2 * c + h) * BLOCK
-                update(src, dst, across_ref, down_ref, sum_ref, row, BLOCK)
+            update(src, dst, across_ref, down_ref, sum_ref, s + 1 + c * BLOCK, BLOCK)
             return carry
 
-        lax.fori_loop(0, steps, step, 0)
-        done = steps * 2 * BLOCK
-        while done < count:
-            take = min(BLOCK, count - done)
-            update(src, dst, across_ref, down_ref, sum_ref, s + 1 + done, take)
-            done += take
+        lax.fori_loop(0, count // BLOCK, step, 0)
+        if odd_pair:
+            update(src, dst, across_ref, down_ref, sum_ref, s + count - 1, 2)
+
+    def two(t, carry):
+        sweep(2 * t, first_ref, second_ref, (tall - 2) % BLOCK == 2)
+        sweep(2 * t + 1, second_ref, first_ref, (tall - 4) % BLOCK == 2)
+        return carry
+
+    lax.fori_loop(0, SWEEPS // 2, two, 0)
 
     near = HALO + 1
     leaving = []
@@ -471,9 +471,13 @@
         fetch.wait()
 
     def sweep(s, src, dst):
-        for start in (s + 1, rows - 1 - HALO - s):
-            for c in range(HALO // take):
-                update(src, dst, across_ref, down_ref, sum_ref, start + c * take, take)
+        def step(c, carry):
+            bottom = c // 2
+            row = jnp.where(bottom == 0, s + 1, rows - 1 - HALO - s) + (c % 2) * take
+            update(src, dst, across_ref, down_ref, sum_ref, row, take)
+            return carry
+
+        lax.fori_loop(0, 4, step, 0)
 
         @pl.when(ends_ref[0] == 1)
         def _():
@@ -521,7 +525,7 @@
         scratch_shapes=[pltpu.VMEM(shape, f32)] * 5
         + [pltpu.VMEM(north.shape, bf16)] * 2
         + [pltpu.SemaphoreType.DMA((10,))],
-        compiler_params=pltpu.CompilerParams(vmem_limit_bytes=VMEM_BYTES // 2),
+        compiler_params=pltpu.CompilerParams(vmem_limit_bytes=VMEM_BYTES),
         name="outer_sweeps",
     )(ends, inverse, total, north, south, first, second, *across_down)
 

time: 92.4 us -> 83.8 us (0.907)
  local copies, waits for them, and re-layouts: 6.45 us -> 2.05 us
  Pallas kernels: 49 us -> 45.7 us
    unnamed x20 -> x12, local copies, waits for them, and re-layouts: 4.31 us -> 0.9 us
    pallas_call x1, Pallas kernels: 16.3 us -> 12.9 us  [outer_sweeps(): pl.pallas_call(functools.partial(outer_kernel, scale), out_shape=jax.Shap...]
    slice x1, local copies, waits for them, and re-layouts: 1.05 us -> 0.06 us  [per_device(): south = from_after(raw[:HALO], 'lat', False)]
  transfers between devices with their start and end apart: 10 -> 10, of which waited for: 5 -> 5; matrix products, arithmetic and copies ran while one was open for 2% -> 3% of each run, Pallas kernels for 27% -> 30%
where the time goes in v9:
time: 83.8 us; the launch traced here: 83.1 us
  Pallas kernels  45.7 us (55%)
  starting transfers between devices  20.7 us (25%)
  waiting for transfers between devices  12.4 us (15%)
  local copies, waits for them, and re-layouts  2.05 us (2%)
  other arithmetic  1.56 us (2%)
    pallas_call x1, Pallas kernels, outer_sweeps(): pl.pallas_call(functools.partial(outer_kernel, scale), out_shape=jax.Shap...  12.9 us
    pallas_call x1, Pallas kernels, inner_sweeps(): pl.pallas_call(inner_kernel, out_shape=(jax.ShapeDtypeStruct(shape, f32),...  12.9 us
    ppermute x7, waiting for transfers between devices, ahead(): lax.ppermute(values, axis, [((i + step) % count, i) for i in range(count)])  12.3 us
    ppermute x7, starting transfers between devices, ahead(): lax.ppermute(values, axis, [((i + step) % count, i) for i in range(count)])  9.25 us
    pallas_call x1, Pallas kernels, deal(): pl.pallas_call(functools.partial(deal_kernel, tiles_lon), out_shape=jax.S...  7.64 us
    pallas_call x1, Pallas kernels, weights(): pl.pallas_call(weight_kernel, out_shape=(jax.ShapeDtypeStruct(shape, f32)...  6.32 us
    pallas_call x1, Pallas kernels, factor_inverse(): pl.pallas_call(inverse_kernel, out_shape=jax.ShapeDtypeStruct(gram.shape,...  5.91 us
    all_to_all x1, starting transfers between devices, per_device(): raw = lax.all_to_all(moving, axes, split_axis=0, concat_axis=0, tiled=True)  5.62 us
  transfers between devices with their start and end apart: 10, of which 5 were waited for; matrix products, arithmetic and copies ran while one was open for 3% of the time, Pallas kernels for 30%

profile of v9, /device:TPU:0, one launch (start us, length us, event | category | flops | bytes accessed | tf_op | source)
XLA Modules:
  0.0 83.1 jit_solution(4573819371469338551)
XLA Ops:
  0.0 7.6 %deal.1 = bf16[32,152,128]{2,1,0:T(8,128)(2,1)} custom-call(bf16[4096,128]{1,0:T(8,128)(2,1)} %basis_ref.1, s32[32,128]{1,0:T(8,128)} %bitcast.19), custom_call_target="tpu_custom_call" | custom-call | flops 5100273664 | bytes 2097152 | tf_op jit(solution)/shard_map/deal/pallas_call | solution.py:129
  7.7 0.5 fusion.5
  8.2 5.1 %collective-permute-start.1 = (f32[152,128]{1,0:T(8,128)S(1)}, f32[152,128]{1,0:T(8,128)S(1)}, u32[]{:S(2)}, u32[]{:S(2)}) collective-permute-start(f32[152,128]{1,0:T(8,128)S(1)} %pad_maximum_fusion.1), channel_id=1, source_target_pairs={{8,0},{16,8},{24,16},{0,24},{9,1},{17,9},{25,17},{1,25},{10,2},{18... | collective-permute-start | bytes 233480 | tf_op jit(solution)/shard_map/ppermute | solution.py:549
  13.3 1.0 %collective-permute-start.2 = (f32[128,128]{1,0:T(8,128)S(1)}, f32[128,128]{1,0:T(8,128)S(1)}, u32[]{:S(2)}, u32[]{:S(2)}) collective-permute-start(f32[128,128]{1,0:T(8,128)S(1)} %fusion.5), channel_id=1, source_target_pairs={{16,0},{24,8},{0,16},{8,24},{17,1},{25,9},{1,17},{9,25},{18,2},{26... | collective-permute-start | bytes 196616 | tf_op jit(solution)/shard_map/ppermute | solution.py:549
  14.3 5.6 %all-to-all-start = ((bf16[32,152,128]{2,1,0:T(8,128)(2,1)}), bf16[32,152,128]{2,1,0:T(8,128)(2,1)S(1)}, u32[]{:S(2)}, u32[]{:S(2)}) async-start(bf16[32,152,128]{2,1,0:T(8,128)(2,1)} %deal.1), calls=%async_computation | async-start | bytes 2490368 | tf_op jit(solution)/shard_map/all_to_all | solution.py:581
  20.0 0.1 pad.21.clone
  20.1 1.0 %collective-permute-done.2 = f32[128,128]{1,0:T(8,128)S(1)} collective-permute-done((f32[128,128]{1,0:T(8,128)S(1)}, f32[128,128]{1,0:T(8,128)S(1)}, u32[]{:S(2)}, u32[]{:S(2)}) %collective-permute-start.2) | collective-permute-done | bytes 65568 | tf_op jit(solution)/shard_map/ppermute | solution.py:549
  21.1 2.5 %collective-permute-start.5 = (f32[128,128]{1,0:T(8,128)S(1)}, f32[128,128]{1,0:T(8,128)S(1)}, u32[]{:S(2)}, u32[]{:S(2)}) collective-permute-start(f32[128,128]{1,0:T(8,128)S(1)} %fusion.1), channel_id=1, source_target_pairs={{2,0},{3,1},{4,2},{5,3},{6,4},{7,5},{0,6},{1,7},{10,8},{11,9},{12,... | collective-permute-start | bytes 196616 | tf_op jit(solution)/shard_map/ppermute | solution.py:549
  23.6 0.1 fusion.3
  23.7 0.1 select_maximum_fusion
  23.8 0.1 collective-permute-start.4
  23.8 0.5 collective-permute-start.3
  24.3 0.7 add_convert_fusion.ends_ref
  25.0 7.7 %collective-permute-done.5 = f32[128,128]{1,0:T(8,128)S(1)} collective-permute-done((f32[128,128]{1,0:T(8,128)S(1)}, f32[128,128]{1,0:T(8,128)S(1)}, u32[]{:S(2)}, u32[]{:S(2)}) %collective-permute-start.5) | collective-permute-done | bytes 65568 | tf_op jit(solution)/shard_map/ppermute | solution.py:549
  32.8 0.8 collective-permute-done.4
  33.5 2.8 %collective-permute-done.3 = f32[184,128]{1,0:T(8,128)S(1)} collective-permute-done((f32[184,128]{1,0:T(8,128)S(1)}, f32[184,128]{1,0:T(8,128)S(1)}, u32[]{:S(2)}, u32[]{:S(2)}) %collective-permute-start.3) | collective-permute-done | bytes 94240 | tf_op jit(solution)/shard_map/ppermute | solution.py:549
  36.4 0.1 collective-permute-start.6
  36.4 0.1 slice.75
  36.5 0.1 pad_maximum_fusion.2
  36.6 0.1 copy.15
  36.8 0.1 copy.17
  36.8 0.6 pad.14.coef_ref
  37.5 6.3 %weights.1 = (f32[52,19,8,128]{3,2,1,0:T(8,128)}, f32[52,19,8,128]{3,2,1,0:T(8,128)}) custom-call(f32[64,256]{1,0:T(8,128)} %pad.14.coef_ref), custom_call_target="tpu_custom_call" | custom-call | flops 101171200 | bytes 8093696 | tf_op jit(solution)/shard_map/weights/pallas_call | solution.py:251
  43.8 0.6 add.41.gram_ref
  44.5 5.9 %factor_inverse.1.inverse_ref = f32[128,128]{1,0:T(8,128)} custom-call(f32[128,128]{1,0:T(8,128)} %add.41.gram_ref), custom_call_target="tpu_custom_call" | custom-call | flops 10737418240 | bytes 131072 | tf_op jit(solution)/shard_map/factor_inverse/pallas_call | solution.py:203
  50.4 0.1 all-to-all-done
  50.5 1.3 %collective-permute-start.8 = (bf16[10,152,128]{2,1,0:T(8,128)(2,1)S(1)}, bf16[10,152,128]{2,1,0:T(8,128)(2,1)S(1)}, u32[]{:S(2)}, u32[]{:S(2)}) collective-permute-start(bf16[10,152,128]{2,1,0:T(8,128)(2,1)S(1)} %get-tuple-element.33), channel_id=1, source_target_pairs={{8,0},{16,8},{24,16},{9,1},{17,9},{25,17},{10,2},{18,10},{26,18},{... | collective-permute-start | bytes 1167368 | tf_op jit(solution)/shard_map/ppermute | solution.py:542
  51.8 4.6 %collective-permute-start.7 = (bf16[10,152,128]{2,1,0:T(8,128)(2,1)S(1)}, bf16[10,152,128]{2,1,0:T(8,128)(2,1)S(1)}, u32[]{:S(2)}, u32[]{:S(2)}) collective-permute-start(bf16[10,152,128]{2,1,0:T(8,128)(2,1)S(1)} %get-tuple-element.34), channel_id=1, source_target_pairs={{0,8},{8,16},{16,24},{1,9},{9,17},{17,25},{2,10},{10,18},{18,26},{... | collective-permute-start | bytes 1167368 | tf_op jit(solution)/shard_map/ppermute | solution.py:535
  56.4 12.9 %inner_sweeps.1 = (f32[32,19,8,128]{3,2,1,0:T(8,128)}, f32[32,19,8,128]{3,2,1,0:T(8,128)}, f32[152,128]{1,0:T(8,128)}) custom-call(bf16[4864,128]{1,0:T(8,128)(2,1)} %bitcast.14, f32[128,128]{1,0:T(8,128)} %factor_inverse.1.inverse_ref, f32[52,19,8,128]{3,2,1,0:T(8,128)} %get-tuple-element.28.across_hbm, f32[52,19,8,128]{3,2,1,0:T(8,128)} %get-tuple-element.29.down_hbm), custom_call_target="tpu_custom_call" | custom-call | flops 12000000000 | bytes 4980736 | tf_op jit(solution)/shard_map/inner_sweeps/pallas_call | solution.py:403
  69.3 0.7 copy-done.2
  70.0 0.2 copy-done.3
  70.2 12.9 %outer_sweeps.1 = f32[32,128]{1,0:T(8,128)} custom-call(s32[2]{0:T(128)} %add_convert_fusion.ends_ref, f32[128,128]{1,0:T(8,128)} %factor_inverse.1.inverse_ref, f32[152,128]{1,0:T(8,128)} %get-tuple-element.30.inner_ref, bf16[1520,128]{1,0:T(8,128)(2,1)} %bitcast.17, bf16[1520,128]{1,0:T(8,128)(2,1)} %bitcast.16, ...), custom_call_target="tpu_custom_call" | custom-call | tf_op jit(solution)/shard_map/outer_sweeps/pallas_call | solution.py:520
  (31 shorter events, 0.2 us)
Async XLA Ops:
  0.0 7.7 %copy-start.4 = (f32[32,128]{1,0:T(8,128)S(1)}, f32[32,128]{1,0:T(8,128)}, u32[]{:S(2)}) copy-start(f32[32,128]{1,0:T(8,128)} %param.7) | copy-start | bytes 49156
  0.0 7.7 %copy-start.5 = (s32[32,128]{1,0:T(8,128)S(1)}, s32[32,128]{1,0:T(8,128)}, u32[]{:S(2)}) copy-start(s32[32,128]{1,0:T(8,128)} %param.6) | copy-start | bytes 49156
  0.0 7.7 %copy-start = (bf16[4096,128]{1,0:T(8,128)(2,1)S(1)}, bf16[4096,128]{1,0:T(8,128)(2,1)}, u32[]{:S(2)}) copy-start(bf16[4096,128]{1,0:T(8,128)(2,1)} %basis_ref.1) | copy-start | bytes 3145732
  8.2 12.8 %collective-permute-start.1 = (f32[152,128]{1,0:T(8,128)S(1)}, f32[152,128]{1,0:T(8,128)S(1)}, u32[]{:S(2)}, u32[]{:S(2)}) collective-permute-start(f32[152,128]{1,0:T(8,128)S(1)} %pad_maximum_fusion.1), channel_id=1, source_target_pairs={{8,0},{16,8},{24,16},{0,24},{9,1},{17,9},{25,17},{1,25},{10,2},{18... | collective-permute-start | bytes 233480 | tf_op jit(solution)/shard_map/ppermute | solution.py:549
  13.3 7.7 %collective-permute-start = (f32[152,128]{1,0:T(8,128)S(1)}, f32[152,128]{1,0:T(8,128)S(1)}, u32[]{:S(2)}, u32[]{:S(2)}) collective-permute-start(f32[152,128]{1,0:T(8,128)S(1)} %pad_maximum_fusion.1), channel_id=1, source_target_pairs={{24,0},{0,8},{8,16},{16,24},{25,1},{1,9},{9,17},{17,25},{26,2},{2,... | collective-permute-start | bytes 233480 | tf_op jit(solution)/shard_map/ppermute | solution.py:549
  13.3 7.7 %collective-permute-start.2 = (f32[128,128]{1,0:T(8,128)S(1)}, f32[128,128]{1,0:T(8,128)S(1)}, u32[]{:S(2)}, u32[]{:S(2)}) collective-permute-start(f32[128,128]{1,0:T(8,128)S(1)} %fusion.5), channel_id=1, source_target_pairs={{16,0},{24,8},{0,16},{8,24},{17,1},{25,9},{1,17},{9,25},{18,2},{26... | collective-permute-start | bytes 196616 | tf_op jit(solution)/shard_map/ppermute | solution.py:549
  14.3 36.1 %all-to-all-start = ((bf16[32,152,128]{2,1,0:T(8,128)(2,1)}), bf16[32,152,128]{2,1,0:T(8,128)(2,1)S(1)}, u32[]{:S(2)}, u32[]{:S(2)}) async-start(bf16[32,152,128]{2,1,0:T(8,128)(2,1)} %deal.1), calls=%async_computation | async-start | bytes 2490368 | tf_op jit(solution)/shard_map/all_to_all | solution.py:581
  21.1 11.7 %collective-permute-start.5 = (f32[128,128]{1,0:T(8,128)S(1)}, f32[128,128]{1,0:T(8,128)S(1)}, u32[]{:S(2)}, u32[]{:S(2)}) collective-permute-start(f32[128,128]{1,0:T(8,128)S(1)} %fusion.1), channel_id=1, source_target_pairs={{2,0},{3,1},{4,2},{5,3},{6,4},{7,5},{0,6},{1,7},{10,8},{11,9},{12,... | collective-permute-start | bytes 196616 | tf_op jit(solution)/shard_map/ppermute | solution.py:549
  23.8 9.7 %collective-permute-start.4 = (f32[184,128]{1,0:T(8,128)S(1)}, f32[184,128]{1,0:T(8,128)S(1)}, u32[]{:S(2)}, u32[]{:S(2)}) collective-permute-start(f32[184,128]{1,0:T(8,128)S(1)} %pad_maximum_fusion), channel_id=1, source_target_pairs={{1,0},{2,1},{3,2},{4,3},{5,4},{6,5},{7,6},{0,7},{9,8},{10,9},{11,1... | collective-permute-start | bytes 282632 | tf_op jit(solution)/shard_map/ppermute | solution.py:549
  23.8 12.5 %collective-permute-start.3 = (f32[184,128]{1,0:T(8,128)S(1)}, f32[184,128]{1,0:T(8,128)S(1)}, u32[]{:S(2)}, u32[]{:S(2)}) collective-permute-start(f32[184,128]{1,0:T(8,128)S(1)} %pad_maximum_fusion), channel_id=1, source_target_pairs={{7,0},{0,1},{1,2},{2,3},{3,4},{4,5},{5,6},{6,7},{15,8},{8,9},{9,10... | collective-permute-start | bytes 282632 | tf_op jit(solution)/shard_map/ppermute | solution.py:549
  36.4 7.5 %collective-permute-start.6 = (f32[128,128]{1,0:T(8,128)S(1)}, f32[128,128]{1,0:T(8,128)S(1)}, u32[]{:S(2)}, u32[]{:S(2)}) collective-permute-start(f32[128,128]{1,0:T(8,128)S(1)} %fusion), channel_id=1, source_target_pairs={{4,0},{5,1},{6,2},{7,3},{0,4},{1,5},{2,6},{3,7},{12,8},{13,9},{14,... | collective-permute-start | bytes 196616 | tf_op jit(solution)/shard_map/ppermute | solution.py:549
  50.5 5.9 %copy-start.1 = (bf16[32,152,128]{2,1,0:T(8,128)(2,1)}, bf16[32,152,128]{2,1,0:T(8,128)(2,1)S(1)}, u32[]{:S(2)}) copy-start(bf16[32,152,128]{2,1,0:T(8,128)(2,1)S(1)} %all-to-all-done) | copy-start | bytes 3735556
  50.5 18.8 %collective-permute-start.8 = (bf16[10,152,128]{2,1,0:T(8,128)(2,1)S(1)}, bf16[10,152,128]{2,1,0:T(8,128)(2,1)S(1)}, u32[]{:S(2)}, u32[]{:S(2)}) collective-permute-start(bf16[10,152,128]{2,1,0:T(8,128)(2,1)S(1)} %get-tuple-element.33), channel_id=1, source_target_pairs={{8,0},{16,8},{24,16},{9,1},{17,9},{25,17},{10,2},{18,10},{26,18},{... | collective-permute-start | bytes 1167368 | tf_op jit(solution)/shard_map/ppermute | solution.py:542
  51.8 17.5 %collective-permute-start.7 = (bf16[10,152,128]{2,1,0:T(8,128)(2,1)S(1)}, bf16[10,152,128]{2,1,0:T(8,128)(2,1)S(1)}, u32[]{:S(2)}, u32[]{:S(2)}) collective-permute-start(bf16[10,152,128]{2,1,0:T(8,128)(2,1)S(1)} %get-tuple-element.34), channel_id=1, source_target_pairs={{0,8},{8,16},{16,24},{1,9},{9,17},{17,25},{2,10},{10,18},{18,26},{... | collective-permute-start | bytes 1167368 | tf_op jit(solution)/shard_map/ppermute | solution.py:535
  69.3 0.7 copy-start.2
  69.3 0.9 %copy-start.3 = (bf16[10,152,128]{2,1,0:T(8,128)(2,1)}, bf16[10,152,128]{2,1,0:T(8,128)(2,1)S(1)}, u32[]{:S(2)}) copy-start(bf16[10,152,128]{2,1,0:T(8,128)(2,1)S(1)} %collective-permute-done.7) | copy-start | bytes 1167364

commit v10 on v9

--- a/solution.py
+++ b/solution.py
@@ -211,7 +211,7 @@
     )(gram)
 
 
-def weight_kernel(coef_ref, across_ref, down_ref, spread):
+def weight_kernel(coef_ref, across_hbm, down_hbm, spread, across_ref, down_ref, sems):
     rows, groups, _, lanes = spread.shape
     places = groups * SUB
     turned = coef_ref[...].T
@@ -239,9 +239,19 @@
             down_ref[r, g] = 0.124 * (here + spread[r + 1, g])
         return carry
 
-    lax.fori_loop(0, rows - 1, weigh, 0)
     across_ref[rows - 1] = jnp.zeros((groups, SUB, lanes), f32)
     down_ref[rows - 1] = jnp.zeros((groups, SUB, lanes), f32)
+    leaving = []
+    for c in range(4):
+        lax.fori_loop(c * per_step, min((c + 1) * per_step, rows - 1), weigh, 0)
+        part = pl.ds(c * per_step, per_step)
+        for k, (source, target) in enumerate(((across_ref, across_hbm), (down_ref, down_hbm))):
+            leaving.append(
+                pltpu.make_async_copy(source.at[part], target.at[part], sems.at[2 * c + k])
+            )
+            leaving[-1].start()
+    for copy in leaving:
+        copy.wait()
 
 
 def weights(coef, lanes):
@@ -251,7 +261,8 @@
     return pl.pallas_call(
         weight_kernel,
         out_shape=(jax.ShapeDtypeStruct(shape, f32),) * 2,
-        scratch_shapes=[pltpu.VMEM(shape, f32)],
+        out_specs=(pl.BlockSpec(memory_space=pl.ANY),) * 2,
+        scratch_shapes=[pltpu.VMEM(shape, f32)] * 3 + [pltpu.SemaphoreType.DMA((8,))],
         compiler_params=pltpu.CompilerParams(vmem_limit_bytes=VMEM_BYTES),
         cost_estimate=pl.CostEstimate(
             flops=rows * places * lanes * 100, bytes_accessed=8 * rows * places * lanes, transcendentals=0
@@ -274,7 +285,7 @@
     return (parts[:, :lanes] + parts[:, lanes:]).astype(bf16).astype(f32)
 
 
-def update(src, dst, across, down, sums, row, take):
+def update(src, dst, across, down, sums, row, take, counted):
     groups = src.shape[1]
     last = groups - 1
     span = range(take)
@@ -295,9 +306,10 @@
             above = under
         return change
 
-    def finish(r, g, new):
+    def finish(r, g, old, new):
         dst[row + r, g] = new
-        sums[row + r, g] += new * new
+        if counted:
+            sums[row + r, g] += old * old + new * new
 
     here = [src[row + r, 1] for r in span]
     west = [across[row + r, 0] * (here[r] - start[r]) for r in span]
@@ -311,10 +323,10 @@
             following, flux = None, closing
         change = vertical(g, here)
         for r in span:
-            finish(r, g, here[r] + (change[r] + (flux[r] - west[r])))
+            finish(r, g, here[r], here[r] + (change[r] + (flux[r] - west[r])))
         here, west = following, flux
     for r in span:
-        finish(r, 0, pending[r] - wrapped[r])
+        finish(r, 0, start[r], pending[r] - wrapped[r])
 
 
 def summed_lanes(sums, rows, totals):
@@ -342,32 +354,30 @@
     take = 4
     cells = take * groups * SUB
 
-    def fill(c, carry):
-        field = rotated(own_ref[pl.ds(pl.multiple_of(c * cells, 16), cells), :], turn)
-        first_ref[pl.ds(c * take, take)] = field.reshape(take, groups, SUB, lanes)
-        return carry
-
-    lax.fori_loop(0, tall // take, fill, 0)
+    for c in range(tall // take):
+        field = rotated(own_ref[c * cells : (c + 1) * cells, :], turn)
+        first_ref[c * take : (c + 1) * take] = field.reshape(take, groups, SUB, lanes)
     sum_ref[...] = jnp.zeros_like(sum_ref)
     second_ref[0] = jnp.zeros(second_ref.shape[1:], f32)
     second_ref[tall - 1] = jnp.zeros(second_ref.shape[1:], f32)
     for fetch in fetches:
         fetch.wait()
 
-    def sweep(s, src, dst, odd_pair):
+    def sweep(s, src, dst, odd_pair, counted):
         count = tall - 2 - 2 * s
 
         def step(c, carry):
-            update(src, dst, across_ref, down_ref, sum_ref, s + 1 + c * BLOCK, BLOCK)
+            row = s + 1 + c * BLOCK
+            update(src, dst, across_ref, down_ref, sum_ref, row, BLOCK, counted)
             return carry
 
         lax.fori_loop(0, count // BLOCK, step, 0)
         if odd_pair:
-            update(src, dst, across_ref, down_ref, sum_ref, s + count - 1, 2)
+            update(src, dst, across_ref, down_ref, sum_ref, s + count - 1, 2, counted)
 
     def two(t, carry):
-        sweep(2 * t, first_ref, second_ref, (tall - 2) % BLOCK == 2)
-        sweep(2 * t + 1, second_ref, first_ref, (tall - 4) % BLOCK == 2)
+        sweep(2 * t, first_ref, second_ref, (tall - 2) % BLOCK == 2, False)
+        sweep(2 * t + 1, second_ref, first_ref, (tall - 4) % BLOCK == 2, True)
         return carry
 
     lax.fori_loop(0, SWEEPS // 2, two, 0)
@@ -428,30 +438,38 @@
     places = groups * SUB
     near = HALO + 1
     halos = [
-        pltpu.make_async_copy(north_hbm, north_ref, sems.at[8]),
-        pltpu.make_async_copy(south_hbm, south_ref, sems.at[9]),
+        pltpu.make_async_copy(north_hbm, north_ref, sems.at[0]),
+        pltpu.make_async_copy(south_hbm, south_ref, sems.at[1]),
     ]
     for halo in halos:
         halo.start()
-    fetches = []
-    for k, (source, target) in enumerate(((first_hbm, first_ref), (second_hbm, second_ref))):
-        for side, row in enumerate((0, tall - near)):
-            fetches.append(
-                pltpu.make_async_copy(
-                    source.at[pl.ds(row, near)],
-                    target.at[pl.ds(HALO + row, near)],
-                    sems.at[2 * k + side],
-                )
+    soon, late = [], []
+
+    def fetch(wave, source, target, start, take, shift):
+        wave.append(
+            pltpu.make_async_copy(
+                source.at[pl.ds(start, take)],
+                target.at[pl.ds(start + shift, take)],
+                sems.at[2 + len(soon) + len(late)],
             )
+        )
+
+    reach = HALO + 2
     wide_part = 2 * HALO + 1
-    for k, (source, target) in enumerate(((across_hbm, across_ref), (down_hbm, down_ref))):
-        for side, row in enumerate((0, rows - wide_part)):
-            part = pl.ds(row, wide_part)
-            fetches.append(
-                pltpu.make_async_copy(source.at[part], target.at[part], sems.at[4 + 2 * k + side])
-            )
-    for fetch in fetches:
-        fetch.start()
+    for source, target in ((across_hbm, across_ref), (down_hbm, down_ref)):
+        fetch(soon, source, target, 0, reach, 0)
+        fetch(soon, source, target, rows - reach, reach, 0)
+    fetch(soon, first_hbm, first_ref, 0, 2, HALO)
+    fetch(soon, first_hbm, first_ref, tall - 2, 2, HALO)
+    fetch(late, second_hbm, second_ref, 1, near - 1, HALO)
+    fetch(late, second_hbm, second_ref, tall - near, near - 1, HALO)
+    for source, target in ((across_hbm, across_ref), (down_hbm, down_ref)):
+        fetch(late, source, target, reach, wide_part - reach, 0)
+        fetch(late, source, target, rows - wide_part, wide_part - reach, 0)
+    fetch(late, first_hbm, first_ref, 2, near - 2, HALO)
+    fetch(late, first_hbm, first_ref, tall - near, near - 2, HALO)
+    for copy in soon + late:
+        copy.start()
     sum_ref[...] = jnp.zeros_like(sum_ref)
     turn = rotation(inverse_ref[...])
     for halo in halos:
@@ -459,22 +477,21 @@
     take = 2
     cells = take * places
 
-    def fill(c, carry):
+    for c in range(HALO // take):
         for source, offset in ((north_ref, 0), (south_ref, HALO + tall)):
-            field = rotated(source[pl.ds(pl.multiple_of(c * cells, 16), cells), :], turn)
-            first_ref[pl.ds(offset + c * take, take)] = field.reshape(take, groups, SUB, lanes)
-        return carry
-
-    lax.fori_loop(0, HALO // take, fill, 0)
+            field = rotated(source[c * cells : (c + 1) * cells, :], turn)
+            first_ref[offset + c * take : offset + (c + 1) * take] = field.reshape(
+                take, groups, SUB, lanes
+            )
     take = HALO // 2
-    for fetch in fetches:
-        fetch.wait()
-
-    def sweep(s, src, dst):
+    for copy in soon:
+        copy.wait()
+
+    def sweep(s, src, dst, counted):
         def step(c, carry):
             bottom = c // 2
             row = jnp.where(bottom == 0, s + 1, rows - 1 - HALO - s) + (c % 2) * take
-            update(src, dst, across_ref, down_ref, sum_ref, row, take)
+            update(src, dst, across_ref, down_ref, sum_ref, row, take, counted)
             return carry
 
         lax.fori_loop(0, 4, step, 0)
@@ -487,12 +504,17 @@
         def _():
             dst[HALO + tall] = jnp.zeros(dst.shape[1:], f32)
 
+    sweep(0, first_ref, second_ref, False)
+    for copy in late:
+        copy.wait()
+    sweep(1, second_ref, first_ref, True)
+
     def two(t, carry):
-        sweep(2 * t, first_ref, second_ref)
-        sweep(2 * t + 1, second_ref, first_ref)
+        sweep(2 * t, first_ref, second_ref, False)
+        sweep(2 * t + 1, second_ref, first_ref, True)
         return carry
 
-    lax.fori_loop(0, SWEEPS // 2, two, 0)
+    lax.fori_loop(1, SWEEPS // 2, two, 0)
 
     def gather(c, totals):
         pairs = []
@@ -524,7 +546,7 @@
         out_specs=vmem,
         scratch_shapes=[pltpu.VMEM(shape, f32)] * 5
         + [pltpu.VMEM(north.shape, bf16)] * 2
-        + [pltpu.SemaphoreType.DMA((10,))],
+        + [pltpu.SemaphoreType.DMA((16,))],
         compiler_params=pltpu.CompilerParams(vmem_limit_bytes=VMEM_BYTES),
         name="outer_sweeps",
     )(ends, inverse, total, north, south, first, second, *across_down)

time: 83.8 us -> 82.9 us (0.989)
  Pallas kernels: 45.7 us -> 44 us
  transfers between devices with their start and end apart: 10 -> 10, of which waited for: 5 -> 5; matrix products, arithmetic and copies ran while one was open for 3% -> 3% of each run, Pallas kernels for 30% -> 29%
where the time goes in v10:
time: 82.9 us; the launch traced here: 82.4 us
  Pallas kernels  44 us (53%)
  starting transfers between devices  20.9 us (25%)
  waiting for transfers between devices  13.1 us (16%)
  local copies, waits for them, and re-layouts  2.05 us (2%)
  other arithmetic  1.56 us (2%)
    pallas_call x1, Pallas kernels, inner_sweeps(): pl.pallas_call(inner_kernel, out_shape=(jax.ShapeDtypeStruct(shape, f32),...  12.5 us
    ppermute x7, waiting for transfers between devices, ahead(): lax.ppermute(values, axis, [((i + step) % count, i) for i in range(count)])  12.3 us
    pallas_call x1, Pallas kernels, outer_sweeps(): pl.pallas_call(functools.partial(outer_kernel, scale), out_shape=jax.Shap...  12.3 us
    ppermute x7, starting transfers between devices, ahead(): lax.ppermute(values, axis, [((i + step) % count, i) for i in range(count)])  9.24 us
    pallas_call x1, Pallas kernels, deal(): pl.pallas_call(functools.partial(deal_kernel, tiles_lon), out_shape=jax.S...  7.64 us
    pallas_call x1, Pallas kernels, factor_inverse(): pl.pallas_call(inverse_kernel, out_shape=jax.ShapeDtypeStruct(gram.shape,...  5.91 us
    pallas_call x1, Pallas kernels, weights(): pl.pallas_call(weight_kernel, out_shape=(jax.ShapeDtypeStruct(shape, f32)...  5.66 us
    all_to_all x1, starting transfers between devices, per_device(): raw = lax.all_to_all(moving, axes, split_axis=0, concat_axis=0, tiled=True)  5.62 us
  transfers between devices with their start and end apart: 10, of which 5 were waited for; matrix products, arithmetic and copies ran while one was open for 3% of the time, Pallas kernels for 29%

profile of v10, /device:TPU:0, one launch (start us, length us, event | category | flops | bytes accessed | tf_op | source)
XLA Modules:
  0.0 82.4 jit_solution(16030378444677930509)
XLA Ops:
  0.0 7.6 %deal.1 = bf16[32,152,128]{2,1,0:T(8,128)(2,1)} custom-call(bf16[4096,128]{1,0:T(8,128)(2,1)} %basis_ref.1, s32[32,128]{1,0:T(8,128)} %bitcast.19), custom_call_target="tpu_custom_call" | custom-call | flops 5100273664 | bytes 2097152 | tf_op jit(solution)/shard_map/deal/pallas_call | solution.py:129
  7.7 0.5 fusion.5
  8.2 5.1 %collective-permute-start.1 = (f32[152,128]{1,0:T(8,128)S(1)}, f32[152,128]{1,0:T(8,128)S(1)}, u32[]{:S(2)}, u32[]{:S(2)}) collective-permute-start(f32[152,128]{1,0:T(8,128)S(1)} %pad_maximum_fusion.1), channel_id=1, source_target_pairs={{8,0},{16,8},{24,16},{0,24},{9,1},{17,9},{25,17},{1,25},{10,2},{18... | collective-permute-start | bytes 233480 | tf_op jit(solution)/shard_map/ppermute | solution.py:571
  13.3 1.0 %collective-permute-start.2 = (f32[128,128]{1,0:T(8,128)S(1)}, f32[128,128]{1,0:T(8,128)S(1)}, u32[]{:S(2)}, u32[]{:S(2)}) collective-permute-start(f32[128,128]{1,0:T(8,128)S(1)} %fusion.5), channel_id=1, source_target_pairs={{16,0},{24,8},{0,16},{8,24},{17,1},{25,9},{1,17},{9,25},{18,2},{26... | collective-permute-start | bytes 196616 | tf_op jit(solution)/shard_map/ppermute | solution.py:571
  14.3 5.6 %all-to-all-start = ((bf16[32,152,128]{2,1,0:T(8,128)(2,1)}), bf16[32,152,128]{2,1,0:T(8,128)(2,1)S(1)}, u32[]{:S(2)}, u32[]{:S(2)}) async-start(bf16[32,152,128]{2,1,0:T(8,128)(2,1)} %deal.1), calls=%async_computation | async-start | bytes 2490368 | tf_op jit(solution)/shard_map/all_to_all | solution.py:603
  20.0 0.1 pad.21.clone
  20.1 1.0 %collective-permute-done.2 = f32[128,128]{1,0:T(8,128)S(1)} collective-permute-done((f32[128,128]{1,0:T(8,128)S(1)}, f32[128,128]{1,0:T(8,128)S(1)}, u32[]{:S(2)}, u32[]{:S(2)}) %collective-permute-start.2) | collective-permute-done | bytes 65568 | tf_op jit(solution)/shard_map/ppermute | solution.py:571
  21.1 2.5 %collective-permute-start.5 = (f32[128,128]{1,0:T(8,128)S(1)}, f32[128,128]{1,0:T(8,128)S(1)}, u32[]{:S(2)}, u32[]{:S(2)}) collective-permute-start(f32[128,128]{1,0:T(8,128)S(1)} %fusion.1), channel_id=1, source_target_pairs={{2,0},{3,1},{4,2},{5,3},{6,4},{7,5},{0,6},{1,7},{10,8},{11,9},{12,... | collective-permute-start | bytes 196616 | tf_op jit(solution)/shard_map/ppermute | solution.py:571
  23.6 0.1 fusion.3
  23.7 0.1 select_maximum_fusion
  23.8 0.1 collective-permute-start.4
  23.8 0.5 collective-permute-start.3
  24.3 0.7 add_convert_fusion.ends_ref
  25.0 7.8 %collective-permute-done.5 = f32[128,128]{1,0:T(8,128)S(1)} collective-permute-done((f32[128,128]{1,0:T(8,128)S(1)}, f32[128,128]{1,0:T(8,128)S(1)}, u32[]{:S(2)}, u32[]{:S(2)}) %collective-permute-start.5) | collective-permute-done | bytes 65568 | tf_op jit(solution)/shard_map/ppermute | solution.py:571
  32.8 0.8 collective-permute-done.4
  33.5 2.8 %collective-permute-done.3 = f32[184,128]{1,0:T(8,128)S(1)} collective-permute-done((f32[184,128]{1,0:T(8,128)S(1)}, f32[184,128]{1,0:T(8,128)S(1)}, u32[]{:S(2)}, u32[]{:S(2)}) %collective-permute-start.3) | collective-permute-done | bytes 94240 | tf_op jit(solution)/shard_map/ppermute | solution.py:571
  36.4 0.1 collective-permute-start.6
  36.4 0.1 slice.75
  36.5 0.1 pad_maximum_fusion.2
  36.6 0.1 copy.15
  36.8 0.1 copy.17
  36.8 0.6 pad.14.coef_ref
  37.5 5.7 %weights.1 = (f32[52,19,8,128]{3,2,1,0:T(8,128)}, f32[52,19,8,128]{3,2,1,0:T(8,128)}) custom-call(f32[64,256]{1,0:T(8,128)} %pad.14.coef_ref), custom_call_target="tpu_custom_call" | custom-call | flops 101171200 | bytes 8093696 | tf_op jit(solution)/shard_map/weights/pallas_call | solution.py:261
  43.2 0.6 add.41.gram_ref
  43.8 5.9 %factor_inverse.1.inverse_ref = f32[128,128]{1,0:T(8,128)} custom-call(f32[128,128]{1,0:T(8,128)} %add.41.gram_ref), custom_call_target="tpu_custom_call" | custom-call | flops 10737418240 | bytes 131072 | tf_op jit(solution)/shard_map/factor_inverse/pallas_call | solution.py:203
  49.7 0.7 all-to-all-done
  50.5 1.3 %collective-permute-start.8 = (bf16[10,152,128]{2,1,0:T(8,128)(2,1)S(1)}, bf16[10,152,128]{2,1,0:T(8,128)(2,1)S(1)}, u32[]{:S(2)}, u32[]{:S(2)}) collective-permute-start(bf16[10,152,128]{2,1,0:T(8,128)(2,1)S(1)} %get-tuple-element.33), channel_id=1, source_target_pairs={{8,0},{16,8},{24,16},{9,1},{17,9},{25,17},{10,2},{18,10},{26,18},{... | collective-permute-start | bytes 1167368 | tf_op jit(solution)/shard_map/ppermute | solution.py:564
  51.8 4.8 %collective-permute-start.7 = (bf16[10,152,128]{2,1,0:T(8,128)(2,1)S(1)}, bf16[10,152,128]{2,1,0:T(8,128)(2,1)S(1)}, u32[]{:S(2)}, u32[]{:S(2)}) collective-permute-start(bf16[10,152,128]{2,1,0:T(8,128)(2,1)S(1)} %get-tuple-element.34), channel_id=1, source_target_pairs={{0,8},{8,16},{16,24},{1,9},{9,17},{17,25},{2,10},{10,18},{18,26},{... | collective-permute-start | bytes 1167368 | tf_op jit(solution)/shard_map/ppermute | solution.py:557
  56.6 12.5 %inner_sweeps.1 = (f32[32,19,8,128]{3,2,1,0:T(8,128)}, f32[32,19,8,128]{3,2,1,0:T(8,128)}, f32[152,128]{1,0:T(8,128)}) custom-call(bf16[4864,128]{1,0:T(8,128)(2,1)} %bitcast.14, f32[128,128]{1,0:T(8,128)} %factor_inverse.1.inverse_ref, f32[52,19,8,128]{3,2,1,0:T(8,128)} %get-tuple-element.28.across_hbm, f32[52,19,8,128]{3,2,1,0:T(8,128)} %get-tuple-element.29.down_hbm), custom_call_target="tpu_custom_call" | custom-call | flops 12000000000 | bytes 4980736 | tf_op jit(solution)/shard_map/inner_sweeps/pallas_call | solution.py:413
  69.1 0.7 copy-done.2
  69.8 0.2 copy-done.3
  70.0 12.3 %outer_sweeps.1 = f32[32,128]{1,0:T(8,128)} custom-call(s32[2]{0:T(128)} %add_convert_fusion.ends_ref, f32[128,128]{1,0:T(8,128)} %factor_inverse.1.inverse_ref, f32[152,128]{1,0:T(8,128)} %get-tuple-element.30.inner_ref, bf16[1520,128]{1,0:T(8,128)(2,1)} %bitcast.17, bf16[1520,128]{1,0:T(8,128)(2,1)} %bitcast.16, ...), custom_call_target="tpu_custom_call" | custom-call | tf_op jit(solution)/shard_map/outer_sweeps/pallas_call | solution.py:542
  (31 shorter events, 0.2 us)
Async XLA Ops:
  0.0 7.7 %copy-start.4 = (f32[32,128]{1,0:T(8,128)S(1)}, f32[32,128]{1,0:T(8,128)}, u32[]{:S(2)}) copy-start(f32[32,128]{1,0:T(8,128)} %param.7) | copy-start | bytes 49156
  0.0 7.7 %copy-start.5 = (s32[32,128]{1,0:T(8,128)S(1)}, s32[32,128]{1,0:T(8,128)}, u32[]{:S(2)}) copy-start(s32[32,128]{1,0:T(8,128)} %param.6) | copy-start | bytes 49156
  0.0 7.7 %copy-start = (bf16[4096,128]{1,0:T(8,128)(2,1)S(1)}, bf16[4096,128]{1,0:T(8,128)(2,1)}, u32[]{:S(2)}) copy-start(bf16[4096,128]{1,0:T(8,128)(2,1)} %basis_ref.1) | copy-start | bytes 3145732
  8.2 12.8 %collective-permute-start.1 = (f32[152,128]{1,0:T(8,128)S(1)}, f32[152,128]{1,0:T(8,128)S(1)}, u32[]{:S(2)}, u32[]{:S(2)}) collective-permute-start(f32[152,128]{1,0:T(8,128)S(1)} %pad_maximum_fusion.1), channel_id=1, source_target_pairs={{8,0},{16,8},{24,16},{0,24},{9,1},{17,9},{25,17},{1,25},{10,2},{18... | collective-permute-start | bytes 233480 | tf_op jit(solution)/shard_map/ppermute | solution.py:571
  13.3 7.7 %collective-permute-start = (f32[152,128]{1,0:T(8,128)S(1)}, f32[152,128]{1,0:T(8,128)S(1)}, u32[]{:S(2)}, u32[]{:S(2)}) collective-permute-start(f32[152,128]{1,0:T(8,128)S(1)} %pad_maximum_fusion.1), channel_id=1, source_target_pairs={{24,0},{0,8},{8,16},{16,24},{25,1},{1,9},{9,17},{17,25},{26,2},{2,... | collective-permute-start | bytes 233480 | tf_op jit(solution)/shard_map/ppermute | solution.py:571
  13.3 7.7 %collective-permute-start.2 = (f32[128,128]{1,0:T(8,128)S(1)}, f32[128,128]{1,0:T(8,128)S(1)}, u32[]{:S(2)}, u32[]{:S(2)}) collective-permute-start(f32[128,128]{1,0:T(8,128)S(1)} %fusion.5), channel_id=1, source_target_pairs={{16,0},{24,8},{0,16},{8,24},{17,1},{25,9},{1,17},{9,25},{18,2},{26... | collective-permute-start | bytes 196616 | tf_op jit(solution)/shard_map/ppermute | solution.py:571
  14.3 36.1 %all-to-all-start = ((bf16[32,152,128]{2,1,0:T(8,128)(2,1)}), bf16[32,152,128]{2,1,0:T(8,128)(2,1)S(1)}, u32[]{:S(2)}, u32[]{:S(2)}) async-start(bf16[32,152,128]{2,1,0:T(8,128)(2,1)} %deal.1), calls=%async_computation | async-start | bytes 2490368 | tf_op jit(solution)/shard_map/all_to_all | solution.py:603
  21.1 11.7 %collective-permute-start.5 = (f32[128,128]{1,0:T(8,128)S(1)}, f32[128,128]{1,0:T(8,128)S(1)}, u32[]{:S(2)}, u32[]{:S(2)}) collective-permute-start(f32[128,128]{1,0:T(8,128)S(1)} %fusion.1), channel_id=1, source_target_pairs={{2,0},{3,1},{4,2},{5,3},{6,4},{7,5},{0,6},{1,7},{10,8},{11,9},{12,... | collective-permute-start | bytes 196616 | tf_op jit(solution)/shard_map/ppermute | solution.py:571
  23.8 9.7 %collective-permute-start.4 = (f32[184,128]{1,0:T(8,128)S(1)}, f32[184,128]{1,0:T(8,128)S(1)}, u32[]{:S(2)}, u32[]{:S(2)}) collective-permute-start(f32[184,128]{1,0:T(8,128)S(1)} %pad_maximum_fusion), channel_id=1, source_target_pairs={{1,0},{2,1},{3,2},{4,3},{5,4},{6,5},{7,6},{0,7},{9,8},{10,9},{11,1... | collective-permute-start | bytes 282632 | tf_op jit(solution)/shard_map/ppermute | solution.py:571
  23.8 12.5 %collective-permute-start.3 = (f32[184,128]{1,0:T(8,128)S(1)}, f32[184,128]{1,0:T(8,128)S(1)}, u32[]{:S(2)}, u32[]{:S(2)}) collective-permute-start(f32[184,128]{1,0:T(8,128)S(1)} %pad_maximum_fusion), channel_id=1, source_target_pairs={{7,0},{0,1},{1,2},{2,3},{3,4},{4,5},{5,6},{6,7},{15,8},{8,9},{9,10... | collective-permute-start | bytes 282632 | tf_op jit(solution)/shard_map/ppermute | solution.py:571
  36.4 6.8 %collective-permute-start.6 = (f32[128,128]{1,0:T(8,128)S(1)}, f32[128,128]{1,0:T(8,128)S(1)}, u32[]{:S(2)}, u32[]{:S(2)}) collective-permute-start(f32[128,128]{1,0:T(8,128)S(1)} %fusion), channel_id=1, source_target_pairs={{4,0},{5,1},{6,2},{7,3},{0,4},{1,5},{2,6},{3,7},{12,8},{13,9},{14,... | collective-permute-start | bytes 196616 | tf_op jit(solution)/shard_map/ppermute | solution.py:571
  50.5 6.1 %copy-start.1 = (bf16[32,152,128]{2,1,0:T(8,128)(2,1)}, bf16[32,152,128]{2,1,0:T(8,128)(2,1)S(1)}, u32[]{:S(2)}) copy-start(bf16[32,152,128]{2,1,0:T(8,128)(2,1)S(1)} %all-to-all-done) | copy-start | bytes 3735556
  50.5 18.5 %collective-permute-start.8 = (bf16[10,152,128]{2,1,0:T(8,128)(2,1)S(1)}, bf16[10,152,128]{2,1,0:T(8,128)(2,1)S(1)}, u32[]{:S(2)}, u32[]{:S(2)}) collective-permute-start(bf16[10,152,128]{2,1,0:T(8,128)(2,1)S(1)} %get-tuple-element.33), channel_id=1, source_target_pairs={{8,0},{16,8},{24,16},{9,1},{17,9},{25,17},{10,2},{18,10},{26,18},{... | collective-permute-start | bytes 1167368 | tf_op jit(solution)/shard_map/ppermute | solution.py:564
  51.8 17.3 %collective-permute-start.7 = (bf16[10,152,128]{2,1,0:T(8,128)(2,1)S(1)}, bf16[10,152,128]{2,1,0:T(8,128)(2,1)S(1)}, u32[]{:S(2)}, u32[]{:S(2)}) collective-permute-start(bf16[10,152,128]{2,1,0:T(8,128)(2,1)S(1)} %get-tuple-element.34), channel_id=1, source_target_pairs={{0,8},{8,16},{16,24},{1,9},{9,17},{17,25},{2,10},{10,18},{18,26},{... | collective-permute-start | bytes 1167368 | tf_op jit(solution)/shard_map/ppermute | solution.py:557
  69.1 0.7 copy-start.2
  69.1 0.9 %copy-start.3 = (bf16[10,152,128]{2,1,0:T(8,128)(2,1)}, bf16[10,152,128]{2,1,0:T(8,128)(2,1)S(1)}, u32[]{:S(2)}) copy-start(bf16[10,152,128]{2,1,0:T(8,128)(2,1)S(1)} %collective-permute-done.7) | copy-start | bytes 1167364

commit v11 on v10

--- a/solution.py
+++ b/solution.py
@@ -13,7 +13,7 @@
 SUB = 8
 ONE_HOT = 1024
 TILES = 4
-BLOCK = 4
+BLOCK = 8
 VMEM_BYTES = 56 * 1024 * 1024
 
 bf16, f32, i32 = jnp.bfloat16, jnp.float32, jnp.int32
@@ -285,7 +285,7 @@
     return (parts[:, :lanes] + parts[:, lanes:]).astype(bf16).astype(f32)
 
 
-def update(src, dst, across, down, sums, row, take, counted):
+def update(src, dst, across, down, sums, row, take, counted, kept=True):
     groups = src.shape[1]
     last = groups - 1
     span = range(take)
@@ -307,7 +307,8 @@
         return change
 
     def finish(r, g, old, new):
-        dst[row + r, g] = new
+        if kept:
+            dst[row + r, g] = new
         if counted:
             sums[row + r, g] += old * old + new * new
 
@@ -363,24 +364,20 @@
     for fetch in fetches:
         fetch.wait()
 
-    def sweep(s, src, dst, odd_pair, counted):
+    for s in range(SWEEPS):
+        src, dst = (first_ref, second_ref) if s % 2 == 0 else (second_ref, first_ref)
         count = tall - 2 - 2 * s
+        size = -(-count // -(-count // BLOCK))
+        run = functools.partial(update, src, dst, across_ref, down_ref, sum_ref)
+        flags = (s % 2 == 1, s < SWEEPS - 1)
 
         def step(c, carry):
-            row = s + 1 + c * BLOCK
-            update(src, dst, across_ref, down_ref, sum_ref, row, BLOCK, counted)
+            run(s + 1 + c * size, size, *flags)
             return carry
 
-        lax.fori_loop(0, count // BLOCK, step, 0)
-        if odd_pair:
-            update(src, dst, across_ref, down_ref, sum_ref, s + count - 1, 2, counted)
-
-    def two(t, carry):
-        sweep(2 * t, first_ref, second_ref, (tall - 2) % BLOCK == 2, False)
-        sweep(2 * t + 1, second_ref, first_ref, (tall - 4) % BLOCK == 2, True)
-        return carry
-
-    lax.fori_loop(0, SWEEPS // 2, two, 0)
+        lax.fori_loop(0, count // size, step, 0)
+        if count % size:
+            run(s + 1 + count - count % size, count % size, *flags)
 
     near = HALO + 1
     leaving = []
@@ -487,34 +484,40 @@
     for copy in soon:
         copy.wait()
 
-    def sweep(s, src, dst, counted):
-        def step(c, carry):
-            bottom = c // 2
-            row = jnp.where(bottom == 0, s + 1, rows - 1 - HALO - s) + (c % 2) * take
-            update(src, dst, across_ref, down_ref, sum_ref, row, take, counted)
+    for s in range(SWEEPS):
+        src, dst = (first_ref, second_ref) if s % 2 == 0 else (second_ref, first_ref)
+        run = functools.partial(update, src, dst, across_ref, down_ref, sum_ref)
+        if s == 1:
+            for copy in late:
+                copy.wait()
+
+        def both(side, carry):
+            halo = HALO - 1 - s
+            if s % 2 == 0:
+                start = jnp.where(side == 0, s + 1, rows - 1 - HALO - s)
+                run(start, take, False)
+                run(start + take, take, False)
+                return carry
+            if halo > 0:
+                run(jnp.where(side == 0, s + 1, HALO + tall), halo, False)
+            start = jnp.where(side == 0, HALO, rows - 1 - HALO - s)
+            done = 0
+            while done < s + 1:
+                size = min(s + 1 - done, 2 * take if s + 1 < 2 * take else take)
+                run(start + done, size, True, s < SWEEPS - 1)
+                done += size
             return carry
 
-        lax.fori_loop(0, 4, step, 0)
-
-        @pl.when(ends_ref[0] == 1)
-        def _():
-            dst[HALO - 1] = jnp.zeros(dst.shape[1:], f32)
-
-        @pl.when(ends_ref[1] == 1)
-        def _():
-            dst[HALO + tall] = jnp.zeros(dst.shape[1:], f32)
-
-    sweep(0, first_ref, second_ref, False)
-    for copy in late:
-        copy.wait()
-    sweep(1, second_ref, first_ref, True)
-
-    def two(t, carry):
-        sweep(2 * t, first_ref, second_ref, False)
-        sweep(2 * t + 1, second_ref, first_ref, True)
-        return carry
-
-    lax.fori_loop(1, SWEEPS // 2, two, 0)
+        lax.fori_loop(0, 2, both, 0)
+        if s < SWEEPS - 1:
+
+            @pl.when(ends_ref[0] == 1)
+            def _():
+                dst[HALO - 1] = jnp.zeros(dst.shape[1:], f32)
+
+            @pl.when(ends_ref[1] == 1)
+            def _():
+                dst[HALO + tall] = jnp.zeros(dst.shape[1:], f32)
 
     def gather(c, totals):
         pairs = []

time: 82.9 us -> 81.2 us (0.979)
  Pallas kernels: 44 us -> 42.3 us
where the time goes in v11:
time: 81.2 us; the launch traced here: 80.8 us
  Pallas kernels  42.3 us (52%)
  starting transfers between devices  20.9 us (26%)
  waiting for transfers between devices  13.1 us (16%)
  local copies, waits for them, and re-layouts  2.05 us (3%)
  other arithmetic  1.56 us (2%)
    ppermute x7, waiting for transfers between devices, ahead(): lax.ppermute(values, axis, [((i + step) % count, i) for i in range(count)])  12.3 us
    pallas_call x1, Pallas kernels, inner_sweeps(): pl.pallas_call(inner_kernel, out_shape=(jax.ShapeDtypeStruct(shape, f32),...  11.7 us
    pallas_call x1, Pallas kernels, outer_sweeps(): pl.pallas_call(functools.partial(outer_kernel, scale), out_shape=jax.Shap...  11.5 us
    ppermute x7, starting transfers between devices, ahead(): lax.ppermute(values, axis, [((i + step) % count, i) for i in range(count)])  9.24 us
    pallas_call x1, Pallas kernels, deal(): pl.pallas_call(functools.partial(deal_kernel, tiles_lon), out_shape=jax.S...  7.64 us
    pallas_call x1, Pallas kernels, factor_inverse(): pl.pallas_call(inverse_kernel, out_shape=jax.ShapeDtypeStruct(gram.shape,...  5.91 us
    pallas_call x1, Pallas kernels, weights(): pl.pallas_call(weight_kernel, out_shape=(jax.ShapeDtypeStruct(shape, f32)...  5.66 us
    all_to_all x1, starting transfers between devices, per_device(): raw = lax.all_to_all(moving, axes, split_axis=0, concat_axis=0, tiled=True)  5.62 us
  transfers between devices with their start and end apart: 10, of which 5 were waited for; matrix products, arithmetic and copies ran while one was open for 3% of the time, Pallas kernels for 29%

profile of v11, /device:TPU:0, one launch (start us, length us, event | category | flops | bytes accessed | tf_op | source)
XLA Modules:
  0.0 80.8 jit_solution(10023531082747054856)
XLA Ops:
  0.0 7.6 %deal.1 = bf16[32,152,128]{2,1,0:T(8,128)(2,1)} custom-call(bf16[4096,128]{1,0:T(8,128)(2,1)} %basis_ref.1, s32[32,128]{1,0:T(8,128)} %bitcast.19), custom_call_target="tpu_custom_call" | custom-call | flops 5100273664 | bytes 2097152 | tf_op jit(solution)/shard_map/deal/pallas_call | solution.py:129
  7.7 0.5 fusion.5
  8.2 5.1 %collective-permute-start.1 = (f32[152,128]{1,0:T(8,128)S(1)}, f32[152,128]{1,0:T(8,128)S(1)}, u32[]{:S(2)}, u32[]{:S(2)}) collective-permute-start(f32[152,128]{1,0:T(8,128)S(1)} %pad_maximum_fusion.1), channel_id=1, source_target_pairs={{8,0},{16,8},{24,16},{0,24},{9,1},{17,9},{25,17},{1,25},{10,2},{18... | collective-permute-start | bytes 233480 | tf_op jit(solution)/shard_map/ppermute | solution.py:574
  13.3 1.0 %collective-permute-start.2 = (f32[128,128]{1,0:T(8,128)S(1)}, f32[128,128]{1,0:T(8,128)S(1)}, u32[]{:S(2)}, u32[]{:S(2)}) collective-permute-start(f32[128,128]{1,0:T(8,128)S(1)} %fusion.5), channel_id=1, source_target_pairs={{16,0},{24,8},{0,16},{8,24},{17,1},{25,9},{1,17},{9,25},{18,2},{26... | collective-permute-start | bytes 196616 | tf_op jit(solution)/shard_map/ppermute | solution.py:574
  14.3 5.6 %all-to-all-start = ((bf16[32,152,128]{2,1,0:T(8,128)(2,1)}), bf16[32,152,128]{2,1,0:T(8,128)(2,1)S(1)}, u32[]{:S(2)}, u32[]{:S(2)}) async-start(bf16[32,152,128]{2,1,0:T(8,128)(2,1)} %deal.1), calls=%async_computation | async-start | bytes 2490368 | tf_op jit(solution)/shard_map/all_to_all | solution.py:606
  20.0 0.1 pad.21.clone
  20.1 1.0 %collective-permute-done.2 = f32[128,128]{1,0:T(8,128)S(1)} collective-permute-done((f32[128,128]{1,0:T(8,128)S(1)}, f32[128,128]{1,0:T(8,128)S(1)}, u32[]{:S(2)}, u32[]{:S(2)}) %collective-permute-start.2) | collective-permute-done | bytes 65568 | tf_op jit(solution)/shard_map/ppermute | solution.py:574
  21.1 2.5 %collective-permute-start.5 = (f32[128,128]{1,0:T(8,128)S(1)}, f32[128,128]{1,0:T(8,128)S(1)}, u32[]{:S(2)}, u32[]{:S(2)}) collective-permute-start(f32[128,128]{1,0:T(8,128)S(1)} %fusion.1), channel_id=1, source_target_pairs={{2,0},{3,1},{4,2},{5,3},{6,4},{7,5},{0,6},{1,7},{10,8},{11,9},{12,... | collective-permute-start | bytes 196616 | tf_op jit(solution)/shard_map/ppermute | solution.py:574
  23.6 0.1 fusion.3
  23.7 0.1 select_maximum_fusion
  23.8 0.1 collective-permute-start.4
  23.8 0.5 collective-permute-start.3
  24.3 0.7 add_convert_fusion.ends_ref
  25.0 7.8 %collective-permute-done.5 = f32[128,128]{1,0:T(8,128)S(1)} collective-permute-done((f32[128,128]{1,0:T(8,128)S(1)}, f32[128,128]{1,0:T(8,128)S(1)}, u32[]{:S(2)}, u32[]{:S(2)}) %collective-permute-start.5) | collective-permute-done | bytes 65568 | tf_op jit(solution)/shard_map/ppermute | solution.py:574
  32.8 0.8 collective-permute-done.4
  33.5 2.8 %collective-permute-done.3 = f32[184,128]{1,0:T(8,128)S(1)} collective-permute-done((f32[184,128]{1,0:T(8,128)S(1)}, f32[184,128]{1,0:T(8,128)S(1)}, u32[]{:S(2)}, u32[]{:S(2)}) %collective-permute-start.3) | collective-permute-done | bytes 94240 | tf_op jit(solution)/shard_map/ppermute | solution.py:574
  36.4 0.1 collective-permute-start.6
  36.4 0.1 slice.75
  36.5 0.1 pad_maximum_fusion.2
  36.6 0.1 copy.15
  36.8 0.1 copy.17
  36.8 0.6 pad.14.coef_ref
  37.5 5.7 %weights.1 = (f32[52,19,8,128]{3,2,1,0:T(8,128)}, f32[52,19,8,128]{3,2,1,0:T(8,128)}) custom-call(f32[64,256]{1,0:T(8,128)} %pad.14.coef_ref), custom_call_target="tpu_custom_call" | custom-call | flops 101171200 | bytes 8093696 | tf_op jit(solution)/shard_map/weights/pallas_call | solution.py:261
  43.2 0.6 add.41.gram_ref
  43.8 5.9 %factor_inverse.1.inverse_ref = f32[128,128]{1,0:T(8,128)} custom-call(f32[128,128]{1,0:T(8,128)} %add.41.gram_ref), custom_call_target="tpu_custom_call" | custom-call | flops 10737418240 | bytes 131072 | tf_op jit(solution)/shard_map/factor_inverse/pallas_call | solution.py:203
  49.7 0.7 all-to-all-done
  50.5 1.3 %collective-permute-start.8 = (bf16[10,152,128]{2,1,0:T(8,128)(2,1)S(1)}, bf16[10,152,128]{2,1,0:T(8,128)(2,1)S(1)}, u32[]{:S(2)}, u32[]{:S(2)}) collective-permute-start(bf16[10,152,128]{2,1,0:T(8,128)(2,1)S(1)} %get-tuple-element.33), channel_id=1, source_target_pairs={{8,0},{16,8},{24,16},{9,1},{17,9},{25,17},{10,2},{18,10},{26,18},{... | collective-permute-start | bytes 1167368 | tf_op jit(solution)/shard_map/ppermute | solution.py:567
  51.8 4.8 %collective-permute-start.7 = (bf16[10,152,128]{2,1,0:T(8,128)(2,1)S(1)}, bf16[10,152,128]{2,1,0:T(8,128)(2,1)S(1)}, u32[]{:S(2)}, u32[]{:S(2)}) collective-permute-start(bf16[10,152,128]{2,1,0:T(8,128)(2,1)S(1)} %get-tuple-element.34), channel_id=1, source_target_pairs={{0,8},{8,16},{16,24},{1,9},{9,17},{17,25},{2,10},{10,18},{18,26},{... | collective-permute-start | bytes 1167368 | tf_op jit(solution)/shard_map/ppermute | solution.py:560
  56.6 11.7 %inner_sweeps.1 = (f32[32,19,8,128]{3,2,1,0:T(8,128)}, f32[32,19,8,128]{3,2,1,0:T(8,128)}, f32[152,128]{1,0:T(8,128)}) custom-call(bf16[4864,128]{1,0:T(8,128)(2,1)} %bitcast.14, f32[128,128]{1,0:T(8,128)} %factor_inverse.1.inverse_ref, f32[52,19,8,128]{3,2,1,0:T(8,128)} %get-tuple-element.28.across_hbm, f32[52,19,8,128]{3,2,1,0:T(8,128)} %get-tuple-element.29.down_hbm), custom_call_target="tpu_custom_call" | custom-call | flops 12000000000 | bytes 4980736 | tf_op jit(solution)/shard_map/inner_sweeps/pallas_call | solution.py:410
  68.3 0.7 copy-done.2
  69.0 0.2 copy-done.3
  69.2 11.5 %outer_sweeps.1 = f32[32,128]{1,0:T(8,128)} custom-call(s32[2]{0:T(128)} %add_convert_fusion.ends_ref, f32[128,128]{1,0:T(8,128)} %factor_inverse.1.inverse_ref, f32[152,128]{1,0:T(8,128)} %get-tuple-element.30.inner_ref, bf16[1520,128]{1,0:T(8,128)(2,1)} %bitcast.17, bf16[1520,128]{1,0:T(8,128)(2,1)} %bitcast.16, ...), custom_call_target="tpu_custom_call" | custom-call | tf_op jit(solution)/shard_map/outer_sweeps/pallas_call | solution.py:545
  (31 shorter events, 0.2 us)
Async XLA Ops:
  0.0 7.7 %copy-start.4 = (f32[32,128]{1,0:T(8,128)S(1)}, f32[32,128]{1,0:T(8,128)}, u32[]{:S(2)}) copy-start(f32[32,128]{1,0:T(8,128)} %param.7) | copy-start | bytes 49156
  0.0 7.7 %copy-start.5 = (s32[32,128]{1,0:T(8,128)S(1)}, s32[32,128]{1,0:T(8,128)}, u32[]{:S(2)}) copy-start(s32[32,128]{1,0:T(8,128)} %param.6) | copy-start | bytes 49156
  0.0 7.7 %copy-start = (bf16[4096,128]{1,0:T(8,128)(2,1)S(1)}, bf16[4096,128]{1,0:T(8,128)(2,1)}, u32[]{:S(2)}) copy-start(bf16[4096,128]{1,0:T(8,128)(2,1)} %basis_ref.1) | copy-start | bytes 3145732
  8.2 12.8 %collective-permute-start.1 = (f32[152,128]{1,0:T(8,128)S(1)}, f32[152,128]{1,0:T(8,128)S(1)}, u32[]{:S(2)}, u32[]{:S(2)}) collective-permute-start(f32[152,128]{1,0:T(8,128)S(1)} %pad_maximum_fusion.1), channel_id=1, source_target_pairs={{8,0},{16,8},{24,16},{0,24},{9,1},{17,9},{25,17},{1,25},{10,2},{18... | collective-permute-start | bytes 233480 | tf_op jit(solution)/shard_map/ppermute | solution.py:574
  13.3 7.7 %collective-permute-start = (f32[152,128]{1,0:T(8,128)S(1)}, f32[152,128]{1,0:T(8,128)S(1)}, u32[]{:S(2)}, u32[]{:S(2)}) collective-permute-start(f32[152,128]{1,0:T(8,128)S(1)} %pad_maximum_fusion.1), channel_id=1, source_target_pairs={{24,0},{0,8},{8,16},{16,24},{25,1},{1,9},{9,17},{17,25},{26,2},{2,... | collective-permute-start | bytes 233480 | tf_op jit(solution)/shard_map/ppermute | solution.py:574
  13.3 7.7 %collective-permute-start.2 = (f32[128,128]{1,0:T(8,128)S(1)}, f32[128,128]{1,0:T(8,128)S(1)}, u32[]{:S(2)}, u32[]{:S(2)}) collective-permute-start(f32[128,128]{1,0:T(8,128)S(1)} %fusion.5), channel_id=1, source_target_pairs={{16,0},{24,8},{0,16},{8,24},{17,1},{25,9},{1,17},{9,25},{18,2},{26... | collective-permute-start | bytes 196616 | tf_op jit(solution)/shard_map/ppermute | solution.py:574
  14.3 36.1 %all-to-all-start = ((bf16[32,152,128]{2,1,0:T(8,128)(2,1)}), bf16[32,152,128]{2,1,0:T(8,128)(2,1)S(1)}, u32[]{:S(2)}, u32[]{:S(2)}) async-start(bf16[32,152,128]{2,1,0:T(8,128)(2,1)} %deal.1), calls=%async_computation | async-start | bytes 2490368 | tf_op jit(solution)/shard_map/all_to_all | solution.py:606
  21.1 11.7 %collective-permute-start.5 = (f32[128,128]{1,0:T(8,128)S(1)}, f32[128,128]{1,0:T(8,128)S(1)}, u32[]{:S(2)}, u32[]{:S(2)}) collective-permute-start(f32[128,128]{1,0:T(8,128)S(1)} %fusion.1), channel_id=1, source_target_pairs={{2,0},{3,1},{4,2},{5,3},{6,4},{7,5},{0,6},{1,7},{10,8},{11,9},{12,... | collective-permute-start | bytes 196616 | tf_op jit(solution)/shard_map/ppermute | solution.py:574
  23.8 9.7 %collective-permute-start.4 = (f32[184,128]{1,0:T(8,128)S(1)}, f32[184,128]{1,0:T(8,128)S(1)}, u32[]{:S(2)}, u32[]{:S(2)}) collective-permute-start(f32[184,128]{1,0:T(8,128)S(1)} %pad_maximum_fusion), channel_id=1, source_target_pairs={{1,0},{2,1},{3,2},{4,3},{5,4},{6,5},{7,6},{0,7},{9,8},{10,9},{11,1... | collective-permute-start | bytes 282632 | tf_op jit(solution)/shard_map/ppermute | solution.py:574
  23.8 12.5 %collective-permute-start.3 = (f32[184,128]{1,0:T(8,128)S(1)}, f32[184,128]{1,0:T(8,128)S(1)}, u32[]{:S(2)}, u32[]{:S(2)}) collective-permute-start(f32[184,128]{1,0:T(8,128)S(1)} %pad_maximum_fusion), channel_id=1, source_target_pairs={{7,0},{0,1},{1,2},{2,3},{3,4},{4,5},{5,6},{6,7},{15,8},{8,9},{9,10... | collective-permute-start | bytes 282632 | tf_op jit(solution)/shard_map/ppermute | solution.py:574
  36.4 6.8 %collective-permute-start.6 = (f32[128,128]{1,0:T(8,128)S(1)}, f32[128,128]{1,0:T(8,128)S(1)}, u32[]{:S(2)}, u32[]{:S(2)}) collective-permute-start(f32[128,128]{1,0:T(8,128)S(1)} %fusion), channel_id=1, source_target_pairs={{4,0},{5,1},{6,2},{7,3},{0,4},{1,5},{2,6},{3,7},{12,8},{13,9},{14,... | collective-permute-start | bytes 196616 | tf_op jit(solution)/shard_map/ppermute | solution.py:574
  50.5 6.1 %copy-start.1 = (bf16[32,152,128]{2,1,0:T(8,128)(2,1)}, bf16[32,152,128]{2,1,0:T(8,128)(2,1)S(1)}, u32[]{:S(2)}) copy-start(bf16[32,152,128]{2,1,0:T(8,128)(2,1)S(1)} %all-to-all-done) | copy-start | bytes 3735556
  50.5 17.7 %collective-permute-start.8 = (bf16[10,152,128]{2,1,0:T(8,128)(2,1)S(1)}, bf16[10,152,128]{2,1,0:T(8,128)(2,1)S(1)}, u32[]{:S(2)}, u32[]{:S(2)}) collective-permute-start(bf16[10,152,128]{2,1,0:T(8,128)(2,1)S(1)} %get-tuple-element.33), channel_id=1, source_target_pairs={{8,0},{16,8},{24,16},{9,1},{17,9},{25,17},{10,2},{18,10},{26,18},{... | collective-permute-start | bytes 1167368 | tf_op jit(solution)/shard_map/ppermute | solution.py:567
  51.8 16.5 %collective-permute-start.7 = (bf16[10,152,128]{2,1,0:T(8,128)(2,1)S(1)}, bf16[10,152,128]{2,1,0:T(8,128)(2,1)S(1)}, u32[]{:S(2)}, u32[]{:S(2)}) collective-permute-start(bf16[10,152,128]{2,1,0:T(8,128)(2,1)S(1)} %get-tuple-element.34), channel_id=1, source_target_pairs={{0,8},{8,16},{16,24},{1,9},{9,17},{17,25},{2,10},{10,18},{18,26},{... | collective-permute-start | bytes 1167368 | tf_op jit(solution)/shard_map/ppermute | solution.py:560
  68.3 0.7 copy-start.2
  68.3 0.9 %copy-start.3 = (bf16[10,152,128]{2,1,0:T(8,128)(2,1)}, bf16[10,152,128]{2,1,0:T(8,128)(2,1)S(1)}, u32[]{:S(2)}) copy-start(bf16[10,152,128]{2,1,0:T(8,128)(2,1)S(1)} %collective-permute-done.7) | copy-start | bytes 1167364

commit v12 on v11

--- a/solution.py
+++ b/solution.py
@@ -15,6 +15,7 @@
 TILES = 4
 BLOCK = 8
 VMEM_BYTES = 56 * 1024 * 1024
+OUTER_BYTES = 52 * 1024 * 1024
 
 bf16, f32, i32 = jnp.bfloat16, jnp.float32, jnp.int32
 
@@ -146,7 +147,7 @@
     )(basis, order.reshape(tiles, wide))
 
 
-def inverse_kernel(gram_ref, out_ref):
+def inverse_kernel(gram_ref, turn_ref, out_ref):
     size = gram_ref.shape[0]
     count = size // SUB
     shape = (SUB, size)
@@ -196,13 +197,15 @@
             pivot = jnp.where(sub == c, core[c, c], pivot)
         kept = jnp.where(lane <= sub + first, merged, 0.0)
         out_ref[first : first + SUB, :] = kept * (1.0 / jnp.sqrt(pivot))
+    turn_ref[...] = rotation(out_ref[...])
 
 
 def factor_inverse(gram):
     size = gram.shape[0]
     return pl.pallas_call(
         inverse_kernel,
-        out_shape=jax.ShapeDtypeStruct(gram.shape, f32),
+        out_shape=jax.ShapeDtypeStruct((2 * size, 2 * size), bf16),
+        scratch_shapes=[pltpu.VMEM(gram.shape, f32)],
         compiler_params=pltpu.CompilerParams(vmem_limit_bytes=VMEM_BYTES),
         cost_estimate=pl.CostEstimate(
             flops=40 * size**4, bytes_accessed=8 * size * size, transcendentals=0
@@ -340,10 +343,10 @@
 
 
 def inner_kernel(
-    own_ref, inverse_ref, across_hbm, down_hbm, first_hbm, second_hbm, total_ref,
+    own_ref, turn_ref, across_hbm, down_hbm, first_hbm, second_hbm,
     first_ref, second_ref, across_ref, down_ref, sum_ref, sems,
 ):
-    tall, groups, _, lanes = first_ref.shape
+    tall, groups, _, lanes = second_ref.shape
     inside = pl.ds(HALO, tall)
     fetches = [
         pltpu.make_async_copy(across_hbm.at[inside], across_ref, sems.at[0]),
@@ -351,7 +354,7 @@
     ]
     for fetch in fetches:
         fetch.start()
-    turn = rotation(inverse_ref[...])
+    turn = turn_ref[...]
     take = 4
     cells = take * groups * SUB
 
@@ -396,7 +399,11 @@
 
     zeros = tuple(jnp.zeros((SUB, lanes), f32) for _ in range(groups))
     totals = lax.fori_loop(0, tall // 4, gather, zeros)
-    total_ref[...] = jnp.concatenate(totals, axis=0)
+    for g in range(groups):
+        first_ref[tall, g] = totals[g]
+    part = pl.ds(tall, 1)
+    leaving.append(pltpu.make_async_copy(first_ref.at[part], first_hbm.at[part], sems.at[6]))
+    leaving[-1].start()
     for copy in leaving:
         copy.wait()
 
@@ -407,16 +414,15 @@
     vmem = pl.BlockSpec(memory_space=pltpu.VMEM)
     far = pl.BlockSpec(memory_space=pl.ANY)
     shape = (tall, places // SUB, SUB, lanes)
+    longer = (tall + 1,) + shape[1:]
     return pl.pallas_call(
         inner_kernel,
-        out_shape=(
-            jax.ShapeDtypeStruct(shape, f32),
-            jax.ShapeDtypeStruct(shape, f32),
-            jax.ShapeDtypeStruct((places, lanes), f32),
-        ),
+        out_shape=(jax.ShapeDtypeStruct(longer, f32), jax.ShapeDtypeStruct(shape, f32)),
         in_specs=[vmem, vmem, far, far],
-        out_specs=(far, far, vmem),
-        scratch_shapes=[pltpu.VMEM(shape, f32)] * 5 + [pltpu.SemaphoreType.DMA((6,))],
+        out_specs=(far, far),
+        scratch_shapes=[pltpu.VMEM(longer, f32)]
+        + [pltpu.VMEM(shape, f32)] * 4
+        + [pltpu.SemaphoreType.DMA((7,))],
         compiler_params=pltpu.CompilerParams(vmem_limit_bytes=VMEM_BYTES),
         cost_estimate=pl.CostEstimate(
             flops=12 * 10**9, bytes_accessed=8 * own.size, transcendentals=0
@@ -426,9 +432,9 @@
 
 
 def outer_kernel(
-    scale, ends_ref, inverse_ref, inner_ref, north_hbm, south_hbm, first_hbm, second_hbm,
+    scale, ends_ref, turn_ref, north_hbm, south_hbm, first_hbm, second_hbm,
     across_hbm, down_hbm, out_ref, first_ref, second_ref, across_ref, down_ref, sum_ref,
-    north_ref, south_ref, sems,
+    north_ref, south_ref, inner_ref, sems,
 ):
     rows, groups, _, lanes = first_ref.shape
     tall = rows - 2 * HALO
@@ -465,10 +471,11 @@
         fetch(late, source, target, rows - wide_part, wide_part - reach, 0)
     fetch(late, first_hbm, first_ref, 2, near - 2, HALO)
     fetch(late, first_hbm, first_ref, tall - near, near - 2, HALO)
+    fetch(late, first_hbm, inner_ref, tall, 1, -tall)
     for copy in soon + late:
         copy.start()
     sum_ref[...] = jnp.zeros_like(sum_ref)
-    turn = rotation(inverse_ref[...])
+    turn = turn_ref[...]
     for halo in halos:
         halo.wait()
     take = 2
@@ -525,7 +532,7 @@
             pairs += [(HALO + row, row), (tall + row, tall - HALO + row)]
         return tuple(summed_lanes(sum_ref, pairs, list(totals)))
 
-    totals = tuple(inner_ref[g * SUB : (g + 1) * SUB, :] for g in range(groups))
+    totals = tuple(inner_ref[0, g] for g in range(groups))
     totals = lax.fori_loop(0, HALO // 2, gather, totals)
     totals = jnp.concatenate(totals, axis=0).T[:tall]
     slot = iota((places, out_ref.shape[1]), 0)
@@ -536,8 +543,8 @@
 
 
 def outer_sweeps(scale, ends, north, south, inverse, inner, across_down, wide):
-    first, second, total = inner
-    tall, groups, _, lanes = first.shape
+    first, second = inner
+    tall, groups, _, lanes = second.shape
     shape = (tall + 2 * HALO, groups, SUB, lanes)
     north, south = (x.reshape(-1, lanes) for x in (north, south))
     vmem = pl.BlockSpec(memory_space=pltpu.VMEM)
@@ -545,14 +552,14 @@
     return pl.pallas_call(
         functools.partial(outer_kernel, scale),
         out_shape=jax.ShapeDtypeStruct((tall, wide), f32),
-        in_specs=[pl.BlockSpec(memory_space=pltpu.SMEM)] + [vmem] * 2 + [far] * 6,
+        in_specs=[pl.BlockSpec(memory_space=pltpu.SMEM), vmem] + [far] * 6,
         out_specs=vmem,
         scratch_shapes=[pltpu.VMEM(shape, f32)] * 5
         + [pltpu.VMEM(north.shape, bf16)] * 2
-        + [pltpu.SemaphoreType.DMA((16,))],
-        compiler_params=pltpu.CompilerParams(vmem_limit_bytes=VMEM_BYTES),
+        + [pltpu.VMEM((1,) + shape[1:], f32), pltpu.SemaphoreType.DMA((17,))],
+        compiler_params=pltpu.CompilerParams(vmem_limit_bytes=OUTER_BYTES),
         name="outer_sweeps",
-    )(ends, inverse, total, north, south, first, second, *across_down)
+    )(ends, inverse, north, south, first, second, *across_down)
 
 
 def from_before(x, axis, closed):

time: 81.2 us -> 80.1 us (0.986)
  local copies, waits for them, and re-layouts: 2.05 us -> 1.18 us
    unnamed x12 -> x10, local copies, waits for them, and re-layouts: 0.9 us -> 0.02 us
  transfers between devices with their start and end apart: 10 -> 10, of which waited for: 5 -> 5; matrix products, arithmetic and copies ran while one was open for 3% -> 3% of each run, Pallas kernels for 29% -> 30%
where the time goes in v12:
time: 80.1 us; the launch traced here: 79.7 us
  Pallas kernels  42.4 us (53%)
  starting transfers between devices  20.9 us (26%)
  waiting for transfers between devices  13.4 us (17%)
  local copies, waits for them, and re-layouts  1.18 us (1%)
  other arithmetic  0.97 us (1%)
    ppermute x7, waiting for transfers between devices, ahead(): lax.ppermute(values, axis, [((i + step) % count, i) for i in range(count)])  12.9 us
    pallas_call x1, Pallas kernels, inner_sweeps(): pl.pallas_call(inner_kernel, out_shape=(jax.ShapeDtypeStruct(longer, f32)...  11.7 us
    pallas_call x1, Pallas kernels, outer_sweeps(): pl.pallas_call(functools.partial(outer_kernel, scale), out_shape=jax.Shap...  11.2 us
    ppermute x7, starting transfers between devices, ahead(): lax.ppermute(values, axis, [((i + step) % count, i) for i in range(count)])  9.24 us
    pallas_call x1, Pallas kernels, deal(): pl.pallas_call(functools.partial(deal_kernel, tiles_lon), out_shape=jax.S...  7.64 us
    pallas_call x1, Pallas kernels, factor_inverse(): pl.pallas_call(inverse_kernel, out_shape=jax.ShapeDtypeStruct((2 * size,...  6.18 us
    pallas_call x1, Pallas kernels, weights(): pl.pallas_call(weight_kernel, out_shape=(jax.ShapeDtypeStruct(shape, f32)...  5.67 us
    all_to_all x1, starting transfers between devices, per_device(): raw = lax.all_to_all(moving, axes, split_axis=0, concat_axis=0, tiled=True)  5.62 us
  transfers between devices with their start and end apart: 10, of which 5 were waited for; matrix products, arithmetic and copies ran while one was open for 3% of the time, Pallas kernels for 30%

profile of v12, /device:TPU:0, one launch (start us, length us, event | category | flops | bytes accessed | tf_op | source)
XLA Modules:
  0.0 79.7 jit_solution(4188573080793444326)
XLA Ops:
  0.0 7.6 %deal.1 = bf16[32,152,128]{2,1,0:T(8,128)(2,1)} custom-call(bf16[4096,128]{1,0:T(8,128)(2,1)} %basis_ref.1, s32[32,128]{1,0:T(8,128)} %bitcast.19), custom_call_target="tpu_custom_call" | custom-call | flops 5100273664 | bytes 2097152 | tf_op jit(solution)/shard_map/deal/pallas_call | solution.py:130
  7.7 0.5 fusion.5
  8.2 5.1 %collective-permute-start.1 = (f32[152,128]{1,0:T(8,128)S(1)}, f32[152,128]{1,0:T(8,128)S(1)}, u32[]{:S(2)}, u32[]{:S(2)}) collective-permute-start(f32[152,128]{1,0:T(8,128)S(1)} %pad_maximum_fusion.1), channel_id=1, source_target_pairs={{8,0},{16,8},{24,16},{0,24},{9,1},{17,9},{25,17},{1,25},{10,2},{18... | collective-permute-start | bytes 233480 | tf_op jit(solution)/shard_map/ppermute | solution.py:581
  13.3 1.0 %collective-permute-start.2 = (f32[128,128]{1,0:T(8,128)S(1)}, f32[128,128]{1,0:T(8,128)S(1)}, u32[]{:S(2)}, u32[]{:S(2)}) collective-permute-start(f32[128,128]{1,0:T(8,128)S(1)} %fusion.5), channel_id=1, source_target_pairs={{16,0},{24,8},{0,16},{8,24},{17,1},{25,9},{1,17},{9,25},{18,2},{26... | collective-permute-start | bytes 196616 | tf_op jit(solution)/shard_map/ppermute | solution.py:581
  14.3 5.6 %all-to-all-start = ((bf16[32,152,128]{2,1,0:T(8,128)(2,1)}), bf16[32,152,128]{2,1,0:T(8,128)(2,1)S(1)}, u32[]{:S(2)}, u32[]{:S(2)}) async-start(bf16[32,152,128]{2,1,0:T(8,128)(2,1)} %deal.1), calls=%async_computation | async-start | bytes 2490368 | tf_op jit(solution)/shard_map/all_to_all | solution.py:613
  20.0 0.1 pad.21.clone
  20.1 1.0 %collective-permute-done.2 = f32[128,128]{1,0:T(8,128)S(1)} collective-permute-done((f32[128,128]{1,0:T(8,128)S(1)}, f32[128,128]{1,0:T(8,128)S(1)}, u32[]{:S(2)}, u32[]{:S(2)}) %collective-permute-start.2) | collective-permute-done | bytes 65568 | tf_op jit(solution)/shard_map/ppermute | solution.py:581
  21.1 0.0 collective-permute-done.1
  21.1 2.5 %collective-permute-start.5 = (f32[128,128]{1,0:T(8,128)S(1)}, f32[128,128]{1,0:T(8,128)S(1)}, u32[]{:S(2)}, u32[]{:S(2)}) collective-permute-start(f32[128,128]{1,0:T(8,128)S(1)} %fusion.1), channel_id=1, source_target_pairs={{2,0},{3,1},{4,2},{5,3},{6,4},{7,5},{0,6},{1,7},{10,8},{11,9},{12,... | collective-permute-start | bytes 196616 | tf_op jit(solution)/shard_map/ppermute | solution.py:581
  23.6 0.1 fusion.3
  23.7 0.1 select_maximum_fusion
  23.8 0.1 collective-permute-start.4
  23.8 0.5 collective-permute-start.3
  24.3 0.1 add_convert_fusion.ends_ref
  24.4 8.3 %collective-permute-done.5 = f32[128,128]{1,0:T(8,128)S(1)} collective-permute-done((f32[128,128]{1,0:T(8,128)S(1)}, f32[128,128]{1,0:T(8,128)S(1)}, u32[]{:S(2)}, u32[]{:S(2)}) %collective-permute-start.5) | collective-permute-done | bytes 65568 | tf_op jit(solution)/shard_map/ppermute | solution.py:581
  32.8 0.8 collective-permute-done.4
  33.5 2.8 %collective-permute-done.3 = f32[184,128]{1,0:T(8,128)S(1)} collective-permute-done((f32[184,128]{1,0:T(8,128)S(1)}, f32[184,128]{1,0:T(8,128)S(1)}, u32[]{:S(2)}, u32[]{:S(2)}) %collective-permute-start.3) | collective-permute-done | bytes 94240 | tf_op jit(solution)/shard_map/ppermute | solution.py:581
  36.4 0.1 collective-permute-start.6
  36.5 0.1 slice.75
  36.5 0.1 pad_maximum_fusion.2
  36.6 0.1 copy.15
  36.8 0.1 copy.17
  36.8 0.6 pad.14.coef_ref
  37.5 5.7 %weights.1 = (f32[52,19,8,128]{3,2,1,0:T(8,128)}, f32[52,19,8,128]{3,2,1,0:T(8,128)}) custom-call(f32[64,256]{1,0:T(8,128)} %pad.14.coef_ref), custom_call_target="tpu_custom_call" | custom-call | flops 101171200 | bytes 8093696 | tf_op jit(solution)/shard_map/weights/pallas_call | solution.py:264
  43.2 0.6 add.41.gram_ref
  43.8 6.2 %factor_inverse.1.turn_ref = bf16[256,256]{1,0:T(8,128)(2,1)} custom-call(f32[128,128]{1,0:T(8,128)} %add.41.gram_ref), custom_call_target="tpu_custom_call" | custom-call | flops 10737418240 | bytes 131072 | tf_op jit(solution)/shard_map/factor_inverse/pallas_call | solution.py:205
  50.0 0.5 all-to-all-done
  50.5 0.1 fusion.2
  50.5 1.3 %collective-permute-start.8 = (bf16[10,152,128]{2,1,0:T(8,128)(2,1)S(1)}, bf16[10,152,128]{2,1,0:T(8,128)(2,1)S(1)}, u32[]{:S(2)}, u32[]{:S(2)}) collective-permute-start(bf16[10,152,128]{2,1,0:T(8,128)(2,1)S(1)} %get-tuple-element.31), channel_id=1, source_target_pairs={{8,0},{16,8},{24,16},{9,1},{17,9},{25,17},{10,2},{18,10},{26,18},{... | collective-permute-start | bytes 1167368 | tf_op jit(solution)/shard_map/ppermute | solution.py:574
  51.8 4.8 %collective-permute-start.7 = (bf16[10,152,128]{2,1,0:T(8,128)(2,1)S(1)}, bf16[10,152,128]{2,1,0:T(8,128)(2,1)S(1)}, u32[]{:S(2)}, u32[]{:S(2)}) collective-permute-start(bf16[10,152,128]{2,1,0:T(8,128)(2,1)S(1)} %get-tuple-element.32), channel_id=1, source_target_pairs={{0,8},{8,16},{16,24},{1,9},{9,17},{17,25},{2,10},{10,18},{18,26},{... | collective-permute-start | bytes 1167368 | tf_op jit(solution)/shard_map/ppermute | solution.py:567
  56.6 11.7 %inner_sweeps.1 = (f32[33,19,8,128]{3,2,1,0:T(8,128)}, f32[32,19,8,128]{3,2,1,0:T(8,128)}) custom-call(bf16[4864,128]{1,0:T(8,128)(2,1)} %bitcast.16, bf16[256,256]{1,0:T(8,128)(2,1)} %factor_inverse.1.turn_ref, f32[52,19,8,128]{3,2,1,0:T(8,128)} %get-tuple-element.27.across_hbm, f32[52,19,8,128]{3,2,1,0:T(8,128)} %get-tuple-element.28.down_hbm), custom_call_target="tpu_custom_call" | custom-call | flops 12000000000 | bytes 4980736 | tf_op jit(solution)/shard_map/inner_sweeps/pallas_call | solution.py:418
  68.4 11.2 %outer_sweeps.1 = f32[32,128]{1,0:T(8,128)} custom-call(s32[2]{0:T(128)S(1)} %add_convert_fusion.ends_ref, bf16[256,256]{1,0:T(8,128)(2,1)S(1)} %copy-done, bf16[1520,128]{1,0:T(8,128)(2,1)S(1)} %bitcast.15, bf16[1520,128]{1,0:T(8,128)(2,1)S(1)} %bitcast.14, f32[33,19,8,128]{3,2,1,0:T(8,128)} %get-tuple-element.29.first_hbm, ...), custom_call_target="tpu_custom_call" | custom-call | tf_op jit(solution)/shard_map/outer_sweeps/pallas_call | solution.py:552
  (29 shorter events, 0.2 us)
Async XLA Ops:
  0.0 7.7 %copy-start.3 = (f32[32,128]{1,0:T(8,128)S(1)}, f32[32,128]{1,0:T(8,128)}, u32[]{:S(2)}) copy-start(f32[32,128]{1,0:T(8,128)} %param.7) | copy-start | bytes 49156
  0.0 7.7 %copy-start.4 = (s32[32,128]{1,0:T(8,128)S(1)}, s32[32,128]{1,0:T(8,128)}, u32[]{:S(2)}) copy-start(s32[32,128]{1,0:T(8,128)} %param.6) | copy-start | bytes 49156
  0.0 7.7 %copy-start.1 = (bf16[4096,128]{1,0:T(8,128)(2,1)S(1)}, bf16[4096,128]{1,0:T(8,128)(2,1)}, u32[]{:S(2)}) copy-start(bf16[4096,128]{1,0:T(8,128)(2,1)} %basis_ref.1) | copy-start | bytes 3145732
  8.2 12.8 %collective-permute-start.1 = (f32[152,128]{1,0:T(8,128)S(1)}, f32[152,128]{1,0:T(8,128)S(1)}, u32[]{:S(2)}, u32[]{:S(2)}) collective-permute-start(f32[152,128]{1,0:T(8,128)S(1)} %pad_maximum_fusion.1), channel_id=1, source_target_pairs={{8,0},{16,8},{24,16},{0,24},{9,1},{17,9},{25,17},{1,25},{10,2},{18... | collective-permute-start | bytes 233480 | tf_op jit(solution)/shard_map/ppermute | solution.py:581
  13.3 7.7 %collective-permute-start = (f32[152,128]{1,0:T(8,128)S(1)}, f32[152,128]{1,0:T(8,128)S(1)}, u32[]{:S(2)}, u32[]{:S(2)}) collective-permute-start(f32[152,128]{1,0:T(8,128)S(1)} %pad_maximum_fusion.1), channel_id=1, source_target_pairs={{24,0},{0,8},{8,16},{16,24},{25,1},{1,9},{9,17},{17,25},{26,2},{2,... | collective-permute-start | bytes 233480 | tf_op jit(solution)/shard_map/ppermute | solution.py:581
  13.3 7.7 %collective-permute-start.2 = (f32[128,128]{1,0:T(8,128)S(1)}, f32[128,128]{1,0:T(8,128)S(1)}, u32[]{:S(2)}, u32[]{:S(2)}) collective-permute-start(f32[128,128]{1,0:T(8,128)S(1)} %fusion.5), channel_id=1, source_target_pairs={{16,0},{24,8},{0,16},{8,24},{17,1},{25,9},{1,17},{9,25},{18,2},{26... | collective-permute-start | bytes 196616 | tf_op jit(solution)/shard_map/ppermute | solution.py:581
  14.3 36.1 %all-to-all-start = ((bf16[32,152,128]{2,1,0:T(8,128)(2,1)}), bf16[32,152,128]{2,1,0:T(8,128)(2,1)S(1)}, u32[]{:S(2)}, u32[]{:S(2)}) async-start(bf16[32,152,128]{2,1,0:T(8,128)(2,1)} %deal.1), calls=%async_computation | async-start | bytes 2490368 | tf_op jit(solution)/shard_map/all_to_all | solution.py:613
  21.1 11.7 %collective-permute-start.5 = (f32[128,128]{1,0:T(8,128)S(1)}, f32[128,128]{1,0:T(8,128)S(1)}, u32[]{:S(2)}, u32[]{:S(2)}) collective-permute-start(f32[128,128]{1,0:T(8,128)S(1)} %fusion.1), channel_id=1, source_target_pairs={{2,0},{3,1},{4,2},{5,3},{6,4},{7,5},{0,6},{1,7},{10,8},{11,9},{12,... | collective-permute-start | bytes 196616 | tf_op jit(solution)/shard_map/ppermute | solution.py:581
  23.8 9.7 %collective-permute-start.4 = (f32[184,128]{1,0:T(8,128)S(1)}, f32[184,128]{1,0:T(8,128)S(1)}, u32[]{:S(2)}, u32[]{:S(2)}) collective-permute-start(f32[184,128]{1,0:T(8,128)S(1)} %pad_maximum_fusion), channel_id=1, source_target_pairs={{1,0},{2,1},{3,2},{4,3},{5,4},{6,5},{7,6},{0,7},{9,8},{10,9},{11,1... | collective-permute-start | bytes 282632 | tf_op jit(solution)/shard_map/ppermute | solution.py:581
  23.8 12.5 %collective-permute-start.3 = (f32[184,128]{1,0:T(8,128)S(1)}, f32[184,128]{1,0:T(8,128)S(1)}, u32[]{:S(2)}, u32[]{:S(2)}) collective-permute-start(f32[184,128]{1,0:T(8,128)S(1)} %pad_maximum_fusion), channel_id=1, source_target_pairs={{7,0},{0,1},{1,2},{2,3},{3,4},{4,5},{5,6},{6,7},{15,8},{8,9},{9,10... | collective-permute-start | bytes 282632 | tf_op jit(solution)/shard_map/ppermute | solution.py:581
  36.4 6.8 %collective-permute-start.6 = (f32[128,128]{1,0:T(8,128)S(1)}, f32[128,128]{1,0:T(8,128)S(1)}, u32[]{:S(2)}, u32[]{:S(2)}) collective-permute-start(f32[128,128]{1,0:T(8,128)S(1)} %fusion), channel_id=1, source_target_pairs={{4,0},{5,1},{6,2},{7,3},{0,4},{1,5},{2,6},{3,7},{12,8},{13,9},{14,... | collective-permute-start | bytes 196616 | tf_op jit(solution)/shard_map/ppermute | solution.py:581
  50.5 6.1 %copy-start.2 = (bf16[32,152,128]{2,1,0:T(8,128)(2,1)}, bf16[32,152,128]{2,1,0:T(8,128)(2,1)S(1)}, u32[]{:S(2)}) copy-start(bf16[32,152,128]{2,1,0:T(8,128)(2,1)S(1)} %all-to-all-done) | copy-start | bytes 3735556
  50.5 17.8 %collective-permute-start.8 = (bf16[10,152,128]{2,1,0:T(8,128)(2,1)S(1)}, bf16[10,152,128]{2,1,0:T(8,128)(2,1)S(1)}, u32[]{:S(2)}, u32[]{:S(2)}) collective-permute-start(bf16[10,152,128]{2,1,0:T(8,128)(2,1)S(1)} %get-tuple-element.31), channel_id=1, source_target_pairs={{8,0},{16,8},{24,16},{9,1},{17,9},{25,17},{10,2},{18,10},{26,18},{... | collective-permute-start | bytes 1167368 | tf_op jit(solution)/shard_map/ppermute | solution.py:574
  51.8 16.5 %collective-permute-start.7 = (bf16[10,152,128]{2,1,0:T(8,128)(2,1)S(1)}, bf16[10,152,128]{2,1,0:T(8,128)(2,1)S(1)}, u32[]{:S(2)}, u32[]{:S(2)}) collective-permute-start(bf16[10,152,128]{2,1,0:T(8,128)(2,1)S(1)} %get-tuple-element.32), channel_id=1, source_target_pairs={{0,8},{8,16},{16,24},{1,9},{9,17},{17,25},{2,10},{10,18},{18,26},{... | collective-permute-start | bytes 1167368 | tf_op jit(solution)/shard_map/ppermute | solution.py:567
  56.6 11.7 %copy-start = (bf16[256,256]{1,0:T(8,128)(2,1)S(1)}, bf16[256,256]{1,0:T(8,128)(2,1)}, u32[]{:S(2)}) copy-start(bf16[256,256]{1,0:T(8,128)(2,1)} %factor_inverse.1.turn_ref) | copy-start | bytes 393220

commit v13 on v12

--- a/solution.py
+++ b/solution.py
@@ -12,7 +12,7 @@
 LANES = 128
 SUB = 8
 ONE_HOT = 1024
-TILES = 4
+TILES = 2
 BLOCK = 8
 VMEM_BYTES = 56 * 1024 * 1024
 OUTER_BYTES = 52 * 1024 * 1024

time: 80.1 us -> 80.2 us (level)
  transfers between devices with their start and end apart: 10 -> 10, of which waited for: 5 -> 5; matrix products, arithmetic and copies ran while one was open for 3% -> 3% of each run, Pallas kernels for 30% -> 29%
where the time goes in v13:
time: 80.2 us; the launch traced here: 79.8 us
  Pallas kernels  42.4 us (53%)
  starting transfers between devices  20.9 us (26%)
  waiting for transfers between devices  13.4 us (17%)
  local copies, waits for them, and re-layouts  1.18 us (1%)
  other arithmetic  0.97 us (1%)
    ppermute x7, waiting for transfers between devices, ahead(): lax.ppermute(values, axis, [((i + step) % count, i) for i in range(count)])  12.9 us
    pallas_call x1, Pallas kernels, inner_sweeps(): pl.pallas_call(inner_kernel, out_shape=(jax.ShapeDtypeStruct(longer, f32)...  11.7 us
    pallas_call x1, Pallas kernels, outer_sweeps(): pl.pallas_call(functools.partial(outer_kernel, scale), out_shape=jax.Shap...  11.2 us
    ppermute x7, starting transfers between devices, ahead(): lax.ppermute(values, axis, [((i + step) % count, i) for i in range(count)])  9.25 us
    pallas_call x1, Pallas kernels, deal(): pl.pallas_call(functools.partial(deal_kernel, tiles_lon), out_shape=jax.S...  7.69 us
    pallas_call x1, Pallas kernels, factor_inverse(): pl.pallas_call(inverse_kernel, out_shape=jax.ShapeDtypeStruct((2 * size,...  6.18 us
    pallas_call x1, Pallas kernels, weights(): pl.pallas_call(weight_kernel, out_shape=(jax.ShapeDtypeStruct(shape, f32)...  5.66 us
    all_to_all x1, starting transfers between devices, per_device(): raw = lax.all_to_all(moving, axes, split_axis=0, concat_axis=0, tiled=True)  5.62 us
  transfers between devices with their start and end apart: 10, of which 5 were waited for; matrix products, arithmetic and copies ran while one was open for 3% of the time, Pallas kernels for 29%

profile of v13, /device:TPU:0, one launch (start us, length us, event | category | flops | bytes accessed | tf_op | source)
XLA Modules:
  0.0 79.8 jit_solution(17197971831934613160)
XLA Ops:
  0.0 7.7 %deal.1 = bf16[32,152,128]{2,1,0:T(8,128)(2,1)} custom-call(bf16[4096,128]{1,0:T(8,128)(2,1)} %basis_ref.1, s32[32,128]{1,0:T(8,128)} %bitcast.19), custom_call_target="tpu_custom_call" | custom-call | flops 5100273664 | bytes 2097152 | tf_op jit(solution)/shard_map/deal/pallas_call | solution.py:130
  7.8 0.5 fusion.5
  8.3 5.1 %collective-permute-start.1 = (f32[152,128]{1,0:T(8,128)S(1)}, f32[152,128]{1,0:T(8,128)S(1)}, u32[]{:S(2)}, u32[]{:S(2)}) collective-permute-start(f32[152,128]{1,0:T(8,128)S(1)} %pad_maximum_fusion.1), channel_id=1, source_target_pairs={{8,0},{16,8},{24,16},{0,24},{9,1},{17,9},{25,17},{1,25},{10,2},{18... | collective-permute-start | bytes 233480 | tf_op jit(solution)/shard_map/ppermute | solution.py:581
  13.4 1.0 %collective-permute-start.2 = (f32[128,128]{1,0:T(8,128)S(1)}, f32[128,128]{1,0:T(8,128)S(1)}, u32[]{:S(2)}, u32[]{:S(2)}) collective-permute-start(f32[128,128]{1,0:T(8,128)S(1)} %fusion.5), channel_id=1, source_target_pairs={{16,0},{24,8},{0,16},{8,24},{17,1},{25,9},{1,17},{9,25},{18,2},{26... | collective-permute-start | bytes 196616 | tf_op jit(solution)/shard_map/ppermute | solution.py:581
  14.4 5.6 %all-to-all-start = ((bf16[32,152,128]{2,1,0:T(8,128)(2,1)}), bf16[32,152,128]{2,1,0:T(8,128)(2,1)S(1)}, u32[]{:S(2)}, u32[]{:S(2)}) async-start(bf16[32,152,128]{2,1,0:T(8,128)(2,1)} %deal.1), calls=%async_computation | async-start | bytes 2490368 | tf_op jit(solution)/shard_map/all_to_all | solution.py:613
  20.0 0.1 pad.21.clone
  20.1 1.0 %collective-permute-done.2 = f32[128,128]{1,0:T(8,128)S(1)} collective-permute-done((f32[128,128]{1,0:T(8,128)S(1)}, f32[128,128]{1,0:T(8,128)S(1)}, u32[]{:S(2)}, u32[]{:S(2)}) %collective-permute-start.2) | collective-permute-done | bytes 65568 | tf_op jit(solution)/shard_map/ppermute | solution.py:581
  21.1 0.0 collective-permute-done
  21.1 2.5 %collective-permute-start.5 = (f32[128,128]{1,0:T(8,128)S(1)}, f32[128,128]{1,0:T(8,128)S(1)}, u32[]{:S(2)}, u32[]{:S(2)}) collective-permute-start(f32[128,128]{1,0:T(8,128)S(1)} %fusion.1), channel_id=1, source_target_pairs={{2,0},{3,1},{4,2},{5,3},{6,4},{7,5},{0,6},{1,7},{10,8},{11,9},{12,... | collective-permute-start | bytes 196616 | tf_op jit(solution)/shard_map/ppermute | solution.py:581
  23.7 0.1 fusion.3
  23.7 0.1 select_maximum_fusion
  23.8 0.1 collective-permute-start.4
  23.9 0.5 collective-permute-start.3
  24.4 0.1 add_convert_fusion.ends_ref
  24.5 8.3 %collective-permute-done.5 = f32[128,128]{1,0:T(8,128)S(1)} collective-permute-done((f32[128,128]{1,0:T(8,128)S(1)}, f32[128,128]{1,0:T(8,128)S(1)}, u32[]{:S(2)}, u32[]{:S(2)}) %collective-permute-start.5) | collective-permute-done | bytes 65568 | tf_op jit(solution)/shard_map/ppermute | solution.py:581
  32.8 0.8 collective-permute-done.4
  33.6 2.8 %collective-permute-done.3 = f32[184,128]{1,0:T(8,128)S(1)} collective-permute-done((f32[184,128]{1,0:T(8,128)S(1)}, f32[184,128]{1,0:T(8,128)S(1)}, u32[]{:S(2)}, u32[]{:S(2)}) %collective-permute-start.3) | collective-permute-done | bytes 94240 | tf_op jit(solution)/shard_map/ppermute | solution.py:581
  36.4 0.1 collective-permute-start.6
  36.5 0.1 slice.75
  36.6 0.1 pad_maximum_fusion.2
  36.7 0.1 copy.15
  36.8 0.1 copy.17
  36.9 0.6 pad.14.coef_ref
  37.5 5.7 %weights.1 = (f32[52,19,8,128]{3,2,1,0:T(8,128)}, f32[52,19,8,128]{3,2,1,0:T(8,128)}) custom-call(f32[64,256]{1,0:T(8,128)} %pad.14.coef_ref), custom_call_target="tpu_custom_call" | custom-call | flops 101171200 | bytes 8093696 | tf_op jit(solution)/shard_map/weights/pallas_call | solution.py:264
  43.2 0.6 add.41.gram_ref
  43.9 6.2 %factor_inverse.1.turn_ref = bf16[256,256]{1,0:T(8,128)(2,1)} custom-call(f32[128,128]{1,0:T(8,128)} %add.41.gram_ref), custom_call_target="tpu_custom_call" | custom-call | flops 10737418240 | bytes 131072 | tf_op jit(solution)/shard_map/factor_inverse/pallas_call | solution.py:205
  50.0 0.5 all-to-all-done
  50.5 0.1 fusion.2
  50.6 1.3 %collective-permute-start.8 = (bf16[10,152,128]{2,1,0:T(8,128)(2,1)S(1)}, bf16[10,152,128]{2,1,0:T(8,128)(2,1)S(1)}, u32[]{:S(2)}, u32[]{:S(2)}) collective-permute-start(bf16[10,152,128]{2,1,0:T(8,128)(2,1)S(1)} %get-tuple-element.31), channel_id=1, source_target_pairs={{8,0},{16,8},{24,16},{9,1},{17,9},{25,17},{10,2},{18,10},{26,18},{... | collective-permute-start | bytes 1167368 | tf_op jit(solution)/shard_map/ppermute | solution.py:574
  51.9 4.8 %collective-permute-start.7 = (bf16[10,152,128]{2,1,0:T(8,128)(2,1)S(1)}, bf16[10,152,128]{2,1,0:T(8,128)(2,1)S(1)}, u32[]{:S(2)}, u32[]{:S(2)}) collective-permute-start(bf16[10,152,128]{2,1,0:T(8,128)(2,1)S(1)} %get-tuple-element.32), channel_id=1, source_target_pairs={{0,8},{8,16},{16,24},{1,9},{9,17},{17,25},{2,10},{10,18},{18,26},{... | collective-permute-start | bytes 1167368 | tf_op jit(solution)/shard_map/ppermute | solution.py:567
  56.7 11.7 %inner_sweeps.1 = (f32[33,19,8,128]{3,2,1,0:T(8,128)}, f32[32,19,8,128]{3,2,1,0:T(8,128)}) custom-call(bf16[4864,128]{1,0:T(8,128)(2,1)} %bitcast.16, bf16[256,256]{1,0:T(8,128)(2,1)} %factor_inverse.1.turn_ref, f32[52,19,8,128]{3,2,1,0:T(8,128)} %get-tuple-element.27.across_hbm, f32[52,19,8,128]{3,2,1,0:T(8,128)} %get-tuple-element.28.down_hbm), custom_call_target="tpu_custom_call" | custom-call | flops 12000000000 | bytes 4980736 | tf_op jit(solution)/shard_map/inner_sweeps/pallas_call | solution.py:418
  68.4 11.2 %outer_sweeps.1 = f32[32,128]{1,0:T(8,128)} custom-call(s32[2]{0:T(128)S(1)} %add_convert_fusion.ends_ref, bf16[256,256]{1,0:T(8,128)(2,1)S(1)} %copy-done, bf16[1520,128]{1,0:T(8,128)(2,1)S(1)} %bitcast.15, bf16[1520,128]{1,0:T(8,128)(2,1)S(1)} %bitcast.14, f32[33,19,8,128]{3,2,1,0:T(8,128)} %get-tuple-element.29.first_hbm, ...), custom_call_target="tpu_custom_call" | custom-call | tf_op jit(solution)/shard_map/outer_sweeps/pallas_call | solution.py:552
  (29 shorter events, 0.2 us)
Async XLA Ops:
  0.0 7.7 %copy-start.3 = (f32[32,128]{1,0:T(8,128)S(1)}, f32[32,128]{1,0:T(8,128)}, u32[]{:S(2)}) copy-start(f32[32,128]{1,0:T(8,128)} %param.7) | copy-start | bytes 49156
  0.0 7.7 %copy-start.4 = (s32[32,128]{1,0:T(8,128)S(1)}, s32[32,128]{1,0:T(8,128)}, u32[]{:S(2)}) copy-start(s32[32,128]{1,0:T(8,128)} %param.6) | copy-start | bytes 49156
  0.0 7.8 %copy-start.1 = (bf16[4096,128]{1,0:T(8,128)(2,1)S(1)}, bf16[4096,128]{1,0:T(8,128)(2,1)}, u32[]{:S(2)}) copy-start(bf16[4096,128]{1,0:T(8,128)(2,1)} %basis_ref.1) | copy-start | bytes 3145732
  8.3 12.8 %collective-permute-start.1 = (f32[152,128]{1,0:T(8,128)S(1)}, f32[152,128]{1,0:T(8,128)S(1)}, u32[]{:S(2)}, u32[]{:S(2)}) collective-permute-start(f32[152,128]{1,0:T(8,128)S(1)} %pad_maximum_fusion.1), channel_id=1, source_target_pairs={{8,0},{16,8},{24,16},{0,24},{9,1},{17,9},{25,17},{1,25},{10,2},{18... | collective-permute-start | bytes 233480 | tf_op jit(solution)/shard_map/ppermute | solution.py:581
  13.4 7.7 %collective-permute-start = (f32[152,128]{1,0:T(8,128)S(1)}, f32[152,128]{1,0:T(8,128)S(1)}, u32[]{:S(2)}, u32[]{:S(2)}) collective-permute-start(f32[152,128]{1,0:T(8,128)S(1)} %pad_maximum_fusion.1), channel_id=1, source_target_pairs={{24,0},{0,8},{8,16},{16,24},{25,1},{1,9},{9,17},{17,25},{26,2},{2,... | collective-permute-start | bytes 233480 | tf_op jit(solution)/shard_map/ppermute | solution.py:581
  13.4 7.7 %collective-permute-start.2 = (f32[128,128]{1,0:T(8,128)S(1)}, f32[128,128]{1,0:T(8,128)S(1)}, u32[]{:S(2)}, u32[]{:S(2)}) collective-permute-start(f32[128,128]{1,0:T(8,128)S(1)} %fusion.5), channel_id=1, source_target_pairs={{16,0},{24,8},{0,16},{8,24},{17,1},{25,9},{1,17},{9,25},{18,2},{26... | collective-permute-start | bytes 196616 | tf_op jit(solution)/shard_map/ppermute | solution.py:581
  14.4 36.1 %all-to-all-start = ((bf16[32,152,128]{2,1,0:T(8,128)(2,1)}), bf16[32,152,128]{2,1,0:T(8,128)(2,1)S(1)}, u32[]{:S(2)}, u32[]{:S(2)}) async-start(bf16[32,152,128]{2,1,0:T(8,128)(2,1)} %deal.1), calls=%async_computation | async-start | bytes 2490368 | tf_op jit(solution)/shard_map/all_to_all | solution.py:613
  21.1 11.7 %collective-permute-start.5 = (f32[128,128]{1,0:T(8,128)S(1)}, f32[128,128]{1,0:T(8,128)S(1)}, u32[]{:S(2)}, u32[]{:S(2)}) collective-permute-start(f32[128,128]{1,0:T(8,128)S(1)} %fusion.1), channel_id=1, source_target_pairs={{2,0},{3,1},{4,2},{5,3},{6,4},{7,5},{0,6},{1,7},{10,8},{11,9},{12,... | collective-permute-start | bytes 196616 | tf_op jit(solution)/shard_map/ppermute | solution.py:581
  23.8 9.7 %collective-permute-start.4 = (f32[184,128]{1,0:T(8,128)S(1)}, f32[184,128]{1,0:T(8,128)S(1)}, u32[]{:S(2)}, u32[]{:S(2)}) collective-permute-start(f32[184,128]{1,0:T(8,128)S(1)} %pad_maximum_fusion), channel_id=1, source_target_pairs={{1,0},{2,1},{3,2},{4,3},{5,4},{6,5},{7,6},{0,7},{9,8},{10,9},{11,1... | collective-permute-start | bytes 282632 | tf_op jit(solution)/shard_map/ppermute | solution.py:581
  23.9 12.5 %collective-permute-start.3 = (f32[184,128]{1,0:T(8,128)S(1)}, f32[184,128]{1,0:T(8,128)S(1)}, u32[]{:S(2)}, u32[]{:S(2)}) collective-permute-start(f32[184,128]{1,0:T(8,128)S(1)} %pad_maximum_fusion), channel_id=1, source_target_pairs={{7,0},{0,1},{1,2},{2,3},{3,4},{4,5},{5,6},{6,7},{15,8},{8,9},{9,10... | collective-permute-start | bytes 282632 | tf_op jit(solution)/shard_map/ppermute | solution.py:581
  36.4 6.8 %collective-permute-start.6 = (f32[128,128]{1,0:T(8,128)S(1)}, f32[128,128]{1,0:T(8,128)S(1)}, u32[]{:S(2)}, u32[]{:S(2)}) collective-permute-start(f32[128,128]{1,0:T(8,128)S(1)} %fusion), channel_id=1, source_target_pairs={{4,0},{5,1},{6,2},{7,3},{0,4},{1,5},{2,6},{3,7},{12,8},{13,9},{14,... | collective-permute-start | bytes 196616 | tf_op jit(solution)/shard_map/ppermute | solution.py:581
  50.5 6.1 %copy-start.2 = (bf16[32,152,128]{2,1,0:T(8,128)(2,1)}, bf16[32,152,128]{2,1,0:T(8,128)(2,1)S(1)}, u32[]{:S(2)}) copy-start(bf16[32,152,128]{2,1,0:T(8,128)(2,1)S(1)} %all-to-all-done) | copy-start | bytes 3735556
  50.6 17.8 %collective-permute-start.8 = (bf16[10,152,128]{2,1,0:T(8,128)(2,1)S(1)}, bf16[10,152,128]{2,1,0:T(8,128)(2,1)S(1)}, u32[]{:S(2)}, u32[]{:S(2)}) collective-permute-start(bf16[10,152,128]{2,1,0:T(8,128)(2,1)S(1)} %get-tuple-element.31), channel_id=1, source_target_pairs={{8,0},{16,8},{24,16},{9,1},{17,9},{25,17},{10,2},{18,10},{26,18},{... | collective-permute-start | bytes 1167368 | tf_op jit(solution)/shard_map/ppermute | solution.py:574
  51.9 16.5 %collective-permute-start.7 = (bf16[10,152,128]{2,1,0:T(8,128)(2,1)S(1)}, bf16[10,152,128]{2,1,0:T(8,128)(2,1)S(1)}, u32[]{:S(2)}, u32[]{:S(2)}) collective-permute-start(bf16[10,152,128]{2,1,0:T(8,128)(2,1)S(1)} %get-tuple-element.32), channel_id=1, source_target_pairs={{0,8},{8,16},{16,24},{1,9},{9,17},{17,25},{2,10},{10,18},{18,26},{... | collective-permute-start | bytes 1167368 | tf_op jit(solution)/shard_map/ppermute | solution.py:567
  56.7 11.7 %copy-start = (bf16[256,256]{1,0:T(8,128)(2,1)S(1)}, bf16[256,256]{1,0:T(8,128)(2,1)}, u32[]{:S(2)}) copy-start(bf16[256,256]{1,0:T(8,128)(2,1)} %factor_inverse.1.turn_ref) | copy-start | bytes 393220
